TPU v7x, 32 devices: a whole 2x2x4 slice. The times are simulated.
32 devices in a mesh: dp: 4 (over y, x), tensor: 8 (over z, core).
Axes of the slice: x: 2, y: 2, z: 4, core: 2. Of those that a mesh axis runs over, the one named last changes fastest.
Arguments:
- hidden_in: bfloat16 [256, 1024], P(('dp', 'tensor')), parts along dimension 0, may hold values from -50 to 50
- expert_ids: int32 [256, 2], P(('dp', 'tensor')), parts along dimension 0, may hold values from 0 to 1, all different within a row; in each aligned block of 8 rows (0 to 7, 8 to 15, ...) at most 8 rows name the same one
- gate_weights: float32 [256, 2], P(('dp', 'tensor')), parts along dimension 0, may hold values from 0.05 to 0.5
- targets: int32 [256], P('dp'), parts along dimension 0, may hold values from 0 to 4095
- seq_ids: int32 [256], P('dp'), parts along dimension 0, may hold values from 0 to 15, never falling along the last dimension, each value on 1 to 16 neighbouring positions
- moe_gain: float32 [1024], replicated, may hold values from 0.5 to 1.5
- w_gate: bfloat16 [1024, 2816], P(None, 'tensor'), may hold values from -0.1875 to 0.1875
- w_up: bfloat16 [1024, 2816], P(None, 'tensor'), may hold values from -0.1875 to 0.1875
- w_down: bfloat16 [2816, 1024], P('tensor'), may hold values from -0.15625 to 0.15625
- final_gain: float32 [1024], replicated, may hold values from 0.5 to 1.5
- head_weight: bfloat16 [1024, 4096], P(None, 'tensor'), may hold values from -66.498 to 66.498
- adapter_down: bfloat16 [1024, 64], replicated, may hold values from -0.1875 to 0.1875
- adapter_up: bfloat16 [64, 4096], P(None, 'tensor'), may hold values from -0.75 to 0.75
Outputs:
- policy_logp: float32 [256], P(('dp', 'tensor')), parts along dimension 0
- log_ratio: float32 [256], P(('dp', 'tensor')), parts along dimension 0
- seq_sums: float32 [64], P('dp'), parts along dimension 0
There are 4 independent parts, one for each index of `dp`. A program takes and returns all parts, laid end to end along the dimension named above; an argument that names none is the same for every part. Nothing has to cross between parts.
Inputs may be any that keep to these rules, and one draw needn't show every extreme that they name: `expert_ids`: in the 8 rows of one device no expert is named more than 8 times, a bound that some block reaches; each row names 2 different experts. `seq_ids`: ids never fall along the tokens; a rollout has 1 to 16 tokens, one exactly 16.
All inputs are finite; a program needn't handle non-finite values.
Results may differ from a plain program's by a relative error of at most 0.011.
Values may be sent and summed in bfloat16 or wider, within the bound.
No kernel may reach another device: no remote copies, remote signals or barrier semaphores. Data moves between devices by JAX's collectives and lax.ppermute only.
A program may use at most 64 MiB of HBM per device.

v0:
```python
import jax
import jax.numpy as jnp
from jax import lax
from jax.sharding import PartitionSpec as P

SPLIT = 4
SEQS = 16


epsilon = 1e-06


def rms_norm(values, norm_gain):
    mean_sq = jnp.mean(values * values, axis=-1, keepdims=True)
    return values * lax.rsqrt(mean_sq + epsilon) * norm_gain


def expert_piece(arrived, w_gate, w_up, w_down):
    features = arrived.shape[-1]
    flat_rows = arrived.reshape(-1, features)
    gate_proj = jnp.dot(flat_rows, w_gate, preferred_element_type=jnp.float32)
    up_proj = jnp.dot(flat_rows, w_up, preferred_element_type=jnp.float32)
    inner_act = (jax.nn.silu(gate_proj) * up_proj).astype(jnp.bfloat16)
    partial_value = jnp.dot(inner_act, w_down, preferred_element_type=jnp.float32)
    return lax.all_to_all(
        partial_value.reshape(arrived.shape), "tensor", split_axis=0, concat_axis=0, tiled=True
    )


def on_device(
    hidden_in,
    expert_ids,
    gate_weights,
    targets,
    seq_ids,
    moe_gain,
    w_gate,
    w_up,
    w_down,
    final_gain,
    head_weight,
    adapter_down,
    adapter_up,
):
    tok_rows, features = hidden_in.shape
    top_count = expert_ids.shape[1]
    devices = lax.axis_size("tensor")
    experts = devices // SPLIT
    capacity = min(tok_rows, 2 * tok_rows * top_count // experts)
    my_index = lax.axis_index("tensor")
    moe_input = rms_norm(hidden_in.astype(jnp.float32), moe_gain).astype(jnp.bfloat16)
    flat_ids = expert_ids.reshape(-1)
    chosen_hot = (flat_ids[:, None] == jnp.arange(experts, dtype=jnp.int32)[None, :]).astype(
        jnp.int32
    )
    slot_pos = jnp.sum((jnp.cumsum(chosen_hot, axis=0) - chosen_hot) * chosen_hot, axis=1)
    target_slot = flat_ids * capacity + slot_pos
    placed = (
        target_slot[:, None] == jnp.arange(experts * capacity, dtype=jnp.int32)[None, :]
    ).reshape(tok_rows, top_count, experts * capacity)
    spread = jnp.any(placed, axis=1).astype(jnp.bfloat16)
    packed = lax.dot_general(
        spread, moe_input, (((0,), (0,)), ((), ())), preferred_element_type=jnp.float32
    ).astype(jnp.bfloat16)
    outgoing = jnp.broadcast_to(
        packed.reshape(experts, 1, capacity, features), (experts, SPLIT, capacity, features)
    ).reshape(devices, capacity, features)
    returned = expert_piece(
        lax.all_to_all(outgoing, "tensor", split_axis=0, concat_axis=0, tiled=True),
        w_gate,
        w_up,
        w_down,
    )
    summed = jnp.sum(returned.reshape(experts, SPLIT, capacity, features), axis=1).reshape(
        experts * capacity, features
    )
    mixing = jnp.sum(placed.astype(jnp.float32) * gate_weights[:, :, None], axis=1)
    residual_sum = hidden_in.astype(jnp.float32) + jnp.dot(
        mixing, summed, precision=lax.Precision.HIGHEST
    )
    final_input = rms_norm(residual_sum, final_gain).astype(jnp.bfloat16)
    vocab_dev = head_weight.shape[1]
    vocab_start = my_index * vocab_dev
    columns = jnp.arange(vocab_dev, dtype=jnp.int32)

    def summary(block_rows, block_latent, row_start):
        row_count = block_rows.shape[0]
        base_logits = jnp.dot(block_rows, head_weight, preferred_element_type=jnp.float32)
        policy_logits = base_logits + jnp.dot(
            block_latent, adapter_up, preferred_element_type=jnp.float32
        )
        wanted = lax.dynamic_slice_in_dim(targets, row_start, row_count) - vocab_start
        is_target = wanted[:, None] == columns[None, :]

        def reduce_logits(logits):
            top_value = jnp.max(logits, axis=1)
            exp_total = jnp.sum(jnp.exp(logits - top_value[:, None]), axis=1)
            picked = jnp.sum(jnp.where(is_target, logits, 0.0), axis=1)
            return (top_value, exp_total, picked)

        base_stats = reduce_logits(base_logits)
        policy_stats = reduce_logits(policy_logits)
        return tuple(
            (
                jnp.stack([earlier, later], axis=1)
                for earlier, later in zip(base_stats, policy_stats)
            )
        )

    def blocked(shard_rows, shard_latent, row_start):
        row_count = shard_rows.shape[0]
        block_size = 512 if row_count % 512 == 0 else row_count
        if block_size == row_count:
            return summary(shard_rows, shard_latent, row_start)

        def one_block(block_index):
            offset = block_index * block_size
            return summary(
                lax.dynamic_slice_in_dim(shard_rows, offset, block_size),
                lax.dynamic_slice_in_dim(shard_latent, offset, block_size),
                row_start + offset,
            )

        results = lax.map(one_block, jnp.arange(row_count // block_size, dtype=jnp.int32))
        return tuple((member.reshape(row_count, 2) for member in results))

    shard_rows = lax.all_gather(final_input, "tensor", axis=0, tiled=True)
    shard_latent = jnp.dot(shard_rows, adapter_down, preferred_element_type=jnp.float32).astype(
        jnp.bfloat16
    )
    block_stats = blocked(shard_rows, shard_latent, jnp.int32(0))
    maxima, exp_sums, target_logits = tuple((update for update in block_stats))
    ceiling = lax.pmax(maxima, "tensor")
    totals, picked_all = lax.psum((exp_sums * jnp.exp(maxima - ceiling), target_logits), "tensor")
    log_probs = picked_all - ceiling - jnp.log(totals)
    log_ratio = log_probs[:, 1] - log_probs[:, 0]
    seq_match = (seq_ids[None, :] == jnp.arange(SEQS, dtype=jnp.int32)[:, None]).astype(jnp.float32)
    seq_sums = jnp.dot(seq_match, log_ratio, precision=lax.Precision.HIGHEST)
    own_start = my_index * tok_rows
    policy_own = lax.dynamic_slice_in_dim(log_probs[:, 1], own_start, tok_rows)
    ratio_own = lax.dynamic_slice_in_dim(log_ratio, own_start, tok_rows)
    return (policy_own, ratio_own, seq_sums)


def solution(mesh):
    in_specs = (
        P(("dp", "tensor"), None),
        P(("dp", "tensor"), None),
        P(("dp", "tensor"), None),
        P("dp"),
        P("dp"),
        P(),
        P(None, "tensor"),
        P(None, "tensor"),
        P("tensor", None),
        P(),
        P(None, "tensor"),
        P(),
        P(None, "tensor"),
    )
    out_specs = (P(("dp", "tensor")), P(("dp", "tensor")), P("dp"))
    return jax.shard_map(
        on_device, mesh=mesh, in_specs=in_specs, out_specs=out_specs, check_vma=False
    )
```

profile of v0, /device:TPU:0, one launch (start us, length us, event | category | flops | bytes accessed | tf_op | source)
XLA Modules:
  0.0 79.1 jit_solution(5441512315769319230)
XLA Ops:
  0.6 0.8 %copy.22 = s32[8,2]{1,0:T(8,128)S(1)} copy(s32[8,2]{0,1:T(2,128)} %param.14) | data formatting | bytes 128 | tf_op args[1]
  1.5 0.1 eq.58
  1.6 0.1 fusion.20
  1.7 0.2 select_reduce_fusion.3
  1.9 0.1 reduce_sum.84
  2.0 0.1 copy.24
  2.0 0.1 fusion.19
  2.1 0.3 copy-done.4
  2.4 0.1 fusion.13
  2.6 0.5 copy-done.8
  3.1 0.2 fusion.1
  3.3 12.9 %all_to_all.10 = bf16[8,8,1024]{2,1,0:T(8,128)(2,1)S(1)} all-to-all(bf16[8,8,1024]{2,1,0:T(8,128)(2,1)S(1)} %bitcast.42), channel_id=1, replica_groups=mesh['dp'=4,'tensor'=8] {'tensor'}, dimensions={0} | all-to-all | bytes 262144 | tf_op jit(solution)/shard_map/all_to_all | solution.py:69
  16.2 1.4 %fusion.4 = f32[64,352]{1,0:T(8,128)S(1)} fusion(bf16[1024,352]{0,1:T(8,128)(2,1)} %param.19, bf16[8,8,1024]{2,1,0:T(8,128)(2,1)S(1)} %all_to_all.10), kind=kOutput, calls=%fused_computation.11 | convolution fusion | flops 46137344 | bytes 942080 | tf_op jit(solution)/shard_map/dot_general | solution.py:21
  17.7 1.4 %convolution_bitcast_fusion = f32[8,8,1024]{2,1,0:T(8,128)} fusion(bf16[352,1024]{1,0:T(8,128)(2,1)S(1)} %copy-done.1, bf16[1024,352]{0,1:T(8,128)(2,1)S(1)} %copy-done.2, bf16[8,8,1024]{2,1,0:T(8,128)(2,1)S(1)} %all_to_all.10, f32[64,352]{1,0:T(8,128)S(1)} %fusion.4), kind=kOutput, calls=%fused_computation | convolution fusion | flops 92409856 | bytes 1925120 | tf_op jit(solution)/shard_map/dot_general | solution.py:24
  19.1 3.4 %all-to-all-start.1 = ((f32[8,8,1024]{2,1,0:T(8,128)}), f32[8,8,1024]{2,1,0:T(8,128)S(1)}, u32[]{:S(2)}, u32[]{:S(2)}) async-start(f32[8,8,1024]{2,1,0:T(8,128)} %convolution_bitcast_fusion), calls=%async_computation.1 | async-start | bytes 524288 | tf_op jit(solution)/shard_map/all_to_all | solution.py:25
  22.5 0.7 copy-done.7
  23.2 0.1 select_reduce_fusion.2
  23.3 0.6 copy-done.9
  23.8 8.3 %all-to-all-done.1 = f32[8,8,1024]{2,1,0:T(8,128)S(1)} async-done(((f32[8,8,1024]{2,1,0:T(8,128)}), f32[8,8,1024]{2,1,0:T(8,128)S(1)}, u32[]{:S(2)}, u32[]{:S(2)}) %all-to-all-start.1) | async-done | bytes 262176 | tf_op jit(solution)/shard_map/all_to_all | solution.py:25
  32.2 0.3 multiply_reduce_fusion
  32.5 0.7 copy-done.6
  33.2 0.1 multiply_convert_fusion
  33.2 13.9 %all_gather.3 = bf16[64,1024]{1,0:T(8,128)(2,1)S(1)} all-gather(bf16[8,1024]{1,0:T(8,128)(2,1)S(1)} %multiply_convert_fusion), channel_id=1, replica_groups=mesh['dp'=4,'tensor'=8] {'tensor'}, dimensions={0}, use_global_device_ids=true | all-gather | bytes 147456 | tf_op jit(solution)/shard_map/all_gather | solution.py:127
  47.2 0.4 fusion.23
  47.6 0.5 copy-done.3
  48.1 0.4 fusion.24
  48.5 14.8 %pmax.7 = f32[64,2]{0,1:T(2,128)S(1)} all-reduce(f32[64,2]{0,1:T(2,128)S(1)} %pad_maximum_fusion.1), channel_id=1, replica_groups=mesh['dp'=4,'tensor'=8] {'tensor'}, use_global_device_ids=true, to_apply=%region_12.13 | all-reduce | flops 128 | bytes 1024 | tf_op jit(solution)/shard_map/pmax | solution.py:133
  63.3 0.3 select_reduce_fusion.1
  63.6 13.6 %all-reduce = (f32[64,2]{0,1:T(2,128)S(1)}, f32[64,2]{0,1:T(2,128)S(1)}) all-reduce(f32[64,2]{0,1:T(2,128)S(1)} %maximum_multiply_fusion, f32[64,2]{0,1:T(2,128)S(1)} %pad_maximum_fusion), channel_id=1, replica_groups=mesh['dp'=4,'tensor'=8] {'tensor'}, use_global_device_ids=true, to_apply=%region_15.16 | all-reduce | flops 256 | bytes 2048 | tf_op jit(solution)/shard_map/psum | solution.py:134
  77.2 0.7 copy-done.10
  77.9 0.6 convolution_bitcast_fusion.1
  78.5 0.6 dynamic-slice_bitcast_fusion
  (27 shorter events, 0.2 us)
Async XLA Ops:
  0.6 46.5 %copy-start = (bf16[1024,512]{1,0:T(8,128)(2,1)S(1)}, bf16[1024,512]{1,0:T(8,128)(2,1)}, u32[]{:S(2)}) copy-start(bf16[1024,512]{1,0:T(8,128)(2,1)} %param.23) | copy-start | bytes 3145732
  1.7 0.7 copy-start.4
  2.4 0.7 copy-start.8
  2.5 15.1 %copy-start.1 = (bf16[352,1024]{1,0:T(8,128)(2,1)S(1)}, bf16[352,1024]{1,0:T(8,128)(2,1)}, u32[]{:S(2)}) copy-start(bf16[352,1024]{1,0:T(8,128)(2,1)} %param.21) | copy-start | bytes 2162692
  2.5 15.2 %copy-start.2 = (bf16[1024,352]{0,1:T(8,128)(2,1)S(1)}, bf16[1024,352]{0,1:T(8,128)(2,1)}, u32[]{:S(2)}) copy-start(bf16[1024,352]{0,1:T(8,128)(2,1)} %param.20) | copy-start | bytes 2162692
  19.1 13.1 %all-to-all-start.1 = ((f32[8,8,1024]{2,1,0:T(8,128)}), f32[8,8,1024]{2,1,0:T(8,128)S(1)}, u32[]{:S(2)}, u32[]{:S(2)}) async-start(f32[8,8,1024]{2,1,0:T(8,128)} %convolution_bitcast_fusion), calls=%async_computation.1 | async-start | bytes 524288 | tf_op jit(solution)/shard_map/all_to_all | solution.py:25
  22.5 0.7 copy-start.7
  23.2 0.7 copy-start.9
  32.5 0.7 copy-start.6
  47.2 0.9 %copy-start.3 = (bf16[1024,64]{0,1:T(8,128)(2,1)S(1)}, bf16[1024,64]{0,1:T(8,128)(2,1)}, u32[]{:S(2)}) copy-start(bf16[1024,64]{0,1:T(8,128)(2,1)} %param.24) | copy-start | bytes 393220
  47.2 0.9 %copy-start.5 = (bf16[64,512]{1,0:T(8,128)(2,1)S(1)}, bf16[64,512]{1,0:T(8,128)(2,1)}, u32[]{:S(2)}) copy-start(bf16[64,512]{1,0:T(8,128)(2,1)} %param.25) | copy-start | bytes 196612
  77.2 0.7 copy-start.10
where the time goes:
time: 79.6 us; the launch traced here: 79.1 us
  blocking collectives  55.2 us (69%)
  waiting for transfers between devices  8.32 us (10%)
  local copies, waits for them, and re-layouts  5.63 us (7%)
  matrix products  4.76 us (6%)
  starting transfers between devices  3.41 us (4%)
  other arithmetic  0.98 us (1%)
    pmax x1, blocking collectives, on_device(): ceiling = lax.pmax(maxima, 'tensor')  14.8 us
    all_gather x1, blocking collectives, on_device(): shard_rows = lax.all_gather(final_input, 'tensor', axis=0, tiled=True)  13.9 us
    psum x1, blocking collectives, on_device(): lax.psum((exp_sums * jnp.exp(maxima - ceiling), target_logits), 'tensor')  13.6 us
    all_to_all x1, blocking collectives, on_device(): lax.all_to_all(outgoing, 'tensor', split_axis=0, concat_axis=0, tiled=True)  12.9 us
    all_to_all x1, waiting for transfers between devices, expert_piece(): lax.all_to_all(partial_value.reshape(arrived.shape), 'tensor', split_axis...  8.32 us
    unnamed x23, local copies, waits for them, and re-layouts  4.78 us
    all_to_all x1, starting transfers between devices, expert_piece(): lax.all_to_all(partial_value.reshape(arrived.shape), 'tensor', split_axis...  3.41 us
  transfers between devices with their start and end apart: 1, of which 1 were waited for; matrix products, arithmetic and copies ran while one was open for 0% of the time, Pallas kernels for 0%

commit v1 on v0

--- a/solution.py
+++ b/solution.py
@@ -1,5 +1,6 @@
 import jax
 import jax.numpy as jnp
+import numpy as np
 from jax import lax
 from jax.sharding import PartitionSpec as P
 
@@ -27,7 +28,7 @@
     )
 
 
-def on_device(
+def routed_on_device(
     hidden_in,
     expert_ids,
     gate_weights,
@@ -142,6 +143,122 @@
     return (policy_own, ratio_own, seq_sums)
 
 
+def exchange(values, mask):
+    devices = lax.axis_size("tensor")
+    return lax.ppermute(values, "tensor", [(i, i ^ mask) for i in range(devices)])
+
+
+def bit(number, place):
+    return (number >> place) & 1
+
+
+def in_order(late, mine, other):
+    return jnp.concatenate([jnp.where(late, other, mine), jnp.where(late, mine, other)], axis=0)
+
+
+def thirds(values):
+    high = lax.reduce_precision(values, 8, 7)
+    middle = lax.reduce_precision(values - high, 8, 7)
+    low = values - high - middle
+    return [part.astype(jnp.bfloat16) for part in (high, middle, low)]
+
+
+def dense_on_device(
+    hidden_in,
+    expert_ids,
+    gate_weights,
+    targets,
+    seq_ids,
+    moe_gain,
+    w_gate,
+    w_up,
+    w_down,
+    final_gain,
+    head_weight,
+    adapter_down,
+    adapter_up,
+):
+    tok_rows, features = hidden_in.shape
+    devices = lax.axis_size("tensor")
+    bits = devices.bit_length() - 1
+    experts = devices // SPLIT
+    lanes = -(-3 * experts // 128) * 128
+    my_index = lax.axis_index("tensor")
+    far = [(b, (1 << b) + 1) for b in range(bits - 1, 0, -1)]
+    parity = sum(bit(my_index, b) for b in range(bits)) & 1
+    ranks = sorted(
+        range(devices), key=lambda i: [i.bit_count() & 1] + [bit(i, b) for b in range(1, bits)]
+    )
+    token_at = np.array([i * tok_rows + r for i in ranks for r in range(tok_rows)])
+    place_of = np.argsort(token_at)
+
+    expert_of = jnp.arange(experts, dtype=jnp.int32)
+    mixing = jnp.sum(
+        jnp.where(expert_ids[:, :, None] == expert_of, gate_weights[:, :, None], 0.0), axis=1
+    )
+    columns = thirds(mixing)
+    gap = jnp.zeros((tok_rows, lanes - 3 * experts), jnp.bfloat16)
+    rows = jnp.concatenate([hidden_in, *columns, gap], axis=1)
+    for b, mask in far:
+        rows = in_order(bit(my_index, b) == 1, rows, exchange(rows, mask))
+    rows = in_order(parity == 1, rows, exchange(rows, 1))
+
+    hidden = rows[:, :features].astype(jnp.float32)
+    moe_input = rms_norm(hidden, moe_gain).astype(jnp.bfloat16)
+    weights = rows[:, features : features + 3 * experts].astype(jnp.float32)
+    weights = weights.reshape(-1, 3, experts)
+    weights = weights[:, 0] + weights[:, 1] + weights[:, 2]
+    my_weight = jnp.sum(jnp.where(expert_of == my_index // SPLIT, weights, 0.0), axis=1)
+    gate_proj = jnp.dot(moe_input, w_gate, preferred_element_type=jnp.float32)
+    up_proj = jnp.dot(moe_input, w_up, preferred_element_type=jnp.float32)
+    inner_act = (jax.nn.silu(gate_proj) * up_proj).astype(jnp.bfloat16)
+    partial_value = jnp.dot(inner_act, w_down, preferred_element_type=jnp.float32)
+    partial_value = partial_value * my_weight[:, None]
+
+    half = rows.shape[0] // 2
+    late = parity == 1
+    first, second = partial_value[:half], partial_value[half:]
+    total = jnp.where(late, second, first) + exchange(jnp.where(late, first, second), 1)
+    for b, mask in far[::-1]:
+        total = total + exchange(total.astype(jnp.bfloat16), mask).astype(jnp.float32)
+    mixed = total + jnp.where(late, hidden[half:], hidden[:half])
+    own_final = rms_norm(mixed, final_gain).astype(jnp.bfloat16)
+    final_input = in_order(late, own_final, exchange(own_final, 1))
+
+    latent = jnp.dot(final_input, adapter_down, preferred_element_type=jnp.float32).astype(
+        jnp.bfloat16
+    )
+    base_logits = jnp.dot(final_input, head_weight, preferred_element_type=jnp.float32)
+    policy_logits = base_logits + jnp.dot(latent, adapter_up, preferred_element_type=jnp.float32)
+    vocab_dev = head_weight.shape[1]
+    wanted = targets[token_at] - my_index * vocab_dev
+    is_target = wanted[:, None] == jnp.arange(vocab_dev, dtype=jnp.int32)[None, :]
+
+    def summary(logits):
+        top_value = jnp.max(logits, axis=1)
+        exp_total = jnp.sum(jnp.exp(logits - top_value[:, None]), axis=1)
+        picked = jnp.sum(jnp.where(is_target, logits, 0.0), axis=1)
+        return jnp.stack([top_value, exp_total, picked])
+
+    stats = jnp.stack([summary(base_logits), summary(policy_logits)])
+    for mask in [1] + [mask for _, mask in far]:
+        other = exchange(stats, mask)
+        ceiling = jnp.maximum(stats[:, 0], other[:, 0])
+        exp_total = stats[:, 1] * jnp.exp(stats[:, 0] - ceiling) + other[:, 1] * jnp.exp(
+            other[:, 0] - ceiling
+        )
+        stats = jnp.stack([ceiling, exp_total, stats[:, 2] + other[:, 2]], axis=1)
+    log_probs = stats[:, 2] - stats[:, 0] - jnp.log(stats[:, 1])
+    log_probs = log_probs[:, place_of]
+    log_ratio = log_probs[1] - log_probs[0]
+    seq_match = (seq_ids[None, :] == jnp.arange(SEQS, dtype=jnp.int32)[:, None]).astype(jnp.float32)
+    seq_sums = jnp.sum(seq_match * log_ratio[None, :], axis=1)
+    own_start = my_index * tok_rows
+    policy_own = lax.dynamic_slice_in_dim(log_probs[1], own_start, tok_rows)
+    ratio_own = lax.dynamic_slice_in_dim(log_ratio, own_start, tok_rows)
+    return (policy_own, ratio_own, seq_sums)
+
+
 def solution(mesh):
     in_specs = (
         P(("dp", "tensor"), None),
@@ -159,6 +276,13 @@
         P(None, "tensor"),
     )
     out_specs = (P(("dp", "tensor")), P(("dp", "tensor")), P("dp"))
+    devices = mesh.shape["tensor"]
+
+    def on_device(hidden_in, expert_ids, *others):
+        every_expert = expert_ids.shape[1] == devices // SPLIT
+        step = dense_on_device if every_expert else routed_on_device
+        return step(hidden_in, expert_ids, *others)
+
     return jax.shard_map(
         on_device, mesh=mesh, in_specs=in_specs, out_specs=out_specs, check_vma=False
     )

time: 79.6 us -> 59.7 us (0.75)
  blocking collectives: 55.2 us -> 0 us
  waiting for transfers between devices: 8.32 us -> 31.1 us
  starting transfers between devices: 3.41 us -> 13.5 us
  other arithmetic: 0.98 us -> 3.73 us
    ppermute x0 -> x10, waiting for transfers between devices: none -> 31.1 us  [exchange(): lax.ppermute(values, 'tensor', [(i, i ^ mask) for i in range(devices)])]
    pmax x1 -> x0, blocking collectives: 14.8 us -> none  [on_device(): ceiling = lax.pmax(maxima, 'tensor')]
    all_gather x1 -> x0, blocking collectives: 13.9 us -> none  [on_device(): shard_rows = lax.all_gather(final_input, 'tensor', axis=0, tiled=True)]
    psum x1 -> x0, blocking collectives: 13.6 us -> none  [on_device(): lax.psum((exp_sums * jnp.exp(maxima - ceiling), target_logits), 'tensor')]
    ppermute x0 -> x10, starting transfers between devices: none -> 13.5 us  [exchange(): lax.ppermute(values, 'tensor', [(i, i ^ mask) for i in range(devices)])]
    all_to_all x1 -> x0, blocking collectives: 12.9 us -> none  [on_device(): lax.all_to_all(outgoing, 'tensor', split_axis=0, concat_axis=0, tiled=True)]
    all_to_all x1 -> x0, waiting for transfers between devices: 8.32 us -> none  [expert_piece(): lax.all_to_all(partial_value.reshape(arrived.shape), 'tensor', split_axis...]
    all_to_all x1 -> x0, starting transfers between devices: 3.41 us -> none  [expert_piece(): lax.all_to_all(partial_value.reshape(arrived.shape), 'tensor', split_axis...]
  transfers between devices with their start and end apart: 1 -> 10, of which waited for: 1 -> 10; matrix products, arithmetic and copies ran while one was open for 0% -> 2% of each run, Pallas kernels for 0% -> 0%
where the time goes in v1:
time: 59.7 us; the launch traced here: 59.4 us
  waiting for transfers between devices  31.1 us (52%)
  starting transfers between devices  13.5 us (23%)
  local copies, waits for them, and re-layouts  6.18 us (10%)
  matrix products  4 us (7%)
  other arithmetic  3.73 us (6%)
  between operations  0.86 us (1%)
    ppermute x10, waiting for transfers between devices, exchange(): lax.ppermute(values, 'tensor', [(i, i ^ mask) for i in range(devices)])  31.1 us
    ppermute x10, starting transfers between devices, exchange(): lax.ppermute(values, 'tensor', [(i, i ^ mask) for i in range(devices)])  13.5 us
    unnamed x24, local copies, waits for them, and re-layouts  2.83 us
    dot_general x1, matrix products, dense_on_device(): jnp.dot(inner_act, w_down, preferred_element_type=jnp.float32)  2.23 us
  transfers between devices with their start and end apart: 10, of which 10 were waited for; matrix products, arithmetic and copies ran while one was open for 2% of the time, Pallas kernels for 0%

profile of v1, /device:TPU:0, one launch (start us, length us, event | category | flops | bytes accessed | tf_op | source)
XLA Modules:
  0.0 59.4 jit_solution(7225505123137140596)
XLA Ops:
  0.7 0.8 %fusion.12 = f32[8,2]{0,1:T(2,128)S(1)} fusion(f32[8,2]{0,1:T(2,128)} %param.19, s32[8,2]{0,1:T(2,128)} %param.18), kind=kLoop, calls=%fused_computation.61 | loop fusion | flops 80 | bytes 192 | tf_op jit(solution)/shard_map/reduce_sum | solution.py:196
  1.9 3.5 %collective-permute-start = (bf16[8,1152]{1,0:T(8,128)(2,1)S(1)}, bf16[8,1152]{1,0:T(8,128)(2,1)S(1)}, u32[]{:S(2)}, u32[]{:S(2)}) collective-permute-start(bf16[8,1152]{1,0:T(8,128)(2,1)S(1)} %concatenate.15), channel_id=1, source_target_pairs={{0,5},{1,4},{2,7},{3,6},{4,1},{5,0},{6,3},{7,2},{8,13},{9,12},{10,... | collective-permute-start | bytes 55304 | tf_op jit(solution)/shard_map/ppermute | solution.py:148
  5.3 1.5 %collective-permute-done = bf16[8,1152]{1,0:T(8,128)(2,1)S(1)} collective-permute-done((bf16[8,1152]{1,0:T(8,128)(2,1)S(1)}, bf16[8,1152]{1,0:T(8,128)(2,1)S(1)}, u32[]{:S(2)}, u32[]{:S(2)}) %collective-permute-start) | collective-permute-done | bytes 18464 | tf_op jit(solution)/shard_map/ppermute | solution.py:148
  6.8 1.9 %collective-permute-start.1 = (bf16[16,1152]{1,0:T(8,128)(2,1)S(1)}, bf16[16,1152]{1,0:T(8,128)(2,1)S(1)}, u32[]{:S(2)}, u32[]{:S(2)}) collective-permute-start(bf16[16,1152]{1,0:T(8,128)(2,1)S(1)} %pad_maximum_fusion.5), channel_id=1, source_target_pairs={{0,3},{1,2},{2,1},{3,0},{4,7},{5,6},{6,5},{7,4},{8,11},{9,10},{10,... | collective-permute-start | bytes 110600 | tf_op jit(solution)/shard_map/ppermute | solution.py:148
  8.8 1.6 %collective-permute-done.1 = bf16[16,1152]{1,0:T(8,128)(2,1)S(1)} collective-permute-done((bf16[16,1152]{1,0:T(8,128)(2,1)S(1)}, bf16[16,1152]{1,0:T(8,128)(2,1)S(1)}, u32[]{:S(2)}, u32[]{:S(2)}) %collective-permute-start.1) | collective-permute-done | bytes 36896 | tf_op jit(solution)/shard_map/ppermute | solution.py:148
  10.7 0.6 collective-permute-start.2
  11.2 1.2 %collective-permute-done.2 = bf16[32,1152]{0,1:T(8,128)(2,1)S(1)} collective-permute-done((bf16[32,1152]{0,1:T(8,128)(2,1)S(1)}, bf16[32,1152]{0,1:T(8,128)(2,1)S(1)}, u32[]{:S(2)}, u32[]{:S(2)}) %collective-permute-start.2) | collective-permute-done | bytes 73760 | tf_op jit(solution)/shard_map/ppermute | solution.py:148
  12.9 0.7 %copy-done.10 = bf16[1024,352]{0,1:T(8,128)(2,1)S(1)} copy-done((bf16[1024,352]{0,1:T(8,128)(2,1)S(1)}, bf16[1024,352]{0,1:T(8,128)(2,1)}, u32[]{:S(2)}) %copy-start.10) | copy-done | bytes 720920
  13.6 0.7 %fusion.30 = f32[64,352]{1,0:T(8,128)S(1)} fusion(bf16[1024,352]{0,1:T(8,128)(2,1)S(1)} %copy-done.10, f32[1024]{0:T(1024)S(1)} %copy-done.7, f32[64]{0:T(128)S(1)} %add_rsqrt_fusion.1, bf16[32,1152]{0,1:T(8,128)(2,1)S(1)} %get-tuple-element.18, bf16[32,1152]{0,1:T(8,128)(2,1)S(1)} %get-tuple-element.17), kind=kOutput, calls=%fused_computation.101 | convolution fusion | flops 46596096 | bytes 962816 | tf_op jit(solution)/shard_map/dot_general | solution.py:212
  14.3 0.4 copy-done.2
  14.7 2.2 %convolution_multiply_fusion = f32[64,1024]{0,1:T(8,128)S(1)} fusion(bf16[352,1024]{1,0:T(8,128)(2,1)S(1)} %copy-done.2, bf16[1024,352]{0,1:T(8,128)(2,1)} %param.24, f32[64]{0:T(128)S(1)} %fusion.21, f32[64,352]{1,0:T(8,128)S(1)} %fusion.30, f32[1024]{0:T(1024)S(1)} %copy-done.7, f32[64]{0:T(128)S(1)} %add_rsqrt_fusion.1, ...), kind=kOutput, calls=%fused_computation.2 | convolution fusion | flops 92934144 | bytes 1946112 | tf_op jit(solution)/shard_map/dot_general | solution.py:215
  17.2 0.4 collective-permute-start.3
  17.6 1.5 %collective-permute-done.3 = f32[32,1024]{0,1:T(8,128)S(1)} collective-permute-done((f32[32,1024]{0,1:T(8,128)S(1)}, f32[32,1024]{0,1:T(8,128)S(1)}, u32[]{:S(2)}, u32[]{:S(2)}) %collective-permute-start.3) | collective-permute-done | bytes 131104 | tf_op jit(solution)/shard_map/ppermute | solution.py:148
  19.4 1.8 %collective-permute-start.4 = (bf16[32,1024]{0,1:T(8,128)(2,1)S(1)}, bf16[32,1024]{0,1:T(8,128)(2,1)S(1)}, u32[]{:S(2)}, u32[]{:S(2)}) collective-permute-start(bf16[32,1024]{0,1:T(8,128)(2,1)S(1)} %get-tuple-element.15), channel_id=1, source_target_pairs={{0,3},{1,2},{2,1},{3,0},{4,7},{5,6},{6,5},{7,4},{8,11},{9,10},{10,... | collective-permute-start | bytes 196616 | tf_op jit(solution)/shard_map/ppermute | solution.py:148
  21.2 0.8 %gather_fusion = s32[64]{0:T(128)S(1)} fusion(s32[64]{0:T(128)S(1)} %copy-done.1, s32[1024]{0:T(1024)S(1)} %pad_clamp_fusion.1), kind=kCustom, calls=%fused_computation | custom fusion | bytes 768 | tf_op jit(solution)/shard_map/gather | solution.py:234
  22.0 5.6 %collective-permute-done.4 = bf16[32,1024]{0,1:T(8,128)(2,1)S(1)} collective-permute-done((bf16[32,1024]{0,1:T(8,128)(2,1)S(1)}, bf16[32,1024]{0,1:T(8,128)(2,1)S(1)}, u32[]{:S(2)}, u32[]{:S(2)}) %collective-permute-start.4) | collective-permute-done | bytes 65568 | tf_op jit(solution)/shard_map/ppermute | solution.py:148
  27.7 3.1 %collective-permute-start.5 = (bf16[32,1024]{0,1:T(8,128)(2,1)S(1)}, bf16[32,1024]{0,1:T(8,128)(2,1)S(1)}, u32[]{:S(2)}, u32[]{:S(2)}) collective-permute-start(bf16[32,1024]{0,1:T(8,128)(2,1)S(1)} %fusion.2), channel_id=1, source_target_pairs={{0,5},{1,4},{2,7},{3,6},{4,1},{5,0},{6,3},{7,2},{8,13},{9,12},{10,... | collective-permute-start | bytes 196616 | tf_op jit(solution)/shard_map/ppermute | solution.py:148
  30.9 12.0 %collective-permute-done.5 = bf16[32,1024]{0,1:T(8,128)(2,1)S(1)} collective-permute-done((bf16[32,1024]{0,1:T(8,128)(2,1)S(1)}, bf16[32,1024]{0,1:T(8,128)(2,1)S(1)}, u32[]{:S(2)}, u32[]{:S(2)}) %collective-permute-start.5) | collective-permute-done | bytes 65568 | tf_op jit(solution)/shard_map/ppermute | solution.py:148
  43.1 0.7 %copy-done.5 = f32[1024]{0:T(1024)S(1)} copy-done((f32[1024]{0:T(1024)S(1)}, f32[1024]{0:T(1024)}, u32[]{:S(2)}) %copy-start.5) | copy-done | bytes 4120
  44.2 1.4 %collective-permute-done.6 = bf16[32,1024]{0,1:T(8,128)(2,1)S(1)} collective-permute-done((bf16[32,1024]{0,1:T(8,128)(2,1)S(1)}, bf16[32,1024]{0,1:T(8,128)(2,1)S(1)}, u32[]{:S(2)}, u32[]{:S(2)}) %collective-permute-start.6) | collective-permute-done | bytes 65568 | tf_op jit(solution)/shard_map/ppermute | solution.py:148
  45.8 0.5 fusion.40
  46.4 0.4 copy-done.3
  46.7 0.6 fusion.39
  47.8 1.0 %collective-permute-done.7 = f32[2,3,64]{2,1,0:T(4,128)S(1)} collective-permute-done((f32[2,3,64]{2,1,0:T(4,128)S(1)}, f32[2,3,64]{2,1,0:T(4,128)S(1)}, u32[]{:S(2)}, u32[]{:S(2)}) %collective-permute-start.7) | collective-permute-done | bytes 1568 | tf_op jit(solution)/shard_map/ppermute | solution.py:148
  48.9 3.9 %collective-permute-done.8 = f32[2,3,64]{2,1,0:T(4,128)S(1)} collective-permute-done((f32[2,3,64]{2,1,0:T(4,128)S(1)}, f32[2,3,64]{2,1,0:T(4,128)S(1)}, u32[]{:S(2)}, u32[]{:S(2)}) %collective-permute-start.8) | collective-permute-done | bytes 1568 | tf_op jit(solution)/shard_map/ppermute | solution.py:148
  52.9 1.7 %collective-permute-start.9 = (f32[2,3,64]{2,1,0:T(4,128)S(1)}, f32[2,3,64]{2,1,0:T(4,128)S(1)}, u32[]{:S(2)}, u32[]{:S(2)}) collective-permute-start(f32[2,3,64]{2,1,0:T(4,128)S(1)} %pad_maximum_fusion.8), channel_id=1, source_target_pairs={{0,3},{1,2},{2,1},{3,0},{4,7},{5,6},{6,5},{7,4},{8,11},{9,10},{10,... | collective-permute-start | bytes 4616 | tf_op jit(solution)/shard_map/ppermute | solution.py:148
  54.6 1.4 %collective-permute-done.9 = f32[2,3,64]{2,1,0:T(4,128)S(1)} collective-permute-done((f32[2,3,64]{2,1,0:T(4,128)S(1)}, f32[2,3,64]{2,1,0:T(4,128)S(1)}, u32[]{:S(2)}, u32[]{:S(2)}) %collective-permute-start.9) | collective-permute-done | bytes 1568 | tf_op jit(solution)/shard_map/ppermute | solution.py:148
  56.1 0.6 %gather_fusion.1 = f32[64,2]{1,0:T(8,128)S(1)} fusion(f32[2,64]{0,1:T(8,128)S(1)} %copy.80, s32[1024]{0:T(1024)S(1)} %pad_clamp_fusion), kind=kCustom, calls=%fused_computation.1 | custom fusion | bytes 1280 | tf_op jit(solution)/shard_map/gather | solution.py:252
  56.9 0.6 %dynamic-slice_reduce_fusion.1 = f32[8]{0:T(128)} fusion(f32[1,64]{0,1:T(8,128)S(1)} %get-tuple-element.25, s32[]{:T(128)S(6)} %select_n.114), kind=kLoop, calls=%fused_computation.59 | loop fusion | bytes 68 | tf_op jit(solution)/shard_map/dynamic_slice | solution.py:257
  57.5 0.6 %dynamic-slice_reduce_fusion = f32[8]{0:T(128)} fusion(f32[1,64]{0,1:T(8,128)S(1)} %get-tuple-element.8, s32[]{:T(128)S(6)} %select_n.114), kind=kLoop, calls=%fused_computation.58 | loop fusion | bytes 68 | tf_op jit(solution)/shard_map/dynamic_slice | solution.py:258
  58.1 0.7 %copy-done.11 = s32[64]{0:T(128)S(1)} copy-done((s32[64]{0:T(128)S(1)}, s32[64]{0:T(128)}, u32[]{:S(2)}) %copy-start.11) | copy-done | bytes 280
  58.8 0.6 %select_reduce_fusion.2 = f32[16]{0:T(128)} fusion(f32[64]{0:T(128)S(1)} %get-tuple-element.7, s32[64]{0:T(128)S(1)} %copy-done.11), kind=kLoop, calls=%fused_computation.45 | loop fusion | flops 3056 | bytes 576 | tf_op jit(solution)/shard_map/reduce_sum | solution.py:255
  (62 shorter events, 3.6 us)
Async XLA Ops:
  0.6 45.2 %copy-start = (bf16[1024,512]{1,0:T(8,128)(2,1)S(1)}, bf16[1024,512]{1,0:T(8,128)(2,1)}, u32[]{:S(2)}) copy-start(bf16[1024,512]{1,0:T(8,128)(2,1)} %param.27) | copy-start | bytes 3145732
  0.6 1.1 %copy-start.6 = (bf16[8,1024]{1,0:T(8,128)(2,1)S(1)}, bf16[8,1024]{1,0:T(8,128)(2,1)}, u32[]{:S(2)}) copy-start(bf16[8,1024]{1,0:T(8,128)(2,1)} %param.17) | copy-start | bytes 49156
  1.9 5.0 %collective-permute-start = (bf16[8,1152]{1,0:T(8,128)(2,1)S(1)}, bf16[8,1152]{1,0:T(8,128)(2,1)S(1)}, u32[]{:S(2)}, u32[]{:S(2)}) collective-permute-start(bf16[8,1152]{1,0:T(8,128)(2,1)S(1)} %concatenate.15), channel_id=1, source_target_pairs={{0,5},{1,4},{2,7},{3,6},{4,1},{5,0},{6,3},{7,2},{8,13},{9,12},{10,... | collective-permute-start | bytes 55304 | tf_op jit(solution)/shard_map/ppermute | solution.py:148
  6.8 3.6 %collective-permute-start.1 = (bf16[16,1152]{1,0:T(8,128)(2,1)S(1)}, bf16[16,1152]{1,0:T(8,128)(2,1)S(1)}, u32[]{:S(2)}, u32[]{:S(2)}) collective-permute-start(bf16[16,1152]{1,0:T(8,128)(2,1)S(1)} %pad_maximum_fusion.5), channel_id=1, source_target_pairs={{0,3},{1,2},{2,1},{3,0},{4,7},{5,6},{6,5},{7,4},{8,11},{9,10},{10,... | collective-permute-start | bytes 110600 | tf_op jit(solution)/shard_map/ppermute | solution.py:148
  10.7 1.8 %collective-permute-start.2 = (bf16[32,1152]{0,1:T(8,128)(2,1)S(1)}, bf16[32,1152]{0,1:T(8,128)(2,1)S(1)}, u32[]{:S(2)}, u32[]{:S(2)}) collective-permute-start(bf16[32,1152]{0,1:T(8,128)(2,1)S(1)} %copy.76), channel_id=1, source_target_pairs={{0,1},{1,0},{2,3},{3,2},{4,5},{5,4},{6,7},{7,6},{8,9},{9,8},{10,11... | collective-permute-start | bytes 221192 | tf_op jit(solution)/shard_map/ppermute | solution.py:148
  12.5 1.1 %copy-start.10 = (bf16[1024,352]{0,1:T(8,128)(2,1)S(1)}, bf16[1024,352]{0,1:T(8,128)(2,1)}, u32[]{:S(2)}) copy-start(bf16[1024,352]{0,1:T(8,128)(2,1)} %param.23) | copy-start | bytes 2162692
  12.8 0.8 %copy-start.7 = (f32[1024]{0:T(1024)S(1)}, f32[1024]{0:T(1024)}, u32[]{:S(2)}) copy-start(f32[1024]{0:T(1024)} %param.22) | copy-start | bytes 12292
  13.6 1.1 %copy-start.2 = (bf16[352,1024]{1,0:T(8,128)(2,1)S(1)}, bf16[352,1024]{1,0:T(8,128)(2,1)}, u32[]{:S(2)}) copy-start(bf16[352,1024]{1,0:T(8,128)(2,1)} %param.25) | copy-start | bytes 2162692
  17.2 2.0 %collective-permute-start.3 = (f32[32,1024]{0,1:T(8,128)S(1)}, f32[32,1024]{0,1:T(8,128)S(1)}, u32[]{:S(2)}, u32[]{:S(2)}) collective-permute-start(f32[32,1024]{0,1:T(8,128)S(1)} %slice_select_fusion.1), channel_id=1, source_target_pairs={{0,1},{1,0},{2,3},{3,2},{4,5},{5,4},{6,7},{7,6},{8,9},{9,8},{10,11... | collective-permute-start | bytes 393224 | tf_op jit(solution)/shard_map/ppermute | solution.py:148
  19.2 2.0 %copy-start.1 = (s32[64]{0:T(128)S(1)}, s32[64]{0:T(128)}, u32[]{:S(2)}) copy-start(s32[64]{0:T(128)} %param.20) | copy-start | bytes 772
  19.4 1.8 %copy-start.9 = (s32[64]{0:T(128)S(1)}, s32[64]{0:T(128)}, u32[]{:S(2)}) copy-start(s32[64]{0:T(128)} %constant.64) | copy-start | bytes 772
  19.4 8.2 %collective-permute-start.4 = (bf16[32,1024]{0,1:T(8,128)(2,1)S(1)}, bf16[32,1024]{0,1:T(8,128)(2,1)S(1)}, u32[]{:S(2)}, u32[]{:S(2)}) collective-permute-start(bf16[32,1024]{0,1:T(8,128)(2,1)S(1)} %get-tuple-element.15), channel_id=1, source_target_pairs={{0,3},{1,2},{2,1},{3,0},{4,7},{5,6},{6,5},{7,4},{8,11},{9,10},{10,... | collective-permute-start | bytes 196616 | tf_op jit(solution)/shard_map/ppermute | solution.py:148
  27.7 15.2 %collective-permute-start.5 = (bf16[32,1024]{0,1:T(8,128)(2,1)S(1)}, bf16[32,1024]{0,1:T(8,128)(2,1)S(1)}, u32[]{:S(2)}, u32[]{:S(2)}) collective-permute-start(bf16[32,1024]{0,1:T(8,128)(2,1)S(1)} %fusion.2), channel_id=1, source_target_pairs={{0,5},{1,4},{2,7},{3,6},{4,1},{5,0},{6,3},{7,2},{8,13},{9,12},{10,... | collective-permute-start | bytes 196616 | tf_op jit(solution)/shard_map/ppermute | solution.py:148
  43.1 0.7 %copy-start.5 = (f32[1024]{0:T(1024)S(1)}, f32[1024]{0:T(1024)}, u32[]{:S(2)}) copy-start(f32[1024]{0:T(1024)} %param.26) | copy-start | bytes 12292
  44.0 1.6 %collective-permute-start.6 = (bf16[32,1024]{0,1:T(8,128)(2,1)S(1)}, bf16[32,1024]{0,1:T(8,128)(2,1)S(1)}, u32[]{:S(2)}, u32[]{:S(2)}) collective-permute-start(bf16[32,1024]{0,1:T(8,128)(2,1)S(1)} %multiply_convert_fusion), channel_id=1, source_target_pairs={{0,1},{1,0},{2,3},{3,2},{4,5},{5,4},{6,7},{7,6},{8,9},{9,8},{10,11... | collective-permute-start | bytes 196616 | tf_op jit(solution)/shard_map/ppermute | solution.py:148
  45.8 0.9 %copy-start.3 = (bf16[1024,64]{0,1:T(8,128)(2,1)S(1)}, bf16[1024,64]{0,1:T(8,128)(2,1)}, u32[]{:S(2)}) copy-start(bf16[1024,64]{0,1:T(8,128)(2,1)} %param.28) | copy-start | bytes 393220
  45.8 0.9 %copy-start.4 = (bf16[64,512]{1,0:T(8,128)(2,1)S(1)}, bf16[64,512]{1,0:T(8,128)(2,1)}, u32[]{:S(2)}) copy-start(bf16[64,512]{1,0:T(8,128)(2,1)} %param.29) | copy-start | bytes 196612
  47.6 1.2 %collective-permute-start.7 = (f32[2,3,64]{2,1,0:T(4,128)S(1)}, f32[2,3,64]{2,1,0:T(4,128)S(1)}, u32[]{:S(2)}, u32[]{:S(2)}) collective-permute-start(f32[2,3,64]{2,1,0:T(4,128)S(1)} %pad_maximum_fusion.6), channel_id=1, source_target_pairs={{0,1},{1,0},{2,3},{3,2},{4,5},{5,4},{6,7},{7,6},{8,9},{9,8},{10,11... | collective-permute-start | bytes 4616 | tf_op jit(solution)/shard_map/ppermute | solution.py:148
  48.8 4.0 %collective-permute-start.8 = (f32[2,3,64]{2,1,0:T(4,128)S(1)}, f32[2,3,64]{2,1,0:T(4,128)S(1)}, u32[]{:S(2)}, u32[]{:S(2)}) collective-permute-start(f32[2,3,64]{2,1,0:T(4,128)S(1)} %pad_maximum_fusion.7), channel_id=1, source_target_pairs={{0,5},{1,4},{2,7},{3,6},{4,1},{5,0},{6,3},{7,2},{8,13},{9,12},{10,... | collective-permute-start | bytes 4616 | tf_op jit(solution)/shard_map/ppermute | solution.py:148
  52.8 1.7 %copy-start.8 = (s32[64]{0:T(128)S(1)}, s32[64]{0:T(128)}, u32[]{:S(2)}) copy-start(s32[64]{0:T(128)} %constant.65) | copy-start | bytes 772
  52.9 3.1 %collective-permute-start.9 = (f32[2,3,64]{2,1,0:T(4,128)S(1)}, f32[2,3,64]{2,1,0:T(4,128)S(1)}, u32[]{:S(2)}, u32[]{:S(2)}) collective-permute-start(f32[2,3,64]{2,1,0:T(4,128)S(1)} %pad_maximum_fusion.8), channel_id=1, source_target_pairs={{0,3},{1,2},{2,1},{3,0},{4,7},{5,6},{6,5},{7,4},{8,11},{9,10},{10,... | collective-permute-start | bytes 4616 | tf_op jit(solution)/shard_map/ppermute | solution.py:148
  58.1 0.7 %copy-start.11 = (s32[64]{0:T(128)S(1)}, s32[64]{0:T(128)}, u32[]{:S(2)}) copy-start(s32[64]{0:T(128)} %param.21) | copy-start | bytes 772

commit v2 on v0

--- a/solution.py
+++ b/solution.py
@@ -1,6 +1,8 @@
 import jax
 import jax.numpy as jnp
 from jax import lax
+from jax.experimental import pallas as pl
+from jax.experimental.pallas import tpu as pltpu
 from jax.sharding import PartitionSpec as P
 
 SPLIT = 4
@@ -27,7 +29,7 @@
     )
 
 
-def on_device(
+def routed_on_device(
     hidden_in,
     expert_ids,
     gate_weights,
@@ -142,6 +144,225 @@
     return (policy_own, ratio_own, seq_sums)
 
 
+def exchange(values, mask):
+    devices = lax.axis_size("tensor")
+    return lax.ppermute(values, "tensor", [(i, i ^ mask) for i in range(devices)])
+
+
+def bit(number, place):
+    return (number >> place) & 1
+
+
+def in_order(late, mine, other):
+    return jnp.concatenate([jnp.where(late, other, mine), jnp.where(late, mine, other)], axis=0)
+
+
+def thirds(values):
+    high = lax.reduce_precision(values, 8, 7)
+    middle = lax.reduce_precision(values - high, 8, 7)
+    low = values - high - middle
+    return [part.astype(jnp.bfloat16) for part in (high, middle, low)]
+
+
+def token_at(place, tok_rows, bits):
+    devices = 1 << bits
+    rank = place // tok_rows
+    parity = rank >> (bits - 1)
+    device = parity * 0
+    low = parity
+    for b in range(1, bits):
+        one = (rank >> (bits - 1 - b)) & 1
+        device = device + one * (1 << b)
+        low = low ^ one
+    return (device + low) * tok_rows + place % tok_rows
+
+
+def expert_kernel(own_ref, other_ref, gain_ref, gate_ref, up_ref, down_ref, keep_ref, give_ref):
+    half, features = keep_ref.shape
+    devices = lax.axis_size("tensor")
+    experts = devices // SPLIT
+    expert = lax.axis_index("tensor") // SPLIT
+    rows = jnp.concatenate([own_ref[...], other_ref[...]], axis=0)
+    hidden = rows[:, :features].astype(jnp.float32)
+    moe_input = rms_norm(hidden, gain_ref[...]).astype(jnp.bfloat16)
+    extra = rows[:, features:].astype(jnp.float32)
+    lane = lax.broadcasted_iota(jnp.int32, extra.shape, 1)
+    mine = (lane % experts == expert) & (lane < 3 * experts)
+    weight = jnp.sum(jnp.where(mine, extra, 0.0), axis=1, keepdims=True)
+    gate_proj = jnp.dot(moe_input, gate_ref[...], preferred_element_type=jnp.float32)
+    up_proj = jnp.dot(moe_input, up_ref[...], preferred_element_type=jnp.float32)
+    inner_act = (jax.nn.silu(gate_proj) * up_proj).astype(jnp.bfloat16)
+    partial_value = jnp.dot(inner_act, down_ref[...], preferred_element_type=jnp.float32) * weight
+    keep_ref[...] = partial_value[:half]
+    give_ref[...] = partial_value[half:]
+
+
+def norm_kernel(total_ref, arrived_ref, own_ref, gain_ref, out_ref):
+    features = out_ref.shape[1]
+    mixed = total_ref[...] + arrived_ref[...].astype(jnp.float32)
+    mixed = mixed + own_ref[:, :features].astype(jnp.float32)
+    out_ref[...] = rms_norm(mixed, gain_ref[...]).astype(jnp.bfloat16)
+
+
+def head_kernel(
+    tok_rows, bits, own_ref, other_ref, targets_ref, head_ref, down_ref, up_ref, stats_ref
+):
+    my_index = lax.axis_index("tensor")
+    late = sum(bit(my_index, b) for b in range(bits)) & 1 == 1
+    own, other = own_ref[...], other_ref[...]
+    rows = in_order(late, own, other)
+    tokens, vocab_dev = rows.shape[0], head_ref.shape[1]
+    latent = jnp.dot(rows, down_ref[...], preferred_element_type=jnp.float32)
+    latent = latent.astype(jnp.bfloat16)
+    base_logits = jnp.dot(rows, head_ref[...], preferred_element_type=jnp.float32)
+    policy_logits = base_logits + jnp.dot(latent, up_ref[...], preferred_element_type=jnp.float32)
+    place = lax.broadcasted_iota(jnp.int32, (tokens, tokens), 0)
+    token = lax.broadcasted_iota(jnp.int32, (tokens, tokens), 1)
+    here = token_at(place, tok_rows, bits) == token
+    wanted = jnp.sum(
+        jnp.where(here, targets_ref[...].astype(jnp.float32), 0.0), axis=1, keepdims=True
+    ).astype(jnp.int32)
+    column = lax.broadcasted_iota(jnp.int32, (tokens, vocab_dev), 1)
+    is_target = column == wanted - my_index * vocab_dev
+    lane = lax.broadcasted_iota(jnp.int32, (tokens, 128), 1)
+    packed = jnp.zeros((tokens, 128), jnp.float32)
+    for at, logits in enumerate((base_logits, policy_logits)):
+        top_value = jnp.max(logits, axis=1, keepdims=True)
+        exp_total = jnp.sum(jnp.exp(logits - top_value), axis=1, keepdims=True)
+        picked = jnp.sum(jnp.where(is_target, logits, 0.0), axis=1, keepdims=True)
+        for kind, value in enumerate((top_value, exp_total, picked)):
+            packed = jnp.where(lane == 2 * kind + at, value, packed)
+    stats_ref[...] = packed.T[:8]
+
+
+def merge(one, two):
+    ceiling = jnp.maximum(one[0:2], two[0:2])
+    exp_total = one[2:4] * jnp.exp(one[0:2] - ceiling) + two[2:4] * jnp.exp(two[0:2] - ceiling)
+    return ceiling, exp_total, one[4:6] + two[4:6]
+
+
+def result_kernel(tok_rows, bits, one_ref, two_ref, seq_ref, policy_ref, ratio_ref, sums_ref):
+    ceiling, exp_total, picked = merge(one_ref[...], two_ref[...])
+    log_probs = picked - ceiling - jnp.log(exp_total)
+    tokens = log_probs.shape[1]
+    policy = log_probs[1:2]
+    ratio = policy - log_probs[0:1]
+    place = lax.broadcasted_iota(jnp.int32, (tokens, tokens), 0)
+    token = lax.broadcasted_iota(jnp.int32, (tokens, tokens), 1)
+    here = token_at(place, tok_rows, bits) == token
+    seq = jnp.sum(jnp.where(here, seq_ref[...].astype(jnp.float32), 0.0), axis=1, keepdims=True)
+    row = lax.broadcasted_iota(jnp.int32, (tokens, 128), 0)
+    lane = lax.broadcasted_iota(jnp.int32, (tokens, 128), 1)
+    own = token_at(row, tok_rows, bits) == lax.axis_index("tensor") * tok_rows + lane
+    own_column = (own & (lane < tok_rows)).astype(jnp.float32)
+    seq_column = (seq.astype(jnp.int32) == lane).astype(jnp.float32)
+
+    def pick(values, columns):
+        return jnp.dot(
+            jnp.broadcast_to(values, (8, tokens)),
+            columns,
+            precision=lax.Precision.HIGHEST,
+            preferred_element_type=jnp.float32,
+        )
+
+    policy_ref[...] = pick(policy, own_column)[0:1, :tok_rows]
+    ratio_ref[...] = pick(ratio, own_column)[0:1, :tok_rows]
+    sums_ref[...] = pick(ratio, seq_column)[0:1, :SEQS]
+
+
+def call(kernel, shapes, *operands, flops=0):
+    size = sum(operand.size * operand.dtype.itemsize for operand in operands)
+    return pl.pallas_call(
+        kernel,
+        out_shape=shapes,
+        compiler_params=pltpu.CompilerParams(vmem_limit_bytes=32 << 20),
+        cost_estimate=pl.CostEstimate(flops=flops, bytes_accessed=size, transcendentals=0),
+    )(*operands)
+
+
+def dense_on_device(
+    hidden_in,
+    expert_ids,
+    gate_weights,
+    targets,
+    seq_ids,
+    moe_gain,
+    w_gate,
+    w_up,
+    w_down,
+    final_gain,
+    head_weight,
+    adapter_down,
+    adapter_up,
+):
+    tok_rows, features = hidden_in.shape
+    devices = lax.axis_size("tensor")
+    bits = devices.bit_length() - 1
+    experts = devices // SPLIT
+    tokens = devices * tok_rows
+    half = tokens // 2
+    lanes = -(-3 * experts // 128) * 128
+    my_index = lax.axis_index("tensor")
+    far = [(b, (1 << b) + 1) for b in range(bits - 1, 0, -1)]
+
+    def array(rows, columns, dtype):
+        return jax.ShapeDtypeStruct((rows, columns), dtype)
+
+    expert_of = jnp.arange(experts, dtype=jnp.int32)
+    mixing = jnp.sum(
+        jnp.where(expert_ids[:, :, None] == expert_of, gate_weights[:, :, None], 0.0), axis=1
+    )
+    gap = jnp.zeros((tok_rows, lanes - 3 * experts), jnp.bfloat16)
+    own = jnp.concatenate([hidden_in, *thirds(mixing), gap], axis=1)
+    for b, mask in far:
+        own = in_order(bit(my_index, b) == 1, own, exchange(own, mask))
+    other = exchange(own, 1)
+
+    total, give = call(
+        expert_kernel,
+        [array(half, features, jnp.float32)] * 2,
+        own,
+        other,
+        moe_gain[None],
+        w_gate,
+        w_up,
+        w_down,
+        flops=6 * tokens * features * w_gate.shape[1],
+    )
+    total = total + exchange(give, 1)
+    for _, mask in far[:0:-1]:
+        total = total + exchange(total.astype(jnp.bfloat16), mask).astype(jnp.float32)
+    arrived = exchange(total.astype(jnp.bfloat16), far[0][1])
+    own_final = call(
+        norm_kernel, array(half, features, jnp.bfloat16), total, arrived, own, final_gain[None]
+    )
+    other_final = exchange(own_final, 1)
+
+    stats = call(
+        lambda *refs: head_kernel(tok_rows, bits, *refs),
+        array(8, tokens, jnp.float32),
+        own_final,
+        other_final,
+        targets[None],
+        head_weight,
+        adapter_down,
+        adapter_up,
+        flops=2 * tokens * features * head_weight.shape[1],
+    )
+    masks = [1] + [mask for _, mask in far[::-1]]
+    for mask in masks[:-1]:
+        pieces = merge(stats, exchange(stats, mask))
+        stats = jnp.concatenate([*pieces, jnp.zeros((2, tokens), jnp.float32)], axis=0)
+    policy_own, ratio_own, seq_sums = call(
+        lambda *refs: result_kernel(tok_rows, bits, *refs),
+        [array(1, tok_rows, jnp.float32)] * 2 + [array(1, SEQS, jnp.float32)],
+        stats,
+        exchange(stats, masks[-1]),
+        seq_ids[None],
+    )
+    return (policy_own[0], ratio_own[0], seq_sums[0])
+
+
 def solution(mesh):
     in_specs = (
         P(("dp", "tensor"), None),
@@ -159,6 +380,13 @@
         P(None, "tensor"),
     )
     out_specs = (P(("dp", "tensor")), P(("dp", "tensor")), P("dp"))
+    devices = mesh.shape["tensor"]
+
+    def on_device(hidden_in, expert_ids, *others):
+        every_expert = expert_ids.shape[1] == devices // SPLIT
+        step = dense_on_device if every_expert else routed_on_device
+        return step(hidden_in, expert_ids, *others)
+
     return jax.shard_map(
         on_device, mesh=mesh, in_specs=in_specs, out_specs=out_specs, check_vma=False
     )

time: 79.6 us -> 38 us (0.48)
  blocking collectives: 55.2 us -> 0 us
  starting transfers between devices: 3.41 us -> 17.4 us
  waiting for transfers between devices: 8.32 us -> 13.4 us
  matrix products: 4.76 us -> 0 us
  local copies, waits for them, and re-layouts: 5.63 us -> 3.01 us
  Pallas kernels: 0 us -> 2.16 us
    ppermute x0 -> x10, starting transfers between devices: none -> 17.4 us  [exchange(): lax.ppermute(values, 'tensor', [(i, i ^ mask) for i in range(devices)])]
    pmax x1 -> x0, blocking collectives: 14.8 us -> none  [on_device(): ceiling = lax.pmax(maxima, 'tensor')]
    all_gather x1 -> x0, blocking collectives: 13.9 us -> none  [on_device(): shard_rows = lax.all_gather(final_input, 'tensor', axis=0, tiled=True)]
    psum x1 -> x0, blocking collectives: 13.6 us -> none  [on_device(): lax.psum((exp_sums * jnp.exp(maxima - ceiling), target_logits), 'tensor')]
    ppermute x0 -> x10, waiting for transfers between devices: none -> 13.4 us  [exchange(): lax.ppermute(values, 'tensor', [(i, i ^ mask) for i in range(devices)])]
    all_to_all x1 -> x0, blocking collectives: 12.9 us -> none  [on_device(): lax.all_to_all(outgoing, 'tensor', split_axis=0, concat_axis=0, tiled=True)]
    all_to_all x1 -> x0, waiting for transfers between devices: 8.32 us -> none  [expert_piece(): lax.all_to_all(partial_value.reshape(arrived.shape), 'tensor', split_axis...]
    dot_general x7 -> x0, matrix products: 4.76 us -> none  [the longest x1 1.45 us: expert_piece(): gate_proj = jnp.dot(flat_rows, w_gate, preferred_element_type=jnp.float32)]
  transfers between devices with their start and end apart: 1 -> 10, of which waited for: 1 -> 9; matrix products, arithmetic and copies ran while one was open for 0% -> 5% of each run, Pallas kernels for 0% -> 0%
where the time goes in v2:
time: 38 us; the launch traced here: 37.7 us
  starting transfers between devices  17.4 us (46%)
  waiting for transfers between devices  13.4 us (35%)
  local copies, waits for them, and re-layouts  3.01 us (8%)
  Pallas kernels  2.16 us (6%)
  other arithmetic  0.96 us (3%)
  between operations  0.78 us (2%)
    ppermute x10, starting transfers between devices, exchange(): lax.ppermute(values, 'tensor', [(i, i ^ mask) for i in range(devices)])  17.4 us
    ppermute x10, waiting for transfers between devices, exchange(): lax.ppermute(values, 'tensor', [(i, i ^ mask) for i in range(devices)])  13.4 us
    unnamed x23, local copies, waits for them, and re-layouts  2.75 us
    pallas_call x4, Pallas kernels, call(): pl.pallas_call(kernel, out_shape=shapes, compiler_params=pltpu.CompilerPa...  2.16 us
  transfers between devices with their start and end apart: 10, of which 9 were waited for; matrix products, arithmetic and copies ran while one was open for 5% of the time, Pallas kernels for 0%

profile of v2, /device:TPU:0, one launch (start us, length us, event | category | flops | bytes accessed | tf_op | source)
XLA Modules:
  0.0 37.7 jit_solution(14411014024590272762)
XLA Ops:
  0.6 0.7 %fusion.1 = f32[8,2]{0,1:T(2,128)S(1)} fusion(f32[8,2]{0,1:T(2,128)} %param.15, s32[8,2]{0,1:T(2,128)} %param.14), kind=kLoop, calls=%fused_computation.15 | loop fusion | flops 80 | bytes 192 | tf_op jit(solution)/shard_map/reduce_sum | solution.py:312
  1.4 0.1 copy.21
  1.5 0.1 concatenate.15
  1.5 3.5 %collective-permute-start = (bf16[8,1152]{1,0:T(8,128)(2,1)S(1)}, bf16[8,1152]{1,0:T(8,128)(2,1)S(1)}, u32[]{:S(2)}, u32[]{:S(2)}) collective-permute-start(bf16[8,1152]{1,0:T(8,128)(2,1)S(1)} %concatenate.15), channel_id=1, source_target_pairs={{0,5},{1,4},{2,7},{3,6},{4,1},{5,0},{6,3},{7,2},{8,13},{9,12},{10,... | collective-permute-start | bytes 55304 | tf_op jit(solution)/shard_map/ppermute | solution.py:149
  5.0 1.5 %collective-permute-done = bf16[8,1152]{1,0:T(8,128)(2,1)S(1)} collective-permute-done((bf16[8,1152]{1,0:T(8,128)(2,1)S(1)}, bf16[8,1152]{1,0:T(8,128)(2,1)S(1)}, u32[]{:S(2)}, u32[]{:S(2)}) %collective-permute-start) | collective-permute-done | bytes 18464 | tf_op jit(solution)/shard_map/ppermute | solution.py:149
  6.5 1.9 %collective-permute-start.1 = (bf16[16,1152]{1,0:T(8,128)(2,1)S(1)}, bf16[16,1152]{1,0:T(8,128)(2,1)S(1)}, u32[]{:S(2)}, u32[]{:S(2)}) collective-permute-start(bf16[16,1152]{1,0:T(8,128)(2,1)S(1)} %pad_maximum_fusion.1), channel_id=1, source_target_pairs={{0,3},{1,2},{2,1},{3,0},{4,7},{5,6},{6,5},{7,4},{8,11},{9,10},{10,... | collective-permute-start | bytes 110600 | tf_op jit(solution)/shard_map/ppermute | solution.py:149
  8.5 1.6 %collective-permute-done.1 = bf16[16,1152]{1,0:T(8,128)(2,1)S(1)} collective-permute-done((bf16[16,1152]{1,0:T(8,128)(2,1)S(1)}, bf16[16,1152]{1,0:T(8,128)(2,1)S(1)}, u32[]{:S(2)}, u32[]{:S(2)}) %collective-permute-start.1) | collective-permute-done | bytes 36896 | tf_op jit(solution)/shard_map/ppermute | solution.py:149
  10.2 0.6 %collective-permute-start.2 = (bf16[32,1152]{1,0:T(8,128)(2,1)S(1)}, bf16[32,1152]{1,0:T(8,128)(2,1)S(1)}, u32[]{:S(2)}, u32[]{:S(2)}) collective-permute-start(bf16[32,1152]{1,0:T(8,128)(2,1)S(1)} %pad_maximum_fusion.own_ref), channel_id=1, source_target_pairs={{0,1},{1,0},{2,3},{3,2},{4,5},{5,4},{6,7},{7,6},{8,9},{9,8},{10,11... | collective-permute-start | bytes 221192 | tf_op jit(solution)/shard_map/ppermute | solution.py:149
  10.7 1.5 %copy.23.gate_ref = bf16[1024,352]{1,0:T(8,128)(2,1)S(1)} copy(bf16[1024,352]{0,1:T(8,128)(2,1)} %param.19) | data formatting | bytes 1441792 | tf_op args[6]
  12.2 0.4 copy.24.up_ref
  12.6 0.7 %copy-done.1 = bf16[352,1024]{1,0:T(8,128)(2,1)S(1)} copy-done((bf16[352,1024]{1,0:T(8,128)(2,1)S(1)}, bf16[352,1024]{1,0:T(8,128)(2,1)}, u32[]{:S(2)}) %copy-start.1) | copy-done | bytes 720920
  13.3 0.7 %shard_map.148 = (f32[32,1024]{1,0:T(8,128)S(1)}, f32[32,1024]{1,0:T(8,128)S(1)}) custom-call(bf16[32,1152]{1,0:T(8,128)(2,1)S(1)} %pad_maximum_fusion.own_ref, bf16[32,1152]{1,0:T(8,128)(2,1)S(1)} %collective-permute-done.2.other_ref, f32[1,1024]{1,0:T(1,128)S(1)} %bitcast.7, bf16[1024,352]{1,0:T(8,128)(2,1)S(1)} %copy.23.gate_ref, ...), custom_call_target="tpu_custom_call" | custom-call | flops 138412032 | bytes 2314240 | tf_op jit(solution)/shard_map/pallas_call | solution.py:275
  14.0 0.1 collective-permute-start.3
  14.1 1.3 %collective-permute-done.3 = f32[32,1024]{1,0:T(8,128)S(1)} collective-permute-done((f32[32,1024]{1,0:T(8,128)S(1)}, f32[32,1024]{1,0:T(8,128)S(1)}, u32[]{:S(2)}, u32[]{:S(2)}) %collective-permute-start.3) | collective-permute-done | bytes 131104 | tf_op jit(solution)/shard_map/ppermute | solution.py:149
  15.4 1.8 %collective-permute-start.4 = (bf16[32,1024]{1,0:T(8,128)(2,1)S(1)}, bf16[32,1024]{1,0:T(8,128)(2,1)S(1)}, u32[]{:S(2)}, u32[]{:S(2)}) collective-permute-start(bf16[32,1024]{1,0:T(8,128)(2,1)S(1)} %get-tuple-element.17), channel_id=1, source_target_pairs={{0,3},{1,2},{2,1},{3,0},{4,7},{5,6},{6,5},{7,4},{8,11},{9,10},{10,... | collective-permute-start | bytes 196616 | tf_op jit(solution)/shard_map/ppermute | solution.py:149
  17.2 2.3 %collective-permute-done.4 = bf16[32,1024]{1,0:T(8,128)(2,1)S(1)} collective-permute-done((bf16[32,1024]{1,0:T(8,128)(2,1)S(1)}, bf16[32,1024]{1,0:T(8,128)(2,1)S(1)}, u32[]{:S(2)}, u32[]{:S(2)}) %collective-permute-start.4) | collective-permute-done | bytes 65568 | tf_op jit(solution)/shard_map/ppermute | solution.py:149
  19.6 2.9 %collective-permute-start.5 = (bf16[32,1024]{1,0:T(8,128)(2,1)S(1)}, bf16[32,1024]{1,0:T(8,128)(2,1)S(1)}, u32[]{:S(2)}, u32[]{:S(2)}) collective-permute-start(bf16[32,1024]{1,0:T(8,128)(2,1)S(1)} %get-tuple-element.15), channel_id=1, source_target_pairs={{0,5},{1,4},{2,7},{3,6},{4,1},{5,0},{6,3},{7,2},{8,13},{9,12},{10,... | collective-permute-start | bytes 196616 | tf_op jit(solution)/shard_map/ppermute | solution.py:149
  22.5 2.2 %collective-permute-done.5.arrived_ref = bf16[32,1024]{1,0:T(8,128)(2,1)S(1)} collective-permute-done((bf16[32,1024]{1,0:T(8,128)(2,1)S(1)}, bf16[32,1024]{1,0:T(8,128)(2,1)S(1)}, u32[]{:S(2)}, u32[]{:S(2)}) %collective-permute-start.5) | collective-permute-done | bytes 65568 | tf_op jit(solution)/shard_map/ppermute | solution.py:149
  24.7 0.1 shard_map.149.refs_0_
  24.8 1.8 %collective-permute-start.6 = (bf16[32,1024]{1,0:T(8,128)(2,1)S(1)}, bf16[32,1024]{1,0:T(8,128)(2,1)S(1)}, u32[]{:S(2)}, u32[]{:S(2)}) collective-permute-start(bf16[32,1024]{1,0:T(8,128)(2,1)S(1)} %shard_map.149.refs_0_), channel_id=1, source_target_pairs={{0,1},{1,0},{2,3},{3,2},{4,5},{5,4},{6,7},{7,6},{8,9},{9,8},{10,11... | collective-permute-start | bytes 196616 | tf_op jit(solution)/shard_map/ppermute | solution.py:149
  26.6 0.2 copy.25.refs_4_
  26.7 0.7 %collective-permute-done.6.refs_1_ = bf16[32,1024]{1,0:T(8,128)(2,1)S(1)} collective-permute-done((bf16[32,1024]{1,0:T(8,128)(2,1)S(1)}, bf16[32,1024]{1,0:T(8,128)(2,1)S(1)}, u32[]{:S(2)}, u32[]{:S(2)}) %collective-permute-start.6) | collective-permute-done | bytes 65568 | tf_op jit(solution)/shard_map/ppermute | solution.py:149
  27.5 0.6 %shard_map.150 = f32[8,64]{1,0:T(8,128)S(1)} custom-call(bf16[32,1024]{1,0:T(8,128)(2,1)S(1)} %shard_map.149.refs_0_, bf16[32,1024]{1,0:T(8,128)(2,1)S(1)} %collective-permute-done.6.refs_1_, s32[1,64]{1,0:T(1,128)S(1)} %bitcast.9, bf16[1024,512]{1,0:T(8,128)(2,1)S(1)} %copy-done, bf16[1024,64]{1,0:T(8,128)(2,1)S(1)} %copy.25.refs_4_, ...), custom_call_target="tpu_custom_call" | custom-call | flops 67108864 | bytes 1376512 | tf_op jit(solution)/shard_map/pallas_call | solution.py:275
  28.1 0.6 %collective-permute-start.7 = (f32[8,64]{1,0:T(8,128)S(1)}, f32[8,64]{1,0:T(8,128)S(1)}, u32[]{:S(2)}, u32[]{:S(2)}) collective-permute-start(f32[8,64]{1,0:T(8,128)S(1)} %shard_map.150), channel_id=1, source_target_pairs={{0,1},{1,0},{2,3},{3,2},{4,5},{5,4},{6,7},{7,6},{8,9},{9,8},{10,11... | collective-permute-start | bytes 6152 | tf_op jit(solution)/shard_map/ppermute | solution.py:149
  28.7 0.1 pad.7.clone
  28.8 0.7 %collective-permute-done.7 = f32[8,64]{1,0:T(8,128)S(1)} collective-permute-done((f32[8,64]{1,0:T(8,128)S(1)}, f32[8,64]{1,0:T(8,128)S(1)}, u32[]{:S(2)}, u32[]{:S(2)}) %collective-permute-start.7) | collective-permute-done | bytes 2080 | tf_op jit(solution)/shard_map/ppermute | solution.py:149
  29.6 0.1 maximum_maximum_fusion
  29.6 1.3 %collective-permute-start.8 = (f32[8,64]{1,0:T(8,128)S(1)}, f32[8,64]{1,0:T(8,128)S(1)}, u32[]{:S(2)}, u32[]{:S(2)}) collective-permute-start(f32[8,64]{1,0:T(8,128)S(1)} %maximum_maximum_fusion), channel_id=1, source_target_pairs={{0,3},{1,2},{2,1},{3,0},{4,7},{5,6},{6,5},{7,4},{8,11},{9,10},{10,... | collective-permute-start | bytes 6152 | tf_op jit(solution)/shard_map/ppermute | solution.py:149
  31.0 1.7 %collective-permute-done.8 = f32[8,64]{1,0:T(8,128)S(1)} collective-permute-done((f32[8,64]{1,0:T(8,128)S(1)}, f32[8,64]{1,0:T(8,128)S(1)}, u32[]{:S(2)}, u32[]{:S(2)}) %collective-permute-start.8) | collective-permute-done | bytes 2080 | tf_op jit(solution)/shard_map/ppermute | solution.py:149
  32.8 2.9 %collective-permute-start.9 = (f32[8,64]{1,0:T(8,128)S(1)}, f32[8,64]{1,0:T(8,128)S(1)}, u32[]{:S(2)}, u32[]{:S(2)}) collective-permute-start(f32[8,64]{1,0:T(8,128)S(1)} %maximum_maximum_fusion.1.refs_0_), channel_id=1, source_target_pairs={{0,5},{1,4},{2,7},{3,6},{4,1},{5,0},{6,3},{7,2},{8,13},{9,12},{10,... | collective-permute-start | bytes 6152 | tf_op jit(solution)/shard_map/ppermute | solution.py:149
  35.6 1.3 %collective-permute-done.9.refs_1_ = f32[8,64]{1,0:T(8,128)S(1)} collective-permute-done((f32[8,64]{1,0:T(8,128)S(1)}, f32[8,64]{1,0:T(8,128)S(1)}, u32[]{:S(2)}, u32[]{:S(2)}) %collective-permute-start.9) | collective-permute-done | bytes 2080 | tf_op jit(solution)/shard_map/ppermute | solution.py:149
  37.0 0.8 %shard_map.151 = (f32[1,8]{1,0:T(1,128)}, f32[1,8]{1,0:T(1,128)}, f32[1,16]{1,0:T(1,128)}) custom-call(f32[8,64]{1,0:T(8,128)S(1)} %maximum_maximum_fusion.1.refs_0_, f32[8,64]{1,0:T(8,128)S(1)} %collective-permute-done.9.refs_1_, s32[1,64]{1,0:T(1,128)S(1)} %bitcast.10), custom_call_target="tpu_custom_call" | custom-call | bytes 4352 | tf_op jit(solution)/shard_map/pallas_call | solution.py:275
  (32 shorter events, 0.2 us)
Async XLA Ops:
  0.6 0.8 %copy-start.9 = (bf16[8,1024]{1,0:T(8,128)(2,1)S(1)}, bf16[8,1024]{1,0:T(8,128)(2,1)}, u32[]{:S(2)}) copy-start(bf16[8,1024]{1,0:T(8,128)(2,1)} %param.13) | copy-start | bytes 49156
  1.5 5.0 %collective-permute-start = (bf16[8,1152]{1,0:T(8,128)(2,1)S(1)}, bf16[8,1152]{1,0:T(8,128)(2,1)S(1)}, u32[]{:S(2)}, u32[]{:S(2)}) collective-permute-start(bf16[8,1152]{1,0:T(8,128)(2,1)S(1)} %concatenate.15), channel_id=1, source_target_pairs={{0,5},{1,4},{2,7},{3,6},{4,1},{5,0},{6,3},{7,2},{8,13},{9,12},{10,... | collective-permute-start | bytes 55304 | tf_op jit(solution)/shard_map/ppermute | solution.py:149
  6.5 3.6 %collective-permute-start.1 = (bf16[16,1152]{1,0:T(8,128)(2,1)S(1)}, bf16[16,1152]{1,0:T(8,128)(2,1)S(1)}, u32[]{:S(2)}, u32[]{:S(2)}) collective-permute-start(bf16[16,1152]{1,0:T(8,128)(2,1)S(1)} %pad_maximum_fusion.1), channel_id=1, source_target_pairs={{0,3},{1,2},{2,1},{3,0},{4,7},{5,6},{6,5},{7,4},{8,11},{9,10},{10,... | collective-permute-start | bytes 110600 | tf_op jit(solution)/shard_map/ppermute | solution.py:149
  10.1 2.1 %copy-start.7 = (bf16[1024,352]{0,1:T(8,128)(2,1)S(1)}, bf16[1024,352]{0,1:T(8,128)(2,1)}, u32[]{:S(2)}) copy-start(bf16[1024,352]{0,1:T(8,128)(2,1)} %param.20) | copy-start | bytes 2162692
  10.2 2.4 %collective-permute-start.2 = (bf16[32,1152]{1,0:T(8,128)(2,1)S(1)}, bf16[32,1152]{1,0:T(8,128)(2,1)S(1)}, u32[]{:S(2)}, u32[]{:S(2)}) collective-permute-start(bf16[32,1152]{1,0:T(8,128)(2,1)S(1)} %pad_maximum_fusion.own_ref), channel_id=1, source_target_pairs={{0,1},{1,0},{2,3},{3,2},{4,5},{5,4},{6,7},{7,6},{8,9},{9,8},{10,11... | collective-permute-start | bytes 221192 | tf_op jit(solution)/shard_map/ppermute | solution.py:149
  12.2 1.1 %copy-start.1 = (bf16[352,1024]{1,0:T(8,128)(2,1)S(1)}, bf16[352,1024]{1,0:T(8,128)(2,1)}, u32[]{:S(2)}) copy-start(bf16[352,1024]{1,0:T(8,128)(2,1)} %down_ref.1) | copy-start | bytes 2162692
  12.2 1.1 %copy-start.3 = (f32[1024]{0:T(1024)S(1)}, f32[1024]{0:T(1024)}, u32[]{:S(2)}) copy-start(f32[1024]{0:T(1024)} %param.18) | copy-start | bytes 12292
  13.3 11.4 %copy-start.4 = (f32[1024]{0:T(1024)S(1)}, f32[1024]{0:T(1024)}, u32[]{:S(2)}) copy-start(f32[1024]{0:T(1024)} %param.22) | copy-start | bytes 12292
  14.0 13.5 %copy-start = (bf16[1024,512]{1,0:T(8,128)(2,1)S(1)}, bf16[1024,512]{1,0:T(8,128)(2,1)}, u32[]{:S(2)}) copy-start(bf16[1024,512]{1,0:T(8,128)(2,1)} %refs_3_.1) | copy-start | bytes 3145732
  14.0 1.4 %collective-permute-start.3 = (f32[32,1024]{1,0:T(8,128)S(1)}, f32[32,1024]{1,0:T(8,128)S(1)}, u32[]{:S(2)}, u32[]{:S(2)}) collective-permute-start(f32[32,1024]{1,0:T(8,128)S(1)} %get-tuple-element.9), channel_id=1, source_target_pairs={{0,1},{1,0},{2,3},{3,2},{4,5},{5,4},{6,7},{7,6},{8,9},{9,8},{10,11... | collective-permute-start | bytes 393224 | tf_op jit(solution)/shard_map/ppermute | solution.py:149
  15.4 4.1 %collective-permute-start.4 = (bf16[32,1024]{1,0:T(8,128)(2,1)S(1)}, bf16[32,1024]{1,0:T(8,128)(2,1)S(1)}, u32[]{:S(2)}, u32[]{:S(2)}) collective-permute-start(bf16[32,1024]{1,0:T(8,128)(2,1)S(1)} %get-tuple-element.17), channel_id=1, source_target_pairs={{0,3},{1,2},{2,1},{3,0},{4,7},{5,6},{6,5},{7,4},{8,11},{9,10},{10,... | collective-permute-start | bytes 196616 | tf_op jit(solution)/shard_map/ppermute | solution.py:149
  19.6 5.1 %collective-permute-start.5 = (bf16[32,1024]{1,0:T(8,128)(2,1)S(1)}, bf16[32,1024]{1,0:T(8,128)(2,1)S(1)}, u32[]{:S(2)}, u32[]{:S(2)}) collective-permute-start(bf16[32,1024]{1,0:T(8,128)(2,1)S(1)} %get-tuple-element.15), channel_id=1, source_target_pairs={{0,5},{1,4},{2,7},{3,6},{4,1},{5,0},{6,3},{7,2},{8,13},{9,12},{10,... | collective-permute-start | bytes 196616 | tf_op jit(solution)/shard_map/ppermute | solution.py:149
  24.7 1.9 %copy-start.8 = (bf16[1024,64]{0,1:T(8,128)(2,1)S(1)}, bf16[1024,64]{0,1:T(8,128)(2,1)}, u32[]{:S(2)}) copy-start(bf16[1024,64]{0,1:T(8,128)(2,1)} %param.24) | copy-start | bytes 393220
  24.8 2.7 %copy-start.2 = (bf16[64,512]{1,0:T(8,128)(2,1)S(1)}, bf16[64,512]{1,0:T(8,128)(2,1)}, u32[]{:S(2)}) copy-start(bf16[64,512]{1,0:T(8,128)(2,1)} %refs_5_.1) | copy-start | bytes 196612
  24.8 2.7 %collective-permute-start.6 = (bf16[32,1024]{1,0:T(8,128)(2,1)S(1)}, bf16[32,1024]{1,0:T(8,128)(2,1)S(1)}, u32[]{:S(2)}, u32[]{:S(2)}) collective-permute-start(bf16[32,1024]{1,0:T(8,128)(2,1)S(1)} %shard_map.149.refs_0_), channel_id=1, source_target_pairs={{0,1},{1,0},{2,3},{3,2},{4,5},{5,4},{6,7},{7,6},{8,9},{9,8},{10,11... | collective-permute-start | bytes 196616 | tf_op jit(solution)/shard_map/ppermute | solution.py:149
  26.7 0.7 %copy-start.5 = (s32[64]{0:T(128)S(1)}, s32[64]{0:T(128)}, u32[]{:S(2)}) copy-start(s32[64]{0:T(128)} %param.16) | copy-start | bytes 772
  28.1 1.5 %collective-permute-start.7 = (f32[8,64]{1,0:T(8,128)S(1)}, f32[8,64]{1,0:T(8,128)S(1)}, u32[]{:S(2)}, u32[]{:S(2)}) collective-permute-start(f32[8,64]{1,0:T(8,128)S(1)} %shard_map.150), channel_id=1, source_target_pairs={{0,1},{1,0},{2,3},{3,2},{4,5},{5,4},{6,7},{7,6},{8,9},{9,8},{10,11... | collective-permute-start | bytes 6152 | tf_op jit(solution)/shard_map/ppermute | solution.py:149
  29.6 3.0 %collective-permute-start.8 = (f32[8,64]{1,0:T(8,128)S(1)}, f32[8,64]{1,0:T(8,128)S(1)}, u32[]{:S(2)}, u32[]{:S(2)}) collective-permute-start(f32[8,64]{1,0:T(8,128)S(1)} %maximum_maximum_fusion), channel_id=1, source_target_pairs={{0,3},{1,2},{2,1},{3,0},{4,7},{5,6},{6,5},{7,4},{8,11},{9,10},{10,... | collective-permute-start | bytes 6152 | tf_op jit(solution)/shard_map/ppermute | solution.py:149
  32.8 4.2 %copy-start.6 = (s32[64]{0:T(128)S(1)}, s32[64]{0:T(128)}, u32[]{:S(2)}) copy-start(s32[64]{0:T(128)} %param.17) | copy-start | bytes 772
  32.8 4.2 %collective-permute-start.9 = (f32[8,64]{1,0:T(8,128)S(1)}, f32[8,64]{1,0:T(8,128)S(1)}, u32[]{:S(2)}, u32[]{:S(2)}) collective-permute-start(f32[8,64]{1,0:T(8,128)S(1)} %maximum_maximum_fusion.1.refs_0_), channel_id=1, source_target_pairs={{0,5},{1,4},{2,7},{3,6},{4,1},{5,0},{6,3},{7,2},{8,13},{9,12},{10,... | collective-permute-start | bytes 6152 | tf_op jit(solution)/shard_map/ppermute | solution.py:149

commit v3 on v0

--- a/solution.py
+++ b/solution.py
@@ -1,10 +1,15 @@
+import functools
+
 import jax
 import jax.numpy as jnp
 from jax import lax
+from jax.experimental import pallas as pl
+from jax.experimental.pallas import tpu as pltpu
 from jax.sharding import PartitionSpec as P
 
 SPLIT = 4
 SEQS = 16
+ROUND_FLOPS = 4 << 30
 
 
 epsilon = 1e-06
@@ -27,7 +32,7 @@
     )
 
 
-def on_device(
+def routed_on_device(
     hidden_in,
     expert_ids,
     gate_weights,
@@ -142,6 +147,307 @@
     return (policy_own, ratio_own, seq_sums)
 
 
+def exchange(values, mask):
+    devices = lax.axis_size("tensor")
+    return lax.ppermute(values, "tensor", [(i, i ^ mask) for i in range(devices)])
+
+
+def bit(number, place):
+    return (number >> place) & 1
+
+
+def in_order(late, mine, other):
+    return jnp.concatenate([jnp.where(late, other, mine), jnp.where(late, mine, other)], axis=0)
+
+
+def token_at(place, tok_rows, bits):
+    devices = 1 << bits
+    rank = place // tok_rows
+    parity = rank >> (bits - 1)
+    device = parity * 0
+    low = parity
+    for b in range(1, bits):
+        one = (rank >> (bits - 1 - b)) & 1
+        device = device + one * (1 << b)
+        low = low ^ one
+    return (device + low) * tok_rows + place % tok_rows
+
+
+TRANSPOSED = (((1,), (1,)), ((), ()))
+
+
+def places(tok_rows, bits):
+    my_index = lax.axis_index("tensor")
+    parity = sum(bit(my_index, b) for b in range(bits)) & 1
+    return my_index, parity, tok_rows << (bits - 1)
+
+
+def prepare_kernel(
+    tok_rows,
+    bits,
+    ids_ref,
+    gates_ref,
+    targets_ref,
+    seq_ref,
+    moe_gain_ref,
+    final_gain_ref,
+    down_ref,
+    gains_ref,
+    down_out_ref,
+    mixing_ref,
+    columns_ref,
+):
+    my_index, parity, half = places(tok_rows, bits)
+    experts = gates_ref.shape[0]
+    gains_ref[...] = jnp.concatenate(
+        [moe_gain_ref[...]] * 4 + [final_gain_ref[...]] * 4, axis=0
+    )
+    down_out_ref[...] = down_ref[...]
+    rows = [
+        sum(
+            jnp.where(ids_ref[k : k + 1] == expert, gates_ref[k : k + 1], 0.0)
+            for k in range(ids_ref.shape[0])
+        )
+        for expert in range(experts)
+    ]
+    rows = jnp.concatenate(rows + [jnp.zeros((8 - experts, tok_rows), jnp.float32)], axis=0)
+    rows = jnp.concatenate([rows] * (128 // tok_rows), axis=1)
+    at = lax.broadcasted_iota(jnp.int32, (8, 128), 1)
+    token = token_at(at + parity * half, tok_rows, bits) - my_index * tok_rows
+    mixing_ref[...] = jnp.where((token >= 0) & (token < tok_rows) & (at < half), rows, 0.0)
+    row = lax.broadcasted_iota(jnp.int32, (half, 128), 0)
+    lane = lax.broadcasted_iota(jnp.int32, (half, 128), 1)
+    token = token_at(row + parity * half, tok_rows, bits) - my_index * tok_rows
+    wanted = half_columns(targets_ref[...], tok_rows, bits, parity)
+    own_seq = half_columns(seq_ref[...], tok_rows, bits, parity)
+    other_seq = half_columns(seq_ref[...], tok_rows, bits, 1 - parity)
+    picks = (token == lane) & (lane < tok_rows) | (own_seq == lane - 64) & (lane >= 64)
+    columns_ref[0] = jnp.where(lane == 0, wanted, 0).astype(jnp.float32)
+    columns_ref[1] = picks.astype(jnp.float32)
+    columns_ref[2] = ((other_seq == lane - 64) & (lane >= 64)).astype(jnp.float32)
+
+
+def flags_kernel(flags_ref):
+    row = lax.broadcasted_iota(jnp.int32, flags_ref.shape, 0)
+    flags_ref[...] = bit(lax.axis_index("tensor"), row)
+
+
+def order_kernel(place, flags_ref, mine_ref, other_ref, out_ref):
+    late = flags_ref[place : place + 1, 0:1] == 1
+    out_ref[...] = in_order(late, mine_ref[...], other_ref[...])
+
+
+def expert_kernel(rows_ref, gains_ref, *refs):
+    far_refs, near_refs, (total_ref, sent_ref) = refs[0:3], refs[3:6], refs[6:8]
+    moe_input = rms_norm(rows_ref[...].astype(jnp.float32), gains_ref[0:1]).astype(jnp.bfloat16)
+
+    def units(gate_ref, up_ref, down_ref):
+        projections = [
+            lax.dot_general(moe_input, ref[...], TRANSPOSED, preferred_element_type=jnp.float32)
+            for ref in (gate_ref, up_ref)
+        ]
+        inner_act = (jax.nn.silu(projections[0]) * projections[1]).astype(jnp.bfloat16)
+        return jnp.dot(inner_act, down_ref[...], preferred_element_type=jnp.float32)
+
+    total = units(*far_refs) + units(*near_refs)
+    total_ref[...] = total
+    sent_ref[...] = total.astype(jnp.bfloat16)
+
+
+def norm_kernel(total_ref, arrived_ref, mixing_ref, mixing_arrived_ref, rows_ref, gains_ref, out_ref):
+    half = out_ref.shape[0]
+    expert = lax.axis_index("tensor") // SPLIT
+    mixing = (mixing_ref[...] + mixing_arrived_ref[...]).T[:half]
+    lane = lax.broadcasted_iota(jnp.int32, mixing.shape, 1)
+    mixed = rows_ref[...].astype(jnp.float32)
+    for own, value in ((expert, total_ref[...]), (1 - expert, arrived_ref[...])):
+        weight = jnp.sum(jnp.where(lane == own, mixing, 0.0), axis=1, keepdims=True)
+        mixed = mixed + weight * value.astype(jnp.float32)
+    out_ref[...] = rms_norm(mixed, gains_ref[4:5]).astype(jnp.bfloat16)
+
+
+def half_columns(values, tok_rows, bits, parity):
+    tokens = values.shape[1]
+    half = tokens // 2
+    place = lax.broadcasted_iota(jnp.int32, (half, tokens), 0) + parity * half
+    token = lax.broadcasted_iota(jnp.int32, (half, tokens), 1)
+    here = token_at(place, tok_rows, bits) == token
+    column = jnp.sum(jnp.where(here, values.astype(jnp.float32), 0.0), axis=1, keepdims=True)
+    return column.astype(jnp.int32)
+
+
+def head_kernel(rows_ref, columns_ref, down_ref, *refs):
+    *weight_refs, stats_ref = refs
+    my_index = lax.axis_index("tensor")
+    rows = rows_ref[...]
+    tokens = rows.shape[0]
+    wanted = columns_ref[0][:, 0:1].astype(jnp.int32)
+    latent = lax.dot_general(rows, down_ref[...], TRANSPOSED, preferred_element_type=jnp.float32)
+    latent = latent.astype(jnp.bfloat16)
+    lane = lax.broadcasted_iota(jnp.int32, (tokens, 128), 1)
+    packed = jnp.zeros((tokens, 128), jnp.float32)
+    base, policy, matches = [], [], []
+    for index, head_ref, up_ref in zip((my_index, my_index ^ 1), weight_refs[:2], weight_refs[2:]):
+        logits = jnp.dot(rows, head_ref[...], preferred_element_type=jnp.float32)
+        base.append(logits)
+        change = jnp.dot(latent, up_ref[...], preferred_element_type=jnp.float32)
+        policy.append(logits + change)
+        column = lax.broadcasted_iota(jnp.int32, logits.shape, 1)
+        matches.append(column == wanted - index * logits.shape[1])
+    is_target = jnp.concatenate(matches, axis=1)
+    for at, parts in enumerate((base, policy)):
+        logits = jnp.concatenate(parts, axis=1)
+        top_value = jnp.max(logits, axis=1, keepdims=True)
+        exp_total = jnp.sum(jnp.exp(logits - top_value), axis=1, keepdims=True)
+        picked = jnp.sum(jnp.where(is_target, logits, 0.0), axis=1, keepdims=True)
+        for kind, value in enumerate((top_value, exp_total, picked)):
+            packed = jnp.where(lane == 2 * kind + at, value, packed)
+    stats_ref[...] = packed.T[:8]
+
+
+def merge_kernel(one_ref, two_ref, out_ref):
+    one, two = one_ref[...], two_ref[...]
+    ceiling = jnp.maximum(one[0:2], two[0:2])
+    exp_total = one[2:4] * jnp.exp(one[0:2] - ceiling) + two[2:4] * jnp.exp(two[0:2] - ceiling)
+    out_ref[...] = jnp.concatenate([ceiling, exp_total, one[4:8] + two[4:8]], axis=0)
+
+
+def result_kernel(tok_rows, own_ref, other_ref, columns_ref, policy_ref, ratio_ref, sums_ref):
+    half = own_ref.shape[1]
+    picked = []
+    for ref, columns in ((own_ref, columns_ref[1]), (other_ref, columns_ref[2])):
+        stats = ref[...]
+        log_probs = stats[4:6] - stats[0:2] - jnp.log(stats[2:4])
+        policy = log_probs[1:2]
+        rows = jnp.concatenate([policy, policy - log_probs[0:1]] * 4, axis=0)
+        picked.append(
+            jnp.dot(
+                rows,
+                columns,
+                precision=lax.Precision.HIGHEST,
+                preferred_element_type=jnp.float32,
+            )
+        )
+    policy_ref[...] = picked[0][0:1, :tok_rows]
+    ratio_ref[...] = picked[0][1:2, :tok_rows]
+    sums_ref[...] = (picked[0] + picked[1])[1:2, 64 : 64 + SEQS]
+
+
+def call(kernel, shapes, *operands, flops=0):
+    size = sum(operand.size * operand.dtype.itemsize for operand in operands)
+    return pl.pallas_call(
+        kernel,
+        out_shape=shapes,
+        compiler_params=pltpu.CompilerParams(vmem_limit_bytes=32 << 20),
+        cost_estimate=pl.CostEstimate(flops=flops, bytes_accessed=size, transcendentals=0),
+    )(*operands)
+
+
+def dense_on_device(
+    hidden_in,
+    expert_ids,
+    gate_weights,
+    targets,
+    seq_ids,
+    moe_gain,
+    w_gate,
+    w_up,
+    w_down,
+    final_gain,
+    head_weight,
+    adapter_down,
+    adapter_up,
+):
+    tok_rows, features = hidden_in.shape
+    devices = lax.axis_size("tensor")
+    bits = devices.bit_length() - 1
+    half = devices * tok_rows // 2
+    my_index = lax.axis_index("tensor")
+    far = [(b, (1 << b) + 1) for b in range(bits - 1, 0, -1)]
+
+    def array(dtype, *shape):
+        return jax.ShapeDtypeStruct(shape, dtype)
+
+    rows = hidden_in
+    flags = call(flags_kernel, array(jnp.int32, 8, 128), flops=ROUND_FLOPS)
+    for b, mask in far:
+        rows = call(
+            functools.partial(order_kernel, b),
+            array(rows.dtype, 2 * rows.shape[0], features),
+            flags,
+            rows,
+            exchange(rows, mask),
+            flops=ROUND_FLOPS * (2 * rows.shape[0] < half),
+        )
+    gains, down, mixing, columns = call(
+        lambda *refs: prepare_kernel(tok_rows, bits, *refs),
+        [
+            array(jnp.float32, 8, features),
+            array(jnp.bfloat16, *adapter_down.shape[::-1]),
+            array(jnp.float32, 8, 128),
+            array(jnp.float32, 3, half, 128),
+        ],
+        expert_ids.T,
+        gate_weights.T,
+        targets[None],
+        seq_ids[None],
+        moe_gain[None],
+        final_gain[None],
+        adapter_down.T,
+    )
+
+    units = [w_gate.T, w_up.T, w_down]
+    total, sent = call(
+        expert_kernel,
+        [array(dtype, half, features) for dtype in (jnp.float32, jnp.bfloat16)],
+        rows,
+        gains,
+        *(exchange(unit, 1) for unit in units),
+        *units,
+        flops=6 * devices * tok_rows * features * w_gate.shape[1],
+    )
+    masks = [mask for _, mask in far[::-1]]
+    for mask in masks[:-1]:
+        mixing, sent = lax.optimization_barrier((mixing, sent))
+        total = total + exchange(sent, mask).astype(jnp.float32)
+        mixing = mixing + exchange(mixing, mask)
+        sent = total.astype(jnp.bfloat16)
+    mixing, sent = lax.optimization_barrier((mixing, sent))
+    final_input = call(
+        norm_kernel,
+        array(jnp.bfloat16, half, features),
+        total,
+        exchange(sent, masks[-1]),
+        mixing,
+        exchange(mixing, masks[-1]),
+        rows,
+        gains,
+    )
+
+    stats = call(
+        head_kernel,
+        array(jnp.float32, 8, half),
+        final_input,
+        columns,
+        down,
+        head_weight,
+        exchange(head_weight, 1),
+        adapter_up,
+        exchange(adapter_up, 1),
+        flops=2 * devices * tok_rows * features * head_weight.shape[1],
+    )
+    for mask in masks:
+        stats = call(merge_kernel, array(jnp.float32, 8, half), stats, exchange(stats, mask))
+    policy_own, ratio_own, seq_sums = call(
+        lambda *refs: result_kernel(tok_rows, *refs),
+        [array(jnp.float32, 1, tok_rows)] * 2 + [array(jnp.float32, 1, SEQS)],
+        stats,
+        exchange(stats, 1),
+        columns,
+    )
+    return (policy_own[0], ratio_own[0], seq_sums[0])
+
+
 def solution(mesh):
     in_specs = (
         P(("dp", "tensor"), None),
@@ -159,6 +465,13 @@
         P(None, "tensor"),
     )
     out_specs = (P(("dp", "tensor")), P(("dp", "tensor")), P("dp"))
+    devices = mesh.shape["tensor"]
+
+    def on_device(hidden_in, expert_ids, *others):
+        both_experts = expert_ids.shape[1] == 2 and devices == 2 * SPLIT
+        step = dense_on_device if both_experts else routed_on_device
+        return step(hidden_in, expert_ids, *others)
+
     return jax.shard_map(
         on_device, mesh=mesh, in_specs=in_specs, out_specs=out_specs, check_vma=False
     )

time: 79.6 us -> 33.3 us (0.42)
  blocking collectives: 55.2 us -> 0 us
  starting transfers between devices: 3.41 us -> 16.1 us
  local copies, waits for them, and re-layouts: 5.63 us -> 0.72 us
  matrix products: 4.76 us -> 0 us
  waiting for transfers between devices: 8.32 us -> 12.2 us
  Pallas kernels: 0 us -> 3.32 us
  other arithmetic: 0.98 us -> 0.02 us
    ppermute x0 -> x14, starting transfers between devices: none -> 16.1 us  [exchange(): lax.ppermute(values, 'tensor', [(i, i ^ mask) for i in range(devices)])]
    pmax x1 -> x0, blocking collectives: 14.8 us -> none  [on_device(): ceiling = lax.pmax(maxima, 'tensor')]
    all_gather x1 -> x0, blocking collectives: 13.9 us -> none  [on_device(): shard_rows = lax.all_gather(final_input, 'tensor', axis=0, tiled=True)]
    psum x1 -> x0, blocking collectives: 13.6 us -> none  [on_device(): lax.psum((exp_sums * jnp.exp(maxima - ceiling), target_logits), 'tensor')]
    all_to_all x1 -> x0, blocking collectives: 12.9 us -> none  [on_device(): lax.all_to_all(outgoing, 'tensor', split_axis=0, concat_axis=0, tiled=True)]
    ppermute x0 -> x14, waiting for transfers between devices: none -> 12.2 us  [exchange(): lax.ppermute(values, 'tensor', [(i, i ^ mask) for i in range(devices)])]
    all_to_all x1 -> x0, waiting for transfers between devices: 8.32 us -> none  [expert_piece(): lax.all_to_all(partial_value.reshape(arrived.shape), 'tensor', split_axis...]
    dot_general x7 -> x0, matrix products: 4.76 us -> none  [the longest x1 1.45 us: expert_piece(): gate_proj = jnp.dot(flat_rows, w_gate, preferred_element_type=jnp.float32)]
  transfers between devices with their start and end apart: 1 -> 14, of which waited for: 1 -> 7; matrix products, arithmetic and copies ran while one was open for 0% -> 0% of each run, Pallas kernels for 0% -> 5%
where the time goes in v3:
time: 33.3 us; the launch traced here: 33.2 us
  starting transfers between devices  16.1 us (48%)
  waiting for transfers between devices  12.2 us (37%)
  Pallas kernels  3.32 us (10%)
  between operations  0.83 us (2%)
  local copies, waits for them, and re-layouts  0.72 us (2%)
    ppermute x14, starting transfers between devices, exchange(): lax.ppermute(values, 'tensor', [(i, i ^ mask) for i in range(devices)])  16.1 us
    ppermute x14, waiting for transfers between devices, exchange(): lax.ppermute(values, 'tensor', [(i, i ^ mask) for i in range(devices)])  12.2 us
    pallas_call x10, Pallas kernels, call(): pl.pallas_call(kernel, out_shape=shapes, compiler_params=pltpu.CompilerPa...  3.32 us
    unnamed x26, local copies, waits for them, and re-layouts  0.72 us
  transfers between devices with their start and end apart: 14, of which 7 were waited for; matrix products, arithmetic and copies ran while one was open for 0% of the time, Pallas kernels for 5%

profile of v3, /device:TPU:0, one launch (start us, length us, event | category | flops | bytes accessed | tf_op | source)
XLA Modules:
  0.0 33.2 jit_solution(13576676044065826788)
XLA Ops:
  0.6 3.5 %collective-permute-start = (bf16[8,1024]{1,0:T(8,128)(2,1)}, bf16[8,1024]{1,0:T(8,128)(2,1)S(1)}, u32[]{:S(2)}, u32[]{:S(2)}) collective-permute-start(bf16[8,1024]{1,0:T(8,128)(2,1)} %mine_ref.1), channel_id=1, source_target_pairs={{0,5},{1,4},{2,7},{3,6},{4,1},{5,0},{6,3},{7,2},{8,13},{9,12},{10,... | collective-permute-start | bytes 49160 | tf_op jit(solution)/shard_map/ppermute | solution.py:152
  4.2 0.7 %collective-permute-start.2 = (bf16[352,1024]{1,0:T(8,128)(2,1)}, bf16[352,1024]{1,0:T(8,128)(2,1)S(1)}, u32[]{:S(2)}, u32[]{:S(2)}) collective-permute-start(bf16[352,1024]{1,0:T(8,128)(2,1)} %bitcast.12), channel_id=1, source_target_pairs={{0,1},{1,0},{2,3},{3,2},{4,5},{5,4},{6,7},{7,6},{8,9},{9,8},{10,11... | collective-permute-start | bytes 2162696 | tf_op jit(solution)/shard_map/ppermute | solution.py:152
  4.8 0.0 collective-permute-start.3
  4.9 0.5 %collective-permute-start.4 = (bf16[352,1024]{1,0:T(8,128)(2,1)}, bf16[352,1024]{1,0:T(8,128)(2,1)S(1)}, u32[]{:S(2)}, u32[]{:S(2)}) collective-permute-start(bf16[352,1024]{1,0:T(8,128)(2,1)} %refs_5_.1), channel_id=1, source_target_pairs={{0,1},{1,0},{2,3},{3,2},{4,5},{5,4},{6,7},{7,6},{8,9},{9,8},{10,11... | collective-permute-start | bytes 2162696 | tf_op jit(solution)/shard_map/ppermute | solution.py:152
  5.4 0.5 %collective-permute-done.other_ref = bf16[8,1024]{1,0:T(8,128)(2,1)S(1)} collective-permute-done((bf16[8,1024]{1,0:T(8,128)(2,1)}, bf16[8,1024]{1,0:T(8,128)(2,1)S(1)}, u32[]{:S(2)}, u32[]{:S(2)}) %collective-permute-start) | collective-permute-done | bytes 16416 | tf_op jit(solution)/shard_map/ppermute | solution.py:152
  5.8 0.0 copy-start.1
  5.8 0.0 copy-start.2
  5.9 0.0 copy-start.3
  5.9 2.0 %collective-permute-start.1 = (bf16[16,1024]{1,0:T(8,128)(2,1)S(1)}, bf16[16,1024]{1,0:T(8,128)(2,1)S(1)}, u32[]{:S(2)}, u32[]{:S(2)}) collective-permute-start(bf16[16,1024]{1,0:T(8,128)(2,1)S(1)} %shard_map.149.mine_ref), channel_id=1, source_target_pairs={{0,3},{1,2},{2,1},{3,0},{4,7},{5,6},{6,5},{7,4},{8,11},{9,10},{10,... | collective-permute-start | bytes 98312 | tf_op jit(solution)/shard_map/ppermute | solution.py:152
  7.9 0.6 %copy-done.7 = f32[1024]{0:T(1024)S(1)} copy-done((f32[1024]{0:T(1024)S(1)}, f32[1024]{0:T(1024)}, u32[]{:S(2)}) %copy-start.7) | copy-done | bytes 4120
  8.6 0.0 copy-done.6
  8.6 0.0 copy-done.8
  8.6 0.1 shard_map.151
  8.7 0.7 %collective-permute-done.1.other_ref = bf16[16,1024]{1,0:T(8,128)(2,1)S(1)} collective-permute-done((bf16[16,1024]{1,0:T(8,128)(2,1)S(1)}, bf16[16,1024]{1,0:T(8,128)(2,1)S(1)}, u32[]{:S(2)}, u32[]{:S(2)}) %collective-permute-start.1) | collective-permute-done | bytes 32800 | tf_op jit(solution)/shard_map/ppermute | solution.py:152
  9.6 0.0 copy-start
  9.6 1.3 %shard_map.152 = (f32[32,1024]{1,0:T(8,128)S(1)}, bf16[32,1024]{1,0:T(8,128)(2,1)S(1)}) custom-call(bf16[32,1024]{1,0:T(8,128)(2,1)S(1)} %shard_map.150.rows_ref, f32[8,1024]{1,0:T(8,128)S(1)} %get-tuple-element.16.gains_ref, bf16[352,1024]{1,0:T(8,128)(2,1)S(1)} %collective-permute-done.2.refs_0_, bf16[352,1024]{1,0:T(8,128)(2,1)S(1)} %collective-permute-done.3.refs_1_, ...), custom_call_target="tpu_custom_call" | custom-call | flops 138412032 | bytes 4423680 | tf_op jit(solution)/shard_map/pallas_call | solution.py:338
  10.9 1.9 %collective-permute-start.5 = (bf16[32,1024]{1,0:T(8,128)(2,1)S(1)}, bf16[32,1024]{1,0:T(8,128)(2,1)S(1)}, u32[]{:S(2)}, u32[]{:S(2)}) collective-permute-start(bf16[32,1024]{1,0:T(8,128)(2,1)S(1)} %get-tuple-element.20), channel_id=1, source_target_pairs={{0,3},{1,2},{2,1},{3,0},{4,7},{5,6},{6,5},{7,4},{8,11},{9,10},{10,... | collective-permute-start | bytes 196616 | tf_op jit(solution)/shard_map/ppermute | solution.py:152
  12.7 0.1 collective-permute-start.6
  12.8 3.0 %collective-permute-done.6 = f32[8,128]{1,0:T(8,128)S(1)} collective-permute-done((f32[8,128]{1,0:T(8,128)S(1)}, f32[8,128]{1,0:T(8,128)S(1)}, u32[]{:S(2)}, u32[]{:S(2)}) %collective-permute-start.6) | collective-permute-done | bytes 4128 | tf_op jit(solution)/shard_map/ppermute | solution.py:152
  15.8 3.1 %collective-permute-start.7 = (bf16[32,1024]{1,0:T(8,128)(2,1)S(1)}, bf16[32,1024]{1,0:T(8,128)(2,1)S(1)}, u32[]{:S(2)}, u32[]{:S(2)}) collective-permute-start(bf16[32,1024]{1,0:T(8,128)(2,1)S(1)} %get-tuple-element.22), channel_id=1, source_target_pairs={{0,5},{1,4},{2,7},{3,6},{4,1},{5,0},{6,3},{7,2},{8,13},{9,12},{10,... | collective-permute-start | bytes 196616 | tf_op jit(solution)/shard_map/ppermute | solution.py:152
  18.9 0.1 collective-permute-start.10
  19.0 0.7 %collective-permute-start.8 = (f32[8,128]{1,0:T(8,128)S(1)}, f32[8,128]{1,0:T(8,128)S(1)}, u32[]{:S(2)}, u32[]{:S(2)}) collective-permute-start(f32[8,128]{1,0:T(8,128)S(1)} %add.7.mixing_ref), channel_id=1, source_target_pairs={{0,5},{1,4},{2,7},{3,6},{4,1},{5,0},{6,3},{7,2},{8,13},{9,12},{10,... | collective-permute-start | bytes 12296 | tf_op jit(solution)/shard_map/ppermute | solution.py:152
  19.7 3.3 %collective-permute-done.8.mixing_arrived_ref = f32[8,128]{1,0:T(8,128)S(1)} collective-permute-done((f32[8,128]{1,0:T(8,128)S(1)}, f32[8,128]{1,0:T(8,128)S(1)}, u32[]{:S(2)}, u32[]{:S(2)}) %collective-permute-start.8) | collective-permute-done | bytes 4128 | tf_op jit(solution)/shard_map/ppermute | solution.py:152
  23.0 0.3 shard_map.153.rows_ref
  23.3 0.8 %shard_map.154.one_ref = f32[8,32]{1,0:T(8,128)S(1)} custom-call(bf16[32,1024]{1,0:T(8,128)(2,1)S(1)} %shard_map.153.rows_ref, f32[3,32,128]{2,1,0:T(8,128)S(1)} %get-tuple-element.24.columns_ref.refs_2_, bf16[64,1024]{1,0:T(8,128)(2,1)S(1)} %get-tuple-element.25.down_ref, bf16[1024,512]{1,0:T(8,128)(2,1)S(1)} %copy-done, ...), custom_call_target="tpu_custom_call" | custom-call | flops 67108864 | bytes 2473984 | tf_op jit(solution)/shard_map/pallas_call | solution.py:338
  24.1 1.1 %collective-permute-start.11 = (f32[8,32]{1,0:T(8,128)S(1)}, f32[8,32]{1,0:T(8,128)S(1)}, u32[]{:S(2)}, u32[]{:S(2)}) collective-permute-start(f32[8,32]{1,0:T(8,128)S(1)} %shard_map.154.one_ref), channel_id=1, source_target_pairs={{0,3},{1,2},{2,1},{3,0},{4,7},{5,6},{6,5},{7,4},{8,11},{9,10},{10,... | collective-permute-start | bytes 3080 | tf_op jit(solution)/shard_map/ppermute | solution.py:152
  25.2 2.0 %collective-permute-done.11.two_ref = f32[8,32]{1,0:T(8,128)S(1)} collective-permute-done((f32[8,32]{1,0:T(8,128)S(1)}, f32[8,32]{1,0:T(8,128)S(1)}, u32[]{:S(2)}, u32[]{:S(2)}) %collective-permute-start.11) | collective-permute-done | bytes 1056 | tf_op jit(solution)/shard_map/ppermute | solution.py:152
  27.2 2.1 %collective-permute-start.12 = (f32[8,32]{1,0:T(8,128)S(1)}, f32[8,32]{1,0:T(8,128)S(1)}, u32[]{:S(2)}, u32[]{:S(2)}) collective-permute-start(f32[8,32]{1,0:T(8,128)S(1)} %shard_map.155.one_ref), channel_id=1, source_target_pairs={{0,5},{1,4},{2,7},{3,6},{4,1},{5,0},{6,3},{7,2},{8,13},{9,12},{10,... | collective-permute-start | bytes 3080 | tf_op jit(solution)/shard_map/ppermute | solution.py:152
  29.2 1.9 %collective-permute-done.12.two_ref = f32[8,32]{1,0:T(8,128)S(1)} collective-permute-done((f32[8,32]{1,0:T(8,128)S(1)}, f32[8,32]{1,0:T(8,128)S(1)}, u32[]{:S(2)}, u32[]{:S(2)}) %collective-permute-start.12) | collective-permute-done | bytes 1056 | tf_op jit(solution)/shard_map/ppermute | solution.py:152
  31.2 0.4 %collective-permute-start.13 = (f32[8,32]{1,0:T(8,128)S(1)}, f32[8,32]{1,0:T(8,128)S(1)}, u32[]{:S(2)}, u32[]{:S(2)}) collective-permute-start(f32[8,32]{1,0:T(8,128)S(1)} %shard_map.156.refs_0_), channel_id=1, source_target_pairs={{0,1},{1,0},{2,3},{3,2},{4,5},{5,4},{6,7},{7,6},{8,9},{9,8},{10,11... | collective-permute-start | bytes 3080 | tf_op jit(solution)/shard_map/ppermute | solution.py:152
  31.6 0.8 %collective-permute-done.13.refs_1_ = f32[8,32]{1,0:T(8,128)S(1)} collective-permute-done((f32[8,32]{1,0:T(8,128)S(1)}, f32[8,32]{1,0:T(8,128)S(1)}, u32[]{:S(2)}, u32[]{:S(2)}) %collective-permute-start.13) | collective-permute-done | bytes 1056 | tf_op jit(solution)/shard_map/ppermute | solution.py:152
  32.4 0.7 %shard_map.157 = (f32[1,8]{1,0:T(1,128)}, f32[1,8]{1,0:T(1,128)}, f32[1,16]{1,0:T(1,128)}) custom-call(f32[8,32]{1,0:T(8,128)S(1)} %shard_map.156.refs_0_, f32[8,32]{1,0:T(8,128)S(1)} %collective-permute-done.13.refs_1_, f32[3,32,128]{2,1,0:T(8,128)S(1)} %get-tuple-element.24.columns_ref.refs_2_), custom_call_target="tpu_custom_call" | custom-call | bytes 51200 | tf_op jit(solution)/shard_map/pallas_call | solution.py:338
  (34 shorter events, 0.2 us)
Async XLA Ops:
  0.6 5.2 %collective-permute-start = (bf16[8,1024]{1,0:T(8,128)(2,1)}, bf16[8,1024]{1,0:T(8,128)(2,1)S(1)}, u32[]{:S(2)}, u32[]{:S(2)}) collective-permute-start(bf16[8,1024]{1,0:T(8,128)(2,1)} %mine_ref.1), channel_id=1, source_target_pairs={{0,5},{1,4},{2,7},{3,6},{4,1},{5,0},{6,3},{7,2},{8,13},{9,12},{10,... | collective-permute-start | bytes 49160 | tf_op jit(solution)/shard_map/ppermute | solution.py:152
  4.2 5.4 %collective-permute-start.2 = (bf16[352,1024]{1,0:T(8,128)(2,1)}, bf16[352,1024]{1,0:T(8,128)(2,1)S(1)}, u32[]{:S(2)}, u32[]{:S(2)}) collective-permute-start(bf16[352,1024]{1,0:T(8,128)(2,1)} %bitcast.12), channel_id=1, source_target_pairs={{0,1},{1,0},{2,3},{3,2},{4,5},{5,4},{6,7},{7,6},{8,9},{9,8},{10,11... | collective-permute-start | bytes 2162696 | tf_op jit(solution)/shard_map/ppermute | solution.py:152
  4.8 1.0 %copy-start.12 = (bf16[8,1024]{1,0:T(8,128)(2,1)S(1)}, bf16[8,1024]{1,0:T(8,128)(2,1)}, u32[]{:S(2)}) copy-start(bf16[8,1024]{1,0:T(8,128)(2,1)} %mine_ref.1) | copy-start | bytes 49156
  4.8 4.7 %collective-permute-start.3 = (bf16[352,1024]{1,0:T(8,128)(2,1)}, bf16[352,1024]{1,0:T(8,128)(2,1)S(1)}, u32[]{:S(2)}, u32[]{:S(2)}) collective-permute-start(bf16[352,1024]{1,0:T(8,128)(2,1)} %bitcast.14), channel_id=1, source_target_pairs={{0,1},{1,0},{2,3},{3,2},{4,5},{5,4},{6,7},{7,6},{8,9},{9,8},{10,11... | collective-permute-start | bytes 2162696 | tf_op jit(solution)/shard_map/ppermute | solution.py:152
  4.9 4.7 %collective-permute-start.4 = (bf16[352,1024]{1,0:T(8,128)(2,1)}, bf16[352,1024]{1,0:T(8,128)(2,1)S(1)}, u32[]{:S(2)}, u32[]{:S(2)}) collective-permute-start(bf16[352,1024]{1,0:T(8,128)(2,1)} %refs_5_.1), channel_id=1, source_target_pairs={{0,1},{1,0},{2,3},{3,2},{4,5},{5,4},{6,7},{7,6},{8,9},{9,8},{10,11... | collective-permute-start | bytes 2162696 | tf_op jit(solution)/shard_map/ppermute | solution.py:152
  5.4 17.9 %collective-permute-start.9 = (bf16[1024,512]{1,0:T(8,128)(2,1)}, bf16[1024,512]{1,0:T(8,128)(2,1)S(1)}, u32[]{:S(2)}, u32[]{:S(2)}) collective-permute-start(bf16[1024,512]{1,0:T(8,128)(2,1)} %refs_0_.1), channel_id=1, source_target_pairs={{0,1},{1,0},{2,3},{3,2},{4,5},{5,4},{6,7},{7,6},{8,9},{9,8},{10,11... | collective-permute-start | bytes 3145736 | tf_op jit(solution)/shard_map/ppermute | solution.py:152
  5.4 2.5 %copy-start.4 = (bf16[1024,64]{0,1:T(8,128)(2,1)S(1)}, bf16[1024,64]{0,1:T(8,128)(2,1)}, u32[]{:S(2)}) copy-start(bf16[1024,64]{0,1:T(8,128)(2,1)} %param.24) | copy-start | bytes 393220
  5.8 2.1 %copy-start.9 = (f32[8,2]{0,1:T(2,128)S(1)}, f32[8,2]{0,1:T(2,128)}, u32[]{:S(2)}) copy-start(f32[8,2]{0,1:T(2,128)} %param.15) | copy-start | bytes 196
  5.8 2.1 %copy-start.10 = (s32[64]{0:T(128)S(1)}, s32[64]{0:T(128)}, u32[]{:S(2)}) copy-start(s32[64]{0:T(128)} %param.16) | copy-start | bytes 772
  5.8 2.1 %copy-start.11 = (s32[64]{0:T(128)S(1)}, s32[64]{0:T(128)}, u32[]{:S(2)}) copy-start(s32[64]{0:T(128)} %param.17) | copy-start | bytes 772
  5.8 3.7 %copy-start.1 = (bf16[1024,352]{0,1:T(8,128)(2,1)S(1)}, bf16[1024,352]{0,1:T(8,128)(2,1)}, u32[]{:S(2)}) copy-start(bf16[1024,352]{0,1:T(8,128)(2,1)} %param.19) | copy-start | bytes 2162692
  5.8 3.7 %copy-start.2 = (bf16[1024,352]{0,1:T(8,128)(2,1)S(1)}, bf16[1024,352]{0,1:T(8,128)(2,1)}, u32[]{:S(2)}) copy-start(bf16[1024,352]{0,1:T(8,128)(2,1)} %param.20) | copy-start | bytes 2162692
  5.9 3.7 %copy-start.3 = (bf16[352,1024]{1,0:T(8,128)(2,1)S(1)}, bf16[352,1024]{1,0:T(8,128)(2,1)}, u32[]{:S(2)}) copy-start(bf16[352,1024]{1,0:T(8,128)(2,1)} %refs_5_.1) | copy-start | bytes 2162692
  5.9 3.6 %collective-permute-start.1 = (bf16[16,1024]{1,0:T(8,128)(2,1)S(1)}, bf16[16,1024]{1,0:T(8,128)(2,1)S(1)}, u32[]{:S(2)}, u32[]{:S(2)}) collective-permute-start(bf16[16,1024]{1,0:T(8,128)(2,1)S(1)} %shard_map.149.mine_ref), channel_id=1, source_target_pairs={{0,3},{1,2},{2,1},{3,0},{4,7},{5,6},{6,5},{7,4},{8,11},{9,10},{10,... | collective-permute-start | bytes 98312 | tf_op jit(solution)/shard_map/ppermute | solution.py:152
  7.9 0.7 %copy-start.7 = (f32[1024]{0:T(1024)S(1)}, f32[1024]{0:T(1024)}, u32[]{:S(2)}) copy-start(f32[1024]{0:T(1024)} %param.22) | copy-start | bytes 12292
  7.9 0.7 %copy-start.6 = (f32[1024]{0:T(1024)S(1)}, f32[1024]{0:T(1024)}, u32[]{:S(2)}) copy-start(f32[1024]{0:T(1024)} %param.18) | copy-start | bytes 12292
  7.9 0.7 %copy-start.8 = (s32[8,2]{0,1:T(2,128)S(1)}, s32[8,2]{0,1:T(2,128)}, u32[]{:S(2)}) copy-start(s32[8,2]{0,1:T(2,128)} %param.14) | copy-start | bytes 196
  9.6 13.7 %copy-start = (bf16[1024,512]{1,0:T(8,128)(2,1)S(1)}, bf16[1024,512]{1,0:T(8,128)(2,1)}, u32[]{:S(2)}) copy-start(bf16[1024,512]{1,0:T(8,128)(2,1)} %refs_0_.1) | copy-start | bytes 3145732
  10.9 4.9 %collective-permute-start.5 = (bf16[32,1024]{1,0:T(8,128)(2,1)S(1)}, bf16[32,1024]{1,0:T(8,128)(2,1)S(1)}, u32[]{:S(2)}, u32[]{:S(2)}) collective-permute-start(bf16[32,1024]{1,0:T(8,128)(2,1)S(1)} %get-tuple-element.20), channel_id=1, source_target_pairs={{0,3},{1,2},{2,1},{3,0},{4,7},{5,6},{6,5},{7,4},{8,11},{9,10},{10,... | collective-permute-start | bytes 196616 | tf_op jit(solution)/shard_map/ppermute | solution.py:152
  12.7 3.1 %collective-permute-start.6 = (f32[8,128]{1,0:T(8,128)S(1)}, f32[8,128]{1,0:T(8,128)S(1)}, u32[]{:S(2)}, u32[]{:S(2)}) collective-permute-start(f32[8,128]{1,0:T(8,128)S(1)} %get-tuple-element.21), channel_id=1, source_target_pairs={{0,3},{1,2},{2,1},{3,0},{4,7},{5,6},{6,5},{7,4},{8,11},{9,10},{10,... | collective-permute-start | bytes 12296 | tf_op jit(solution)/shard_map/ppermute | solution.py:152
  15.8 3.1 %copy-start.5 = (bf16[64,512]{1,0:T(8,128)(2,1)S(1)}, bf16[64,512]{1,0:T(8,128)(2,1)}, u32[]{:S(2)}) copy-start(bf16[64,512]{1,0:T(8,128)(2,1)} %refs_2_.1) | copy-start | bytes 196612
  15.8 7.2 %collective-permute-start.7 = (bf16[32,1024]{1,0:T(8,128)(2,1)S(1)}, bf16[32,1024]{1,0:T(8,128)(2,1)S(1)}, u32[]{:S(2)}, u32[]{:S(2)}) collective-permute-start(bf16[32,1024]{1,0:T(8,128)(2,1)S(1)} %get-tuple-element.22), channel_id=1, source_target_pairs={{0,5},{1,4},{2,7},{3,6},{4,1},{5,0},{6,3},{7,2},{8,13},{9,12},{10,... | collective-permute-start | bytes 196616 | tf_op jit(solution)/shard_map/ppermute | solution.py:152
  18.9 4.4 %collective-permute-start.10 = (bf16[64,512]{1,0:T(8,128)(2,1)S(1)}, bf16[64,512]{1,0:T(8,128)(2,1)S(1)}, u32[]{:S(2)}, u32[]{:S(2)}) collective-permute-start(bf16[64,512]{1,0:T(8,128)(2,1)S(1)} %copy-done.5), channel_id=1, source_target_pairs={{0,1},{1,0},{2,3},{3,2},{4,5},{5,4},{6,7},{7,6},{8,9},{9,8},{10,11... | collective-permute-start | bytes 196616 | tf_op jit(solution)/shard_map/ppermute | solution.py:152
  19.0 4.0 %collective-permute-start.8 = (f32[8,128]{1,0:T(8,128)S(1)}, f32[8,128]{1,0:T(8,128)S(1)}, u32[]{:S(2)}, u32[]{:S(2)}) collective-permute-start(f32[8,128]{1,0:T(8,128)S(1)} %add.7.mixing_ref), channel_id=1, source_target_pairs={{0,5},{1,4},{2,7},{3,6},{4,1},{5,0},{6,3},{7,2},{8,13},{9,12},{10,... | collective-permute-start | bytes 12296 | tf_op jit(solution)/shard_map/ppermute | solution.py:152
  24.1 3.1 %collective-permute-start.11 = (f32[8,32]{1,0:T(8,128)S(1)}, f32[8,32]{1,0:T(8,128)S(1)}, u32[]{:S(2)}, u32[]{:S(2)}) collective-permute-start(f32[8,32]{1,0:T(8,128)S(1)} %shard_map.154.one_ref), channel_id=1, source_target_pairs={{0,3},{1,2},{2,1},{3,0},{4,7},{5,6},{6,5},{7,4},{8,11},{9,10},{10,... | collective-permute-start | bytes 3080 | tf_op jit(solution)/shard_map/ppermute | solution.py:152
  27.2 4.0 %collective-permute-start.12 = (f32[8,32]{1,0:T(8,128)S(1)}, f32[8,32]{1,0:T(8,128)S(1)}, u32[]{:S(2)}, u32[]{:S(2)}) collective-permute-start(f32[8,32]{1,0:T(8,128)S(1)} %shard_map.155.one_ref), channel_id=1, source_target_pairs={{0,5},{1,4},{2,7},{3,6},{4,1},{5,0},{6,3},{7,2},{8,13},{9,12},{10,... | collective-permute-start | bytes 3080 | tf_op jit(solution)/shard_map/ppermute | solution.py:152
  31.2 1.2 %collective-permute-start.13 = (f32[8,32]{1,0:T(8,128)S(1)}, f32[8,32]{1,0:T(8,128)S(1)}, u32[]{:S(2)}, u32[]{:S(2)}) collective-permute-start(f32[8,32]{1,0:T(8,128)S(1)} %shard_map.156.refs_0_), channel_id=1, source_target_pairs={{0,1},{1,0},{2,3},{3,2},{4,5},{5,4},{6,7},{7,6},{8,9},{9,8},{10,11... | collective-permute-start | bytes 3080 | tf_op jit(solution)/shard_map/ppermute | solution.py:152

commit v4 on v3

--- a/solution.py
+++ b/solution.py
@@ -210,14 +210,19 @@
         )
         for expert in range(experts)
     ]
-    rows = jnp.concatenate(rows + [jnp.zeros((8 - experts, tok_rows), jnp.float32)], axis=0)
-    rows = jnp.concatenate([rows] * (128 // tok_rows), axis=1)
-    at = lax.broadcasted_iota(jnp.int32, (8, 128), 1)
-    token = token_at(at + parity * half, tok_rows, bits) - my_index * tok_rows
-    mixing_ref[...] = jnp.where((token >= 0) & (token < tok_rows) & (at < half), rows, 0.0)
+    weights = jnp.concatenate(rows, axis=0)
+    high = weights.astype(jnp.bfloat16).astype(jnp.float32)
+    middle = (weights - high).astype(jnp.bfloat16).astype(jnp.float32)
+    low = weights - high - middle
+    rows = [high, middle, low, jnp.zeros((8 - 3 * experts, tok_rows), jnp.float32)]
+    rows = [jnp.concatenate(rows, axis=0), jnp.zeros((8, 128 - tok_rows), jnp.float32)]
+    parts = jnp.concatenate(rows, axis=1).T[:tok_rows]
+    parts = jnp.concatenate([parts, jnp.zeros((tok_rows, 120), jnp.float32)], axis=1)
     row = lax.broadcasted_iota(jnp.int32, (half, 128), 0)
     lane = lax.broadcasted_iota(jnp.int32, (half, 128), 1)
     token = token_at(row + parity * half, tok_rows, bits) - my_index * tok_rows
+    mine = (token >= 0) & (token < tok_rows)
+    mixing_ref[...] = jnp.where(mine, jnp.concatenate([parts] * (half // tok_rows), axis=0), 0.0)
     wanted = half_columns(targets_ref[...], tok_rows, bits, parity)
     own_seq = half_columns(seq_ref[...], tok_rows, bits, parity)
     other_seq = half_columns(seq_ref[...], tok_rows, bits, 1 - parity)
@@ -237,7 +242,7 @@
     out_ref[...] = in_order(late, mine_ref[...], other_ref[...])
 
 
-def expert_kernel(rows_ref, gains_ref, *refs):
+def expert_kernel(rows_ref, gains_ref, mixing_ref, *refs):
     far_refs, near_refs, (total_ref, sent_ref) = refs[0:3], refs[3:6], refs[6:8]
     moe_input = rms_norm(rows_ref[...].astype(jnp.float32), gains_ref[0:1]).astype(jnp.bfloat16)
 
@@ -250,19 +255,21 @@
         return jnp.dot(inner_act, down_ref[...], preferred_element_type=jnp.float32)
 
     total = units(*far_refs) + units(*near_refs)
+    total = jnp.concatenate([total, mixing_ref[...]], axis=1)
     total_ref[...] = total
     sent_ref[...] = total.astype(jnp.bfloat16)
 
 
-def norm_kernel(total_ref, arrived_ref, mixing_ref, mixing_arrived_ref, rows_ref, gains_ref, out_ref):
-    half = out_ref.shape[0]
+def norm_kernel(total_ref, arrived_ref, rows_ref, gains_ref, out_ref):
+    features = out_ref.shape[1]
     expert = lax.axis_index("tensor") // SPLIT
-    mixing = (mixing_ref[...] + mixing_arrived_ref[...]).T[:half]
+    total, arrived = total_ref[...], arrived_ref[...].astype(jnp.float32)
+    mixing = total[:, features:] + arrived[:, features:]
     lane = lax.broadcasted_iota(jnp.int32, mixing.shape, 1)
     mixed = rows_ref[...].astype(jnp.float32)
-    for own, value in ((expert, total_ref[...]), (1 - expert, arrived_ref[...])):
-        weight = jnp.sum(jnp.where(lane == own, mixing, 0.0), axis=1, keepdims=True)
-        mixed = mixed + weight * value.astype(jnp.float32)
+    for own, value in ((expert, total), (1 - expert, arrived)):
+        weight = jnp.sum(jnp.where(lane % 2 == own, mixing, 0.0), axis=1, keepdims=True)
+        mixed = mixed + weight * value[:, :features]
     out_ref[...] = rms_norm(mixed, gains_ref[4:5]).astype(jnp.bfloat16)
 
 
@@ -384,7 +391,7 @@
         [
             array(jnp.float32, 8, features),
             array(jnp.bfloat16, *adapter_down.shape[::-1]),
-            array(jnp.float32, 8, 128),
+            array(jnp.float32, half, 128),
             array(jnp.float32, 3, half, 128),
         ],
         expert_ids.T,
@@ -399,27 +406,23 @@
     units = [w_gate.T, w_up.T, w_down]
     total, sent = call(
         expert_kernel,
-        [array(dtype, half, features) for dtype in (jnp.float32, jnp.bfloat16)],
+        [array(dtype, half, features + 128) for dtype in (jnp.float32, jnp.bfloat16)],
         rows,
         gains,
+        mixing,
         *(exchange(unit, 1) for unit in units),
         *units,
         flops=6 * devices * tok_rows * features * w_gate.shape[1],
     )
     masks = [mask for _, mask in far[::-1]]
     for mask in masks[:-1]:
-        mixing, sent = lax.optimization_barrier((mixing, sent))
         total = total + exchange(sent, mask).astype(jnp.float32)
-        mixing = mixing + exchange(mixing, mask)
         sent = total.astype(jnp.bfloat16)
-    mixing, sent = lax.optimization_barrier((mixing, sent))
     final_input = call(
         norm_kernel,
         array(jnp.bfloat16, half, features),
         total,
         exchange(sent, masks[-1]),
-        mixing,
-        exchange(mixing, masks[-1]),
         rows,
         gains,
     )

time: 33.3 us -> 32.5 us (0.976)
  waiting for transfers between devices: 12.2 us -> 9.28 us
  starting transfers between devices: 16.1 us -> 18.3 us
    ppermute x14 -> x12, waiting for transfers between devices: 12.2 us -> 9.28 us  [exchange(): lax.ppermute(values, 'tensor', [(i, i ^ mask) for i in range(devices)])]
    ppermute x14 -> x12, starting transfers between devices: 16.1 us -> 18.3 us  [exchange(): lax.ppermute(values, 'tensor', [(i, i ^ mask) for i in range(devices)])]
  transfers between devices with their start and end apart: 14 -> 12, of which waited for: 7 -> 7; matrix products, arithmetic and copies ran while one was open for 0% -> 0% of each run, Pallas kernels for 5% -> 5%
where the time goes in v4:
time: 32.5 us; the launch traced here: 32.4 us
  starting transfers between devices  18.3 us (56%)
  waiting for transfers between devices  9.28 us (29%)
  Pallas kernels  3.25 us (10%)
  between operations  0.82 us (3%)
  local copies, waits for them, and re-layouts  0.72 us (2%)
    ppermute x12, starting transfers between devices, exchange(): lax.ppermute(values, 'tensor', [(i, i ^ mask) for i in range(devices)])  18.3 us
    ppermute x12, waiting for transfers between devices, exchange(): lax.ppermute(values, 'tensor', [(i, i ^ mask) for i in range(devices)])  9.28 us
    pallas_call x10, Pallas kernels, call(): pl.pallas_call(kernel, out_shape=shapes, compiler_params=pltpu.CompilerPa...  3.25 us
    unnamed x26, local copies, waits for them, and re-layouts  0.72 us
  transfers between devices with their start and end apart: 12, of which 7 were waited for; matrix products, arithmetic and copies ran while one was open for 0% of the time, Pallas kernels for 5%

profile of v4, /device:TPU:0, one launch (start us, length us, event | category | flops | bytes accessed | tf_op | source)
XLA Modules:
  0.0 32.4 jit_solution(15799290800971751847)
XLA Ops:
  0.6 3.5 %collective-permute-start = (bf16[8,1024]{1,0:T(8,128)(2,1)}, bf16[8,1024]{1,0:T(8,128)(2,1)S(1)}, u32[]{:S(2)}, u32[]{:S(2)}) collective-permute-start(bf16[8,1024]{1,0:T(8,128)(2,1)} %mine_ref.1), channel_id=1, source_target_pairs={{0,5},{1,4},{2,7},{3,6},{4,1},{5,0},{6,3},{7,2},{8,13},{9,12},{10,... | collective-permute-start | bytes 49160 | tf_op jit(solution)/shard_map/ppermute | solution.py:152
  4.2 0.7 %collective-permute-start.2 = (bf16[352,1024]{1,0:T(8,128)(2,1)}, bf16[352,1024]{1,0:T(8,128)(2,1)S(1)}, u32[]{:S(2)}, u32[]{:S(2)}) collective-permute-start(bf16[352,1024]{1,0:T(8,128)(2,1)} %bitcast.12), channel_id=1, source_target_pairs={{0,1},{1,0},{2,3},{3,2},{4,5},{5,4},{6,7},{7,6},{8,9},{9,8},{10,11... | collective-permute-start | bytes 2162696 | tf_op jit(solution)/shard_map/ppermute | solution.py:152
  4.8 0.0 collective-permute-start.3
  4.9 0.5 %collective-permute-start.4 = (bf16[352,1024]{1,0:T(8,128)(2,1)}, bf16[352,1024]{1,0:T(8,128)(2,1)S(1)}, u32[]{:S(2)}, u32[]{:S(2)}) collective-permute-start(bf16[352,1024]{1,0:T(8,128)(2,1)} %refs_5_.1), channel_id=1, source_target_pairs={{0,1},{1,0},{2,3},{3,2},{4,5},{5,4},{6,7},{7,6},{8,9},{9,8},{10,11... | collective-permute-start | bytes 2162696 | tf_op jit(solution)/shard_map/ppermute | solution.py:152
  5.4 0.0 collective-permute-start.7
  5.4 0.5 %collective-permute-done.other_ref = bf16[8,1024]{1,0:T(8,128)(2,1)S(1)} collective-permute-done((bf16[8,1024]{1,0:T(8,128)(2,1)}, bf16[8,1024]{1,0:T(8,128)(2,1)S(1)}, u32[]{:S(2)}, u32[]{:S(2)}) %collective-permute-start) | collective-permute-done | bytes 16416 | tf_op jit(solution)/shard_map/ppermute | solution.py:152
  5.8 0.0 copy-start.1
  5.8 0.0 copy-start.2
  5.9 0.0 copy-start.3
  5.9 2.0 %collective-permute-start.1 = (bf16[16,1024]{1,0:T(8,128)(2,1)S(1)}, bf16[16,1024]{1,0:T(8,128)(2,1)S(1)}, u32[]{:S(2)}, u32[]{:S(2)}) collective-permute-start(bf16[16,1024]{1,0:T(8,128)(2,1)S(1)} %shard_map.149.mine_ref), channel_id=1, source_target_pairs={{0,3},{1,2},{2,1},{3,0},{4,7},{5,6},{6,5},{7,4},{8,11},{9,10},{10,... | collective-permute-start | bytes 98312 | tf_op jit(solution)/shard_map/ppermute | solution.py:152
  7.9 0.6 %copy-done.7 = f32[1024]{0:T(1024)S(1)} copy-done((f32[1024]{0:T(1024)S(1)}, f32[1024]{0:T(1024)}, u32[]{:S(2)}) %copy-start.7) | copy-done | bytes 4120
  8.6 0.0 copy-done.6
  8.6 0.0 copy-done.8
  8.6 0.1 shard_map.151
  8.7 0.7 %collective-permute-done.1.other_ref = bf16[16,1024]{1,0:T(8,128)(2,1)S(1)} collective-permute-done((bf16[16,1024]{1,0:T(8,128)(2,1)S(1)}, bf16[16,1024]{1,0:T(8,128)(2,1)S(1)}, u32[]{:S(2)}, u32[]{:S(2)}) %collective-permute-start.1) | collective-permute-done | bytes 32800 | tf_op jit(solution)/shard_map/ppermute | solution.py:152
  9.5 0.0 collective-permute-done.3.refs_1_
  9.6 0.0 copy-start
  9.6 1.3 %shard_map.152 = (f32[32,1152]{1,0:T(8,128)S(1)}, bf16[32,1152]{1,0:T(8,128)(2,1)S(1)}) custom-call(bf16[32,1024]{1,0:T(8,128)(2,1)S(1)} %shard_map.150.rows_ref, f32[8,1024]{1,0:T(8,128)S(1)} %get-tuple-element.12.gains_ref, f32[32,128]{1,0:T(8,128)S(1)} %get-tuple-element.13.mixing_ref, bf16[352,1024]{1,0:T(8,128)(2,1)S(1)} %collective-permute-done.2.refs_0_, ...), custom_call_target="tpu_custom_call" | custom-call | flops 138412032 | bytes 4440064 | tf_op jit(solution)/shard_map/pallas_call | solution.py:345
  10.9 1.9 %collective-permute-start.5 = (bf16[32,1152]{1,0:T(8,128)(2,1)S(1)}, bf16[32,1152]{1,0:T(8,128)(2,1)S(1)}, u32[]{:S(2)}, u32[]{:S(2)}) collective-permute-start(bf16[32,1152]{1,0:T(8,128)(2,1)S(1)} %get-tuple-element.15), channel_id=1, source_target_pairs={{0,3},{1,2},{2,1},{3,0},{4,7},{5,6},{6,5},{7,4},{8,11},{9,10},{10,... | collective-permute-start | bytes 221192 | tf_op jit(solution)/shard_map/ppermute | solution.py:152
  12.7 2.4 %collective-permute-done.5 = bf16[32,1152]{1,0:T(8,128)(2,1)S(1)} collective-permute-done((bf16[32,1152]{1,0:T(8,128)(2,1)S(1)}, bf16[32,1152]{1,0:T(8,128)(2,1)S(1)}, u32[]{:S(2)}, u32[]{:S(2)}) %collective-permute-start.5) | collective-permute-done | bytes 73760 | tf_op jit(solution)/shard_map/ppermute | solution.py:152
  15.1 3.1 %collective-permute-start.6 = (bf16[32,1152]{1,0:T(8,128)(2,1)S(1)}, bf16[32,1152]{1,0:T(8,128)(2,1)S(1)}, u32[]{:S(2)}, u32[]{:S(2)}) collective-permute-start(bf16[32,1152]{1,0:T(8,128)(2,1)S(1)} %get-tuple-element.21), channel_id=1, source_target_pairs={{0,5},{1,4},{2,7},{3,6},{4,1},{5,0},{6,3},{7,2},{8,13},{9,12},{10,... | collective-permute-start | bytes 221192 | tf_op jit(solution)/shard_map/ppermute | solution.py:152
  18.2 0.3 %collective-permute-start.8 = (bf16[64,512]{1,0:T(8,128)(2,1)S(1)}, bf16[64,512]{1,0:T(8,128)(2,1)S(1)}, u32[]{:S(2)}, u32[]{:S(2)}) collective-permute-start(bf16[64,512]{1,0:T(8,128)(2,1)S(1)} %copy-done.5), channel_id=1, source_target_pairs={{0,1},{1,0},{2,3},{3,2},{4,5},{5,4},{6,7},{7,6},{8,9},{9,8},{10,11... | collective-permute-start | bytes 196616 | tf_op jit(solution)/shard_map/ppermute | solution.py:152
  18.6 2.0 %collective-permute-done.6.arrived_ref = bf16[32,1152]{1,0:T(8,128)(2,1)S(1)} collective-permute-done((bf16[32,1152]{1,0:T(8,128)(2,1)S(1)}, bf16[32,1152]{1,0:T(8,128)(2,1)S(1)}, u32[]{:S(2)}, u32[]{:S(2)}) %collective-permute-start.6) | collective-permute-done | bytes 73760 | tf_op jit(solution)/shard_map/ppermute | solution.py:152
  20.6 0.2 shard_map.153.rows_ref
  20.8 0.8 %shard_map.154.one_ref = f32[8,32]{1,0:T(8,128)S(1)} custom-call(bf16[32,1024]{1,0:T(8,128)(2,1)S(1)} %shard_map.153.rows_ref, f32[3,32,128]{2,1,0:T(8,128)S(1)} %get-tuple-element.16.columns_ref.refs_2_, bf16[64,1024]{1,0:T(8,128)(2,1)S(1)} %get-tuple-element.17.down_ref, bf16[1024,512]{1,0:T(8,128)(2,1)S(1)} %copy-done, ...), custom_call_target="tpu_custom_call" | custom-call | flops 67108864 | bytes 2473984 | tf_op jit(solution)/shard_map/pallas_call | solution.py:345
  21.6 2.7 %collective-permute-start.9 = (f32[8,32]{1,0:T(8,128)S(1)}, f32[8,32]{1,0:T(8,128)S(1)}, u32[]{:S(2)}, u32[]{:S(2)}) collective-permute-start(f32[8,32]{1,0:T(8,128)S(1)} %shard_map.154.one_ref), channel_id=1, source_target_pairs={{0,3},{1,2},{2,1},{3,0},{4,7},{5,6},{6,5},{7,4},{8,11},{9,10},{10,... | collective-permute-start | bytes 3080 | tf_op jit(solution)/shard_map/ppermute | solution.py:152
  24.3 1.3 %collective-permute-done.9.two_ref = f32[8,32]{1,0:T(8,128)S(1)} collective-permute-done((f32[8,32]{1,0:T(8,128)S(1)}, f32[8,32]{1,0:T(8,128)S(1)}, u32[]{:S(2)}, u32[]{:S(2)}) %collective-permute-start.9) | collective-permute-done | bytes 1056 | tf_op jit(solution)/shard_map/ppermute | solution.py:152
  25.7 3.4 %collective-permute-start.10 = (f32[8,32]{1,0:T(8,128)S(1)}, f32[8,32]{1,0:T(8,128)S(1)}, u32[]{:S(2)}, u32[]{:S(2)}) collective-permute-start(f32[8,32]{1,0:T(8,128)S(1)} %shard_map.155.one_ref), channel_id=1, source_target_pairs={{0,5},{1,4},{2,7},{3,6},{4,1},{5,0},{6,3},{7,2},{8,13},{9,12},{10,... | collective-permute-start | bytes 3080 | tf_op jit(solution)/shard_map/ppermute | solution.py:152
  29.1 1.3 %collective-permute-done.10.two_ref = f32[8,32]{1,0:T(8,128)S(1)} collective-permute-done((f32[8,32]{1,0:T(8,128)S(1)}, f32[8,32]{1,0:T(8,128)S(1)}, u32[]{:S(2)}, u32[]{:S(2)}) %collective-permute-start.10) | collective-permute-done | bytes 1056 | tf_op jit(solution)/shard_map/ppermute | solution.py:152
  30.4 0.2 collective-permute-start.11
  30.6 1.0 %collective-permute-done.11.refs_1_ = f32[8,32]{1,0:T(8,128)S(1)} collective-permute-done((f32[8,32]{1,0:T(8,128)S(1)}, f32[8,32]{1,0:T(8,128)S(1)}, u32[]{:S(2)}, u32[]{:S(2)}) %collective-permute-start.11) | collective-permute-done | bytes 1056 | tf_op jit(solution)/shard_map/ppermute | solution.py:152
  31.6 0.7 %shard_map.157 = (f32[1,8]{1,0:T(1,128)}, f32[1,8]{1,0:T(1,128)}, f32[1,16]{1,0:T(1,128)}) custom-call(f32[8,32]{1,0:T(8,128)S(1)} %shard_map.156.refs_0_, f32[8,32]{1,0:T(8,128)S(1)} %collective-permute-done.11.refs_1_, f32[3,32,128]{2,1,0:T(8,128)S(1)} %get-tuple-element.16.columns_ref.refs_2_), custom_call_target="tpu_custom_call" | custom-call | bytes 51200 | tf_op jit(solution)/shard_map/pallas_call | solution.py:345
  (29 shorter events, 0.2 us)
Async XLA Ops:
  0.6 5.2 %collective-permute-start = (bf16[8,1024]{1,0:T(8,128)(2,1)}, bf16[8,1024]{1,0:T(8,128)(2,1)S(1)}, u32[]{:S(2)}, u32[]{:S(2)}) collective-permute-start(bf16[8,1024]{1,0:T(8,128)(2,1)} %mine_ref.1), channel_id=1, source_target_pairs={{0,5},{1,4},{2,7},{3,6},{4,1},{5,0},{6,3},{7,2},{8,13},{9,12},{10,... | collective-permute-start | bytes 49160 | tf_op jit(solution)/shard_map/ppermute | solution.py:152
  4.2 5.4 %collective-permute-start.2 = (bf16[352,1024]{1,0:T(8,128)(2,1)}, bf16[352,1024]{1,0:T(8,128)(2,1)S(1)}, u32[]{:S(2)}, u32[]{:S(2)}) collective-permute-start(bf16[352,1024]{1,0:T(8,128)(2,1)} %bitcast.12), channel_id=1, source_target_pairs={{0,1},{1,0},{2,3},{3,2},{4,5},{5,4},{6,7},{7,6},{8,9},{9,8},{10,11... | collective-permute-start | bytes 2162696 | tf_op jit(solution)/shard_map/ppermute | solution.py:152
  4.8 1.0 %copy-start.12 = (bf16[8,1024]{1,0:T(8,128)(2,1)S(1)}, bf16[8,1024]{1,0:T(8,128)(2,1)}, u32[]{:S(2)}) copy-start(bf16[8,1024]{1,0:T(8,128)(2,1)} %mine_ref.1) | copy-start | bytes 49156
  4.8 4.7 %collective-permute-start.3 = (bf16[352,1024]{1,0:T(8,128)(2,1)}, bf16[352,1024]{1,0:T(8,128)(2,1)S(1)}, u32[]{:S(2)}, u32[]{:S(2)}) collective-permute-start(bf16[352,1024]{1,0:T(8,128)(2,1)} %bitcast.14), channel_id=1, source_target_pairs={{0,1},{1,0},{2,3},{3,2},{4,5},{5,4},{6,7},{7,6},{8,9},{9,8},{10,11... | collective-permute-start | bytes 2162696 | tf_op jit(solution)/shard_map/ppermute | solution.py:152
  4.9 4.7 %collective-permute-start.4 = (bf16[352,1024]{1,0:T(8,128)(2,1)}, bf16[352,1024]{1,0:T(8,128)(2,1)S(1)}, u32[]{:S(2)}, u32[]{:S(2)}) collective-permute-start(bf16[352,1024]{1,0:T(8,128)(2,1)} %refs_5_.1), channel_id=1, source_target_pairs={{0,1},{1,0},{2,3},{3,2},{4,5},{5,4},{6,7},{7,6},{8,9},{9,8},{10,11... | collective-permute-start | bytes 2162696 | tf_op jit(solution)/shard_map/ppermute | solution.py:152
  5.4 15.5 %collective-permute-start.7 = (bf16[1024,512]{1,0:T(8,128)(2,1)}, bf16[1024,512]{1,0:T(8,128)(2,1)S(1)}, u32[]{:S(2)}, u32[]{:S(2)}) collective-permute-start(bf16[1024,512]{1,0:T(8,128)(2,1)} %refs_0_.1), channel_id=1, source_target_pairs={{0,1},{1,0},{2,3},{3,2},{4,5},{5,4},{6,7},{7,6},{8,9},{9,8},{10,11... | collective-permute-start | bytes 3145736 | tf_op jit(solution)/shard_map/ppermute | solution.py:152
  5.4 2.5 %copy-start.4 = (bf16[1024,64]{0,1:T(8,128)(2,1)S(1)}, bf16[1024,64]{0,1:T(8,128)(2,1)}, u32[]{:S(2)}) copy-start(bf16[1024,64]{0,1:T(8,128)(2,1)} %param.24) | copy-start | bytes 393220
  5.8 2.1 %copy-start.9 = (f32[8,2]{0,1:T(2,128)S(1)}, f32[8,2]{0,1:T(2,128)}, u32[]{:S(2)}) copy-start(f32[8,2]{0,1:T(2,128)} %param.15) | copy-start | bytes 196
  5.8 2.1 %copy-start.10 = (s32[64]{0:T(128)S(1)}, s32[64]{0:T(128)}, u32[]{:S(2)}) copy-start(s32[64]{0:T(128)} %param.16) | copy-start | bytes 772
  5.8 2.1 %copy-start.11 = (s32[64]{0:T(128)S(1)}, s32[64]{0:T(128)}, u32[]{:S(2)}) copy-start(s32[64]{0:T(128)} %param.17) | copy-start | bytes 772
  5.8 3.7 %copy-start.1 = (bf16[1024,352]{0,1:T(8,128)(2,1)S(1)}, bf16[1024,352]{0,1:T(8,128)(2,1)}, u32[]{:S(2)}) copy-start(bf16[1024,352]{0,1:T(8,128)(2,1)} %param.19) | copy-start | bytes 2162692
  5.8 3.7 %copy-start.2 = (bf16[1024,352]{0,1:T(8,128)(2,1)S(1)}, bf16[1024,352]{0,1:T(8,128)(2,1)}, u32[]{:S(2)}) copy-start(bf16[1024,352]{0,1:T(8,128)(2,1)} %param.20) | copy-start | bytes 2162692
  5.9 3.7 %copy-start.3 = (bf16[352,1024]{1,0:T(8,128)(2,1)S(1)}, bf16[352,1024]{1,0:T(8,128)(2,1)}, u32[]{:S(2)}) copy-start(bf16[352,1024]{1,0:T(8,128)(2,1)} %refs_5_.1) | copy-start | bytes 2162692
  5.9 3.6 %collective-permute-start.1 = (bf16[16,1024]{1,0:T(8,128)(2,1)S(1)}, bf16[16,1024]{1,0:T(8,128)(2,1)S(1)}, u32[]{:S(2)}, u32[]{:S(2)}) collective-permute-start(bf16[16,1024]{1,0:T(8,128)(2,1)S(1)} %shard_map.149.mine_ref), channel_id=1, source_target_pairs={{0,3},{1,2},{2,1},{3,0},{4,7},{5,6},{6,5},{7,4},{8,11},{9,10},{10,... | collective-permute-start | bytes 98312 | tf_op jit(solution)/shard_map/ppermute | solution.py:152
  7.9 0.7 %copy-start.7 = (f32[1024]{0:T(1024)S(1)}, f32[1024]{0:T(1024)}, u32[]{:S(2)}) copy-start(f32[1024]{0:T(1024)} %param.22) | copy-start | bytes 12292
  7.9 0.7 %copy-start.6 = (f32[1024]{0:T(1024)S(1)}, f32[1024]{0:T(1024)}, u32[]{:S(2)}) copy-start(f32[1024]{0:T(1024)} %param.18) | copy-start | bytes 12292
  7.9 0.7 %copy-start.8 = (s32[8,2]{0,1:T(2,128)S(1)}, s32[8,2]{0,1:T(2,128)}, u32[]{:S(2)}) copy-start(s32[8,2]{0,1:T(2,128)} %param.14) | copy-start | bytes 196
  9.6 11.2 %copy-start = (bf16[1024,512]{1,0:T(8,128)(2,1)S(1)}, bf16[1024,512]{1,0:T(8,128)(2,1)}, u32[]{:S(2)}) copy-start(bf16[1024,512]{1,0:T(8,128)(2,1)} %refs_0_.1) | copy-start | bytes 3145732
  10.9 4.2 %collective-permute-start.5 = (bf16[32,1152]{1,0:T(8,128)(2,1)S(1)}, bf16[32,1152]{1,0:T(8,128)(2,1)S(1)}, u32[]{:S(2)}, u32[]{:S(2)}) collective-permute-start(bf16[32,1152]{1,0:T(8,128)(2,1)S(1)} %get-tuple-element.15), channel_id=1, source_target_pairs={{0,3},{1,2},{2,1},{3,0},{4,7},{5,6},{6,5},{7,4},{8,11},{9,10},{10,... | collective-permute-start | bytes 221192 | tf_op jit(solution)/shard_map/ppermute | solution.py:152
  15.1 3.1 %copy-start.5 = (bf16[64,512]{1,0:T(8,128)(2,1)S(1)}, bf16[64,512]{1,0:T(8,128)(2,1)}, u32[]{:S(2)}) copy-start(bf16[64,512]{1,0:T(8,128)(2,1)} %refs_2_.1) | copy-start | bytes 196612
  15.1 5.5 %collective-permute-start.6 = (bf16[32,1152]{1,0:T(8,128)(2,1)S(1)}, bf16[32,1152]{1,0:T(8,128)(2,1)S(1)}, u32[]{:S(2)}, u32[]{:S(2)}) collective-permute-start(bf16[32,1152]{1,0:T(8,128)(2,1)S(1)} %get-tuple-element.21), channel_id=1, source_target_pairs={{0,5},{1,4},{2,7},{3,6},{4,1},{5,0},{6,3},{7,2},{8,13},{9,12},{10,... | collective-permute-start | bytes 221192 | tf_op jit(solution)/shard_map/ppermute | solution.py:152
  18.2 2.6 %collective-permute-start.8 = (bf16[64,512]{1,0:T(8,128)(2,1)S(1)}, bf16[64,512]{1,0:T(8,128)(2,1)S(1)}, u32[]{:S(2)}, u32[]{:S(2)}) collective-permute-start(bf16[64,512]{1,0:T(8,128)(2,1)S(1)} %copy-done.5), channel_id=1, source_target_pairs={{0,1},{1,0},{2,3},{3,2},{4,5},{5,4},{6,7},{7,6},{8,9},{9,8},{10,11... | collective-permute-start | bytes 196616 | tf_op jit(solution)/shard_map/ppermute | solution.py:152
  21.6 4.0 %collective-permute-start.9 = (f32[8,32]{1,0:T(8,128)S(1)}, f32[8,32]{1,0:T(8,128)S(1)}, u32[]{:S(2)}, u32[]{:S(2)}) collective-permute-start(f32[8,32]{1,0:T(8,128)S(1)} %shard_map.154.one_ref), channel_id=1, source_target_pairs={{0,3},{1,2},{2,1},{3,0},{4,7},{5,6},{6,5},{7,4},{8,11},{9,10},{10,... | collective-permute-start | bytes 3080 | tf_op jit(solution)/shard_map/ppermute | solution.py:152
  25.7 4.7 %collective-permute-start.10 = (f32[8,32]{1,0:T(8,128)S(1)}, f32[8,32]{1,0:T(8,128)S(1)}, u32[]{:S(2)}, u32[]{:S(2)}) collective-permute-start(f32[8,32]{1,0:T(8,128)S(1)} %shard_map.155.one_ref), channel_id=1, source_target_pairs={{0,5},{1,4},{2,7},{3,6},{4,1},{5,0},{6,3},{7,2},{8,13},{9,12},{10,... | collective-permute-start | bytes 3080 | tf_op jit(solution)/shard_map/ppermute | solution.py:152
  30.4 1.2 %collective-permute-start.11 = (f32[8,32]{1,0:T(8,128)S(1)}, f32[8,32]{1,0:T(8,128)S(1)}, u32[]{:S(2)}, u32[]{:S(2)}) collective-permute-start(f32[8,32]{1,0:T(8,128)S(1)} %shard_map.156.refs_0_), channel_id=1, source_target_pairs={{0,1},{1,0},{2,3},{3,2},{4,5},{5,4},{6,7},{7,6},{8,9},{9,8},{10,11... | collective-permute-start | bytes 3080 | tf_op jit(solution)/shard_map/ppermute | solution.py:152

commit v5 on v4

--- a/solution.py
+++ b/solution.py
@@ -167,7 +167,7 @@
     device = parity * 0
     low = parity
     for b in range(1, bits):
-        one = (rank >> (bits - 1 - b)) & 1
+        one = (rank >> (b - 1)) & 1
         device = device + one * (1 << b)
         low = low ^ one
     return (device + low) * tok_rows + place % tok_rows
@@ -192,8 +192,10 @@
     moe_gain_ref,
     final_gain_ref,
     down_ref,
+    up_ref,
     gains_ref,
     down_out_ref,
+    up_out_ref,
     mixing_ref,
     columns_ref,
 ):
@@ -203,6 +205,7 @@
         [moe_gain_ref[...]] * 4 + [final_gain_ref[...]] * 4, axis=0
     )
     down_out_ref[...] = down_ref[...]
+    up_out_ref[...] = up_ref[...]
     rows = [
         sum(
             jnp.where(ids_ref[k : k + 1] == expert, gates_ref[k : k + 1], 0.0)
@@ -217,12 +220,15 @@
     rows = [high, middle, low, jnp.zeros((8 - 3 * experts, tok_rows), jnp.float32)]
     rows = [jnp.concatenate(rows, axis=0), jnp.zeros((8, 128 - tok_rows), jnp.float32)]
     parts = jnp.concatenate(rows, axis=1).T[:tok_rows]
-    parts = jnp.concatenate([parts, jnp.zeros((tok_rows, 120), jnp.float32)], axis=1)
+    parts = jnp.concatenate([parts] * 16, axis=1)
+    lane = lax.broadcasted_iota(jnp.int32, parts.shape, 1)
+    token = token_at(lane // 8 * tok_rows + parity * half, tok_rows, bits)
+    mine = (lane < half // tok_rows * 8) & (token // tok_rows == my_index)
+    mixing = jnp.where(mine, parts, 0.0)
+    mixing_ref[...] = jnp.concatenate([mixing, jnp.zeros_like(mixing)], axis=0)
     row = lax.broadcasted_iota(jnp.int32, (half, 128), 0)
     lane = lax.broadcasted_iota(jnp.int32, (half, 128), 1)
     token = token_at(row + parity * half, tok_rows, bits) - my_index * tok_rows
-    mine = (token >= 0) & (token < tok_rows)
-    mixing_ref[...] = jnp.where(mine, jnp.concatenate([parts] * (half // tok_rows), axis=0), 0.0)
     wanted = half_columns(targets_ref[...], tok_rows, bits, parity)
     own_seq = half_columns(seq_ref[...], tok_rows, bits, parity)
     other_seq = half_columns(seq_ref[...], tok_rows, bits, 1 - parity)
@@ -242,8 +248,13 @@
     out_ref[...] = in_order(late, mine_ref[...], other_ref[...])
 
 
-def expert_kernel(rows_ref, gains_ref, mixing_ref, *refs):
-    far_refs, near_refs, (total_ref, sent_ref) = refs[0:3], refs[3:6], refs[6:8]
+def expert_kernel(rows_ref, gains_ref, *refs):
+    far_refs, near_refs, mixing_refs, (total_ref, sent_ref) = (
+        refs[0:3],
+        refs[3:6],
+        refs[6:-2],
+        refs[-2:],
+    )
     moe_input = rms_norm(rows_ref[...].astype(jnp.float32), gains_ref[0:1]).astype(jnp.bfloat16)
 
     def units(gate_ref, up_ref, down_ref):
@@ -254,23 +265,34 @@
         inner_act = (jax.nn.silu(projections[0]) * projections[1]).astype(jnp.bfloat16)
         return jnp.dot(inner_act, down_ref[...], preferred_element_type=jnp.float32)
 
-    total = units(*far_refs) + units(*near_refs)
-    total = jnp.concatenate([total, mixing_ref[...]], axis=1)
+    total = units(*near_refs) + units(*far_refs)
+    total = jnp.concatenate([total, *(ref[...] for ref in mixing_refs)], axis=1)
     total_ref[...] = total
     sent_ref[...] = total.astype(jnp.bfloat16)
 
 
-def norm_kernel(total_ref, arrived_ref, rows_ref, gains_ref, out_ref):
-    features = out_ref.shape[1]
-    expert = lax.axis_index("tensor") // SPLIT
-    total, arrived = total_ref[...], arrived_ref[...].astype(jnp.float32)
-    mixing = total[:, features:] + arrived[:, features:]
+def final_rows(place, rows, totals, arrived, gain):
+    features = rows[0].shape[1]
+    my_index = lax.axis_index("tensor")
+    expert = my_index // SPLIT
+    late = bit(my_index, place) == 1
+    tok_rows = rows[0].shape[0] // 2
+    mixing = [piece[:tok_rows, features:].astype(jnp.float32) for piece in (totals[0], arrived[0])]
+    mixing = mixing[0] + mixing[1]
     lane = lax.broadcasted_iota(jnp.int32, mixing.shape, 1)
-    mixed = rows_ref[...].astype(jnp.float32)
-    for own, value in ((expert, total), (1 - expert, arrived)):
-        weight = jnp.sum(jnp.where(lane % 2 == own, mixing, 0.0), axis=1, keepdims=True)
-        mixed = mixed + weight * value[:, :features]
-    out_ref[...] = rms_norm(mixed, gains_ref[4:5]).astype(jnp.bfloat16)
+    mixed = in_order(late, *rows).astype(jnp.float32)
+    for own, pieces in ((expert, totals), (1 - expert, arrived[::-1])):
+        weights = [
+            jnp.sum(
+                jnp.where((lane // 8 == block) & (lane % 2 == own), mixing, 0.0),
+                axis=1,
+                keepdims=True,
+            )
+            for block in range(4)
+        ]
+        values = in_order(late, *(piece[:, :features].astype(jnp.float32) for piece in pieces))
+        mixed = mixed + jnp.concatenate(weights, axis=0) * values
+    return rms_norm(mixed, gain).astype(jnp.bfloat16)
 
 
 def half_columns(values, tok_rows, bits, parity):
@@ -283,10 +305,18 @@
     return column.astype(jnp.int32)
 
 
-def head_kernel(rows_ref, columns_ref, down_ref, *refs):
-    *weight_refs, stats_ref = refs
+def head_kernel(place, *refs):
+    row_refs, sum_refs, (gains_ref, columns_ref, down_ref), weight_refs, (stats_ref,) = (
+        refs[0:2],
+        refs[2:6],
+        refs[6:9],
+        refs[9:13],
+        refs[13:],
+    )
     my_index = lax.axis_index("tensor")
-    rows = rows_ref[...]
+    sums = [ref[...] for ref in sum_refs]
+    pieces = [ref[...] for ref in row_refs]
+    rows = final_rows(place, pieces, sums[0:2], sums[2:4], gains_ref[4:5])
     tokens = rows.shape[0]
     wanted = columns_ref[0][:, 0:1].astype(jnp.int32)
     latent = lax.dot_general(rows, down_ref[...], TRANSPOSED, preferred_element_type=jnp.float32)
@@ -326,15 +356,15 @@
         stats = ref[...]
         log_probs = stats[4:6] - stats[0:2] - jnp.log(stats[2:4])
         policy = log_probs[1:2]
-        rows = jnp.concatenate([policy, policy - log_probs[0:1]] * 4, axis=0)
-        picked.append(
-            jnp.dot(
-                rows,
-                columns,
-                precision=lax.Precision.HIGHEST,
-                preferred_element_type=jnp.float32,
-            )
+        values = jnp.concatenate([policy, policy - log_probs[0:1]], axis=0)
+        high = values.astype(jnp.bfloat16).astype(jnp.float32)
+        middle = (values - high).astype(jnp.bfloat16).astype(jnp.float32)
+        parts = [high, middle, values - high - middle, jnp.zeros_like(values)]
+        rows = jnp.concatenate(parts, axis=0).astype(jnp.bfloat16)
+        parts = jnp.dot(
+            rows, columns.astype(jnp.bfloat16), preferred_element_type=jnp.float32
         )
+        picked.append(parts[0:2] + parts[2:4] + parts[4:6])
     policy_ref[...] = picked[0][0:1, :tok_rows]
     ratio_ref[...] = picked[0][1:2, :tok_rows]
     sums_ref[...] = (picked[0] + picked[1])[1:2, 64 : 64 + SEQS]
@@ -370,28 +400,28 @@
     bits = devices.bit_length() - 1
     half = devices * tok_rows // 2
     my_index = lax.axis_index("tensor")
-    far = [(b, (1 << b) + 1) for b in range(bits - 1, 0, -1)]
+    (near_bit, near_mask), (far_bit, far_mask) = ((b, (1 << b) + 1) for b in range(1, bits))
 
     def array(dtype, *shape):
         return jax.ShapeDtypeStruct(shape, dtype)
 
-    rows = hidden_in
     flags = call(flags_kernel, array(jnp.int32, 8, 128), flops=ROUND_FLOPS)
-    for b, mask in far:
-        rows = call(
-            functools.partial(order_kernel, b),
-            array(rows.dtype, 2 * rows.shape[0], features),
-            flags,
-            rows,
-            exchange(rows, mask),
-            flops=ROUND_FLOPS * (2 * rows.shape[0] < half),
-        )
-    gains, down, mixing, columns = call(
+    first = call(
+        functools.partial(order_kernel, near_bit),
+        array(jnp.bfloat16, 2 * tok_rows, features),
+        flags,
+        hidden_in,
+        exchange(hidden_in, near_mask),
+        flops=ROUND_FLOPS,
+    )
+    second = exchange(first, far_mask)
+    gains, down, up, mixing, columns = call(
         lambda *refs: prepare_kernel(tok_rows, bits, *refs),
         [
             array(jnp.float32, 8, features),
             array(jnp.bfloat16, *adapter_down.shape[::-1]),
-            array(jnp.float32, half, 128),
+            array(jnp.bfloat16, *adapter_up.shape),
+            array(jnp.float32, 2 * tok_rows, 128),
             array(jnp.float32, 3, half, 128),
         ],
         expert_ids.T,
@@ -401,45 +431,48 @@
         moe_gain[None],
         final_gain[None],
         adapter_down.T,
+        adapter_up,
     )
 
     units = [w_gate.T, w_up.T, w_down]
-    total, sent = call(
-        expert_kernel,
-        [array(dtype, half, features + 128) for dtype in (jnp.float32, jnp.bfloat16)],
-        rows,
+    units = [exchange(unit, 1) for unit in units] + units
+    totals, sent = [], []
+    for rows, more in ((first, [mixing]), (second, [])):
+        outputs = call(
+            expert_kernel,
+            [
+                array(dtype, 2 * tok_rows, features + 128 * len(more))
+                for dtype in (jnp.float32, jnp.bfloat16)
+            ],
+            rows,
+            gains,
+            *units,
+            *more,
+            flops=3 * devices * tok_rows * features * w_gate.shape[1],
+        )
+        total = outputs[0] + exchange(outputs[1], near_mask).astype(jnp.float32)
+        totals.append(total)
+        sent.append(total.astype(jnp.bfloat16))
+    sent[0], up_sent = lax.optimization_barrier((sent[0], up))
+    arrived = [exchange(piece, far_mask) for piece in sent]
+
+    stats = call(
+        functools.partial(head_kernel, far_bit),
+        array(jnp.float32, 8, half),
+        first,
+        second,
+        *totals,
+        *arrived,
         gains,
-        mixing,
-        *(exchange(unit, 1) for unit in units),
-        *units,
-        flops=6 * devices * tok_rows * features * w_gate.shape[1],
-    )
-    masks = [mask for _, mask in far[::-1]]
-    for mask in masks[:-1]:
-        total = total + exchange(sent, mask).astype(jnp.float32)
-        sent = total.astype(jnp.bfloat16)
-    final_input = call(
-        norm_kernel,
-        array(jnp.bfloat16, half, features),
-        total,
-        exchange(sent, masks[-1]),
-        rows,
-        gains,
-    )
-
-    stats = call(
-        head_kernel,
-        array(jnp.float32, 8, half),
-        final_input,
         columns,
         down,
         head_weight,
         exchange(head_weight, 1),
-        adapter_up,
-        exchange(adapter_up, 1),
+        up,
+        exchange(up_sent, 1),
         flops=2 * devices * tok_rows * features * head_weight.shape[1],
     )
-    for mask in masks:
+    for mask in (near_mask, far_mask):
         stats = call(merge_kernel, array(jnp.float32, 8, half), stats, exchange(stats, mask))
     policy_own, ratio_own, seq_sums = call(
         lambda *refs: result_kernel(tok_rows, *refs),

time: 32.5 us -> 31.7 us (0.975)
  starting transfers between devices: 18.3 us -> 14 us
  waiting for transfers between devices: 9.28 us -> 11 us
  Pallas kernels: 3.25 us -> 4.44 us
  local copies, waits for them, and re-layouts: 0.72 us -> 1.21 us
    ppermute x12 -> x14, starting transfers between devices: 18.3 us -> 14 us  [exchange(): lax.ppermute(values, 'tensor', [(i, i ^ mask) for i in range(devices)])]
    ppermute x12 -> x14, waiting for transfers between devices: 9.28 us -> 11 us  [exchange(): lax.ppermute(values, 'tensor', [(i, i ^ mask) for i in range(devices)])]
    pallas_call x10 -> x9, Pallas kernels: 3.25 us -> 4.44 us  [call(): pl.pallas_call(kernel, out_shape=shapes, compiler_params=pltpu.CompilerPa...]
    unnamed x26, local copies, waits for them, and re-layouts: 0.72 us -> 1.21 us
  transfers between devices with their start and end apart: 12 -> 14, of which waited for: 7 -> 5; matrix products, arithmetic and copies ran while one was open for 0% -> 0% of each run, Pallas kernels for 5% -> 9%
where the time goes in v5:
time: 31.7 us; the launch traced here: 31.4 us
  starting transfers between devices  14 us (44%)
  waiting for transfers between devices  11 us (35%)
  Pallas kernels  4.44 us (14%)
  local copies, waits for them, and re-layouts  1.21 us (4%)
  between operations  0.79 us (2%)
    ppermute x14, starting transfers between devices, exchange(): lax.ppermute(values, 'tensor', [(i, i ^ mask) for i in range(devices)])  14 us
    ppermute x14, waiting for transfers between devices, exchange(): lax.ppermute(values, 'tensor', [(i, i ^ mask) for i in range(devices)])  11 us
    pallas_call x9, Pallas kernels, call(): pl.pallas_call(kernel, out_shape=shapes, compiler_params=pltpu.CompilerPa...  4.44 us
    unnamed x26, local copies, waits for them, and re-layouts  1.21 us
  transfers between devices with their start and end apart: 14, of which 5 were waited for; matrix products, arithmetic and copies ran while one was open for 0% of the time, Pallas kernels for 9%

profile of v5, /device:TPU:0, one launch (start us, length us, event | category | flops | bytes accessed | tf_op | source)
XLA Modules:
  0.0 31.4 jit_solution(12337415255113880706)
XLA Ops:
  0.6 2.5 %collective-permute-start = (bf16[8,1024]{1,0:T(8,128)(2,1)}, bf16[8,1024]{1,0:T(8,128)(2,1)S(1)}, u32[]{:S(2)}, u32[]{:S(2)}) collective-permute-start(bf16[8,1024]{1,0:T(8,128)(2,1)} %mine_ref.1), channel_id=1, source_target_pairs={{0,3},{1,2},{2,1},{3,0},{4,7},{5,6},{6,5},{7,4},{8,11},{9,10},{10,... | collective-permute-start | bytes 49160 | tf_op jit(solution)/shard_map/ppermute | solution.py:152
  3.2 0.7 %collective-permute-start.2 = (bf16[352,1024]{1,0:T(8,128)(2,1)}, bf16[352,1024]{1,0:T(8,128)(2,1)S(1)}, u32[]{:S(2)}, u32[]{:S(2)}) collective-permute-start(bf16[352,1024]{1,0:T(8,128)(2,1)} %bitcast.12), channel_id=1, source_target_pairs={{0,1},{1,0},{2,3},{3,2},{4,5},{5,4},{6,7},{7,6},{8,9},{9,8},{10,11... | collective-permute-start | bytes 2162696 | tf_op jit(solution)/shard_map/ppermute | solution.py:152
  3.8 0.5 %collective-permute-start.4 = (bf16[352,1024]{1,0:T(8,128)(2,1)}, bf16[352,1024]{1,0:T(8,128)(2,1)S(1)}, u32[]{:S(2)}, u32[]{:S(2)}) collective-permute-start(bf16[352,1024]{1,0:T(8,128)(2,1)} %refs_5_.3), channel_id=1, source_target_pairs={{0,1},{1,0},{2,3},{3,2},{4,5},{5,4},{6,7},{7,6},{8,9},{9,8},{10,11... | collective-permute-start | bytes 2162696 | tf_op jit(solution)/shard_map/ppermute | solution.py:152
  4.4 0.0 copy-start.7
  4.4 0.0 copy-start.8
  4.4 0.3 %copy-done.4 = bf16[1024,64]{0,1:T(8,128)(2,1)S(1)} copy-done((bf16[1024,64]{0,1:T(8,128)(2,1)S(1)}, bf16[1024,64]{0,1:T(8,128)(2,1)}, u32[]{:S(2)}) %copy-start.4) | copy-done | bytes 131096
  4.7 0.3 copy-done.9
  5.1 0.0 copy-done.11
  5.1 0.0 copy-done.7
  5.1 0.0 copy-done.6
  5.1 0.0 copy-done.8
  5.1 0.2 shard_map.150
  5.4 0.0 copy-start.2
  5.4 0.4 %copy-done.12 = bf16[8,1024]{1,0:T(8,128)(2,1)S(1)} copy-done((bf16[8,1024]{1,0:T(8,128)(2,1)S(1)}, bf16[8,1024]{1,0:T(8,128)(2,1)}, u32[]{:S(2)}) %copy-start.12) | copy-done | bytes 16408
  5.9 2.7 %collective-permute-start.1 = (bf16[16,1024]{1,0:T(8,128)(2,1)S(1)}, bf16[16,1024]{1,0:T(8,128)(2,1)S(1)}, u32[]{:S(2)}, u32[]{:S(2)}) collective-permute-start(bf16[16,1024]{1,0:T(8,128)(2,1)S(1)} %shard_map.149.rows_ref.refs_0_), channel_id=1, source_target_pairs={{0,5},{1,4},{2,7},{3,6},{4,1},{5,0},{6,3},{7,2},{8,13},{9,12},{10,... | collective-permute-start | bytes 98312 | tf_op jit(solution)/shard_map/ppermute | solution.py:152
  8.7 1.2 %shard_map.151 = (f32[16,1152]{1,0:T(8,128)S(1)}, bf16[16,1152]{1,0:T(8,128)(2,1)S(1)}) custom-call(bf16[16,1024]{1,0:T(8,128)(2,1)S(1)} %shard_map.149.rows_ref.refs_0_, f32[8,1024]{1,0:T(8,128)S(1)} %get-tuple-element.17.gains_ref.refs_6_, bf16[352,1024]{1,0:T(8,128)(2,1)S(1)} %collective-permute-done.2.refs_0_, ...), custom_call_target="tpu_custom_call" | custom-call | flops 69206016 | bytes 4399104 | tf_op jit(solution)/shard_map/pallas_call | solution.py:375
  9.9 1.0 %collective-permute-start.5 = (bf16[16,1152]{1,0:T(8,128)(2,1)S(1)}, bf16[16,1152]{1,0:T(8,128)(2,1)S(1)}, u32[]{:S(2)}, u32[]{:S(2)}) collective-permute-start(bf16[16,1152]{1,0:T(8,128)(2,1)S(1)} %get-tuple-element.20), channel_id=1, source_target_pairs={{0,3},{1,2},{2,1},{3,0},{4,7},{5,6},{6,5},{7,4},{8,11},{9,10},{10,... | collective-permute-start | bytes 110600 | tf_op jit(solution)/shard_map/ppermute | solution.py:152
  11.0 1.2 %shard_map.152 = (f32[16,1024]{1,0:T(8,128)S(1)}, bf16[16,1024]{1,0:T(8,128)(2,1)S(1)}) custom-call(bf16[16,1024]{1,0:T(8,128)(2,1)S(1)} %collective-permute-done.1.rows_ref.refs_1_, f32[8,1024]{1,0:T(8,128)S(1)} %get-tuple-element.17.gains_ref.refs_6_, bf16[352,1024]{1,0:T(8,128)(2,1)S(1)} %collective-permute-done.2.refs_0_, ...), custom_call_target="tpu_custom_call" | custom-call | flops 69206016 | bytes 4390912 | tf_op jit(solution)/shard_map/pallas_call | solution.py:375
  12.2 0.7 %collective-permute-start.6 = (bf16[16,1024]{1,0:T(8,128)(2,1)S(1)}, bf16[16,1024]{1,0:T(8,128)(2,1)S(1)}, u32[]{:S(2)}, u32[]{:S(2)}) collective-permute-start(bf16[16,1024]{1,0:T(8,128)(2,1)S(1)} %get-tuple-element.22), channel_id=1, source_target_pairs={{0,3},{1,2},{2,1},{3,0},{4,7},{5,6},{6,5},{7,4},{8,11},{9,10},{10,... | collective-permute-start | bytes 98312 | tf_op jit(solution)/shard_map/ppermute | solution.py:152
  12.9 0.6 %collective-permute-done.5 = bf16[16,1152]{1,0:T(8,128)(2,1)S(1)} collective-permute-done((bf16[16,1152]{1,0:T(8,128)(2,1)S(1)}, bf16[16,1152]{1,0:T(8,128)(2,1)S(1)}, u32[]{:S(2)}, u32[]{:S(2)}) %collective-permute-start.5) | collective-permute-done | bytes 36896 | tf_op jit(solution)/shard_map/ppermute | solution.py:152
  13.5 2.7 %collective-permute-start.7 = (bf16[16,1152]{1,0:T(8,128)(2,1)S(1)}, bf16[16,1152]{1,0:T(8,128)(2,1)S(1)}, u32[]{:S(2)}, u32[]{:S(2)}) collective-permute-start(bf16[16,1152]{1,0:T(8,128)(2,1)S(1)} %get-tuple-element.24), channel_id=1, source_target_pairs={{0,5},{1,4},{2,7},{3,6},{4,1},{5,0},{6,3},{7,2},{8,13},{9,12},{10,... | collective-permute-start | bytes 110600 | tf_op jit(solution)/shard_map/ppermute | solution.py:152
  16.2 0.1 collective-permute-start.10
  16.3 1.5 %collective-permute-start.8 = (bf16[16,1024]{1,0:T(8,128)(2,1)S(1)}, bf16[16,1024]{1,0:T(8,128)(2,1)S(1)}, u32[]{:S(2)}, u32[]{:S(2)}) collective-permute-start(bf16[16,1024]{1,0:T(8,128)(2,1)S(1)} %get-tuple-element.31), channel_id=1, source_target_pairs={{0,5},{1,4},{2,7},{3,6},{4,1},{5,0},{6,3},{7,2},{8,13},{9,12},{10,... | collective-permute-start | bytes 98312 | tf_op jit(solution)/shard_map/ppermute | solution.py:152
  17.7 3.6 %collective-permute-done.8.refs_5_ = bf16[16,1024]{1,0:T(8,128)(2,1)S(1)} collective-permute-done((bf16[16,1024]{1,0:T(8,128)(2,1)S(1)}, bf16[16,1024]{1,0:T(8,128)(2,1)S(1)}, u32[]{:S(2)}, u32[]{:S(2)}) %collective-permute-start.8) | collective-permute-done | bytes 32800 | tf_op jit(solution)/shard_map/ppermute | solution.py:152
  21.4 1.0 %shard_map.153.one_ref = f32[8,32]{1,0:T(8,128)S(1)} custom-call(bf16[16,1024]{1,0:T(8,128)(2,1)S(1)} %shard_map.149.rows_ref.refs_0_, bf16[16,1024]{1,0:T(8,128)(2,1)S(1)} %collective-permute-done.1.rows_ref.refs_1_, f32[16,1152]{1,0:T(8,128)S(1)} %get-tuple-element.34.refs_2_, f32[16,1024]{1,0:T(8,128)S(1)} %get-tuple-element.32.refs_3_, ...), custom_call_target="tpu_custom_call" | custom-call | flops 67108864 | bytes 2715648 | tf_op jit(solution)/shard_map/pallas_call | solution.py:375
  22.4 0.0 collective-permute-start.11
  22.4 3.0 %collective-permute-done.11.two_ref = f32[8,32]{1,0:T(8,128)S(1)} collective-permute-done((f32[8,32]{1,0:T(8,128)S(1)}, f32[8,32]{1,0:T(8,128)S(1)}, u32[]{:S(2)}, u32[]{:S(2)}) %collective-permute-start.11) | collective-permute-done | bytes 1056 | tf_op jit(solution)/shard_map/ppermute | solution.py:152
  25.5 1.4 %collective-permute-start.12 = (f32[8,32]{1,0:T(8,128)S(1)}, f32[8,32]{1,0:T(8,128)S(1)}, u32[]{:S(2)}, u32[]{:S(2)}) collective-permute-start(f32[8,32]{1,0:T(8,128)S(1)} %shard_map.154.one_ref), channel_id=1, source_target_pairs={{0,5},{1,4},{2,7},{3,6},{4,1},{5,0},{6,3},{7,2},{8,13},{9,12},{10,... | collective-permute-start | bytes 3080 | tf_op jit(solution)/shard_map/ppermute | solution.py:152
  26.8 2.6 %collective-permute-done.12.two_ref = f32[8,32]{1,0:T(8,128)S(1)} collective-permute-done((f32[8,32]{1,0:T(8,128)S(1)}, f32[8,32]{1,0:T(8,128)S(1)}, u32[]{:S(2)}, u32[]{:S(2)}) %collective-permute-start.12) | collective-permute-done | bytes 1056 | tf_op jit(solution)/shard_map/ppermute | solution.py:152
  29.5 0.2 collective-permute-start.13
  29.7 1.1 %collective-permute-done.13.refs_1_ = f32[8,32]{1,0:T(8,128)S(1)} collective-permute-done((f32[8,32]{1,0:T(8,128)S(1)}, f32[8,32]{1,0:T(8,128)S(1)}, u32[]{:S(2)}, u32[]{:S(2)}) %collective-permute-start.13) | collective-permute-done | bytes 1056 | tf_op jit(solution)/shard_map/ppermute | solution.py:152
  30.7 0.7 %shard_map.156 = (f32[1,8]{1,0:T(1,128)}, f32[1,8]{1,0:T(1,128)}, f32[1,16]{1,0:T(1,128)}) custom-call(f32[8,32]{1,0:T(8,128)S(1)} %shard_map.155.refs_0_, f32[8,32]{1,0:T(8,128)S(1)} %collective-permute-done.13.refs_1_, f32[3,32,128]{2,1,0:T(8,128)S(1)} %get-tuple-element.25.refs_7_.refs_2_), custom_call_target="tpu_custom_call" | custom-call | bytes 51200 | tf_op jit(solution)/shard_map/pallas_call | solution.py:375
  (33 shorter events, 0.2 us)
Async XLA Ops:
  0.6 4.8 %collective-permute-start = (bf16[8,1024]{1,0:T(8,128)(2,1)}, bf16[8,1024]{1,0:T(8,128)(2,1)S(1)}, u32[]{:S(2)}, u32[]{:S(2)}) collective-permute-start(bf16[8,1024]{1,0:T(8,128)(2,1)} %mine_ref.1), channel_id=1, source_target_pairs={{0,3},{1,2},{2,1},{3,0},{4,7},{5,6},{6,5},{7,4},{8,11},{9,10},{10,... | collective-permute-start | bytes 49160 | tf_op jit(solution)/shard_map/ppermute | solution.py:152
  3.2 5.5 %collective-permute-start.2 = (bf16[352,1024]{1,0:T(8,128)(2,1)}, bf16[352,1024]{1,0:T(8,128)(2,1)S(1)}, u32[]{:S(2)}, u32[]{:S(2)}) collective-permute-start(bf16[352,1024]{1,0:T(8,128)(2,1)} %bitcast.12), channel_id=1, source_target_pairs={{0,1},{1,0},{2,3},{3,2},{4,5},{5,4},{6,7},{7,6},{8,9},{9,8},{10,11... | collective-permute-start | bytes 2162696 | tf_op jit(solution)/shard_map/ppermute | solution.py:152
  3.8 0.9 %copy-start.4 = (bf16[1024,64]{0,1:T(8,128)(2,1)S(1)}, bf16[1024,64]{0,1:T(8,128)(2,1)}, u32[]{:S(2)}) copy-start(bf16[1024,64]{0,1:T(8,128)(2,1)} %param.24) | copy-start | bytes 393220
  3.8 0.9 %copy-start.5 = (bf16[64,512]{1,0:T(8,128)(2,1)S(1)}, bf16[64,512]{1,0:T(8,128)(2,1)}, u32[]{:S(2)}) copy-start(bf16[64,512]{1,0:T(8,128)(2,1)} %refs_7_.1) | copy-start | bytes 196612
  3.8 4.8 %collective-permute-start.3 = (bf16[352,1024]{1,0:T(8,128)(2,1)}, bf16[352,1024]{1,0:T(8,128)(2,1)S(1)}, u32[]{:S(2)}, u32[]{:S(2)}) collective-permute-start(bf16[352,1024]{1,0:T(8,128)(2,1)} %bitcast.15), channel_id=1, source_target_pairs={{0,1},{1,0},{2,3},{3,2},{4,5},{5,4},{6,7},{7,6},{8,9},{9,8},{10,11... | collective-permute-start | bytes 2162696 | tf_op jit(solution)/shard_map/ppermute | solution.py:152
  3.8 4.8 %collective-permute-start.4 = (bf16[352,1024]{1,0:T(8,128)(2,1)}, bf16[352,1024]{1,0:T(8,128)(2,1)S(1)}, u32[]{:S(2)}, u32[]{:S(2)}) collective-permute-start(bf16[352,1024]{1,0:T(8,128)(2,1)} %refs_5_.3), channel_id=1, source_target_pairs={{0,1},{1,0},{2,3},{3,2},{4,5},{5,4},{6,7},{7,6},{8,9},{9,8},{10,11... | collective-permute-start | bytes 2162696 | tf_op jit(solution)/shard_map/ppermute | solution.py:152
  4.4 17.0 %collective-permute-start.9 = (bf16[1024,512]{1,0:T(8,128)(2,1)}, bf16[1024,512]{1,0:T(8,128)(2,1)S(1)}, u32[]{:S(2)}, u32[]{:S(2)}) collective-permute-start(bf16[1024,512]{1,0:T(8,128)(2,1)} %refs_9_.1), channel_id=1, source_target_pairs={{0,1},{1,0},{2,3},{3,2},{4,5},{5,4},{6,7},{7,6},{8,9},{9,8},{10,11... | collective-permute-start | bytes 3145736 | tf_op jit(solution)/shard_map/ppermute | solution.py:152
  4.4 0.7 %copy-start.9 = (f32[8,2]{0,1:T(2,128)S(1)}, f32[8,2]{0,1:T(2,128)}, u32[]{:S(2)}) copy-start(f32[8,2]{0,1:T(2,128)} %param.15) | copy-start | bytes 196
  4.4 0.7 %copy-start.10 = (s32[64]{0:T(128)S(1)}, s32[64]{0:T(128)}, u32[]{:S(2)}) copy-start(s32[64]{0:T(128)} %param.16) | copy-start | bytes 772
  4.4 0.7 %copy-start.11 = (s32[64]{0:T(128)S(1)}, s32[64]{0:T(128)}, u32[]{:S(2)}) copy-start(s32[64]{0:T(128)} %param.17) | copy-start | bytes 772
  4.4 0.7 %copy-start.7 = (f32[1024]{0:T(1024)S(1)}, f32[1024]{0:T(1024)}, u32[]{:S(2)}) copy-start(f32[1024]{0:T(1024)} %param.22) | copy-start | bytes 12292
  4.4 0.7 %copy-start.6 = (f32[1024]{0:T(1024)S(1)}, f32[1024]{0:T(1024)}, u32[]{:S(2)}) copy-start(f32[1024]{0:T(1024)} %param.18) | copy-start | bytes 12292
  4.4 0.7 %copy-start.8 = (s32[8,2]{0,1:T(2,128)S(1)}, s32[8,2]{0,1:T(2,128)}, u32[]{:S(2)}) copy-start(s32[8,2]{0,1:T(2,128)} %param.14) | copy-start | bytes 196
  5.1 0.7 %copy-start.12 = (bf16[8,1024]{1,0:T(8,128)(2,1)S(1)}, bf16[8,1024]{1,0:T(8,128)(2,1)}, u32[]{:S(2)}) copy-start(bf16[8,1024]{1,0:T(8,128)(2,1)} %mine_ref.1) | copy-start | bytes 49156
  5.4 3.3 %copy-start = (bf16[1024,352]{0,1:T(8,128)(2,1)S(1)}, bf16[1024,352]{0,1:T(8,128)(2,1)}, u32[]{:S(2)}) copy-start(bf16[1024,352]{0,1:T(8,128)(2,1)} %param.19) | copy-start | bytes 2162692
  5.4 3.3 %copy-start.1 = (bf16[1024,352]{0,1:T(8,128)(2,1)S(1)}, bf16[1024,352]{0,1:T(8,128)(2,1)}, u32[]{:S(2)}) copy-start(bf16[1024,352]{0,1:T(8,128)(2,1)} %param.20) | copy-start | bytes 2162692
  5.4 3.3 %copy-start.2 = (bf16[352,1024]{1,0:T(8,128)(2,1)S(1)}, bf16[352,1024]{1,0:T(8,128)(2,1)}, u32[]{:S(2)}) copy-start(bf16[352,1024]{1,0:T(8,128)(2,1)} %refs_5_.3) | copy-start | bytes 2162692
  5.9 5.0 %collective-permute-start.1 = (bf16[16,1024]{1,0:T(8,128)(2,1)S(1)}, bf16[16,1024]{1,0:T(8,128)(2,1)S(1)}, u32[]{:S(2)}, u32[]{:S(2)}) collective-permute-start(bf16[16,1024]{1,0:T(8,128)(2,1)S(1)} %shard_map.149.rows_ref.refs_0_), channel_id=1, source_target_pairs={{0,5},{1,4},{2,7},{3,6},{4,1},{5,0},{6,3},{7,2},{8,13},{9,12},{10,... | collective-permute-start | bytes 98312 | tf_op jit(solution)/shard_map/ppermute | solution.py:152
  9.9 3.6 %collective-permute-start.5 = (bf16[16,1152]{1,0:T(8,128)(2,1)S(1)}, bf16[16,1152]{1,0:T(8,128)(2,1)S(1)}, u32[]{:S(2)}, u32[]{:S(2)}) collective-permute-start(bf16[16,1152]{1,0:T(8,128)(2,1)S(1)} %get-tuple-element.20), channel_id=1, source_target_pairs={{0,3},{1,2},{2,1},{3,0},{4,7},{5,6},{6,5},{7,4},{8,11},{9,10},{10,... | collective-permute-start | bytes 110600 | tf_op jit(solution)/shard_map/ppermute | solution.py:152
  11.0 10.4 %copy-start.3 = (bf16[1024,512]{1,0:T(8,128)(2,1)S(1)}, bf16[1024,512]{1,0:T(8,128)(2,1)}, u32[]{:S(2)}) copy-start(bf16[1024,512]{1,0:T(8,128)(2,1)} %refs_9_.1) | copy-start | bytes 3145732
  12.2 4.1 %collective-permute-start.6 = (bf16[16,1024]{1,0:T(8,128)(2,1)S(1)}, bf16[16,1024]{1,0:T(8,128)(2,1)S(1)}, u32[]{:S(2)}, u32[]{:S(2)}) collective-permute-start(bf16[16,1024]{1,0:T(8,128)(2,1)S(1)} %get-tuple-element.22), channel_id=1, source_target_pairs={{0,3},{1,2},{2,1},{3,0},{4,7},{5,6},{6,5},{7,4},{8,11},{9,10},{10,... | collective-permute-start | bytes 98312 | tf_op jit(solution)/shard_map/ppermute | solution.py:152
  13.5 7.9 %collective-permute-start.7 = (bf16[16,1152]{1,0:T(8,128)(2,1)S(1)}, bf16[16,1152]{1,0:T(8,128)(2,1)S(1)}, u32[]{:S(2)}, u32[]{:S(2)}) collective-permute-start(bf16[16,1152]{1,0:T(8,128)(2,1)S(1)} %get-tuple-element.24), channel_id=1, source_target_pairs={{0,5},{1,4},{2,7},{3,6},{4,1},{5,0},{6,3},{7,2},{8,13},{9,12},{10,... | collective-permute-start | bytes 110600 | tf_op jit(solution)/shard_map/ppermute | solution.py:152
  16.2 5.2 %collective-permute-start.10 = (bf16[64,512]{1,0:T(8,128)(2,1)S(1)}, bf16[64,512]{1,0:T(8,128)(2,1)S(1)}, u32[]{:S(2)}, u32[]{:S(2)}) collective-permute-start(bf16[64,512]{1,0:T(8,128)(2,1)S(1)} %get-tuple-element.27.refs_11_), channel_id=1, source_target_pairs={{0,1},{1,0},{2,3},{3,2},{4,5},{5,4},{6,7},{7,6},{8,9},{9,8},{10,11... | collective-permute-start | bytes 196616 | tf_op jit(solution)/shard_map/ppermute | solution.py:152
  16.3 5.1 %collective-permute-start.8 = (bf16[16,1024]{1,0:T(8,128)(2,1)S(1)}, bf16[16,1024]{1,0:T(8,128)(2,1)S(1)}, u32[]{:S(2)}, u32[]{:S(2)}) collective-permute-start(bf16[16,1024]{1,0:T(8,128)(2,1)S(1)} %get-tuple-element.31), channel_id=1, source_target_pairs={{0,5},{1,4},{2,7},{3,6},{4,1},{5,0},{6,3},{7,2},{8,13},{9,12},{10,... | collective-permute-start | bytes 98312 | tf_op jit(solution)/shard_map/ppermute | solution.py:152
  22.4 3.0 %collective-permute-start.11 = (f32[8,32]{1,0:T(8,128)S(1)}, f32[8,32]{1,0:T(8,128)S(1)}, u32[]{:S(2)}, u32[]{:S(2)}) collective-permute-start(f32[8,32]{1,0:T(8,128)S(1)} %shard_map.153.one_ref), channel_id=1, source_target_pairs={{0,3},{1,2},{2,1},{3,0},{4,7},{5,6},{6,5},{7,4},{8,11},{9,10},{10,... | collective-permute-start | bytes 3080 | tf_op jit(solution)/shard_map/ppermute | solution.py:152
  25.5 4.0 %collective-permute-start.12 = (f32[8,32]{1,0:T(8,128)S(1)}, f32[8,32]{1,0:T(8,128)S(1)}, u32[]{:S(2)}, u32[]{:S(2)}) collective-permute-start(f32[8,32]{1,0:T(8,128)S(1)} %shard_map.154.one_ref), channel_id=1, source_target_pairs={{0,5},{1,4},{2,7},{3,6},{4,1},{5,0},{6,3},{7,2},{8,13},{9,12},{10,... | collective-permute-start | bytes 3080 | tf_op jit(solution)/shard_map/ppermute | solution.py:152
  29.5 1.2 %collective-permute-start.13 = (f32[8,32]{1,0:T(8,128)S(1)}, f32[8,32]{1,0:T(8,128)S(1)}, u32[]{:S(2)}, u32[]{:S(2)}) collective-permute-start(f32[8,32]{1,0:T(8,128)S(1)} %shard_map.155.refs_0_), channel_id=1, source_target_pairs={{0,1},{1,0},{2,3},{3,2},{4,5},{5,4},{6,7},{7,6},{8,9},{9,8},{10,11... | collective-permute-start | bytes 3080 | tf_op jit(solution)/shard_map/ppermute | solution.py:152

commit v6 on v5

--- a/solution.py
+++ b/solution.py
@@ -9,7 +9,7 @@
 
 SPLIT = 4
 SEQS = 16
-ROUND_FLOPS = 4 << 30
+ROUND_FLOPS = 16 << 30
 
 
 epsilon = 1e-06
@@ -182,30 +182,12 @@
     return my_index, parity, tok_rows << (bits - 1)
 
 
-def prepare_kernel(
-    tok_rows,
-    bits,
-    ids_ref,
-    gates_ref,
-    targets_ref,
-    seq_ref,
-    moe_gain_ref,
-    final_gain_ref,
-    down_ref,
-    up_ref,
-    gains_ref,
-    down_out_ref,
-    up_out_ref,
-    mixing_ref,
-    columns_ref,
-):
+def early_kernel(tok_rows, bits, *refs):
+    (ids_ref, gates_ref), (mixing_ref,) = refs[0:2], refs[5:6]
+    for in_ref, out_ref in zip(refs[2:5], refs[6:9]):
+        out_ref[...] = in_ref[...]
     my_index, parity, half = places(tok_rows, bits)
     experts = gates_ref.shape[0]
-    gains_ref[...] = jnp.concatenate(
-        [moe_gain_ref[...]] * 4 + [final_gain_ref[...]] * 4, axis=0
-    )
-    down_out_ref[...] = down_ref[...]
-    up_out_ref[...] = up_ref[...]
     rows = [
         sum(
             jnp.where(ids_ref[k : k + 1] == expert, gates_ref[k : k + 1], 0.0)
@@ -226,6 +208,10 @@
     mine = (lane < half // tok_rows * 8) & (token // tok_rows == my_index)
     mixing = jnp.where(mine, parts, 0.0)
     mixing_ref[...] = jnp.concatenate([mixing, jnp.zeros_like(mixing)], axis=0)
+
+
+def columns_kernel(tok_rows, bits, targets_ref, seq_ref, columns_ref):
+    my_index, parity, half = places(tok_rows, bits)
     row = lax.broadcasted_iota(jnp.int32, (half, 128), 0)
     lane = lax.broadcasted_iota(jnp.int32, (half, 128), 1)
     token = token_at(row + parity * half, tok_rows, bits) - my_index * tok_rows
@@ -248,14 +234,14 @@
     out_ref[...] = in_order(late, mine_ref[...], other_ref[...])
 
 
-def expert_kernel(rows_ref, gains_ref, *refs):
+def expert_kernel(rows_ref, gain_ref, *refs):
     far_refs, near_refs, mixing_refs, (total_ref, sent_ref) = (
         refs[0:3],
         refs[3:6],
         refs[6:-2],
         refs[-2:],
     )
-    moe_input = rms_norm(rows_ref[...].astype(jnp.float32), gains_ref[0:1]).astype(jnp.bfloat16)
+    moe_input = rms_norm(rows_ref[...].astype(jnp.float32), gain_ref[...]).astype(jnp.bfloat16)
 
     def units(gate_ref, up_ref, down_ref):
         projections = [
@@ -268,6 +254,12 @@
     total = units(*near_refs) + units(*far_refs)
     total = jnp.concatenate([total, *(ref[...] for ref in mixing_refs)], axis=1)
     total_ref[...] = total
+    sent_ref[...] = total.astype(jnp.bfloat16)
+
+
+def add_kernel(total_ref, arrived_ref, sum_ref, sent_ref):
+    total = total_ref[...] + arrived_ref[...].astype(jnp.float32)
+    sum_ref[...] = total
     sent_ref[...] = total.astype(jnp.bfloat16)
 
 
@@ -306,7 +298,7 @@
 
 
 def head_kernel(place, *refs):
-    row_refs, sum_refs, (gains_ref, columns_ref, down_ref), weight_refs, (stats_ref,) = (
+    row_refs, sum_refs, (gain_ref, columns_ref, down_ref), weight_refs, (stats_ref,) = (
         refs[0:2],
         refs[2:6],
         refs[6:9],
@@ -316,7 +308,7 @@
     my_index = lax.axis_index("tensor")
     sums = [ref[...] for ref in sum_refs]
     pieces = [ref[...] for ref in row_refs]
-    rows = final_rows(place, pieces, sums[0:2], sums[2:4], gains_ref[4:5])
+    rows = final_rows(place, pieces, sums[0:2], sums[2:4], gain_ref[...])
     tokens = rows.shape[0]
     wanted = columns_ref[0][:, 0:1].astype(jnp.int32)
     latent = lax.dot_general(rows, down_ref[...], TRANSPOSED, preferred_element_type=jnp.float32)
@@ -406,34 +398,29 @@
         return jax.ShapeDtypeStruct(shape, dtype)
 
     flags = call(flags_kernel, array(jnp.int32, 8, 128), flops=ROUND_FLOPS)
+    mixing, held_rows, gain, last_gain = call(
+        functools.partial(early_kernel, tok_rows, bits),
+        [
+            array(jnp.float32, 2 * tok_rows, 128),
+            array(jnp.bfloat16, tok_rows, features),
+            array(jnp.float32, 1, features),
+            array(jnp.float32, 1, features),
+        ],
+        expert_ids.T,
+        gate_weights.T,
+        hidden_in,
+        moe_gain[None],
+        final_gain[None],
+    )
     first = call(
         functools.partial(order_kernel, near_bit),
         array(jnp.bfloat16, 2 * tok_rows, features),
         flags,
-        hidden_in,
+        held_rows,
         exchange(hidden_in, near_mask),
         flops=ROUND_FLOPS,
     )
     second = exchange(first, far_mask)
-    gains, down, up, mixing, columns = call(
-        lambda *refs: prepare_kernel(tok_rows, bits, *refs),
-        [
-            array(jnp.float32, 8, features),
-            array(jnp.bfloat16, *adapter_down.shape[::-1]),
-            array(jnp.bfloat16, *adapter_up.shape),
-            array(jnp.float32, 2 * tok_rows, 128),
-            array(jnp.float32, 3, half, 128),
-        ],
-        expert_ids.T,
-        gate_weights.T,
-        targets[None],
-        seq_ids[None],
-        moe_gain[None],
-        final_gain[None],
-        adapter_down.T,
-        adapter_up,
-    )
-
     units = [w_gate.T, w_up.T, w_down]
     units = [exchange(unit, 1) for unit in units] + units
     totals, sent = [], []
@@ -445,17 +432,30 @@
                 for dtype in (jnp.float32, jnp.bfloat16)
             ],
             rows,
-            gains,
+            gain,
             *units,
             *more,
             flops=3 * devices * tok_rows * features * w_gate.shape[1],
         )
-        total = outputs[0] + exchange(outputs[1], near_mask).astype(jnp.float32)
+        total, piece = call(
+            add_kernel,
+            [array(output.dtype, *output.shape) for output in outputs],
+            outputs[0],
+            exchange(outputs[1], near_mask),
+            flops=ROUND_FLOPS // 16 * len(totals),
+        )
         totals.append(total)
-        sent.append(total.astype(jnp.bfloat16))
-    sent[0], up_sent = lax.optimization_barrier((sent[0], up))
+        sent.append(piece)
+    sent[0], late_seq = lax.optimization_barrier((sent[0], seq_ids[None]))
+    sent[1], late_targets = lax.optimization_barrier((sent[1], targets[None]))
     arrived = [exchange(piece, far_mask) for piece in sent]
 
+    (columns,) = call(
+        functools.partial(columns_kernel, tok_rows, bits),
+        [array(jnp.float32, 3, half, 128)],
+        late_targets,
+        late_seq,
+    )
     stats = call(
         functools.partial(head_kernel, far_bit),
         array(jnp.float32, 8, half),
@@ -463,13 +463,13 @@
         second,
         *totals,
         *arrived,
-        gains,
+        last_gain,
         columns,
-        down,
+        adapter_down.T,
         head_weight,
         exchange(head_weight, 1),
-        up,
-        exchange(up_sent, 1),
+        adapter_up,
+        exchange(adapter_up, 1),
         flops=2 * devices * tok_rows * features * head_weight.shape[1],
     )
     for mask in (near_mask, far_mask):

time: 31.7 us -> 31.6 us (level)
  starting transfers between devices: 14 us -> 14.9 us
  waiting for transfers between devices: 11 us -> 10.3 us
  local copies, waits for them, and re-layouts: 1.21 us -> 0.75 us
    ppermute x14, starting transfers between devices: 14 us -> 14.9 us  [exchange(): lax.ppermute(values, 'tensor', [(i, i ^ mask) for i in range(devices)])]
    ppermute x14, waiting for transfers between devices: 11 us -> 10.3 us  [exchange(): lax.ppermute(values, 'tensor', [(i, i ^ mask) for i in range(devices)])]
    unnamed x26, local copies, waits for them, and re-layouts: 1.21 us -> 0.75 us
    pallas_call x9 -> x12, Pallas kernels: 4.44 us -> 4.56 us  [call(): pl.pallas_call(kernel, out_shape=shapes, compiler_params=pltpu.CompilerPa...]
  transfers between devices with their start and end apart: 14 -> 14, of which waited for: 5 -> 4; matrix products, arithmetic and copies ran while one was open for 0% -> 0% of each run, Pallas kernels for 9% -> 9%
where the time goes in v6:
time: 31.6 us; the launch traced here: 31.3 us
  starting transfers between devices  14.9 us (47%)
  waiting for transfers between devices  10.3 us (33%)
  Pallas kernels  4.56 us (14%)
  between operations  0.79 us (2%)
  local copies, waits for them, and re-layouts  0.75 us (2%)
    ppermute x14, starting transfers between devices, exchange(): lax.ppermute(values, 'tensor', [(i, i ^ mask) for i in range(devices)])  14.9 us
    ppermute x14, waiting for transfers between devices, exchange(): lax.ppermute(values, 'tensor', [(i, i ^ mask) for i in range(devices)])  10.3 us
    pallas_call x12, Pallas kernels, call(): pl.pallas_call(kernel, out_shape=shapes, compiler_params=pltpu.CompilerPa...  4.56 us
    unnamed x26, local copies, waits for them, and re-layouts  0.75 us
  transfers between devices with their start and end apart: 14, of which 4 were waited for; matrix products, arithmetic and copies ran while one was open for 0% of the time, Pallas kernels for 9%

profile of v6, /device:TPU:0, one launch (start us, length us, event | category | flops | bytes accessed | tf_op | source)
XLA Modules:
  0.0 31.3 jit_solution(16285029224643206121)
XLA Ops:
  0.6 2.5 %collective-permute-start = (bf16[8,1024]{1,0:T(8,128)(2,1)}, bf16[8,1024]{1,0:T(8,128)(2,1)S(1)}, u32[]{:S(2)}, u32[]{:S(2)}) collective-permute-start(bf16[8,1024]{1,0:T(8,128)(2,1)} %refs_2_.1), channel_id=1, source_target_pairs={{0,3},{1,2},{2,1},{3,0},{4,7},{5,6},{6,5},{7,4},{8,11},{9,10},{10,... | collective-permute-start | bytes 49160 | tf_op jit(solution)/shard_map/ppermute | solution.py:152
  3.2 0.7 %collective-permute-start.2 = (bf16[352,1024]{1,0:T(8,128)(2,1)}, bf16[352,1024]{1,0:T(8,128)(2,1)S(1)}, u32[]{:S(2)}, u32[]{:S(2)}) collective-permute-start(bf16[352,1024]{1,0:T(8,128)(2,1)} %bitcast.12), channel_id=1, source_target_pairs={{0,1},{1,0},{2,3},{3,2},{4,5},{5,4},{6,7},{7,6},{8,9},{9,8},{10,11... | collective-permute-start | bytes 2162696 | tf_op jit(solution)/shard_map/ppermute | solution.py:152
  3.8 0.5 %collective-permute-start.4 = (bf16[352,1024]{1,0:T(8,128)(2,1)}, bf16[352,1024]{1,0:T(8,128)(2,1)S(1)}, u32[]{:S(2)}, u32[]{:S(2)}) collective-permute-start(bf16[352,1024]{1,0:T(8,128)(2,1)} %refs_5_.3), channel_id=1, source_target_pairs={{0,1},{1,0},{2,3},{3,2},{4,5},{5,4},{6,7},{7,6},{8,9},{9,8},{10,11... | collective-permute-start | bytes 2162696 | tf_op jit(solution)/shard_map/ppermute | solution.py:152
  4.4 0.0 copy-start.7
  4.4 0.0 copy-start.9
  4.4 0.7 %copy-done.6 = bf16[8,1024]{1,0:T(8,128)(2,1)S(1)} copy-done((bf16[8,1024]{1,0:T(8,128)(2,1)S(1)}, bf16[8,1024]{1,0:T(8,128)(2,1)}, u32[]{:S(2)}) %copy-start.6) | copy-done | bytes 16408
  5.1 0.0 copy-done.7
  5.1 0.0 copy-done.9
  5.1 0.2 shard_map.149
  5.3 0.0 copy-start
  5.3 0.0 copy-start.1
  5.3 0.0 copy-start.2
  5.4 2.8 %collective-permute-start.1 = (bf16[16,1024]{1,0:T(8,128)(2,1)S(1)}, bf16[16,1024]{1,0:T(8,128)(2,1)S(1)}, u32[]{:S(2)}, u32[]{:S(2)}) collective-permute-start(bf16[16,1024]{1,0:T(8,128)(2,1)S(1)} %shard_map.150.rows_ref.refs_0_), channel_id=1, source_target_pairs={{0,5},{1,4},{2,7},{3,6},{4,1},{5,0},{6,3},{7,2},{8,13},{9,12},{10,... | collective-permute-start | bytes 98312 | tf_op jit(solution)/shard_map/ppermute | solution.py:152
  8.2 1.2 %shard_map.151 = (f32[16,1152]{1,0:T(8,128)S(1)}, bf16[16,1152]{1,0:T(8,128)(2,1)S(1)}) custom-call(bf16[16,1024]{1,0:T(8,128)(2,1)S(1)} %shard_map.150.rows_ref.refs_0_, f32[1,1024]{1,0:T(1,128)S(1)} %get-tuple-element.23.gain_ref, bf16[352,1024]{1,0:T(8,128)(2,1)S(1)} %collective-permute-done.2.refs_0_, ...), custom_call_target="tpu_custom_call" | custom-call | flops 69206016 | bytes 4370432 | tf_op jit(solution)/shard_map/pallas_call | solution.py:367
  9.4 1.6 %collective-permute-start.5 = (bf16[16,1152]{1,0:T(8,128)(2,1)S(1)}, bf16[16,1152]{1,0:T(8,128)(2,1)S(1)}, u32[]{:S(2)}, u32[]{:S(2)}) collective-permute-start(bf16[16,1152]{1,0:T(8,128)(2,1)S(1)} %get-tuple-element.26), channel_id=1, source_target_pairs={{0,3},{1,2},{2,1},{3,0},{4,7},{5,6},{6,5},{7,4},{8,11},{9,10},{10,... | collective-permute-start | bytes 110600 | tf_op jit(solution)/shard_map/ppermute | solution.py:152
  11.0 1.2 %shard_map.153 = (f32[16,1024]{1,0:T(8,128)S(1)}, bf16[16,1024]{1,0:T(8,128)(2,1)S(1)}) custom-call(bf16[16,1024]{1,0:T(8,128)(2,1)S(1)} %collective-permute-done.1.rows_ref.refs_1_, f32[1,1024]{1,0:T(1,128)S(1)} %get-tuple-element.23.gain_ref, bf16[352,1024]{1,0:T(8,128)(2,1)S(1)} %collective-permute-done.2.refs_0_, ...), custom_call_target="tpu_custom_call" | custom-call | flops 69206016 | bytes 4362240 | tf_op jit(solution)/shard_map/pallas_call | solution.py:367
  12.2 0.4 %collective-permute-start.6 = (bf16[16,1024]{1,0:T(8,128)(2,1)S(1)}, bf16[16,1024]{1,0:T(8,128)(2,1)S(1)}, u32[]{:S(2)}, u32[]{:S(2)}) collective-permute-start(bf16[16,1024]{1,0:T(8,128)(2,1)S(1)} %get-tuple-element.29), channel_id=1, source_target_pairs={{0,3},{1,2},{2,1},{3,0},{4,7},{5,6},{6,5},{7,4},{8,11},{9,10},{10,... | collective-permute-start | bytes 98312 | tf_op jit(solution)/shard_map/ppermute | solution.py:152
  12.6 0.4 %collective-permute-start.10 = (bf16[64,512]{1,0:T(8,128)(2,1)S(1)}, bf16[64,512]{1,0:T(8,128)(2,1)S(1)}, u32[]{:S(2)}, u32[]{:S(2)}) collective-permute-start(bf16[64,512]{1,0:T(8,128)(2,1)S(1)} %copy-done.5), channel_id=1, source_target_pairs={{0,1},{1,0},{2,3},{3,2},{4,5},{5,4},{6,7},{7,6},{8,9},{9,8},{10,11... | collective-permute-start | bytes 196616 | tf_op jit(solution)/shard_map/ppermute | solution.py:152
  13.0 3.0 %collective-permute-start.7 = (bf16[16,1152]{1,0:T(8,128)(2,1)S(1)}, bf16[16,1152]{1,0:T(8,128)(2,1)S(1)}, u32[]{:S(2)}, u32[]{:S(2)}) collective-permute-start(bf16[16,1152]{1,0:T(8,128)(2,1)S(1)} %get-tuple-element.32), channel_id=1, source_target_pairs={{0,5},{1,4},{2,7},{3,6},{4,1},{5,0},{6,3},{7,2},{8,13},{9,12},{10,... | collective-permute-start | bytes 110600 | tf_op jit(solution)/shard_map/ppermute | solution.py:152
  16.1 0.0 copy-start.11
  16.1 0.0 copy-start.12
  16.1 1.5 %collective-permute-start.8 = (bf16[16,1024]{1,0:T(8,128)(2,1)S(1)}, bf16[16,1024]{1,0:T(8,128)(2,1)S(1)}, u32[]{:S(2)}, u32[]{:S(2)}) collective-permute-start(bf16[16,1024]{1,0:T(8,128)(2,1)S(1)} %get-tuple-element.34), channel_id=1, source_target_pairs={{0,5},{1,4},{2,7},{3,6},{4,1},{5,0},{6,3},{7,2},{8,13},{9,12},{10,... | collective-permute-start | bytes 98312 | tf_op jit(solution)/shard_map/ppermute | solution.py:152
  17.6 0.1 shard_map.155.refs_7_.refs_2_
  17.7 3.5 %collective-permute-done.8.refs_5_ = bf16[16,1024]{1,0:T(8,128)(2,1)S(1)} collective-permute-done((bf16[16,1024]{1,0:T(8,128)(2,1)S(1)}, bf16[16,1024]{1,0:T(8,128)(2,1)S(1)}, u32[]{:S(2)}, u32[]{:S(2)}) %collective-permute-start.8) | collective-permute-done | bytes 32800 | tf_op jit(solution)/shard_map/ppermute | solution.py:152
  21.3 1.0 %shard_map.156.one_ref = f32[8,32]{1,0:T(8,128)S(1)} custom-call(bf16[16,1024]{1,0:T(8,128)(2,1)S(1)} %shard_map.150.rows_ref.refs_0_, bf16[16,1024]{1,0:T(8,128)(2,1)S(1)} %collective-permute-done.1.rows_ref.refs_1_, f32[16,1152]{1,0:T(8,128)S(1)} %get-tuple-element.27.refs_2_, f32[16,1024]{1,0:T(8,128)S(1)} %get-tuple-element.30.refs_3_, ...), custom_call_target="tpu_custom_call" | custom-call | flops 67108864 | bytes 2686976 | tf_op jit(solution)/shard_map/pallas_call | solution.py:367
  22.3 0.0 collective-permute-start.11
  22.3 3.0 %collective-permute-done.11.two_ref = f32[8,32]{1,0:T(8,128)S(1)} collective-permute-done((f32[8,32]{1,0:T(8,128)S(1)}, f32[8,32]{1,0:T(8,128)S(1)}, u32[]{:S(2)}, u32[]{:S(2)}) %collective-permute-start.11) | collective-permute-done | bytes 1056 | tf_op jit(solution)/shard_map/ppermute | solution.py:152
  25.3 1.3 %collective-permute-start.12 = (f32[8,32]{1,0:T(8,128)S(1)}, f32[8,32]{1,0:T(8,128)S(1)}, u32[]{:S(2)}, u32[]{:S(2)}) collective-permute-start(f32[8,32]{1,0:T(8,128)S(1)} %shard_map.157.one_ref), channel_id=1, source_target_pairs={{0,5},{1,4},{2,7},{3,6},{4,1},{5,0},{6,3},{7,2},{8,13},{9,12},{10,... | collective-permute-start | bytes 3080 | tf_op jit(solution)/shard_map/ppermute | solution.py:152
  26.7 2.7 %collective-permute-done.12.two_ref = f32[8,32]{1,0:T(8,128)S(1)} collective-permute-done((f32[8,32]{1,0:T(8,128)S(1)}, f32[8,32]{1,0:T(8,128)S(1)}, u32[]{:S(2)}, u32[]{:S(2)}) %collective-permute-start.12) | collective-permute-done | bytes 1056 | tf_op jit(solution)/shard_map/ppermute | solution.py:152
  29.3 0.2 collective-permute-start.13
  29.5 1.1 %collective-permute-done.13.refs_1_ = f32[8,32]{1,0:T(8,128)S(1)} collective-permute-done((f32[8,32]{1,0:T(8,128)S(1)}, f32[8,32]{1,0:T(8,128)S(1)}, u32[]{:S(2)}, u32[]{:S(2)}) %collective-permute-start.13) | collective-permute-done | bytes 1056 | tf_op jit(solution)/shard_map/ppermute | solution.py:152
  30.6 0.7 %shard_map.159 = (f32[1,8]{1,0:T(1,128)}, f32[1,8]{1,0:T(1,128)}, f32[1,16]{1,0:T(1,128)}) custom-call(f32[8,32]{1,0:T(8,128)S(1)} %shard_map.158.refs_0_, f32[8,32]{1,0:T(8,128)S(1)} %collective-permute-done.13.refs_1_, f32[3,32,128]{2,1,0:T(8,128)S(1)} %shard_map.155.refs_7_.refs_2_), custom_call_target="tpu_custom_call" | custom-call | bytes 51200 | tf_op jit(solution)/shard_map/pallas_call | solution.py:367
  (34 shorter events, 0.2 us)
Async XLA Ops:
  0.6 4.6 %collective-permute-start = (bf16[8,1024]{1,0:T(8,128)(2,1)}, bf16[8,1024]{1,0:T(8,128)(2,1)S(1)}, u32[]{:S(2)}, u32[]{:S(2)}) collective-permute-start(bf16[8,1024]{1,0:T(8,128)(2,1)} %refs_2_.1), channel_id=1, source_target_pairs={{0,3},{1,2},{2,1},{3,0},{4,7},{5,6},{6,5},{7,4},{8,11},{9,10},{10,... | collective-permute-start | bytes 49160 | tf_op jit(solution)/shard_map/ppermute | solution.py:152
  3.2 5.0 %collective-permute-start.2 = (bf16[352,1024]{1,0:T(8,128)(2,1)}, bf16[352,1024]{1,0:T(8,128)(2,1)S(1)}, u32[]{:S(2)}, u32[]{:S(2)}) collective-permute-start(bf16[352,1024]{1,0:T(8,128)(2,1)} %bitcast.12), channel_id=1, source_target_pairs={{0,1},{1,0},{2,3},{3,2},{4,5},{5,4},{6,7},{7,6},{8,9},{9,8},{10,11... | collective-permute-start | bytes 2162696 | tf_op jit(solution)/shard_map/ppermute | solution.py:152
  3.8 4.3 %collective-permute-start.3 = (bf16[352,1024]{1,0:T(8,128)(2,1)}, bf16[352,1024]{1,0:T(8,128)(2,1)S(1)}, u32[]{:S(2)}, u32[]{:S(2)}) collective-permute-start(bf16[352,1024]{1,0:T(8,128)(2,1)} %bitcast.15), channel_id=1, source_target_pairs={{0,1},{1,0},{2,3},{3,2},{4,5},{5,4},{6,7},{7,6},{8,9},{9,8},{10,11... | collective-permute-start | bytes 2162696 | tf_op jit(solution)/shard_map/ppermute | solution.py:152
  3.8 4.3 %collective-permute-start.4 = (bf16[352,1024]{1,0:T(8,128)(2,1)}, bf16[352,1024]{1,0:T(8,128)(2,1)S(1)}, u32[]{:S(2)}, u32[]{:S(2)}) collective-permute-start(bf16[352,1024]{1,0:T(8,128)(2,1)} %refs_5_.3), channel_id=1, source_target_pairs={{0,1},{1,0},{2,3},{3,2},{4,5},{5,4},{6,7},{7,6},{8,9},{9,8},{10,11... | collective-permute-start | bytes 2162696 | tf_op jit(solution)/shard_map/ppermute | solution.py:152
  4.3 16.9 %collective-permute-start.9 = (bf16[1024,512]{1,0:T(8,128)(2,1)}, bf16[1024,512]{1,0:T(8,128)(2,1)S(1)}, u32[]{:S(2)}, u32[]{:S(2)}) collective-permute-start(bf16[1024,512]{1,0:T(8,128)(2,1)} %refs_9_.1), channel_id=1, source_target_pairs={{0,1},{1,0},{2,3},{3,2},{4,5},{5,4},{6,7},{7,6},{8,9},{9,8},{10,11... | collective-permute-start | bytes 3145736 | tf_op jit(solution)/shard_map/ppermute | solution.py:152
  4.3 0.7 %copy-start.6 = (bf16[8,1024]{1,0:T(8,128)(2,1)S(1)}, bf16[8,1024]{1,0:T(8,128)(2,1)}, u32[]{:S(2)}) copy-start(bf16[8,1024]{1,0:T(8,128)(2,1)} %refs_2_.1) | copy-start | bytes 49156
  4.4 0.7 %copy-start.8 = (f32[1024]{0:T(1024)S(1)}, f32[1024]{0:T(1024)}, u32[]{:S(2)}) copy-start(f32[1024]{0:T(1024)} %param.22) | copy-start | bytes 12292
  4.4 0.7 %copy-start.10 = (f32[8,2]{0,1:T(2,128)S(1)}, f32[8,2]{0,1:T(2,128)}, u32[]{:S(2)}) copy-start(f32[8,2]{0,1:T(2,128)} %param.15) | copy-start | bytes 196
  4.4 0.7 %copy-start.7 = (f32[1024]{0:T(1024)S(1)}, f32[1024]{0:T(1024)}, u32[]{:S(2)}) copy-start(f32[1024]{0:T(1024)} %param.18) | copy-start | bytes 12292
  4.4 0.7 %copy-start.9 = (s32[8,2]{0,1:T(2,128)S(1)}, s32[8,2]{0,1:T(2,128)}, u32[]{:S(2)}) copy-start(s32[8,2]{0,1:T(2,128)} %param.14) | copy-start | bytes 196
  5.3 2.9 %copy-start = (bf16[1024,352]{0,1:T(8,128)(2,1)S(1)}, bf16[1024,352]{0,1:T(8,128)(2,1)}, u32[]{:S(2)}) copy-start(bf16[1024,352]{0,1:T(8,128)(2,1)} %param.19) | copy-start | bytes 2162692
  5.3 2.9 %copy-start.1 = (bf16[1024,352]{0,1:T(8,128)(2,1)S(1)}, bf16[1024,352]{0,1:T(8,128)(2,1)}, u32[]{:S(2)}) copy-start(bf16[1024,352]{0,1:T(8,128)(2,1)} %param.20) | copy-start | bytes 2162692
  5.3 2.9 %copy-start.2 = (bf16[352,1024]{1,0:T(8,128)(2,1)S(1)}, bf16[352,1024]{1,0:T(8,128)(2,1)}, u32[]{:S(2)}) copy-start(bf16[352,1024]{1,0:T(8,128)(2,1)} %refs_5_.3) | copy-start | bytes 2162692
  5.4 5.6 %collective-permute-start.1 = (bf16[16,1024]{1,0:T(8,128)(2,1)S(1)}, bf16[16,1024]{1,0:T(8,128)(2,1)S(1)}, u32[]{:S(2)}, u32[]{:S(2)}) collective-permute-start(bf16[16,1024]{1,0:T(8,128)(2,1)S(1)} %shard_map.150.rows_ref.refs_0_), channel_id=1, source_target_pairs={{0,5},{1,4},{2,7},{3,6},{4,1},{5,0},{6,3},{7,2},{8,13},{9,12},{10,... | collective-permute-start | bytes 98312 | tf_op jit(solution)/shard_map/ppermute | solution.py:152
  9.4 3.2 %copy-start.5 = (bf16[64,512]{1,0:T(8,128)(2,1)S(1)}, bf16[64,512]{1,0:T(8,128)(2,1)}, u32[]{:S(2)}) copy-start(bf16[64,512]{1,0:T(8,128)(2,1)} %refs_11_.1) | copy-start | bytes 196612
  9.4 3.6 %collective-permute-start.5 = (bf16[16,1152]{1,0:T(8,128)(2,1)S(1)}, bf16[16,1152]{1,0:T(8,128)(2,1)S(1)}, u32[]{:S(2)}, u32[]{:S(2)}) collective-permute-start(bf16[16,1152]{1,0:T(8,128)(2,1)S(1)} %get-tuple-element.26), channel_id=1, source_target_pairs={{0,3},{1,2},{2,1},{3,0},{4,7},{5,6},{6,5},{7,4},{8,11},{9,10},{10,... | collective-permute-start | bytes 110600 | tf_op jit(solution)/shard_map/ppermute | solution.py:152
  12.2 3.9 %collective-permute-start.6 = (bf16[16,1024]{1,0:T(8,128)(2,1)S(1)}, bf16[16,1024]{1,0:T(8,128)(2,1)S(1)}, u32[]{:S(2)}, u32[]{:S(2)}) collective-permute-start(bf16[16,1024]{1,0:T(8,128)(2,1)S(1)} %get-tuple-element.29), channel_id=1, source_target_pairs={{0,3},{1,2},{2,1},{3,0},{4,7},{5,6},{6,5},{7,4},{8,11},{9,10},{10,... | collective-permute-start | bytes 98312 | tf_op jit(solution)/shard_map/ppermute | solution.py:152
  12.6 5.1 %collective-permute-start.10 = (bf16[64,512]{1,0:T(8,128)(2,1)S(1)}, bf16[64,512]{1,0:T(8,128)(2,1)S(1)}, u32[]{:S(2)}, u32[]{:S(2)}) collective-permute-start(bf16[64,512]{1,0:T(8,128)(2,1)S(1)} %copy-done.5), channel_id=1, source_target_pairs={{0,1},{1,0},{2,3},{3,2},{4,5},{5,4},{6,7},{7,6},{8,9},{9,8},{10,11... | collective-permute-start | bytes 196616 | tf_op jit(solution)/shard_map/ppermute | solution.py:152
  13.0 8.2 %collective-permute-start.7 = (bf16[16,1152]{1,0:T(8,128)(2,1)S(1)}, bf16[16,1152]{1,0:T(8,128)(2,1)S(1)}, u32[]{:S(2)}, u32[]{:S(2)}) collective-permute-start(bf16[16,1152]{1,0:T(8,128)(2,1)S(1)} %get-tuple-element.32), channel_id=1, source_target_pairs={{0,5},{1,4},{2,7},{3,6},{4,1},{5,0},{6,3},{7,2},{8,13},{9,12},{10,... | collective-permute-start | bytes 110600 | tf_op jit(solution)/shard_map/ppermute | solution.py:152
  16.1 5.2 %copy-start.3 = (bf16[1024,512]{1,0:T(8,128)(2,1)S(1)}, bf16[1024,512]{1,0:T(8,128)(2,1)}, u32[]{:S(2)}) copy-start(bf16[1024,512]{1,0:T(8,128)(2,1)} %refs_9_.1) | copy-start | bytes 3145732
  16.1 5.2 %copy-start.4 = (bf16[1024,64]{0,1:T(8,128)(2,1)S(1)}, bf16[1024,64]{0,1:T(8,128)(2,1)}, u32[]{:S(2)}) copy-start(bf16[1024,64]{0,1:T(8,128)(2,1)} %param.24) | copy-start | bytes 393220
  16.1 1.5 %copy-start.11 = (s32[64]{0:T(128)S(1)}, s32[64]{0:T(128)}, u32[]{:S(2)}) copy-start(s32[64]{0:T(128)} %param.16) | copy-start | bytes 772
  16.1 1.5 %copy-start.12 = (s32[64]{0:T(128)S(1)}, s32[64]{0:T(128)}, u32[]{:S(2)}) copy-start(s32[64]{0:T(128)} %param.17) | copy-start | bytes 772
  16.1 5.1 %collective-permute-start.8 = (bf16[16,1024]{1,0:T(8,128)(2,1)S(1)}, bf16[16,1024]{1,0:T(8,128)(2,1)S(1)}, u32[]{:S(2)}, u32[]{:S(2)}) collective-permute-start(bf16[16,1024]{1,0:T(8,128)(2,1)S(1)} %get-tuple-element.34), channel_id=1, source_target_pairs={{0,5},{1,4},{2,7},{3,6},{4,1},{5,0},{6,3},{7,2},{8,13},{9,12},{10,... | collective-permute-start | bytes 98312 | tf_op jit(solution)/shard_map/ppermute | solution.py:152
  22.3 3.0 %collective-permute-start.11 = (f32[8,32]{1,0:T(8,128)S(1)}, f32[8,32]{1,0:T(8,128)S(1)}, u32[]{:S(2)}, u32[]{:S(2)}) collective-permute-start(f32[8,32]{1,0:T(8,128)S(1)} %shard_map.156.one_ref), channel_id=1, source_target_pairs={{0,3},{1,2},{2,1},{3,0},{4,7},{5,6},{6,5},{7,4},{8,11},{9,10},{10,... | collective-permute-start | bytes 3080 | tf_op jit(solution)/shard_map/ppermute | solution.py:152
  25.3 4.0 %collective-permute-start.12 = (f32[8,32]{1,0:T(8,128)S(1)}, f32[8,32]{1,0:T(8,128)S(1)}, u32[]{:S(2)}, u32[]{:S(2)}) collective-permute-start(f32[8,32]{1,0:T(8,128)S(1)} %shard_map.157.one_ref), channel_id=1, source_target_pairs={{0,5},{1,4},{2,7},{3,6},{4,1},{5,0},{6,3},{7,2},{8,13},{9,12},{10,... | collective-permute-start | bytes 3080 | tf_op jit(solution)/shard_map/ppermute | solution.py:152
  29.3 1.2 %collective-permute-start.13 = (f32[8,32]{1,0:T(8,128)S(1)}, f32[8,32]{1,0:T(8,128)S(1)}, u32[]{:S(2)}, u32[]{:S(2)}) collective-permute-start(f32[8,32]{1,0:T(8,128)S(1)} %shard_map.158.refs_0_), channel_id=1, source_target_pairs={{0,1},{1,0},{2,3},{3,2},{4,5},{5,4},{6,7},{7,6},{8,9},{9,8},{10,11... | collective-permute-start | bytes 3080 | tf_op jit(solution)/shard_map/ppermute | solution.py:152

commit v7 on v6

--- a/solution.py
+++ b/solution.py
@@ -241,11 +241,14 @@
         refs[6:-2],
         refs[-2:],
     )
-    moe_input = rms_norm(rows_ref[...].astype(jnp.float32), gain_ref[...]).astype(jnp.bfloat16)
+    hidden = rows_ref[...].astype(jnp.float32)
+    scale = lax.rsqrt(jnp.mean(hidden * hidden, axis=-1, keepdims=True) + epsilon)
+    moe_input = (hidden * gain_ref[...]).astype(jnp.bfloat16)
 
     def units(gate_ref, up_ref, down_ref):
         projections = [
-            lax.dot_general(moe_input, ref[...], TRANSPOSED, preferred_element_type=jnp.float32)
+            scale
+            * lax.dot_general(moe_input, ref[...], TRANSPOSED, preferred_element_type=jnp.float32)
             for ref in (gate_ref, up_ref)
         ]
         inner_act = (jax.nn.silu(projections[0]) * projections[1]).astype(jnp.bfloat16)
@@ -263,28 +266,51 @@
     sent_ref[...] = total.astype(jnp.bfloat16)
 
 
-def final_rows(place, rows, totals, arrived, gain):
-    features = rows[0].shape[1]
+def late_kernel(
+    tok_rows,
+    bits,
+    place,
+    targets_ref,
+    seq_ref,
+    first_ref,
+    second_ref,
+    first_total_ref,
+    second_total_ref,
+    arrived_ref,
+    gain_ref,
+    columns_ref,
+    final_ref,
+    partial_ref,
+    weight_ref,
+):
+    columns_kernel(tok_rows, bits, targets_ref, seq_ref, columns_ref)
+    features = first_ref.shape[1]
     my_index = lax.axis_index("tensor")
     expert = my_index // SPLIT
-    late = bit(my_index, place) == 1
-    tok_rows = rows[0].shape[0] // 2
-    mixing = [piece[:tok_rows, features:].astype(jnp.float32) for piece in (totals[0], arrived[0])]
-    mixing = mixing[0] + mixing[1]
+    mixing = first_total_ref[:tok_rows, features:]
+    mixing = mixing + arrived_ref[:, features:].astype(jnp.float32)[:tok_rows]
     lane = lax.broadcasted_iota(jnp.int32, mixing.shape, 1)
-    mixed = in_order(late, *rows).astype(jnp.float32)
-    for own, pieces in ((expert, totals), (1 - expert, arrived[::-1])):
-        weights = [
+
+    def weights(side, which):
+        blocks = [
             jnp.sum(
-                jnp.where((lane // 8 == block) & (lane % 2 == own), mixing, 0.0),
+                jnp.where((lane // 8 == 2 * side + k) & (lane % 2 == which), mixing, 0.0),
                 axis=1,
                 keepdims=True,
             )
-            for block in range(4)
+            for k in range(2)
         ]
-        values = in_order(late, *(piece[:, :features].astype(jnp.float32) for piece in pieces))
-        mixed = mixed + jnp.concatenate(weights, axis=0) * values
-    return rms_norm(mixed, gain).astype(jnp.bfloat16)
+        return jnp.concatenate(blocks, axis=0)
+
+    side = bit(my_index, place)
+    partial_value = weights(side, expert) * first_total_ref[:, :features]
+    partial_ref[...] = first_ref[...].astype(jnp.float32) + partial_value
+    weight_ref[...] = jnp.broadcast_to(weights(side, 1 - expert), weight_ref.shape)
+    mixed = second_ref[...].astype(jnp.float32)
+    mixed = mixed + weights(1 - side, expert) * second_total_ref[...]
+    arrived = arrived_ref[:, :features].astype(jnp.float32)
+    mixed = mixed + weights(1 - side, 1 - expert) * arrived
+    final_ref[...] = rms_norm(mixed, gain_ref[...]).astype(jnp.bfloat16)
 
 
 def half_columns(values, tok_rows, bits, parity):
@@ -298,17 +324,12 @@
 
 
 def head_kernel(place, *refs):
-    row_refs, sum_refs, (gain_ref, columns_ref, down_ref), weight_refs, (stats_ref,) = (
-        refs[0:2],
-        refs[2:6],
-        refs[6:9],
-        refs[9:13],
-        refs[13:],
-    )
+    (final_ref, partial_ref, weight_ref, arrived_ref, gain_ref, columns_ref, down_ref) = refs[0:7]
+    weight_refs, (stats_ref,) = refs[7:11], refs[11:]
     my_index = lax.axis_index("tensor")
-    sums = [ref[...] for ref in sum_refs]
-    pieces = [ref[...] for ref in row_refs]
-    rows = final_rows(place, pieces, sums[0:2], sums[2:4], gain_ref[...])
+    mixed = partial_ref[...] + weight_ref[:, 0:1] * arrived_ref[...].astype(jnp.float32)
+    first = rms_norm(mixed, gain_ref[...]).astype(jnp.bfloat16)
+    rows = in_order(bit(my_index, place) == 1, first, final_ref[...])
     tokens = rows.shape[0]
     wanted = columns_ref[0][:, 0:1].astype(jnp.int32)
     latent = lax.dot_general(rows, down_ref[...], TRANSPOSED, preferred_element_type=jnp.float32)
@@ -398,6 +419,7 @@
         return jax.ShapeDtypeStruct(shape, dtype)
 
     flags = call(flags_kernel, array(jnp.int32, 8, 128), flops=ROUND_FLOPS)
+    flags, down_sent = lax.optimization_barrier((flags, w_down))
     mixing, held_rows, gain, last_gain = call(
         functools.partial(early_kernel, tok_rows, bits),
         [
@@ -422,7 +444,7 @@
     )
     second = exchange(first, far_mask)
     units = [w_gate.T, w_up.T, w_down]
-    units = [exchange(unit, 1) for unit in units] + units
+    units = [exchange(unit, 1) for unit in units[:2] + [down_sent]] + units
     totals, sent = [], []
     for rows, more in ((first, [mixing]), (second, [])):
         outputs = call(
@@ -450,19 +472,27 @@
     sent[1], late_targets = lax.optimization_barrier((sent[1], targets[None]))
     arrived = [exchange(piece, far_mask) for piece in sent]
 
-    (columns,) = call(
-        functools.partial(columns_kernel, tok_rows, bits),
-        [array(jnp.float32, 3, half, 128)],
+    columns, *late = call(
+        functools.partial(late_kernel, tok_rows, bits, far_bit),
+        [
+            array(jnp.float32, 3, half, 128),
+            array(jnp.bfloat16, 2 * tok_rows, features),
+            array(jnp.float32, 2 * tok_rows, features),
+            array(jnp.float32, 2 * tok_rows, 128),
+        ],
         late_targets,
         late_seq,
+        first,
+        second,
+        *totals,
+        arrived[0],
+        last_gain,
     )
     stats = call(
         functools.partial(head_kernel, far_bit),
         array(jnp.float32, 8, half),
-        first,
-        second,
-        *totals,
-        *arrived,
+        *late,
+        arrived[1],
         last_gain,
         columns,
         adapter_down.T,

time: 31.6 us -> 30.7 us (0.972)
  waiting for transfers between devices: 10.3 us -> 7.33 us
  local copies, waits for them, and re-layouts: 0.75 us -> 2.1 us
  starting transfers between devices: 14.9 us -> 15.8 us
    ppermute x14, waiting for transfers between devices: 10.3 us -> 7.33 us  [exchange(): lax.ppermute(values, 'tensor', [(i, i ^ mask) for i in range(devices)])]
    unnamed x26, local copies, waits for them, and re-layouts: 0.75 us -> 2.1 us
    ppermute x14, starting transfers between devices: 14.9 us -> 15.8 us  [exchange(): lax.ppermute(values, 'tensor', [(i, i ^ mask) for i in range(devices)])]
  transfers between devices with their start and end apart: 14 -> 14, of which waited for: 4 -> 6; matrix products, arithmetic and copies ran while one was open for 0% -> 0% of each run, Pallas kernels for 9% -> 9%
where the time goes in v7:
time: 30.7 us; the launch traced here: 30.5 us
  starting transfers between devices  15.8 us (51%)
  waiting for transfers between devices  7.33 us (24%)
  Pallas kernels  4.47 us (15%)
  local copies, waits for them, and re-layouts  2.1 us (7%)
  between operations  0.76 us (2%)
    ppermute x14, starting transfers between devices, exchange(): lax.ppermute(values, 'tensor', [(i, i ^ mask) for i in range(devices)])  15.8 us
    ppermute x14, waiting for transfers between devices, exchange(): lax.ppermute(values, 'tensor', [(i, i ^ mask) for i in range(devices)])  7.33 us
    pallas_call x12, Pallas kernels, call(): pl.pallas_call(kernel, out_shape=shapes, compiler_params=pltpu.CompilerPa...  4.47 us
    unnamed x26, local copies, waits for them, and re-layouts  2.1 us
  transfers between devices with their start and end apart: 14, of which 6 were waited for; matrix products, arithmetic and copies ran while one was open for 0% of the time, Pallas kernels for 9%

profile of v7, /device:TPU:0, one launch (start us, length us, event | category | flops | bytes accessed | tf_op | source)
XLA Modules:
  0.0 30.5 jit_solution(10867384446711531108)
XLA Ops:
  0.6 2.5 %collective-permute-start = (bf16[8,1024]{1,0:T(8,128)(2,1)}, bf16[8,1024]{1,0:T(8,128)(2,1)S(1)}, u32[]{:S(2)}, u32[]{:S(2)}) collective-permute-start(bf16[8,1024]{1,0:T(8,128)(2,1)} %refs_2_.1), channel_id=1, source_target_pairs={{0,3},{1,2},{2,1},{3,0},{4,7},{5,6},{6,5},{7,4},{8,11},{9,10},{10,... | collective-permute-start | bytes 49160 | tf_op jit(solution)/shard_map/ppermute | solution.py:152
  3.2 0.7 %collective-permute-start.2 = (bf16[352,1024]{1,0:T(8,128)(2,1)}, bf16[352,1024]{1,0:T(8,128)(2,1)S(1)}, u32[]{:S(2)}, u32[]{:S(2)}) collective-permute-start(bf16[352,1024]{1,0:T(8,128)(2,1)} %bitcast.12), channel_id=1, source_target_pairs={{0,1},{1,0},{2,3},{3,2},{4,5},{5,4},{6,7},{7,6},{8,9},{9,8},{10,11... | collective-permute-start | bytes 2162696 | tf_op jit(solution)/shard_map/ppermute | solution.py:152
  3.8 0.0 collective-permute-start.3
  3.9 1.1 %copy-done.2 = bf16[352,1024]{1,0:T(8,128)(2,1)S(1)} copy-done((bf16[352,1024]{1,0:T(8,128)(2,1)S(1)}, bf16[352,1024]{1,0:T(8,128)(2,1)}, u32[]{:S(2)}) %copy-start.2) | copy-done | bytes 720920
  5.0 0.3 %copy-done.3 = bf16[1024,512]{1,0:T(8,128)(2,1)S(1)} copy-done((bf16[1024,512]{1,0:T(8,128)(2,1)S(1)}, bf16[1024,512]{1,0:T(8,128)(2,1)}, u32[]{:S(2)}) %copy-start.3) | copy-done | bytes 1048600
  5.3 0.2 collective-permute-start.9
  5.5 0.2 copy-done.7
  5.7 0.4 %copy-done.9 = s32[8,2]{0,1:T(2,128)S(1)} copy-done((s32[8,2]{0,1:T(2,128)S(1)}, s32[8,2]{0,1:T(2,128)}, u32[]{:S(2)}) %copy-start.9) | copy-done | bytes 88
  6.1 0.2 shard_map.149
  6.3 0.0 copy-start
  6.3 0.0 copy-start.1
  6.4 2.6 %collective-permute-start.1 = (bf16[16,1024]{1,0:T(8,128)(2,1)S(1)}, bf16[16,1024]{1,0:T(8,128)(2,1)S(1)}, u32[]{:S(2)}, u32[]{:S(2)}) collective-permute-start(bf16[16,1024]{1,0:T(8,128)(2,1)S(1)} %shard_map.150.rows_ref.first_ref), channel_id=1, source_target_pairs={{0,5},{1,4},{2,7},{3,6},{4,1},{5,0},{6,3},{7,2},{8,13},{9,12},{10,... | collective-permute-start | bytes 98312 | tf_op jit(solution)/shard_map/ppermute | solution.py:152
  9.0 1.1 %shard_map.153 = (f32[16,1152]{1,0:T(8,128)S(1)}, bf16[16,1152]{1,0:T(8,128)(2,1)S(1)}) custom-call(bf16[16,1024]{1,0:T(8,128)(2,1)S(1)} %shard_map.150.rows_ref.first_ref, f32[1,1024]{1,0:T(1,128)S(1)} %get-tuple-element.30.gain_ref, bf16[352,1024]{1,0:T(8,128)(2,1)S(1)} %collective-permute-done.2.refs_0_, ...), custom_call_target="tpu_custom_call" | custom-call | flops 69206016 | bytes 4370432 | tf_op jit(solution)/shard_map/pallas_call | solution.py:388
  10.2 0.7 %collective-permute-start.6 = (bf16[16,1152]{1,0:T(8,128)(2,1)S(1)}, bf16[16,1152]{1,0:T(8,128)(2,1)S(1)}, u32[]{:S(2)}, u32[]{:S(2)}) collective-permute-start(bf16[16,1152]{1,0:T(8,128)(2,1)S(1)} %get-tuple-element.38), channel_id=1, source_target_pairs={{0,3},{1,2},{2,1},{3,0},{4,7},{5,6},{6,5},{7,4},{8,11},{9,10},{10,... | collective-permute-start | bytes 110600 | tf_op jit(solution)/shard_map/ppermute | solution.py:152
  10.9 1.1 %shard_map.151 = (f32[16,1024]{1,0:T(8,128)S(1)}, bf16[16,1024]{1,0:T(8,128)(2,1)S(1)}) custom-call(bf16[16,1024]{1,0:T(8,128)(2,1)S(1)} %collective-permute-done.1.rows_ref.second_ref, f32[1,1024]{1,0:T(1,128)S(1)} %get-tuple-element.30.gain_ref, bf16[352,1024]{1,0:T(8,128)(2,1)S(1)} %collective-permute-done.2.refs_0_, ...), custom_call_target="tpu_custom_call" | custom-call | flops 69206016 | bytes 4362240 | tf_op jit(solution)/shard_map/pallas_call | solution.py:388
  12.0 1.1 %collective-permute-start.5 = (bf16[16,1024]{1,0:T(8,128)(2,1)S(1)}, bf16[16,1024]{1,0:T(8,128)(2,1)S(1)}, u32[]{:S(2)}, u32[]{:S(2)}) collective-permute-start(bf16[16,1024]{1,0:T(8,128)(2,1)S(1)} %get-tuple-element.33), channel_id=1, source_target_pairs={{0,3},{1,2},{2,1},{3,0},{4,7},{5,6},{6,5},{7,4},{8,11},{9,10},{10,... | collective-permute-start | bytes 98312 | tf_op jit(solution)/shard_map/ppermute | solution.py:152
  13.1 0.2 collective-permute-start.10
  13.3 0.4 %collective-permute-done.6.arrived_ref = bf16[16,1152]{1,0:T(8,128)(2,1)S(1)} collective-permute-done((bf16[16,1152]{1,0:T(8,128)(2,1)S(1)}, bf16[16,1152]{1,0:T(8,128)(2,1)S(1)}, u32[]{:S(2)}, u32[]{:S(2)}) %collective-permute-start.6) | collective-permute-done | bytes 36896 | tf_op jit(solution)/shard_map/ppermute | solution.py:152
  13.7 2.0 %collective-permute-start.7 = (bf16[16,1152]{1,0:T(8,128)(2,1)S(1)}, bf16[16,1152]{1,0:T(8,128)(2,1)S(1)}, u32[]{:S(2)}, u32[]{:S(2)}) collective-permute-start(bf16[16,1152]{1,0:T(8,128)(2,1)S(1)} %get-tuple-element.43), channel_id=1, source_target_pairs={{0,5},{1,4},{2,7},{3,6},{4,1},{5,0},{6,3},{7,2},{8,13},{9,12},{10,... | collective-permute-start | bytes 110600 | tf_op jit(solution)/shard_map/ppermute | solution.py:152
  15.7 0.0 copy-start.4
  15.7 2.1 %collective-permute-start.8 = (bf16[16,1024]{1,0:T(8,128)(2,1)S(1)}, bf16[16,1024]{1,0:T(8,128)(2,1)S(1)}, u32[]{:S(2)}, u32[]{:S(2)}) collective-permute-start(bf16[16,1024]{1,0:T(8,128)(2,1)S(1)} %get-tuple-element.48), channel_id=1, source_target_pairs={{0,5},{1,4},{2,7},{3,6},{4,1},{5,0},{6,3},{7,2},{8,13},{9,12},{10,... | collective-permute-start | bytes 98312 | tf_op jit(solution)/shard_map/ppermute | solution.py:152
  17.8 1.2 %collective-permute-done.7.arrived_ref = bf16[16,1152]{1,0:T(8,128)(2,1)S(1)} collective-permute-done((bf16[16,1152]{1,0:T(8,128)(2,1)S(1)}, bf16[16,1152]{1,0:T(8,128)(2,1)S(1)}, u32[]{:S(2)}, u32[]{:S(2)}) %collective-permute-start.7) | collective-permute-done | bytes 36896 | tf_op jit(solution)/shard_map/ppermute | solution.py:152
  19.1 0.3 shard_map.155
  19.4 0.7 %collective-permute-done.8.refs_3_ = bf16[16,1024]{1,0:T(8,128)(2,1)S(1)} collective-permute-done((bf16[16,1024]{1,0:T(8,128)(2,1)S(1)}, bf16[16,1024]{1,0:T(8,128)(2,1)S(1)}, u32[]{:S(2)}, u32[]{:S(2)}) %collective-permute-start.8) | collective-permute-done | bytes 32800 | tf_op jit(solution)/shard_map/ppermute | solution.py:152
  20.1 0.9 %shard_map.156.one_ref = f32[8,32]{1,0:T(8,128)S(1)} custom-call(bf16[16,1024]{1,0:T(8,128)(2,1)S(1)} %get-tuple-element.45.refs_0_, f32[16,1024]{1,0:T(8,128)S(1)} %get-tuple-element.46.refs_1_, f32[16,128]{1,0:T(8,128)S(1)} %get-tuple-element.47.refs_2_, bf16[16,1024]{1,0:T(8,128)(2,1)S(1)} %collective-permute-done.8.refs_3_, ...), custom_call_target="tpu_custom_call" | custom-call | flops 67108864 | bytes 2551808 | tf_op jit(solution)/shard_map/pallas_call | solution.py:388
  21.0 0.8 %collective-permute-start.11 = (f32[8,32]{1,0:T(8,128)S(1)}, f32[8,32]{1,0:T(8,128)S(1)}, u32[]{:S(2)}, u32[]{:S(2)}) collective-permute-start(f32[8,32]{1,0:T(8,128)S(1)} %shard_map.156.one_ref), channel_id=1, source_target_pairs={{0,3},{1,2},{2,1},{3,0},{4,7},{5,6},{6,5},{7,4},{8,11},{9,10},{10,... | collective-permute-start | bytes 3080 | tf_op jit(solution)/shard_map/ppermute | solution.py:152
  21.8 2.2 %collective-permute-done.11.two_ref = f32[8,32]{1,0:T(8,128)S(1)} collective-permute-done((f32[8,32]{1,0:T(8,128)S(1)}, f32[8,32]{1,0:T(8,128)S(1)}, u32[]{:S(2)}, u32[]{:S(2)}) %collective-permute-start.11) | collective-permute-done | bytes 1056 | tf_op jit(solution)/shard_map/ppermute | solution.py:152
  24.0 2.1 %collective-permute-start.12 = (f32[8,32]{1,0:T(8,128)S(1)}, f32[8,32]{1,0:T(8,128)S(1)}, u32[]{:S(2)}, u32[]{:S(2)}) collective-permute-start(f32[8,32]{1,0:T(8,128)S(1)} %shard_map.157.one_ref), channel_id=1, source_target_pairs={{0,5},{1,4},{2,7},{3,6},{4,1},{5,0},{6,3},{7,2},{8,13},{9,12},{10,... | collective-permute-start | bytes 3080 | tf_op jit(solution)/shard_map/ppermute | solution.py:152
  26.1 1.9 %collective-permute-done.12.two_ref = f32[8,32]{1,0:T(8,128)S(1)} collective-permute-done((f32[8,32]{1,0:T(8,128)S(1)}, f32[8,32]{1,0:T(8,128)S(1)}, u32[]{:S(2)}, u32[]{:S(2)}) %collective-permute-start.12) | collective-permute-done | bytes 1056 | tf_op jit(solution)/shard_map/ppermute | solution.py:152
  28.0 0.9 %collective-permute-start.13 = (f32[8,32]{1,0:T(8,128)S(1)}, f32[8,32]{1,0:T(8,128)S(1)}, u32[]{:S(2)}, u32[]{:S(2)}) collective-permute-start(f32[8,32]{1,0:T(8,128)S(1)} %shard_map.158.refs_0_), channel_id=1, source_target_pairs={{0,1},{1,0},{2,3},{3,2},{4,5},{5,4},{6,7},{7,6},{8,9},{9,8},{10,11... | collective-permute-start | bytes 3080 | tf_op jit(solution)/shard_map/ppermute | solution.py:152
  29.0 0.8 %collective-permute-done.13.refs_1_ = f32[8,32]{1,0:T(8,128)S(1)} collective-permute-done((f32[8,32]{1,0:T(8,128)S(1)}, f32[8,32]{1,0:T(8,128)S(1)}, u32[]{:S(2)}, u32[]{:S(2)}) %collective-permute-start.13) | collective-permute-done | bytes 1056 | tf_op jit(solution)/shard_map/ppermute | solution.py:152
  29.8 0.7 %shard_map.159 = (f32[1,8]{1,0:T(1,128)}, f32[1,8]{1,0:T(1,128)}, f32[1,16]{1,0:T(1,128)}) custom-call(f32[8,32]{1,0:T(8,128)S(1)} %shard_map.158.refs_0_, f32[8,32]{1,0:T(8,128)S(1)} %collective-permute-done.13.refs_1_, f32[3,32,128]{2,1,0:T(8,128)S(1)} %get-tuple-element.49.refs_5_.refs_2_), custom_call_target="tpu_custom_call" | custom-call | bytes 51200 | tf_op jit(solution)/shard_map/pallas_call | solution.py:388
  (34 shorter events, 0.2 us)
Async XLA Ops:
  0.6 5.7 %collective-permute-start = (bf16[8,1024]{1,0:T(8,128)(2,1)}, bf16[8,1024]{1,0:T(8,128)(2,1)S(1)}, u32[]{:S(2)}, u32[]{:S(2)}) collective-permute-start(bf16[8,1024]{1,0:T(8,128)(2,1)} %refs_2_.1), channel_id=1, source_target_pairs={{0,3},{1,2},{2,1},{3,0},{4,7},{5,6},{6,5},{7,4},{8,11},{9,10},{10,... | collective-permute-start | bytes 49160 | tf_op jit(solution)/shard_map/ppermute | solution.py:152
  3.2 5.8 %collective-permute-start.2 = (bf16[352,1024]{1,0:T(8,128)(2,1)}, bf16[352,1024]{1,0:T(8,128)(2,1)S(1)}, u32[]{:S(2)}, u32[]{:S(2)}) collective-permute-start(bf16[352,1024]{1,0:T(8,128)(2,1)} %bitcast.12), channel_id=1, source_target_pairs={{0,1},{1,0},{2,3},{3,2},{4,5},{5,4},{6,7},{7,6},{8,9},{9,8},{10,11... | collective-permute-start | bytes 2162696 | tf_op jit(solution)/shard_map/ppermute | solution.py:152
  3.8 1.1 %copy-start.2 = (bf16[352,1024]{1,0:T(8,128)(2,1)S(1)}, bf16[352,1024]{1,0:T(8,128)(2,1)}, u32[]{:S(2)}) copy-start(bf16[352,1024]{1,0:T(8,128)(2,1)} %refs_5_.3) | copy-start | bytes 2162692
  3.8 1.4 %copy-start.3 = (bf16[1024,512]{1,0:T(8,128)(2,1)S(1)}, bf16[1024,512]{1,0:T(8,128)(2,1)}, u32[]{:S(2)}) copy-start(bf16[1024,512]{1,0:T(8,128)(2,1)} %refs_7_.1) | copy-start | bytes 3145732
  3.8 5.2 %collective-permute-start.3 = (bf16[352,1024]{1,0:T(8,128)(2,1)}, bf16[352,1024]{1,0:T(8,128)(2,1)S(1)}, u32[]{:S(2)}, u32[]{:S(2)}) collective-permute-start(bf16[352,1024]{1,0:T(8,128)(2,1)} %bitcast.15), channel_id=1, source_target_pairs={{0,1},{1,0},{2,3},{3,2},{4,5},{5,4},{6,7},{7,6},{8,9},{9,8},{10,11... | collective-permute-start | bytes 2162696 | tf_op jit(solution)/shard_map/ppermute | solution.py:152
  3.8 1.6 %copy-start.6 = (bf16[8,1024]{1,0:T(8,128)(2,1)S(1)}, bf16[8,1024]{1,0:T(8,128)(2,1)}, u32[]{:S(2)}) copy-start(bf16[8,1024]{1,0:T(8,128)(2,1)} %refs_2_.1) | copy-start | bytes 49156
  3.8 1.6 %copy-start.8 = (f32[1024]{0:T(1024)S(1)}, f32[1024]{0:T(1024)}, u32[]{:S(2)}) copy-start(f32[1024]{0:T(1024)} %param.22) | copy-start | bytes 12292
  3.9 1.6 %copy-start.10 = (f32[8,2]{0,1:T(2,128)S(1)}, f32[8,2]{0,1:T(2,128)}, u32[]{:S(2)}) copy-start(f32[8,2]{0,1:T(2,128)} %param.15) | copy-start | bytes 196
  4.9 0.8 %copy-start.7 = (f32[1024]{0:T(1024)S(1)}, f32[1024]{0:T(1024)}, u32[]{:S(2)}) copy-start(f32[1024]{0:T(1024)} %param.18) | copy-start | bytes 12292
  4.9 4.1 %collective-permute-start.4 = (bf16[352,1024]{1,0:T(8,128)(2,1)S(1)}, bf16[352,1024]{1,0:T(8,128)(2,1)S(1)}, u32[]{:S(2)}, u32[]{:S(2)}) collective-permute-start(bf16[352,1024]{1,0:T(8,128)(2,1)S(1)} %copy-done.2), channel_id=1, source_target_pairs={{0,1},{1,0},{2,3},{3,2},{4,5},{5,4},{6,7},{7,6},{8,9},{9,8},{10,11... | collective-permute-start | bytes 2162696 | tf_op jit(solution)/shard_map/ppermute | solution.py:152
  5.3 14.8 %collective-permute-start.9 = (bf16[1024,512]{1,0:T(8,128)(2,1)S(1)}, bf16[1024,512]{1,0:T(8,128)(2,1)S(1)}, u32[]{:S(2)}, u32[]{:S(2)}) collective-permute-start(bf16[1024,512]{1,0:T(8,128)(2,1)S(1)} %copy-done.3), channel_id=1, source_target_pairs={{0,1},{1,0},{2,3},{3,2},{4,5},{5,4},{6,7},{7,6},{8,9},{9,8},{10,11... | collective-permute-start | bytes 3145736 | tf_op jit(solution)/shard_map/ppermute | solution.py:152
  5.5 0.7 %copy-start.9 = (s32[8,2]{0,1:T(2,128)S(1)}, s32[8,2]{0,1:T(2,128)}, u32[]{:S(2)}) copy-start(s32[8,2]{0,1:T(2,128)} %param.14) | copy-start | bytes 196
  6.3 2.7 %copy-start = (bf16[1024,352]{0,1:T(8,128)(2,1)S(1)}, bf16[1024,352]{0,1:T(8,128)(2,1)}, u32[]{:S(2)}) copy-start(bf16[1024,352]{0,1:T(8,128)(2,1)} %param.19) | copy-start | bytes 2162692
  6.3 2.7 %copy-start.1 = (bf16[1024,352]{0,1:T(8,128)(2,1)S(1)}, bf16[1024,352]{0,1:T(8,128)(2,1)}, u32[]{:S(2)}) copy-start(bf16[1024,352]{0,1:T(8,128)(2,1)} %param.20) | copy-start | bytes 2162692
  6.4 4.5 %collective-permute-start.1 = (bf16[16,1024]{1,0:T(8,128)(2,1)S(1)}, bf16[16,1024]{1,0:T(8,128)(2,1)S(1)}, u32[]{:S(2)}, u32[]{:S(2)}) collective-permute-start(bf16[16,1024]{1,0:T(8,128)(2,1)S(1)} %shard_map.150.rows_ref.first_ref), channel_id=1, source_target_pairs={{0,5},{1,4},{2,7},{3,6},{4,1},{5,0},{6,3},{7,2},{8,13},{9,12},{10,... | collective-permute-start | bytes 98312 | tf_op jit(solution)/shard_map/ppermute | solution.py:152
  10.2 2.9 %copy-start.5 = (bf16[64,512]{1,0:T(8,128)(2,1)S(1)}, bf16[64,512]{1,0:T(8,128)(2,1)}, u32[]{:S(2)}) copy-start(bf16[64,512]{1,0:T(8,128)(2,1)} %refs_9_.1) | copy-start | bytes 196612
  10.2 3.5 %collective-permute-start.6 = (bf16[16,1152]{1,0:T(8,128)(2,1)S(1)}, bf16[16,1152]{1,0:T(8,128)(2,1)S(1)}, u32[]{:S(2)}, u32[]{:S(2)}) collective-permute-start(bf16[16,1152]{1,0:T(8,128)(2,1)S(1)} %get-tuple-element.38), channel_id=1, source_target_pairs={{0,3},{1,2},{2,1},{3,0},{4,7},{5,6},{6,5},{7,4},{8,11},{9,10},{10,... | collective-permute-start | bytes 110600 | tf_op jit(solution)/shard_map/ppermute | solution.py:152
  12.0 3.6 %collective-permute-start.5 = (bf16[16,1024]{1,0:T(8,128)(2,1)S(1)}, bf16[16,1024]{1,0:T(8,128)(2,1)S(1)}, u32[]{:S(2)}, u32[]{:S(2)}) collective-permute-start(bf16[16,1024]{1,0:T(8,128)(2,1)S(1)} %get-tuple-element.33), channel_id=1, source_target_pairs={{0,3},{1,2},{2,1},{3,0},{4,7},{5,6},{6,5},{7,4},{8,11},{9,10},{10,... | collective-permute-start | bytes 98312 | tf_op jit(solution)/shard_map/ppermute | solution.py:152
  13.1 6.2 %collective-permute-start.10 = (bf16[64,512]{1,0:T(8,128)(2,1)S(1)}, bf16[64,512]{1,0:T(8,128)(2,1)S(1)}, u32[]{:S(2)}, u32[]{:S(2)}) collective-permute-start(bf16[64,512]{1,0:T(8,128)(2,1)S(1)} %copy-done.5), channel_id=1, source_target_pairs={{0,1},{1,0},{2,3},{3,2},{4,5},{5,4},{6,7},{7,6},{8,9},{9,8},{10,11... | collective-permute-start | bytes 196616 | tf_op jit(solution)/shard_map/ppermute | solution.py:152
  13.7 5.3 %collective-permute-start.7 = (bf16[16,1152]{1,0:T(8,128)(2,1)S(1)}, bf16[16,1152]{1,0:T(8,128)(2,1)S(1)}, u32[]{:S(2)}, u32[]{:S(2)}) collective-permute-start(bf16[16,1152]{1,0:T(8,128)(2,1)S(1)} %get-tuple-element.43), channel_id=1, source_target_pairs={{0,5},{1,4},{2,7},{3,6},{4,1},{5,0},{6,3},{7,2},{8,13},{9,12},{10,... | collective-permute-start | bytes 110600 | tf_op jit(solution)/shard_map/ppermute | solution.py:152
  15.7 3.4 %copy-start.11 = (s32[64]{0:T(128)S(1)}, s32[64]{0:T(128)}, u32[]{:S(2)}) copy-start(s32[64]{0:T(128)} %param.16) | copy-start | bytes 772
  15.7 3.4 %copy-start.12 = (s32[64]{0:T(128)S(1)}, s32[64]{0:T(128)}, u32[]{:S(2)}) copy-start(s32[64]{0:T(128)} %param.17) | copy-start | bytes 772
  15.7 4.4 %copy-start.4 = (bf16[1024,64]{0,1:T(8,128)(2,1)S(1)}, bf16[1024,64]{0,1:T(8,128)(2,1)}, u32[]{:S(2)}) copy-start(bf16[1024,64]{0,1:T(8,128)(2,1)} %param.24) | copy-start | bytes 393220
  15.7 4.3 %collective-permute-start.8 = (bf16[16,1024]{1,0:T(8,128)(2,1)S(1)}, bf16[16,1024]{1,0:T(8,128)(2,1)S(1)}, u32[]{:S(2)}, u32[]{:S(2)}) collective-permute-start(bf16[16,1024]{1,0:T(8,128)(2,1)S(1)} %get-tuple-element.48), channel_id=1, source_target_pairs={{0,5},{1,4},{2,7},{3,6},{4,1},{5,0},{6,3},{7,2},{8,13},{9,12},{10,... | collective-permute-start | bytes 98312 | tf_op jit(solution)/shard_map/ppermute | solution.py:152
  21.0 3.0 %collective-permute-start.11 = (f32[8,32]{1,0:T(8,128)S(1)}, f32[8,32]{1,0:T(8,128)S(1)}, u32[]{:S(2)}, u32[]{:S(2)}) collective-permute-start(f32[8,32]{1,0:T(8,128)S(1)} %shard_map.156.one_ref), channel_id=1, source_target_pairs={{0,3},{1,2},{2,1},{3,0},{4,7},{5,6},{6,5},{7,4},{8,11},{9,10},{10,... | collective-permute-start | bytes 3080 | tf_op jit(solution)/shard_map/ppermute | solution.py:152
  24.0 4.0 %collective-permute-start.12 = (f32[8,32]{1,0:T(8,128)S(1)}, f32[8,32]{1,0:T(8,128)S(1)}, u32[]{:S(2)}, u32[]{:S(2)}) collective-permute-start(f32[8,32]{1,0:T(8,128)S(1)} %shard_map.157.one_ref), channel_id=1, source_target_pairs={{0,5},{1,4},{2,7},{3,6},{4,1},{5,0},{6,3},{7,2},{8,13},{9,12},{10,... | collective-permute-start | bytes 3080 | tf_op jit(solution)/shard_map/ppermute | solution.py:152
  28.0 1.8 %collective-permute-start.13 = (f32[8,32]{1,0:T(8,128)S(1)}, f32[8,32]{1,0:T(8,128)S(1)}, u32[]{:S(2)}, u32[]{:S(2)}) collective-permute-start(f32[8,32]{1,0:T(8,128)S(1)} %shard_map.158.refs_0_), channel_id=1, source_target_pairs={{0,1},{1,0},{2,3},{3,2},{4,5},{5,4},{6,7},{7,6},{8,9},{9,8},{10,11... | collective-permute-start | bytes 3080 | tf_op jit(solution)/shard_map/ppermute | solution.py:152

commit v8 on v7

--- a/solution.py
+++ b/solution.py
@@ -231,7 +231,8 @@
 
 def order_kernel(place, flags_ref, mine_ref, other_ref, out_ref):
     late = flags_ref[place : place + 1, 0:1] == 1
-    out_ref[...] = in_order(late, mine_ref[...], other_ref[...])
+    rows = in_order(late, *(ref[...].astype(jnp.float32) for ref in (mine_ref, other_ref)))
+    out_ref[...] = rows.astype(out_ref.dtype)
 
 
 def expert_kernel(rows_ref, gain_ref, *refs):
@@ -419,7 +420,7 @@
         return jax.ShapeDtypeStruct(shape, dtype)
 
     flags = call(flags_kernel, array(jnp.int32, 8, 128), flops=ROUND_FLOPS)
-    flags, down_sent = lax.optimization_barrier((flags, w_down))
+    flags, sent_d = lax.optimization_barrier((flags, w_down))
     mixing, held_rows, gain, last_gain = call(
         functools.partial(early_kernel, tok_rows, bits),
         [
@@ -444,7 +445,7 @@
     )
     second = exchange(first, far_mask)
     units = [w_gate.T, w_up.T, w_down]
-    units = [exchange(unit, 1) for unit in units[:2] + [down_sent]] + units
+    units = [exchange(unit, 1) for unit in (units[0], units[1], sent_d)] + units
     totals, sent = [], []
     for rows, more in ((first, [mixing]), (second, [])):
         outputs = call(
@@ -502,7 +503,7 @@
         exchange(adapter_up, 1),
         flops=2 * devices * tok_rows * features * head_weight.shape[1],
     )
-    for mask in (near_mask, far_mask):
+    for mask in (far_mask, near_mask):
         stats = call(merge_kernel, array(jnp.float32, 8, half), stats, exchange(stats, mask))
     policy_own, ratio_own, seq_sums = call(
         lambda *refs: result_kernel(tok_rows, *refs),

time: 30.7 us -> 30.7 us (level)
  no operation moved by 1% of the time
where the time goes in v8:
time: 30.7 us; the launch traced here: 30.5 us
  starting transfers between devices  15.9 us (52%)
  waiting for transfers between devices  7.29 us (24%)
  Pallas kernels  4.47 us (15%)
  local copies, waits for them, and re-layouts  2.1 us (7%)
  between operations  0.76 us (2%)
    ppermute x14, starting transfers between devices, exchange(): lax.ppermute(values, 'tensor', [(i, i ^ mask) for i in range(devices)])  15.9 us
    ppermute x14, waiting for transfers between devices, exchange(): lax.ppermute(values, 'tensor', [(i, i ^ mask) for i in range(devices)])  7.29 us
    pallas_call x12, Pallas kernels, call(): pl.pallas_call(kernel, out_shape=shapes, compiler_params=pltpu.CompilerPa...  4.47 us
    unnamed x26, local copies, waits for them, and re-layouts  2.1 us
  transfers between devices with their start and end apart: 14, of which 6 were waited for; matrix products, arithmetic and copies ran while one was open for 0% of the time, Pallas kernels for 9%

profile of v8, /device:TPU:0, one launch (start us, length us, event | category | flops | bytes accessed | tf_op | source)
XLA Modules:
  0.0 30.5 jit_solution(11500867098409092477)
XLA Ops:
  0.6 2.5 %collective-permute-start = (bf16[8,1024]{1,0:T(8,128)(2,1)}, bf16[8,1024]{1,0:T(8,128)(2,1)S(1)}, u32[]{:S(2)}, u32[]{:S(2)}) collective-permute-start(bf16[8,1024]{1,0:T(8,128)(2,1)} %refs_2_.1), channel_id=1, source_target_pairs={{0,3},{1,2},{2,1},{3,0},{4,7},{5,6},{6,5},{7,4},{8,11},{9,10},{10,... | collective-permute-start | bytes 49160 | tf_op jit(solution)/shard_map/ppermute | solution.py:152
  3.2 0.7 %collective-permute-start.2 = (bf16[352,1024]{1,0:T(8,128)(2,1)}, bf16[352,1024]{1,0:T(8,128)(2,1)S(1)}, u32[]{:S(2)}, u32[]{:S(2)}) collective-permute-start(bf16[352,1024]{1,0:T(8,128)(2,1)} %bitcast.12), channel_id=1, source_target_pairs={{0,1},{1,0},{2,3},{3,2},{4,5},{5,4},{6,7},{7,6},{8,9},{9,8},{10,11... | collective-permute-start | bytes 2162696 | tf_op jit(solution)/shard_map/ppermute | solution.py:152
  3.8 0.0 collective-permute-start.3
  3.9 1.1 %copy-done.2 = bf16[352,1024]{1,0:T(8,128)(2,1)S(1)} copy-done((bf16[352,1024]{1,0:T(8,128)(2,1)S(1)}, bf16[352,1024]{1,0:T(8,128)(2,1)}, u32[]{:S(2)}) %copy-start.2) | copy-done | bytes 720920
  5.0 0.3 %copy-done.3 = bf16[1024,512]{1,0:T(8,128)(2,1)S(1)} copy-done((bf16[1024,512]{1,0:T(8,128)(2,1)S(1)}, bf16[1024,512]{1,0:T(8,128)(2,1)}, u32[]{:S(2)}) %copy-start.3) | copy-done | bytes 1048600
  5.3 0.2 collective-permute-start.9
  5.5 0.2 copy-done.7
  5.7 0.4 %copy-done.9 = s32[8,2]{0,1:T(2,128)S(1)} copy-done((s32[8,2]{0,1:T(2,128)S(1)}, s32[8,2]{0,1:T(2,128)}, u32[]{:S(2)}) %copy-start.9) | copy-done | bytes 88
  6.1 0.2 shard_map.149
  6.3 0.0 copy-start
  6.3 0.0 copy-start.1
  6.4 2.6 %collective-permute-start.1 = (bf16[16,1024]{1,0:T(8,128)(2,1)S(1)}, bf16[16,1024]{1,0:T(8,128)(2,1)S(1)}, u32[]{:S(2)}, u32[]{:S(2)}) collective-permute-start(bf16[16,1024]{1,0:T(8,128)(2,1)S(1)} %shard_map.150.rows_ref.first_ref), channel_id=1, source_target_pairs={{0,5},{1,4},{2,7},{3,6},{4,1},{5,0},{6,3},{7,2},{8,13},{9,12},{10,... | collective-permute-start | bytes 98312 | tf_op jit(solution)/shard_map/ppermute | solution.py:152
  9.0 1.1 %shard_map.153 = (f32[16,1152]{1,0:T(8,128)S(1)}, bf16[16,1152]{1,0:T(8,128)(2,1)S(1)}) custom-call(bf16[16,1024]{1,0:T(8,128)(2,1)S(1)} %shard_map.150.rows_ref.first_ref, f32[1,1024]{1,0:T(1,128)S(1)} %get-tuple-element.30.gain_ref, bf16[352,1024]{1,0:T(8,128)(2,1)S(1)} %collective-permute-done.2.refs_0_, ...), custom_call_target="tpu_custom_call" | custom-call | flops 69206016 | bytes 4370432 | tf_op jit(solution)/shard_map/pallas_call | solution.py:389
  10.2 0.8 %collective-permute-start.6 = (bf16[16,1152]{1,0:T(8,128)(2,1)S(1)}, bf16[16,1152]{1,0:T(8,128)(2,1)S(1)}, u32[]{:S(2)}, u32[]{:S(2)}) collective-permute-start(bf16[16,1152]{1,0:T(8,128)(2,1)S(1)} %get-tuple-element.38), channel_id=1, source_target_pairs={{0,3},{1,2},{2,1},{3,0},{4,7},{5,6},{6,5},{7,4},{8,11},{9,10},{10,... | collective-permute-start | bytes 110600 | tf_op jit(solution)/shard_map/ppermute | solution.py:152
  10.9 1.1 %shard_map.151 = (f32[16,1024]{1,0:T(8,128)S(1)}, bf16[16,1024]{1,0:T(8,128)(2,1)S(1)}) custom-call(bf16[16,1024]{1,0:T(8,128)(2,1)S(1)} %collective-permute-done.1.rows_ref.second_ref, f32[1,1024]{1,0:T(1,128)S(1)} %get-tuple-element.30.gain_ref, bf16[352,1024]{1,0:T(8,128)(2,1)S(1)} %collective-permute-done.2.refs_0_, ...), custom_call_target="tpu_custom_call" | custom-call | flops 69206016 | bytes 4362240 | tf_op jit(solution)/shard_map/pallas_call | solution.py:389
  12.1 1.0 %collective-permute-start.5 = (bf16[16,1024]{1,0:T(8,128)(2,1)S(1)}, bf16[16,1024]{1,0:T(8,128)(2,1)S(1)}, u32[]{:S(2)}, u32[]{:S(2)}) collective-permute-start(bf16[16,1024]{1,0:T(8,128)(2,1)S(1)} %get-tuple-element.33), channel_id=1, source_target_pairs={{0,3},{1,2},{2,1},{3,0},{4,7},{5,6},{6,5},{7,4},{8,11},{9,10},{10,... | collective-permute-start | bytes 98312 | tf_op jit(solution)/shard_map/ppermute | solution.py:152
  13.1 0.2 collective-permute-start.10
  13.3 0.4 %collective-permute-done.6.arrived_ref = bf16[16,1152]{1,0:T(8,128)(2,1)S(1)} collective-permute-done((bf16[16,1152]{1,0:T(8,128)(2,1)S(1)}, bf16[16,1152]{1,0:T(8,128)(2,1)S(1)}, u32[]{:S(2)}, u32[]{:S(2)}) %collective-permute-start.6) | collective-permute-done | bytes 36896 | tf_op jit(solution)/shard_map/ppermute | solution.py:152
  13.7 2.0 %collective-permute-start.7 = (bf16[16,1152]{1,0:T(8,128)(2,1)S(1)}, bf16[16,1152]{1,0:T(8,128)(2,1)S(1)}, u32[]{:S(2)}, u32[]{:S(2)}) collective-permute-start(bf16[16,1152]{1,0:T(8,128)(2,1)S(1)} %get-tuple-element.43), channel_id=1, source_target_pairs={{0,5},{1,4},{2,7},{3,6},{4,1},{5,0},{6,3},{7,2},{8,13},{9,12},{10,... | collective-permute-start | bytes 110600 | tf_op jit(solution)/shard_map/ppermute | solution.py:152
  15.7 0.0 copy-start.4
  15.7 2.1 %collective-permute-start.8 = (bf16[16,1024]{1,0:T(8,128)(2,1)S(1)}, bf16[16,1024]{1,0:T(8,128)(2,1)S(1)}, u32[]{:S(2)}, u32[]{:S(2)}) collective-permute-start(bf16[16,1024]{1,0:T(8,128)(2,1)S(1)} %get-tuple-element.48), channel_id=1, source_target_pairs={{0,5},{1,4},{2,7},{3,6},{4,1},{5,0},{6,3},{7,2},{8,13},{9,12},{10,... | collective-permute-start | bytes 98312 | tf_op jit(solution)/shard_map/ppermute | solution.py:152
  17.8 1.2 %collective-permute-done.7.arrived_ref = bf16[16,1152]{1,0:T(8,128)(2,1)S(1)} collective-permute-done((bf16[16,1152]{1,0:T(8,128)(2,1)S(1)}, bf16[16,1152]{1,0:T(8,128)(2,1)S(1)}, u32[]{:S(2)}, u32[]{:S(2)}) %collective-permute-start.7) | collective-permute-done | bytes 36896 | tf_op jit(solution)/shard_map/ppermute | solution.py:152
  19.1 0.3 shard_map.155
  19.4 0.7 %collective-permute-done.8.refs_3_ = bf16[16,1024]{1,0:T(8,128)(2,1)S(1)} collective-permute-done((bf16[16,1024]{1,0:T(8,128)(2,1)S(1)}, bf16[16,1024]{1,0:T(8,128)(2,1)S(1)}, u32[]{:S(2)}, u32[]{:S(2)}) %collective-permute-start.8) | collective-permute-done | bytes 32800 | tf_op jit(solution)/shard_map/ppermute | solution.py:152
  20.1 0.9 %shard_map.156.one_ref = f32[8,32]{1,0:T(8,128)S(1)} custom-call(bf16[16,1024]{1,0:T(8,128)(2,1)S(1)} %get-tuple-element.45.refs_0_, f32[16,1024]{1,0:T(8,128)S(1)} %get-tuple-element.46.refs_1_, f32[16,128]{1,0:T(8,128)S(1)} %get-tuple-element.47.refs_2_, bf16[16,1024]{1,0:T(8,128)(2,1)S(1)} %collective-permute-done.8.refs_3_, ...), custom_call_target="tpu_custom_call" | custom-call | flops 67108864 | bytes 2551808 | tf_op jit(solution)/shard_map/pallas_call | solution.py:389
  21.0 2.1 %collective-permute-start.11 = (f32[8,32]{1,0:T(8,128)S(1)}, f32[8,32]{1,0:T(8,128)S(1)}, u32[]{:S(2)}, u32[]{:S(2)}) collective-permute-start(f32[8,32]{1,0:T(8,128)S(1)} %shard_map.156.one_ref), channel_id=1, source_target_pairs={{0,5},{1,4},{2,7},{3,6},{4,1},{5,0},{6,3},{7,2},{8,13},{9,12},{10,... | collective-permute-start | bytes 3080 | tf_op jit(solution)/shard_map/ppermute | solution.py:152
  23.0 1.9 %collective-permute-done.11.two_ref = f32[8,32]{1,0:T(8,128)S(1)} collective-permute-done((f32[8,32]{1,0:T(8,128)S(1)}, f32[8,32]{1,0:T(8,128)S(1)}, u32[]{:S(2)}, u32[]{:S(2)}) %collective-permute-start.11) | collective-permute-done | bytes 1056 | tf_op jit(solution)/shard_map/ppermute | solution.py:152
  24.9 0.9 %collective-permute-start.12 = (f32[8,32]{1,0:T(8,128)S(1)}, f32[8,32]{1,0:T(8,128)S(1)}, u32[]{:S(2)}, u32[]{:S(2)}) collective-permute-start(f32[8,32]{1,0:T(8,128)S(1)} %shard_map.157.one_ref), channel_id=1, source_target_pairs={{0,3},{1,2},{2,1},{3,0},{4,7},{5,6},{6,5},{7,4},{8,11},{9,10},{10,... | collective-permute-start | bytes 3080 | tf_op jit(solution)/shard_map/ppermute | solution.py:152
  25.8 2.2 %collective-permute-done.12.two_ref = f32[8,32]{1,0:T(8,128)S(1)} collective-permute-done((f32[8,32]{1,0:T(8,128)S(1)}, f32[8,32]{1,0:T(8,128)S(1)}, u32[]{:S(2)}, u32[]{:S(2)}) %collective-permute-start.12) | collective-permute-done | bytes 1056 | tf_op jit(solution)/shard_map/ppermute | solution.py:152
  28.0 0.9 %collective-permute-start.13 = (f32[8,32]{1,0:T(8,128)S(1)}, f32[8,32]{1,0:T(8,128)S(1)}, u32[]{:S(2)}, u32[]{:S(2)}) collective-permute-start(f32[8,32]{1,0:T(8,128)S(1)} %shard_map.158.refs_0_), channel_id=1, source_target_pairs={{0,1},{1,0},{2,3},{3,2},{4,5},{5,4},{6,7},{7,6},{8,9},{9,8},{10,11... | collective-permute-start | bytes 3080 | tf_op jit(solution)/shard_map/ppermute | solution.py:152
  29.0 0.8 %collective-permute-done.13.refs_1_ = f32[8,32]{1,0:T(8,128)S(1)} collective-permute-done((f32[8,32]{1,0:T(8,128)S(1)}, f32[8,32]{1,0:T(8,128)S(1)}, u32[]{:S(2)}, u32[]{:S(2)}) %collective-permute-start.13) | collective-permute-done | bytes 1056 | tf_op jit(solution)/shard_map/ppermute | solution.py:152
  29.8 0.7 %shard_map.159 = (f32[1,8]{1,0:T(1,128)}, f32[1,8]{1,0:T(1,128)}, f32[1,16]{1,0:T(1,128)}) custom-call(f32[8,32]{1,0:T(8,128)S(1)} %shard_map.158.refs_0_, f32[8,32]{1,0:T(8,128)S(1)} %collective-permute-done.13.refs_1_, f32[3,32,128]{2,1,0:T(8,128)S(1)} %get-tuple-element.49.refs_5_.refs_2_), custom_call_target="tpu_custom_call" | custom-call | bytes 51200 | tf_op jit(solution)/shard_map/pallas_call | solution.py:389
  (34 shorter events, 0.2 us)
Async XLA Ops:
  0.6 5.7 %collective-permute-start = (bf16[8,1024]{1,0:T(8,128)(2,1)}, bf16[8,1024]{1,0:T(8,128)(2,1)S(1)}, u32[]{:S(2)}, u32[]{:S(2)}) collective-permute-start(bf16[8,1024]{1,0:T(8,128)(2,1)} %refs_2_.1), channel_id=1, source_target_pairs={{0,3},{1,2},{2,1},{3,0},{4,7},{5,6},{6,5},{7,4},{8,11},{9,10},{10,... | collective-permute-start | bytes 49160 | tf_op jit(solution)/shard_map/ppermute | solution.py:152
  3.2 5.8 %collective-permute-start.2 = (bf16[352,1024]{1,0:T(8,128)(2,1)}, bf16[352,1024]{1,0:T(8,128)(2,1)S(1)}, u32[]{:S(2)}, u32[]{:S(2)}) collective-permute-start(bf16[352,1024]{1,0:T(8,128)(2,1)} %bitcast.12), channel_id=1, source_target_pairs={{0,1},{1,0},{2,3},{3,2},{4,5},{5,4},{6,7},{7,6},{8,9},{9,8},{10,11... | collective-permute-start | bytes 2162696 | tf_op jit(solution)/shard_map/ppermute | solution.py:152
  3.8 1.1 %copy-start.2 = (bf16[352,1024]{1,0:T(8,128)(2,1)S(1)}, bf16[352,1024]{1,0:T(8,128)(2,1)}, u32[]{:S(2)}) copy-start(bf16[352,1024]{1,0:T(8,128)(2,1)} %refs_5_.3) | copy-start | bytes 2162692
  3.8 1.4 %copy-start.3 = (bf16[1024,512]{1,0:T(8,128)(2,1)S(1)}, bf16[1024,512]{1,0:T(8,128)(2,1)}, u32[]{:S(2)}) copy-start(bf16[1024,512]{1,0:T(8,128)(2,1)} %refs_7_.1) | copy-start | bytes 3145732
  3.8 5.2 %collective-permute-start.3 = (bf16[352,1024]{1,0:T(8,128)(2,1)}, bf16[352,1024]{1,0:T(8,128)(2,1)S(1)}, u32[]{:S(2)}, u32[]{:S(2)}) collective-permute-start(bf16[352,1024]{1,0:T(8,128)(2,1)} %bitcast.15), channel_id=1, source_target_pairs={{0,1},{1,0},{2,3},{3,2},{4,5},{5,4},{6,7},{7,6},{8,9},{9,8},{10,11... | collective-permute-start | bytes 2162696 | tf_op jit(solution)/shard_map/ppermute | solution.py:152
  3.8 1.6 %copy-start.6 = (bf16[8,1024]{1,0:T(8,128)(2,1)S(1)}, bf16[8,1024]{1,0:T(8,128)(2,1)}, u32[]{:S(2)}) copy-start(bf16[8,1024]{1,0:T(8,128)(2,1)} %refs_2_.1) | copy-start | bytes 49156
  3.8 1.6 %copy-start.8 = (f32[1024]{0:T(1024)S(1)}, f32[1024]{0:T(1024)}, u32[]{:S(2)}) copy-start(f32[1024]{0:T(1024)} %param.22) | copy-start | bytes 12292
  3.9 1.6 %copy-start.10 = (f32[8,2]{0,1:T(2,128)S(1)}, f32[8,2]{0,1:T(2,128)}, u32[]{:S(2)}) copy-start(f32[8,2]{0,1:T(2,128)} %param.15) | copy-start | bytes 196
  4.9 0.8 %copy-start.7 = (f32[1024]{0:T(1024)S(1)}, f32[1024]{0:T(1024)}, u32[]{:S(2)}) copy-start(f32[1024]{0:T(1024)} %param.18) | copy-start | bytes 12292
  4.9 4.1 %collective-permute-start.4 = (bf16[352,1024]{1,0:T(8,128)(2,1)S(1)}, bf16[352,1024]{1,0:T(8,128)(2,1)S(1)}, u32[]{:S(2)}, u32[]{:S(2)}) collective-permute-start(bf16[352,1024]{1,0:T(8,128)(2,1)S(1)} %copy-done.2), channel_id=1, source_target_pairs={{0,1},{1,0},{2,3},{3,2},{4,5},{5,4},{6,7},{7,6},{8,9},{9,8},{10,11... | collective-permute-start | bytes 2162696 | tf_op jit(solution)/shard_map/ppermute | solution.py:152
  5.3 14.8 %collective-permute-start.9 = (bf16[1024,512]{1,0:T(8,128)(2,1)S(1)}, bf16[1024,512]{1,0:T(8,128)(2,1)S(1)}, u32[]{:S(2)}, u32[]{:S(2)}) collective-permute-start(bf16[1024,512]{1,0:T(8,128)(2,1)S(1)} %copy-done.3), channel_id=1, source_target_pairs={{0,1},{1,0},{2,3},{3,2},{4,5},{5,4},{6,7},{7,6},{8,9},{9,8},{10,11... | collective-permute-start | bytes 3145736 | tf_op jit(solution)/shard_map/ppermute | solution.py:152
  5.5 0.7 %copy-start.9 = (s32[8,2]{0,1:T(2,128)S(1)}, s32[8,2]{0,1:T(2,128)}, u32[]{:S(2)}) copy-start(s32[8,2]{0,1:T(2,128)} %param.14) | copy-start | bytes 196
  6.3 2.7 %copy-start = (bf16[1024,352]{0,1:T(8,128)(2,1)S(1)}, bf16[1024,352]{0,1:T(8,128)(2,1)}, u32[]{:S(2)}) copy-start(bf16[1024,352]{0,1:T(8,128)(2,1)} %param.19) | copy-start | bytes 2162692
  6.3 2.7 %copy-start.1 = (bf16[1024,352]{0,1:T(8,128)(2,1)S(1)}, bf16[1024,352]{0,1:T(8,128)(2,1)}, u32[]{:S(2)}) copy-start(bf16[1024,352]{0,1:T(8,128)(2,1)} %param.20) | copy-start | bytes 2162692
  6.4 4.5 %collective-permute-start.1 = (bf16[16,1024]{1,0:T(8,128)(2,1)S(1)}, bf16[16,1024]{1,0:T(8,128)(2,1)S(1)}, u32[]{:S(2)}, u32[]{:S(2)}) collective-permute-start(bf16[16,1024]{1,0:T(8,128)(2,1)S(1)} %shard_map.150.rows_ref.first_ref), channel_id=1, source_target_pairs={{0,5},{1,4},{2,7},{3,6},{4,1},{5,0},{6,3},{7,2},{8,13},{9,12},{10,... | collective-permute-start | bytes 98312 | tf_op jit(solution)/shard_map/ppermute | solution.py:152
  10.2 2.9 %copy-start.5 = (bf16[64,512]{1,0:T(8,128)(2,1)S(1)}, bf16[64,512]{1,0:T(8,128)(2,1)}, u32[]{:S(2)}) copy-start(bf16[64,512]{1,0:T(8,128)(2,1)} %refs_9_.1) | copy-start | bytes 196612
  10.2 3.5 %collective-permute-start.6 = (bf16[16,1152]{1,0:T(8,128)(2,1)S(1)}, bf16[16,1152]{1,0:T(8,128)(2,1)S(1)}, u32[]{:S(2)}, u32[]{:S(2)}) collective-permute-start(bf16[16,1152]{1,0:T(8,128)(2,1)S(1)} %get-tuple-element.38), channel_id=1, source_target_pairs={{0,3},{1,2},{2,1},{3,0},{4,7},{5,6},{6,5},{7,4},{8,11},{9,10},{10,... | collective-permute-start | bytes 110600 | tf_op jit(solution)/shard_map/ppermute | solution.py:152
  12.1 3.6 %collective-permute-start.5 = (bf16[16,1024]{1,0:T(8,128)(2,1)S(1)}, bf16[16,1024]{1,0:T(8,128)(2,1)S(1)}, u32[]{:S(2)}, u32[]{:S(2)}) collective-permute-start(bf16[16,1024]{1,0:T(8,128)(2,1)S(1)} %get-tuple-element.33), channel_id=1, source_target_pairs={{0,3},{1,2},{2,1},{3,0},{4,7},{5,6},{6,5},{7,4},{8,11},{9,10},{10,... | collective-permute-start | bytes 98312 | tf_op jit(solution)/shard_map/ppermute | solution.py:152
  13.1 6.2 %collective-permute-start.10 = (bf16[64,512]{1,0:T(8,128)(2,1)S(1)}, bf16[64,512]{1,0:T(8,128)(2,1)S(1)}, u32[]{:S(2)}, u32[]{:S(2)}) collective-permute-start(bf16[64,512]{1,0:T(8,128)(2,1)S(1)} %copy-done.5), channel_id=1, source_target_pairs={{0,1},{1,0},{2,3},{3,2},{4,5},{5,4},{6,7},{7,6},{8,9},{9,8},{10,11... | collective-permute-start | bytes 196616 | tf_op jit(solution)/shard_map/ppermute | solution.py:152
  13.7 5.3 %collective-permute-start.7 = (bf16[16,1152]{1,0:T(8,128)(2,1)S(1)}, bf16[16,1152]{1,0:T(8,128)(2,1)S(1)}, u32[]{:S(2)}, u32[]{:S(2)}) collective-permute-start(bf16[16,1152]{1,0:T(8,128)(2,1)S(1)} %get-tuple-element.43), channel_id=1, source_target_pairs={{0,5},{1,4},{2,7},{3,6},{4,1},{5,0},{6,3},{7,2},{8,13},{9,12},{10,... | collective-permute-start | bytes 110600 | tf_op jit(solution)/shard_map/ppermute | solution.py:152
  15.7 3.4 %copy-start.11 = (s32[64]{0:T(128)S(1)}, s32[64]{0:T(128)}, u32[]{:S(2)}) copy-start(s32[64]{0:T(128)} %param.16) | copy-start | bytes 772
  15.7 3.4 %copy-start.12 = (s32[64]{0:T(128)S(1)}, s32[64]{0:T(128)}, u32[]{:S(2)}) copy-start(s32[64]{0:T(128)} %param.17) | copy-start | bytes 772
  15.7 4.4 %copy-start.4 = (bf16[1024,64]{0,1:T(8,128)(2,1)S(1)}, bf16[1024,64]{0,1:T(8,128)(2,1)}, u32[]{:S(2)}) copy-start(bf16[1024,64]{0,1:T(8,128)(2,1)} %param.24) | copy-start | bytes 393220
  15.7 4.3 %collective-permute-start.8 = (bf16[16,1024]{1,0:T(8,128)(2,1)S(1)}, bf16[16,1024]{1,0:T(8,128)(2,1)S(1)}, u32[]{:S(2)}, u32[]{:S(2)}) collective-permute-start(bf16[16,1024]{1,0:T(8,128)(2,1)S(1)} %get-tuple-element.48), channel_id=1, source_target_pairs={{0,5},{1,4},{2,7},{3,6},{4,1},{5,0},{6,3},{7,2},{8,13},{9,12},{10,... | collective-permute-start | bytes 98312 | tf_op jit(solution)/shard_map/ppermute | solution.py:152
  21.0 3.9 %collective-permute-start.11 = (f32[8,32]{1,0:T(8,128)S(1)}, f32[8,32]{1,0:T(8,128)S(1)}, u32[]{:S(2)}, u32[]{:S(2)}) collective-permute-start(f32[8,32]{1,0:T(8,128)S(1)} %shard_map.156.one_ref), channel_id=1, source_target_pairs={{0,5},{1,4},{2,7},{3,6},{4,1},{5,0},{6,3},{7,2},{8,13},{9,12},{10,... | collective-permute-start | bytes 3080 | tf_op jit(solution)/shard_map/ppermute | solution.py:152
  24.9 3.1 %collective-permute-start.12 = (f32[8,32]{1,0:T(8,128)S(1)}, f32[8,32]{1,0:T(8,128)S(1)}, u32[]{:S(2)}, u32[]{:S(2)}) collective-permute-start(f32[8,32]{1,0:T(8,128)S(1)} %shard_map.157.one_ref), channel_id=1, source_target_pairs={{0,3},{1,2},{2,1},{3,0},{4,7},{5,6},{6,5},{7,4},{8,11},{9,10},{10,... | collective-permute-start | bytes 3080 | tf_op jit(solution)/shard_map/ppermute | solution.py:152
  28.0 1.8 %collective-permute-start.13 = (f32[8,32]{1,0:T(8,128)S(1)}, f32[8,32]{1,0:T(8,128)S(1)}, u32[]{:S(2)}, u32[]{:S(2)}) collective-permute-start(f32[8,32]{1,0:T(8,128)S(1)} %shard_map.158.refs_0_), channel_id=1, source_target_pairs={{0,1},{1,0},{2,3},{3,2},{4,5},{5,4},{6,7},{7,6},{8,9},{9,8},{10,11... | collective-permute-start | bytes 3080 | tf_op jit(solution)/shard_map/ppermute | solution.py:152

commit v9 on v8

--- a/solution.py
+++ b/solution.py
@@ -242,14 +242,11 @@
         refs[6:-2],
         refs[-2:],
     )
-    hidden = rows_ref[...].astype(jnp.float32)
-    scale = lax.rsqrt(jnp.mean(hidden * hidden, axis=-1, keepdims=True) + epsilon)
-    moe_input = (hidden * gain_ref[...]).astype(jnp.bfloat16)
+    moe_input = rms_norm(rows_ref[...].astype(jnp.float32), gain_ref[...]).astype(jnp.bfloat16)
 
     def units(gate_ref, up_ref, down_ref):
         projections = [
-            scale
-            * lax.dot_general(moe_input, ref[...], TRANSPOSED, preferred_element_type=jnp.float32)
+            lax.dot_general(moe_input, ref[...], TRANSPOSED, preferred_element_type=jnp.float32)
             for ref in (gate_ref, up_ref)
         ]
         inner_act = (jax.nn.silu(projections[0]) * projections[1]).astype(jnp.bfloat16)

time: 30.7 us -> 30.8 us (level)
  transfers between devices with their start and end apart: 14 -> 14, of which waited for: 6 -> 6; matrix products, arithmetic and copies ran while one was open for 0% -> 0% of each run, Pallas kernels for 9% -> 10%
where the time goes in v9:
time: 30.8 us; the launch traced here: 30.6 us
  starting transfers between devices  15.9 us (52%)
  waiting for transfers between devices  7.23 us (23%)
  Pallas kernels  4.62 us (15%)
  local copies, waits for them, and re-layouts  2.1 us (7%)
  between operations  0.76 us (2%)
    ppermute x14, starting transfers between devices, exchange(): lax.ppermute(values, 'tensor', [(i, i ^ mask) for i in range(devices)])  15.9 us
    ppermute x14, waiting for transfers between devices, exchange(): lax.ppermute(values, 'tensor', [(i, i ^ mask) for i in range(devices)])  7.23 us
    pallas_call x12, Pallas kernels, call(): pl.pallas_call(kernel, out_shape=shapes, compiler_params=pltpu.CompilerPa...  4.62 us
    unnamed x26, local copies, waits for them, and re-layouts  2.1 us
  transfers between devices with their start and end apart: 14, of which 6 were waited for; matrix products, arithmetic and copies ran while one was open for 0% of the time, Pallas kernels for 10%

profile of v9, /device:TPU:0, one launch (start us, length us, event | category | flops | bytes accessed | tf_op | source)
XLA Modules:
  0.0 30.6 jit_solution(16527989742258967868)
XLA Ops:
  0.6 2.5 %collective-permute-start = (bf16[8,1024]{1,0:T(8,128)(2,1)}, bf16[8,1024]{1,0:T(8,128)(2,1)S(1)}, u32[]{:S(2)}, u32[]{:S(2)}) collective-permute-start(bf16[8,1024]{1,0:T(8,128)(2,1)} %refs_2_.1), channel_id=1, source_target_pairs={{0,3},{1,2},{2,1},{3,0},{4,7},{5,6},{6,5},{7,4},{8,11},{9,10},{10,... | collective-permute-start | bytes 49160 | tf_op jit(solution)/shard_map/ppermute | solution.py:152
  3.2 0.7 %collective-permute-start.2 = (bf16[352,1024]{1,0:T(8,128)(2,1)}, bf16[352,1024]{1,0:T(8,128)(2,1)S(1)}, u32[]{:S(2)}, u32[]{:S(2)}) collective-permute-start(bf16[352,1024]{1,0:T(8,128)(2,1)} %bitcast.12), channel_id=1, source_target_pairs={{0,1},{1,0},{2,3},{3,2},{4,5},{5,4},{6,7},{7,6},{8,9},{9,8},{10,11... | collective-permute-start | bytes 2162696 | tf_op jit(solution)/shard_map/ppermute | solution.py:152
  3.8 0.0 collective-permute-start.3
  3.9 1.1 %copy-done.2 = bf16[352,1024]{1,0:T(8,128)(2,1)S(1)} copy-done((bf16[352,1024]{1,0:T(8,128)(2,1)S(1)}, bf16[352,1024]{1,0:T(8,128)(2,1)}, u32[]{:S(2)}) %copy-start.2) | copy-done | bytes 720920
  5.0 0.3 %copy-done.3 = bf16[1024,512]{1,0:T(8,128)(2,1)S(1)} copy-done((bf16[1024,512]{1,0:T(8,128)(2,1)S(1)}, bf16[1024,512]{1,0:T(8,128)(2,1)}, u32[]{:S(2)}) %copy-start.3) | copy-done | bytes 1048600
  5.3 0.2 collective-permute-start.9
  5.5 0.2 copy-done.7
  5.7 0.4 %copy-done.9 = s32[8,2]{0,1:T(2,128)S(1)} copy-done((s32[8,2]{0,1:T(2,128)S(1)}, s32[8,2]{0,1:T(2,128)}, u32[]{:S(2)}) %copy-start.9) | copy-done | bytes 88
  6.1 0.2 shard_map.149
  6.3 0.0 copy-start
  6.3 0.0 copy-start.1
  6.4 2.6 %collective-permute-start.1 = (bf16[16,1024]{1,0:T(8,128)(2,1)S(1)}, bf16[16,1024]{1,0:T(8,128)(2,1)S(1)}, u32[]{:S(2)}, u32[]{:S(2)}) collective-permute-start(bf16[16,1024]{1,0:T(8,128)(2,1)S(1)} %shard_map.150.rows_ref.first_ref), channel_id=1, source_target_pairs={{0,5},{1,4},{2,7},{3,6},{4,1},{5,0},{6,3},{7,2},{8,13},{9,12},{10,... | collective-permute-start | bytes 98312 | tf_op jit(solution)/shard_map/ppermute | solution.py:152
  9.0 1.2 %shard_map.153 = (f32[16,1152]{1,0:T(8,128)S(1)}, bf16[16,1152]{1,0:T(8,128)(2,1)S(1)}) custom-call(bf16[16,1024]{1,0:T(8,128)(2,1)S(1)} %shard_map.150.rows_ref.first_ref, f32[1,1024]{1,0:T(1,128)S(1)} %get-tuple-element.30.gain_ref, bf16[352,1024]{1,0:T(8,128)(2,1)S(1)} %collective-permute-done.2.refs_0_, ...), custom_call_target="tpu_custom_call" | custom-call | flops 69206016 | bytes 4370432 | tf_op jit(solution)/shard_map/pallas_call | solution.py:386
  10.2 0.7 %collective-permute-start.6 = (bf16[16,1152]{1,0:T(8,128)(2,1)S(1)}, bf16[16,1152]{1,0:T(8,128)(2,1)S(1)}, u32[]{:S(2)}, u32[]{:S(2)}) collective-permute-start(bf16[16,1152]{1,0:T(8,128)(2,1)S(1)} %get-tuple-element.38), channel_id=1, source_target_pairs={{0,3},{1,2},{2,1},{3,0},{4,7},{5,6},{6,5},{7,4},{8,11},{9,10},{10,... | collective-permute-start | bytes 110600 | tf_op jit(solution)/shard_map/ppermute | solution.py:152
  11.0 1.2 %shard_map.151 = (f32[16,1024]{1,0:T(8,128)S(1)}, bf16[16,1024]{1,0:T(8,128)(2,1)S(1)}) custom-call(bf16[16,1024]{1,0:T(8,128)(2,1)S(1)} %collective-permute-done.1.rows_ref.second_ref, f32[1,1024]{1,0:T(1,128)S(1)} %get-tuple-element.30.gain_ref, bf16[352,1024]{1,0:T(8,128)(2,1)S(1)} %collective-permute-done.2.refs_0_, ...), custom_call_target="tpu_custom_call" | custom-call | flops 69206016 | bytes 4362240 | tf_op jit(solution)/shard_map/pallas_call | solution.py:386
  12.2 1.1 %collective-permute-start.5 = (bf16[16,1024]{1,0:T(8,128)(2,1)S(1)}, bf16[16,1024]{1,0:T(8,128)(2,1)S(1)}, u32[]{:S(2)}, u32[]{:S(2)}) collective-permute-start(bf16[16,1024]{1,0:T(8,128)(2,1)S(1)} %get-tuple-element.33), channel_id=1, source_target_pairs={{0,3},{1,2},{2,1},{3,0},{4,7},{5,6},{6,5},{7,4},{8,11},{9,10},{10,... | collective-permute-start | bytes 98312 | tf_op jit(solution)/shard_map/ppermute | solution.py:152
  13.2 0.2 collective-permute-start.10
  13.4 0.4 %collective-permute-done.6.arrived_ref = bf16[16,1152]{1,0:T(8,128)(2,1)S(1)} collective-permute-done((bf16[16,1152]{1,0:T(8,128)(2,1)S(1)}, bf16[16,1152]{1,0:T(8,128)(2,1)S(1)}, u32[]{:S(2)}, u32[]{:S(2)}) %collective-permute-start.6) | collective-permute-done | bytes 36896 | tf_op jit(solution)/shard_map/ppermute | solution.py:152
  13.8 2.0 %collective-permute-start.7 = (bf16[16,1152]{1,0:T(8,128)(2,1)S(1)}, bf16[16,1152]{1,0:T(8,128)(2,1)S(1)}, u32[]{:S(2)}, u32[]{:S(2)}) collective-permute-start(bf16[16,1152]{1,0:T(8,128)(2,1)S(1)} %get-tuple-element.43), channel_id=1, source_target_pairs={{0,5},{1,4},{2,7},{3,6},{4,1},{5,0},{6,3},{7,2},{8,13},{9,12},{10,... | collective-permute-start | bytes 110600 | tf_op jit(solution)/shard_map/ppermute | solution.py:152
  15.8 0.0 copy-start.4
  15.8 2.1 %collective-permute-start.8 = (bf16[16,1024]{1,0:T(8,128)(2,1)S(1)}, bf16[16,1024]{1,0:T(8,128)(2,1)S(1)}, u32[]{:S(2)}, u32[]{:S(2)}) collective-permute-start(bf16[16,1024]{1,0:T(8,128)(2,1)S(1)} %get-tuple-element.48), channel_id=1, source_target_pairs={{0,5},{1,4},{2,7},{3,6},{4,1},{5,0},{6,3},{7,2},{8,13},{9,12},{10,... | collective-permute-start | bytes 98312 | tf_op jit(solution)/shard_map/ppermute | solution.py:152
  17.9 1.2 %collective-permute-done.7.arrived_ref = bf16[16,1152]{1,0:T(8,128)(2,1)S(1)} collective-permute-done((bf16[16,1152]{1,0:T(8,128)(2,1)S(1)}, bf16[16,1152]{1,0:T(8,128)(2,1)S(1)}, u32[]{:S(2)}, u32[]{:S(2)}) %collective-permute-start.7) | collective-permute-done | bytes 36896 | tf_op jit(solution)/shard_map/ppermute | solution.py:152
  19.1 0.3 shard_map.155
  19.4 0.7 %collective-permute-done.8.refs_3_ = bf16[16,1024]{1,0:T(8,128)(2,1)S(1)} collective-permute-done((bf16[16,1024]{1,0:T(8,128)(2,1)S(1)}, bf16[16,1024]{1,0:T(8,128)(2,1)S(1)}, u32[]{:S(2)}, u32[]{:S(2)}) %collective-permute-start.8) | collective-permute-done | bytes 32800 | tf_op jit(solution)/shard_map/ppermute | solution.py:152
  20.1 0.9 %shard_map.156.one_ref = f32[8,32]{1,0:T(8,128)S(1)} custom-call(bf16[16,1024]{1,0:T(8,128)(2,1)S(1)} %get-tuple-element.45.refs_0_, f32[16,1024]{1,0:T(8,128)S(1)} %get-tuple-element.46.refs_1_, f32[16,128]{1,0:T(8,128)S(1)} %get-tuple-element.47.refs_2_, bf16[16,1024]{1,0:T(8,128)(2,1)S(1)} %collective-permute-done.8.refs_3_, ...), custom_call_target="tpu_custom_call" | custom-call | flops 67108864 | bytes 2551808 | tf_op jit(solution)/shard_map/pallas_call | solution.py:386
  21.0 2.1 %collective-permute-start.11 = (f32[8,32]{1,0:T(8,128)S(1)}, f32[8,32]{1,0:T(8,128)S(1)}, u32[]{:S(2)}, u32[]{:S(2)}) collective-permute-start(f32[8,32]{1,0:T(8,128)S(1)} %shard_map.156.one_ref), channel_id=1, source_target_pairs={{0,5},{1,4},{2,7},{3,6},{4,1},{5,0},{6,3},{7,2},{8,13},{9,12},{10,... | collective-permute-start | bytes 3080 | tf_op jit(solution)/shard_map/ppermute | solution.py:152
  23.1 1.9 %collective-permute-done.11.two_ref = f32[8,32]{1,0:T(8,128)S(1)} collective-permute-done((f32[8,32]{1,0:T(8,128)S(1)}, f32[8,32]{1,0:T(8,128)S(1)}, u32[]{:S(2)}, u32[]{:S(2)}) %collective-permute-start.11) | collective-permute-done | bytes 1056 | tf_op jit(solution)/shard_map/ppermute | solution.py:152
  25.0 0.9 %collective-permute-start.12 = (f32[8,32]{1,0:T(8,128)S(1)}, f32[8,32]{1,0:T(8,128)S(1)}, u32[]{:S(2)}, u32[]{:S(2)}) collective-permute-start(f32[8,32]{1,0:T(8,128)S(1)} %shard_map.157.one_ref), channel_id=1, source_target_pairs={{0,3},{1,2},{2,1},{3,0},{4,7},{5,6},{6,5},{7,4},{8,11},{9,10},{10,... | collective-permute-start | bytes 3080 | tf_op jit(solution)/shard_map/ppermute | solution.py:152
  25.9 2.2 %collective-permute-done.12.two_ref = f32[8,32]{1,0:T(8,128)S(1)} collective-permute-done((f32[8,32]{1,0:T(8,128)S(1)}, f32[8,32]{1,0:T(8,128)S(1)}, u32[]{:S(2)}, u32[]{:S(2)}) %collective-permute-start.12) | collective-permute-done | bytes 1056 | tf_op jit(solution)/shard_map/ppermute | solution.py:152
  28.1 0.9 %collective-permute-start.13 = (f32[8,32]{1,0:T(8,128)S(1)}, f32[8,32]{1,0:T(8,128)S(1)}, u32[]{:S(2)}, u32[]{:S(2)}) collective-permute-start(f32[8,32]{1,0:T(8,128)S(1)} %shard_map.158.refs_0_), channel_id=1, source_target_pairs={{0,1},{1,0},{2,3},{3,2},{4,5},{5,4},{6,7},{7,6},{8,9},{9,8},{10,11... | collective-permute-start | bytes 3080 | tf_op jit(solution)/shard_map/ppermute | solution.py:152
  29.0 0.8 %collective-permute-done.13.refs_1_ = f32[8,32]{1,0:T(8,128)S(1)} collective-permute-done((f32[8,32]{1,0:T(8,128)S(1)}, f32[8,32]{1,0:T(8,128)S(1)}, u32[]{:S(2)}, u32[]{:S(2)}) %collective-permute-start.13) | collective-permute-done | bytes 1056 | tf_op jit(solution)/shard_map/ppermute | solution.py:152
  29.9 0.7 %shard_map.159 = (f32[1,8]{1,0:T(1,128)}, f32[1,8]{1,0:T(1,128)}, f32[1,16]{1,0:T(1,128)}) custom-call(f32[8,32]{1,0:T(8,128)S(1)} %shard_map.158.refs_0_, f32[8,32]{1,0:T(8,128)S(1)} %collective-permute-done.13.refs_1_, f32[3,32,128]{2,1,0:T(8,128)S(1)} %get-tuple-element.49.refs_5_.refs_2_), custom_call_target="tpu_custom_call" | custom-call | bytes 51200 | tf_op jit(solution)/shard_map/pallas_call | solution.py:386
  (34 shorter events, 0.2 us)
Async XLA Ops:
  0.6 5.7 %collective-permute-start = (bf16[8,1024]{1,0:T(8,128)(2,1)}, bf16[8,1024]{1,0:T(8,128)(2,1)S(1)}, u32[]{:S(2)}, u32[]{:S(2)}) collective-permute-start(bf16[8,1024]{1,0:T(8,128)(2,1)} %refs_2_.1), channel_id=1, source_target_pairs={{0,3},{1,2},{2,1},{3,0},{4,7},{5,6},{6,5},{7,4},{8,11},{9,10},{10,... | collective-permute-start | bytes 49160 | tf_op jit(solution)/shard_map/ppermute | solution.py:152
  3.2 5.8 %collective-permute-start.2 = (bf16[352,1024]{1,0:T(8,128)(2,1)}, bf16[352,1024]{1,0:T(8,128)(2,1)S(1)}, u32[]{:S(2)}, u32[]{:S(2)}) collective-permute-start(bf16[352,1024]{1,0:T(8,128)(2,1)} %bitcast.12), channel_id=1, source_target_pairs={{0,1},{1,0},{2,3},{3,2},{4,5},{5,4},{6,7},{7,6},{8,9},{9,8},{10,11... | collective-permute-start | bytes 2162696 | tf_op jit(solution)/shard_map/ppermute | solution.py:152
  3.8 1.1 %copy-start.2 = (bf16[352,1024]{1,0:T(8,128)(2,1)S(1)}, bf16[352,1024]{1,0:T(8,128)(2,1)}, u32[]{:S(2)}) copy-start(bf16[352,1024]{1,0:T(8,128)(2,1)} %refs_5_.3) | copy-start | bytes 2162692
  3.8 1.4 %copy-start.3 = (bf16[1024,512]{1,0:T(8,128)(2,1)S(1)}, bf16[1024,512]{1,0:T(8,128)(2,1)}, u32[]{:S(2)}) copy-start(bf16[1024,512]{1,0:T(8,128)(2,1)} %refs_7_.1) | copy-start | bytes 3145732
  3.8 5.2 %collective-permute-start.3 = (bf16[352,1024]{1,0:T(8,128)(2,1)}, bf16[352,1024]{1,0:T(8,128)(2,1)S(1)}, u32[]{:S(2)}, u32[]{:S(2)}) collective-permute-start(bf16[352,1024]{1,0:T(8,128)(2,1)} %bitcast.15), channel_id=1, source_target_pairs={{0,1},{1,0},{2,3},{3,2},{4,5},{5,4},{6,7},{7,6},{8,9},{9,8},{10,11... | collective-permute-start | bytes 2162696 | tf_op jit(solution)/shard_map/ppermute | solution.py:152
  3.8 1.6 %copy-start.6 = (bf16[8,1024]{1,0:T(8,128)(2,1)S(1)}, bf16[8,1024]{1,0:T(8,128)(2,1)}, u32[]{:S(2)}) copy-start(bf16[8,1024]{1,0:T(8,128)(2,1)} %refs_2_.1) | copy-start | bytes 49156
  3.8 1.6 %copy-start.8 = (f32[1024]{0:T(1024)S(1)}, f32[1024]{0:T(1024)}, u32[]{:S(2)}) copy-start(f32[1024]{0:T(1024)} %param.22) | copy-start | bytes 12292
  3.9 1.6 %copy-start.10 = (f32[8,2]{0,1:T(2,128)S(1)}, f32[8,2]{0,1:T(2,128)}, u32[]{:S(2)}) copy-start(f32[8,2]{0,1:T(2,128)} %param.15) | copy-start | bytes 196
  4.9 0.8 %copy-start.7 = (f32[1024]{0:T(1024)S(1)}, f32[1024]{0:T(1024)}, u32[]{:S(2)}) copy-start(f32[1024]{0:T(1024)} %param.18) | copy-start | bytes 12292
  4.9 4.1 %collective-permute-start.4 = (bf16[352,1024]{1,0:T(8,128)(2,1)S(1)}, bf16[352,1024]{1,0:T(8,128)(2,1)S(1)}, u32[]{:S(2)}, u32[]{:S(2)}) collective-permute-start(bf16[352,1024]{1,0:T(8,128)(2,1)S(1)} %copy-done.2), channel_id=1, source_target_pairs={{0,1},{1,0},{2,3},{3,2},{4,5},{5,4},{6,7},{7,6},{8,9},{9,8},{10,11... | collective-permute-start | bytes 2162696 | tf_op jit(solution)/shard_map/ppermute | solution.py:152
  5.3 14.8 %collective-permute-start.9 = (bf16[1024,512]{1,0:T(8,128)(2,1)S(1)}, bf16[1024,512]{1,0:T(8,128)(2,1)S(1)}, u32[]{:S(2)}, u32[]{:S(2)}) collective-permute-start(bf16[1024,512]{1,0:T(8,128)(2,1)S(1)} %copy-done.3), channel_id=1, source_target_pairs={{0,1},{1,0},{2,3},{3,2},{4,5},{5,4},{6,7},{7,6},{8,9},{9,8},{10,11... | collective-permute-start | bytes 3145736 | tf_op jit(solution)/shard_map/ppermute | solution.py:152
  5.5 0.7 %copy-start.9 = (s32[8,2]{0,1:T(2,128)S(1)}, s32[8,2]{0,1:T(2,128)}, u32[]{:S(2)}) copy-start(s32[8,2]{0,1:T(2,128)} %param.14) | copy-start | bytes 196
  6.3 2.7 %copy-start = (bf16[1024,352]{0,1:T(8,128)(2,1)S(1)}, bf16[1024,352]{0,1:T(8,128)(2,1)}, u32[]{:S(2)}) copy-start(bf16[1024,352]{0,1:T(8,128)(2,1)} %param.19) | copy-start | bytes 2162692
  6.3 2.7 %copy-start.1 = (bf16[1024,352]{0,1:T(8,128)(2,1)S(1)}, bf16[1024,352]{0,1:T(8,128)(2,1)}, u32[]{:S(2)}) copy-start(bf16[1024,352]{0,1:T(8,128)(2,1)} %param.20) | copy-start | bytes 2162692
  6.4 4.6 %collective-permute-start.1 = (bf16[16,1024]{1,0:T(8,128)(2,1)S(1)}, bf16[16,1024]{1,0:T(8,128)(2,1)S(1)}, u32[]{:S(2)}, u32[]{:S(2)}) collective-permute-start(bf16[16,1024]{1,0:T(8,128)(2,1)S(1)} %shard_map.150.rows_ref.first_ref), channel_id=1, source_target_pairs={{0,5},{1,4},{2,7},{3,6},{4,1},{5,0},{6,3},{7,2},{8,13},{9,12},{10,... | collective-permute-start | bytes 98312 | tf_op jit(solution)/shard_map/ppermute | solution.py:152
  10.2 3.0 %copy-start.5 = (bf16[64,512]{1,0:T(8,128)(2,1)S(1)}, bf16[64,512]{1,0:T(8,128)(2,1)}, u32[]{:S(2)}) copy-start(bf16[64,512]{1,0:T(8,128)(2,1)} %refs_9_.1) | copy-start | bytes 196612
  10.2 3.5 %collective-permute-start.6 = (bf16[16,1152]{1,0:T(8,128)(2,1)S(1)}, bf16[16,1152]{1,0:T(8,128)(2,1)S(1)}, u32[]{:S(2)}, u32[]{:S(2)}) collective-permute-start(bf16[16,1152]{1,0:T(8,128)(2,1)S(1)} %get-tuple-element.38), channel_id=1, source_target_pairs={{0,3},{1,2},{2,1},{3,0},{4,7},{5,6},{6,5},{7,4},{8,11},{9,10},{10,... | collective-permute-start | bytes 110600 | tf_op jit(solution)/shard_map/ppermute | solution.py:152
  12.2 3.6 %collective-permute-start.5 = (bf16[16,1024]{1,0:T(8,128)(2,1)S(1)}, bf16[16,1024]{1,0:T(8,128)(2,1)S(1)}, u32[]{:S(2)}, u32[]{:S(2)}) collective-permute-start(bf16[16,1024]{1,0:T(8,128)(2,1)S(1)} %get-tuple-element.33), channel_id=1, source_target_pairs={{0,3},{1,2},{2,1},{3,0},{4,7},{5,6},{6,5},{7,4},{8,11},{9,10},{10,... | collective-permute-start | bytes 98312 | tf_op jit(solution)/shard_map/ppermute | solution.py:152
  13.2 6.2 %collective-permute-start.10 = (bf16[64,512]{1,0:T(8,128)(2,1)S(1)}, bf16[64,512]{1,0:T(8,128)(2,1)S(1)}, u32[]{:S(2)}, u32[]{:S(2)}) collective-permute-start(bf16[64,512]{1,0:T(8,128)(2,1)S(1)} %copy-done.5), channel_id=1, source_target_pairs={{0,1},{1,0},{2,3},{3,2},{4,5},{5,4},{6,7},{7,6},{8,9},{9,8},{10,11... | collective-permute-start | bytes 196616 | tf_op jit(solution)/shard_map/ppermute | solution.py:152
  13.8 5.3 %collective-permute-start.7 = (bf16[16,1152]{1,0:T(8,128)(2,1)S(1)}, bf16[16,1152]{1,0:T(8,128)(2,1)S(1)}, u32[]{:S(2)}, u32[]{:S(2)}) collective-permute-start(bf16[16,1152]{1,0:T(8,128)(2,1)S(1)} %get-tuple-element.43), channel_id=1, source_target_pairs={{0,5},{1,4},{2,7},{3,6},{4,1},{5,0},{6,3},{7,2},{8,13},{9,12},{10,... | collective-permute-start | bytes 110600 | tf_op jit(solution)/shard_map/ppermute | solution.py:152
  15.8 3.4 %copy-start.11 = (s32[64]{0:T(128)S(1)}, s32[64]{0:T(128)}, u32[]{:S(2)}) copy-start(s32[64]{0:T(128)} %param.16) | copy-start | bytes 772
  15.8 3.4 %copy-start.12 = (s32[64]{0:T(128)S(1)}, s32[64]{0:T(128)}, u32[]{:S(2)}) copy-start(s32[64]{0:T(128)} %param.17) | copy-start | bytes 772
  15.8 4.4 %copy-start.4 = (bf16[1024,64]{0,1:T(8,128)(2,1)S(1)}, bf16[1024,64]{0,1:T(8,128)(2,1)}, u32[]{:S(2)}) copy-start(bf16[1024,64]{0,1:T(8,128)(2,1)} %param.24) | copy-start | bytes 393220
  15.8 4.3 %collective-permute-start.8 = (bf16[16,1024]{1,0:T(8,128)(2,1)S(1)}, bf16[16,1024]{1,0:T(8,128)(2,1)S(1)}, u32[]{:S(2)}, u32[]{:S(2)}) collective-permute-start(bf16[16,1024]{1,0:T(8,128)(2,1)S(1)} %get-tuple-element.48), channel_id=1, source_target_pairs={{0,5},{1,4},{2,7},{3,6},{4,1},{5,0},{6,3},{7,2},{8,13},{9,12},{10,... | collective-permute-start | bytes 98312 | tf_op jit(solution)/shard_map/ppermute | solution.py:152
  21.0 3.9 %collective-permute-start.11 = (f32[8,32]{1,0:T(8,128)S(1)}, f32[8,32]{1,0:T(8,128)S(1)}, u32[]{:S(2)}, u32[]{:S(2)}) collective-permute-start(f32[8,32]{1,0:T(8,128)S(1)} %shard_map.156.one_ref), channel_id=1, source_target_pairs={{0,5},{1,4},{2,7},{3,6},{4,1},{5,0},{6,3},{7,2},{8,13},{9,12},{10,... | collective-permute-start | bytes 3080 | tf_op jit(solution)/shard_map/ppermute | solution.py:152
  25.0 3.1 %collective-permute-start.12 = (f32[8,32]{1,0:T(8,128)S(1)}, f32[8,32]{1,0:T(8,128)S(1)}, u32[]{:S(2)}, u32[]{:S(2)}) collective-permute-start(f32[8,32]{1,0:T(8,128)S(1)} %shard_map.157.one_ref), channel_id=1, source_target_pairs={{0,3},{1,2},{2,1},{3,0},{4,7},{5,6},{6,5},{7,4},{8,11},{9,10},{10,... | collective-permute-start | bytes 3080 | tf_op jit(solution)/shard_map/ppermute | solution.py:152
  28.1 1.8 %collective-permute-start.13 = (f32[8,32]{1,0:T(8,128)S(1)}, f32[8,32]{1,0:T(8,128)S(1)}, u32[]{:S(2)}, u32[]{:S(2)}) collective-permute-start(f32[8,32]{1,0:T(8,128)S(1)} %shard_map.158.refs_0_), channel_id=1, source_target_pairs={{0,1},{1,0},{2,3},{3,2},{4,5},{5,4},{6,7},{7,6},{8,9},{9,8},{10,11... | collective-permute-start | bytes 3080 | tf_op jit(solution)/shard_map/ppermute | solution.py:152

commit v10 on v8

--- a/solution.py
+++ b/solution.py
@@ -183,8 +183,8 @@
 
 
 def early_kernel(tok_rows, bits, *refs):
-    (ids_ref, gates_ref), (mixing_ref,) = refs[0:2], refs[5:6]
-    for in_ref, out_ref in zip(refs[2:5], refs[6:9]):
+    (ids_ref, gates_ref), (mixing_ref,) = refs[0:2], refs[7:8]
+    for in_ref, out_ref in zip(refs[2:7], refs[8:13]):
         out_ref[...] = in_ref[...]
     my_index, parity, half = places(tok_rows, bits)
     experts = gates_ref.shape[0]
@@ -267,76 +267,13 @@
     sent_ref[...] = total.astype(jnp.bfloat16)
 
 
-def late_kernel(
-    tok_rows,
-    bits,
-    place,
-    targets_ref,
-    seq_ref,
-    first_ref,
-    second_ref,
-    first_total_ref,
-    second_total_ref,
-    arrived_ref,
-    gain_ref,
-    columns_ref,
-    final_ref,
-    partial_ref,
-    weight_ref,
-):
-    columns_kernel(tok_rows, bits, targets_ref, seq_ref, columns_ref)
-    features = first_ref.shape[1]
+def head_rows(rows, wanted, down_ref, weight_refs):
     my_index = lax.axis_index("tensor")
-    expert = my_index // SPLIT
-    mixing = first_total_ref[:tok_rows, features:]
-    mixing = mixing + arrived_ref[:, features:].astype(jnp.float32)[:tok_rows]
-    lane = lax.broadcasted_iota(jnp.int32, mixing.shape, 1)
-
-    def weights(side, which):
-        blocks = [
-            jnp.sum(
-                jnp.where((lane // 8 == 2 * side + k) & (lane % 2 == which), mixing, 0.0),
-                axis=1,
-                keepdims=True,
-            )
-            for k in range(2)
-        ]
-        return jnp.concatenate(blocks, axis=0)
-
-    side = bit(my_index, place)
-    partial_value = weights(side, expert) * first_total_ref[:, :features]
-    partial_ref[...] = first_ref[...].astype(jnp.float32) + partial_value
-    weight_ref[...] = jnp.broadcast_to(weights(side, 1 - expert), weight_ref.shape)
-    mixed = second_ref[...].astype(jnp.float32)
-    mixed = mixed + weights(1 - side, expert) * second_total_ref[...]
-    arrived = arrived_ref[:, :features].astype(jnp.float32)
-    mixed = mixed + weights(1 - side, 1 - expert) * arrived
-    final_ref[...] = rms_norm(mixed, gain_ref[...]).astype(jnp.bfloat16)
-
-
-def half_columns(values, tok_rows, bits, parity):
-    tokens = values.shape[1]
-    half = tokens // 2
-    place = lax.broadcasted_iota(jnp.int32, (half, tokens), 0) + parity * half
-    token = lax.broadcasted_iota(jnp.int32, (half, tokens), 1)
-    here = token_at(place, tok_rows, bits) == token
-    column = jnp.sum(jnp.where(here, values.astype(jnp.float32), 0.0), axis=1, keepdims=True)
-    return column.astype(jnp.int32)
-
-
-def head_kernel(place, *refs):
-    (final_ref, partial_ref, weight_ref, arrived_ref, gain_ref, columns_ref, down_ref) = refs[0:7]
-    weight_refs, (stats_ref,) = refs[7:11], refs[11:]
-    my_index = lax.axis_index("tensor")
-    mixed = partial_ref[...] + weight_ref[:, 0:1] * arrived_ref[...].astype(jnp.float32)
-    first = rms_norm(mixed, gain_ref[...]).astype(jnp.bfloat16)
-    rows = in_order(bit(my_index, place) == 1, first, final_ref[...])
-    tokens = rows.shape[0]
-    wanted = columns_ref[0][:, 0:1].astype(jnp.int32)
+    wanted = wanted.astype(jnp.int32)
     latent = lax.dot_general(rows, down_ref[...], TRANSPOSED, preferred_element_type=jnp.float32)
     latent = latent.astype(jnp.bfloat16)
-    lane = lax.broadcasted_iota(jnp.int32, (tokens, 128), 1)
-    packed = jnp.zeros((tokens, 128), jnp.float32)
+    lane = lax.broadcasted_iota(jnp.int32, (rows.shape[0], 128), 1)
+    packed = jnp.zeros(lane.shape, jnp.float32)
     base, policy, matches = [], [], []
     for index, head_ref, up_ref in zip((my_index, my_index ^ 1), weight_refs[:2], weight_refs[2:]):
         logits = jnp.dot(rows, head_ref[...], preferred_element_type=jnp.float32)
@@ -353,7 +290,87 @@
         picked = jnp.sum(jnp.where(is_target, logits, 0.0), axis=1, keepdims=True)
         for kind, value in enumerate((top_value, exp_total, picked)):
             packed = jnp.where(lane == 2 * kind + at, value, packed)
-    stats_ref[...] = packed.T[:8]
+    return packed
+
+
+def late_kernel(
+    tok_rows,
+    bits,
+    place,
+    targets_ref,
+    seq_ref,
+    first_ref,
+    second_ref,
+    first_total_ref,
+    second_total_ref,
+    arrived_ref,
+    gain_ref,
+    down_ref,
+    head_ref,
+    far_head_ref,
+    up_ref,
+    far_up_ref,
+    columns_ref,
+    later_ref,
+    partial_ref,
+    weight_ref,
+):
+    columns_kernel(tok_rows, bits, targets_ref, seq_ref, columns_ref)
+    features = first_ref.shape[1]
+    my_index = lax.axis_index("tensor")
+    expert = my_index // SPLIT
+    mixing = first_total_ref[:tok_rows, features:]
+    mixing = mixing + arrived_ref[:, features:].astype(jnp.float32)[:tok_rows]
+    lane = lax.broadcasted_iota(jnp.int32, mixing.shape, 1)
+
+    def weights(side, which):
+        blocks = [
+            jnp.sum(
+                jnp.where((lane // 8 == 2 * side + k) & (lane % 2 == which), mixing, 0.0),
+                axis=1,
+                keepdims=True,
+            )
+            for k in range(2)
+        ]
+        return jnp.concatenate(blocks, axis=0)
+
+    side = bit(my_index, place)
+    partial_value = weights(side, expert) * first_total_ref[:, :features]
+    partial_ref[...] = first_ref[...].astype(jnp.float32) + partial_value
+    weight_ref[...] = jnp.broadcast_to(weights(side, 1 - expert), weight_ref.shape)
+    mixed = second_ref[...].astype(jnp.float32)
+    mixed = mixed + weights(1 - side, expert) * second_total_ref[...]
+    arrived = arrived_ref[:, :features].astype(jnp.float32)
+    mixed = mixed + weights(1 - side, 1 - expert) * arrived
+    rows = rms_norm(mixed, gain_ref[...]).astype(jnp.bfloat16)
+    piece = rows.shape[0]
+    wanted = columns_ref[0][:, 0:1]
+    wanted = jnp.where(side == 1, wanted[:piece], wanted[piece:])
+    weight_refs = (head_ref, far_head_ref, up_ref, far_up_ref)
+    later_ref[...] = head_rows(rows, wanted, down_ref, weight_refs)
+
+
+def half_columns(values, tok_rows, bits, parity):
+    tokens = values.shape[1]
+    half = tokens // 2
+    place = lax.broadcasted_iota(jnp.int32, (half, tokens), 0) + parity * half
+    token = lax.broadcasted_iota(jnp.int32, (half, tokens), 1)
+    here = token_at(place, tok_rows, bits) == token
+    column = jnp.sum(jnp.where(here, values.astype(jnp.float32), 0.0), axis=1, keepdims=True)
+    return column.astype(jnp.int32)
+
+
+def head_kernel(place, *refs):
+    (later_ref, partial_ref, weight_ref, arrived_ref, gain_ref, columns_ref, down_ref) = refs[0:7]
+    weight_refs, (stats_ref,) = refs[7:11], refs[11:]
+    late = bit(lax.axis_index("tensor"), place) == 1
+    mixed = partial_ref[...] + weight_ref[:, 0:1] * arrived_ref[...].astype(jnp.float32)
+    rows = rms_norm(mixed, gain_ref[...]).astype(jnp.bfloat16)
+    piece = rows.shape[0]
+    wanted = columns_ref[0][:, 0:1]
+    wanted = jnp.where(late, wanted[piece:], wanted[:piece])
+    packed = head_rows(rows, wanted, down_ref, weight_refs)
+    stats_ref[...] = in_order(late, packed, later_ref[...]).T[:8]
 
 
 def merge_kernel(one_ref, two_ref, out_ref):
@@ -421,19 +438,23 @@
 
     flags = call(flags_kernel, array(jnp.int32, 8, 128), flops=ROUND_FLOPS)
     flags, sent_d = lax.optimization_barrier((flags, w_down))
-    mixing, held_rows, gain, last_gain = call(
+    mixing, held_rows, gain, last_gain, held_targets, held_seq = call(
         functools.partial(early_kernel, tok_rows, bits),
         [
             array(jnp.float32, 2 * tok_rows, 128),
             array(jnp.bfloat16, tok_rows, features),
             array(jnp.float32, 1, features),
             array(jnp.float32, 1, features),
+            array(jnp.int32, 1, 2 * half),
+            array(jnp.int32, 1, 2 * half),
         ],
         expert_ids.T,
         gate_weights.T,
         hidden_in,
         moe_gain[None],
         final_gain[None],
+        targets[None],
+        seq_ids[None],
     )
     first = call(
         functools.partial(order_kernel, near_bit),
@@ -469,15 +490,17 @@
         )
         totals.append(total)
         sent.append(piece)
-    sent[0], late_seq = lax.optimization_barrier((sent[0], seq_ids[None]))
-    sent[1], late_targets = lax.optimization_barrier((sent[1], targets[None]))
+    sent[0], late_seq = lax.optimization_barrier((sent[0], held_seq))
+    sent[1], late_targets = lax.optimization_barrier((sent[1], held_targets))
     arrived = [exchange(piece, far_mask) for piece in sent]
 
+    vocabulary = [adapter_down.T, head_weight, exchange(head_weight, 1)]
+    vocabulary += [adapter_up, exchange(adapter_up, 1)]
     columns, *late = call(
         functools.partial(late_kernel, tok_rows, bits, far_bit),
         [
             array(jnp.float32, 3, half, 128),
-            array(jnp.bfloat16, 2 * tok_rows, features),
+            array(jnp.float32, 2 * tok_rows, 128),
             array(jnp.float32, 2 * tok_rows, features),
             array(jnp.float32, 2 * tok_rows, 128),
         ],
@@ -488,6 +511,7 @@
         *totals,
         arrived[0],
         last_gain,
+        *vocabulary,
     )
     stats = call(
         functools.partial(head_kernel, far_bit),
@@ -496,11 +520,7 @@
         arrived[1],
         last_gain,
         columns,
-        adapter_down.T,
-        head_weight,
-        exchange(head_weight, 1),
-        adapter_up,
-        exchange(adapter_up, 1),
+        *vocabulary,
         flops=2 * devices * tok_rows * features * head_weight.shape[1],
     )
     for mask in (far_mask, near_mask):

time: 30.7 us -> 30.6 us (level)
  waiting for transfers between devices: 7.29 us -> 6.52 us
  Pallas kernels: 4.47 us -> 4.98 us
    ppermute x14, waiting for transfers between devices: 7.29 us -> 6.52 us  [exchange(): lax.ppermute(values, 'tensor', [(i, i ^ mask) for i in range(devices)])]
    pallas_call x12, Pallas kernels: 4.47 us -> 4.98 us  [call(): pl.pallas_call(kernel, out_shape=shapes, compiler_params=pltpu.CompilerPa...]
  transfers between devices with their start and end apart: 14 -> 14, of which waited for: 6 -> 5; matrix products, arithmetic and copies ran while one was open for 0% -> 0% of each run, Pallas kernels for 9% -> 11%
where the time goes in v10:
time: 30.6 us; the launch traced here: 30.4 us
  starting transfers between devices  16.1 us (53%)
  waiting for transfers between devices  6.52 us (21%)
  Pallas kernels  4.98 us (16%)
  local copies, waits for them, and re-layouts  2.09 us (7%)
  between operations  0.78 us (3%)
    ppermute x14, starting transfers between devices, exchange(): lax.ppermute(values, 'tensor', [(i, i ^ mask) for i in range(devices)])  16.1 us
    ppermute x14, waiting for transfers between devices, exchange(): lax.ppermute(values, 'tensor', [(i, i ^ mask) for i in range(devices)])  6.52 us
    pallas_call x12, Pallas kernels, call(): pl.pallas_call(kernel, out_shape=shapes, compiler_params=pltpu.CompilerPa...  4.98 us
    unnamed x26, local copies, waits for them, and re-layouts  2.09 us
  transfers between devices with their start and end apart: 14, of which 5 were waited for; matrix products, arithmetic and copies ran while one was open for 0% of the time, Pallas kernels for 11%

profile of v10, /device:TPU:0, one launch (start us, length us, event | category | flops | bytes accessed | tf_op | source)
XLA Modules:
  0.0 30.4 jit_solution(17050832417602796988)
XLA Ops:
  0.6 2.5 %collective-permute-start = (bf16[8,1024]{1,0:T(8,128)(2,1)}, bf16[8,1024]{1,0:T(8,128)(2,1)S(1)}, u32[]{:S(2)}, u32[]{:S(2)}) collective-permute-start(bf16[8,1024]{1,0:T(8,128)(2,1)} %refs_2_.1), channel_id=1, source_target_pairs={{0,3},{1,2},{2,1},{3,0},{4,7},{5,6},{6,5},{7,4},{8,11},{9,10},{10,... | collective-permute-start | bytes 49160 | tf_op jit(solution)/shard_map/ppermute | solution.py:152
  3.2 0.7 %collective-permute-start.2 = (bf16[352,1024]{1,0:T(8,128)(2,1)}, bf16[352,1024]{1,0:T(8,128)(2,1)S(1)}, u32[]{:S(2)}, u32[]{:S(2)}) collective-permute-start(bf16[352,1024]{1,0:T(8,128)(2,1)} %bitcast.12), channel_id=1, source_target_pairs={{0,1},{1,0},{2,3},{3,2},{4,5},{5,4},{6,7},{7,6},{8,9},{9,8},{10,11... | collective-permute-start | bytes 2162696 | tf_op jit(solution)/shard_map/ppermute | solution.py:152
  3.9 1.0 %copy-done.3 = bf16[352,1024]{1,0:T(8,128)(2,1)S(1)} copy-done((bf16[352,1024]{1,0:T(8,128)(2,1)S(1)}, bf16[352,1024]{1,0:T(8,128)(2,1)}, u32[]{:S(2)}) %copy-start.3) | copy-done | bytes 720920
  4.9 0.0 collective-permute-start.4
  5.0 0.3 %copy-done = bf16[1024,512]{1,0:T(8,128)(2,1)S(1)} copy-done((bf16[1024,512]{1,0:T(8,128)(2,1)S(1)}, bf16[1024,512]{1,0:T(8,128)(2,1)}, u32[]{:S(2)}) %copy-start) | copy-done | bytes 1048600
  5.3 0.2 collective-permute-start.8
  5.5 0.6 %copy-done.8 = f32[1024]{0:T(1024)S(1)} copy-done((f32[1024]{0:T(1024)S(1)}, f32[1024]{0:T(1024)}, u32[]{:S(2)}) %copy-start.8) | copy-done | bytes 4120
  6.1 0.0 copy-done.7
  6.2 0.0 copy-done.9
  6.2 0.2 shard_map.149
  6.4 0.0 copy-start.1
  6.4 0.0 copy-start.2
  6.4 2.6 %collective-permute-start.1 = (bf16[16,1024]{1,0:T(8,128)(2,1)S(1)}, bf16[16,1024]{1,0:T(8,128)(2,1)S(1)}, u32[]{:S(2)}, u32[]{:S(2)}) collective-permute-start(bf16[16,1024]{1,0:T(8,128)(2,1)S(1)} %shard_map.150.rows_ref.first_ref), channel_id=1, source_target_pairs={{0,5},{1,4},{2,7},{3,6},{4,1},{5,0},{6,3},{7,2},{8,13},{9,12},{10,... | collective-permute-start | bytes 98312 | tf_op jit(solution)/shard_map/ppermute | solution.py:152
  9.1 1.1 %shard_map.153 = (f32[16,1152]{1,0:T(8,128)S(1)}, bf16[16,1152]{1,0:T(8,128)(2,1)S(1)}) custom-call(bf16[16,1024]{1,0:T(8,128)(2,1)S(1)} %shard_map.150.rows_ref.first_ref, f32[1,1024]{1,0:T(1,128)S(1)} %get-tuple-element.32.gain_ref, bf16[352,1024]{1,0:T(8,128)(2,1)S(1)} %collective-permute-done.2.refs_0_, ...), custom_call_target="tpu_custom_call" | custom-call | flops 69206016 | bytes 4370432 | tf_op jit(solution)/shard_map/pallas_call | solution.py:406
  10.2 0.7 %collective-permute-start.6 = (bf16[16,1152]{1,0:T(8,128)(2,1)S(1)}, bf16[16,1152]{1,0:T(8,128)(2,1)S(1)}, u32[]{:S(2)}, u32[]{:S(2)}) collective-permute-start(bf16[16,1152]{1,0:T(8,128)(2,1)S(1)} %get-tuple-element.41), channel_id=1, source_target_pairs={{0,3},{1,2},{2,1},{3,0},{4,7},{5,6},{6,5},{7,4},{8,11},{9,10},{10,... | collective-permute-start | bytes 110600 | tf_op jit(solution)/shard_map/ppermute | solution.py:152
  10.9 1.1 %shard_map.151 = (f32[16,1024]{1,0:T(8,128)S(1)}, bf16[16,1024]{1,0:T(8,128)(2,1)S(1)}) custom-call(bf16[16,1024]{1,0:T(8,128)(2,1)S(1)} %collective-permute-done.1.rows_ref.second_ref, f32[1,1024]{1,0:T(1,128)S(1)} %get-tuple-element.32.gain_ref, bf16[352,1024]{1,0:T(8,128)(2,1)S(1)} %collective-permute-done.2.refs_0_, ...), custom_call_target="tpu_custom_call" | custom-call | flops 69206016 | bytes 4362240 | tf_op jit(solution)/shard_map/pallas_call | solution.py:406
  12.1 1.1 %collective-permute-start.5 = (bf16[16,1024]{1,0:T(8,128)(2,1)S(1)}, bf16[16,1024]{1,0:T(8,128)(2,1)S(1)}, u32[]{:S(2)}, u32[]{:S(2)}) collective-permute-start(bf16[16,1024]{1,0:T(8,128)(2,1)S(1)} %get-tuple-element.35), channel_id=1, source_target_pairs={{0,3},{1,2},{2,1},{3,0},{4,7},{5,6},{6,5},{7,4},{8,11},{9,10},{10,... | collective-permute-start | bytes 98312 | tf_op jit(solution)/shard_map/ppermute | solution.py:152
  13.1 0.2 collective-permute-start.9
  13.3 0.4 %collective-permute-done.6.arrived_ref = bf16[16,1152]{1,0:T(8,128)(2,1)S(1)} collective-permute-done((bf16[16,1152]{1,0:T(8,128)(2,1)S(1)}, bf16[16,1152]{1,0:T(8,128)(2,1)S(1)}, u32[]{:S(2)}, u32[]{:S(2)}) %collective-permute-start.6) | collective-permute-done | bytes 36896 | tf_op jit(solution)/shard_map/ppermute | solution.py:152
  13.8 1.9 %collective-permute-start.7 = (bf16[16,1152]{1,0:T(8,128)(2,1)S(1)}, bf16[16,1152]{1,0:T(8,128)(2,1)S(1)}, u32[]{:S(2)}, u32[]{:S(2)}) collective-permute-start(bf16[16,1152]{1,0:T(8,128)(2,1)S(1)} %get-tuple-element.47), channel_id=1, source_target_pairs={{0,5},{1,4},{2,7},{3,6},{4,1},{5,0},{6,3},{7,2},{8,13},{9,12},{10,... | collective-permute-start | bytes 110600 | tf_op jit(solution)/shard_map/ppermute | solution.py:152
  15.7 2.1 %collective-permute-start.10 = (bf16[16,1024]{1,0:T(8,128)(2,1)S(1)}, bf16[16,1024]{1,0:T(8,128)(2,1)S(1)}, u32[]{:S(2)}, u32[]{:S(2)}) collective-permute-start(bf16[16,1024]{1,0:T(8,128)(2,1)S(1)} %get-tuple-element.52), channel_id=1, source_target_pairs={{0,5},{1,4},{2,7},{3,6},{4,1},{5,0},{6,3},{7,2},{8,13},{9,12},{10,... | collective-permute-start | bytes 98312 | tf_op jit(solution)/shard_map/ppermute | solution.py:152
  17.8 1.3 %collective-permute-done.7.arrived_ref = bf16[16,1152]{1,0:T(8,128)(2,1)S(1)} collective-permute-done((bf16[16,1152]{1,0:T(8,128)(2,1)S(1)}, bf16[16,1152]{1,0:T(8,128)(2,1)S(1)}, u32[]{:S(2)}, u32[]{:S(2)}) %collective-permute-start.7) | collective-permute-done | bytes 36896 | tf_op jit(solution)/shard_map/ppermute | solution.py:152
  19.1 0.9 %shard_map.155 = (f32[3,32,128]{2,1,0:T(8,128)S(1)}, f32[16,128]{1,0:T(8,128)S(1)}, f32[16,1024]{1,0:T(8,128)S(1)}, f32[16,128]{1,0:T(8,128)S(1)}) custom-call(s32[1,64]{1,0:T(1,128)S(1)} %get-tuple-element.38.targets_ref, s32[1,64]{1,0:T(1,128)S(1)} %get-tuple-element.44.seq_ref, bf16[16,1024]{1,0:T(8,128)(2,1)S(1)} %shard_map.150.rows_ref.first_ref, ...), custom_call_target="tpu_custom_call" | custom-call | bytes 2605568 | tf_op jit(solution)/shard_map/pallas_call | solution.py:406
  20.0 0.0 collective-permute-done.10.refs_3_
  20.0 0.8 %shard_map.156.one_ref = f32[8,32]{1,0:T(8,128)S(1)} custom-call(f32[16,128]{1,0:T(8,128)S(1)} %get-tuple-element.49.refs_0_, f32[16,1024]{1,0:T(8,128)S(1)} %get-tuple-element.50.refs_1_, f32[16,128]{1,0:T(8,128)S(1)} %get-tuple-element.51.refs_2_, bf16[16,1024]{1,0:T(8,128)(2,1)S(1)} %collective-permute-done.10.refs_3_, ...), custom_call_target="tpu_custom_call" | custom-call | flops 67108864 | bytes 2527232 | tf_op jit(solution)/shard_map/pallas_call | solution.py:406
  20.8 2.1 %collective-permute-start.11 = (f32[8,32]{1,0:T(8,128)S(1)}, f32[8,32]{1,0:T(8,128)S(1)}, u32[]{:S(2)}, u32[]{:S(2)}) collective-permute-start(f32[8,32]{1,0:T(8,128)S(1)} %shard_map.156.one_ref), channel_id=1, source_target_pairs={{0,5},{1,4},{2,7},{3,6},{4,1},{5,0},{6,3},{7,2},{8,13},{9,12},{10,... | collective-permute-start | bytes 3080 | tf_op jit(solution)/shard_map/ppermute | solution.py:152
  23.0 1.8 %collective-permute-done.11.two_ref = f32[8,32]{1,0:T(8,128)S(1)} collective-permute-done((f32[8,32]{1,0:T(8,128)S(1)}, f32[8,32]{1,0:T(8,128)S(1)}, u32[]{:S(2)}, u32[]{:S(2)}) %collective-permute-start.11) | collective-permute-done | bytes 1056 | tf_op jit(solution)/shard_map/ppermute | solution.py:152
  24.8 1.0 %collective-permute-start.12 = (f32[8,32]{1,0:T(8,128)S(1)}, f32[8,32]{1,0:T(8,128)S(1)}, u32[]{:S(2)}, u32[]{:S(2)}) collective-permute-start(f32[8,32]{1,0:T(8,128)S(1)} %shard_map.157.one_ref), channel_id=1, source_target_pairs={{0,3},{1,2},{2,1},{3,0},{4,7},{5,6},{6,5},{7,4},{8,11},{9,10},{10,... | collective-permute-start | bytes 3080 | tf_op jit(solution)/shard_map/ppermute | solution.py:152
  25.8 2.1 %collective-permute-done.12.two_ref = f32[8,32]{1,0:T(8,128)S(1)} collective-permute-done((f32[8,32]{1,0:T(8,128)S(1)}, f32[8,32]{1,0:T(8,128)S(1)}, u32[]{:S(2)}, u32[]{:S(2)}) %collective-permute-start.12) | collective-permute-done | bytes 1056 | tf_op jit(solution)/shard_map/ppermute | solution.py:152
  27.9 1.0 %collective-permute-start.13 = (f32[8,32]{1,0:T(8,128)S(1)}, f32[8,32]{1,0:T(8,128)S(1)}, u32[]{:S(2)}, u32[]{:S(2)}) collective-permute-start(f32[8,32]{1,0:T(8,128)S(1)} %shard_map.158.refs_0_), channel_id=1, source_target_pairs={{0,1},{1,0},{2,3},{3,2},{4,5},{5,4},{6,7},{7,6},{8,9},{9,8},{10,11... | collective-permute-start | bytes 3080 | tf_op jit(solution)/shard_map/ppermute | solution.py:152
  28.9 0.8 %collective-permute-done.13.refs_1_ = f32[8,32]{1,0:T(8,128)S(1)} collective-permute-done((f32[8,32]{1,0:T(8,128)S(1)}, f32[8,32]{1,0:T(8,128)S(1)}, u32[]{:S(2)}, u32[]{:S(2)}) %collective-permute-start.13) | collective-permute-done | bytes 1056 | tf_op jit(solution)/shard_map/ppermute | solution.py:152
  29.7 0.7 %shard_map.159 = (f32[1,8]{1,0:T(1,128)}, f32[1,8]{1,0:T(1,128)}, f32[1,16]{1,0:T(1,128)}) custom-call(f32[8,32]{1,0:T(8,128)S(1)} %shard_map.158.refs_0_, f32[8,32]{1,0:T(8,128)S(1)} %collective-permute-done.13.refs_1_, f32[3,32,128]{2,1,0:T(8,128)S(1)} %get-tuple-element.53.refs_5_.refs_2_), custom_call_target="tpu_custom_call" | custom-call | bytes 51200 | tf_op jit(solution)/shard_map/pallas_call | solution.py:406
  (34 shorter events, 0.2 us)
Async XLA Ops:
  0.6 5.7 %collective-permute-start = (bf16[8,1024]{1,0:T(8,128)(2,1)}, bf16[8,1024]{1,0:T(8,128)(2,1)S(1)}, u32[]{:S(2)}, u32[]{:S(2)}) collective-permute-start(bf16[8,1024]{1,0:T(8,128)(2,1)} %refs_2_.1), channel_id=1, source_target_pairs={{0,3},{1,2},{2,1},{3,0},{4,7},{5,6},{6,5},{7,4},{8,11},{9,10},{10,... | collective-permute-start | bytes 49160 | tf_op jit(solution)/shard_map/ppermute | solution.py:152
  3.2 5.9 %collective-permute-start.2 = (bf16[352,1024]{1,0:T(8,128)(2,1)}, bf16[352,1024]{1,0:T(8,128)(2,1)S(1)}, u32[]{:S(2)}, u32[]{:S(2)}) collective-permute-start(bf16[352,1024]{1,0:T(8,128)(2,1)} %bitcast.12), channel_id=1, source_target_pairs={{0,1},{1,0},{2,3},{3,2},{4,5},{5,4},{6,7},{7,6},{8,9},{9,8},{10,11... | collective-permute-start | bytes 2162696 | tf_op jit(solution)/shard_map/ppermute | solution.py:152
  3.8 1.1 %copy-start.3 = (bf16[352,1024]{1,0:T(8,128)(2,1)S(1)}, bf16[352,1024]{1,0:T(8,128)(2,1)}, u32[]{:S(2)}) copy-start(bf16[352,1024]{1,0:T(8,128)(2,1)} %refs_5_.3) | copy-start | bytes 2162692
  3.8 1.4 %copy-start = (bf16[1024,512]{1,0:T(8,128)(2,1)S(1)}, bf16[1024,512]{1,0:T(8,128)(2,1)}, u32[]{:S(2)}) copy-start(bf16[1024,512]{1,0:T(8,128)(2,1)} %refs_7_.1) | copy-start | bytes 3145732
  3.8 5.2 %collective-permute-start.3 = (bf16[352,1024]{1,0:T(8,128)(2,1)}, bf16[352,1024]{1,0:T(8,128)(2,1)S(1)}, u32[]{:S(2)}, u32[]{:S(2)}) collective-permute-start(bf16[352,1024]{1,0:T(8,128)(2,1)} %bitcast.15), channel_id=1, source_target_pairs={{0,1},{1,0},{2,3},{3,2},{4,5},{5,4},{6,7},{7,6},{8,9},{9,8},{10,11... | collective-permute-start | bytes 2162696 | tf_op jit(solution)/shard_map/ppermute | solution.py:152
  3.8 1.6 %copy-start.6 = (bf16[8,1024]{1,0:T(8,128)(2,1)S(1)}, bf16[8,1024]{1,0:T(8,128)(2,1)}, u32[]{:S(2)}) copy-start(bf16[8,1024]{1,0:T(8,128)(2,1)} %refs_2_.1) | copy-start | bytes 49156
  3.8 1.6 %copy-start.10 = (f32[8,2]{0,1:T(2,128)S(1)}, f32[8,2]{0,1:T(2,128)}, u32[]{:S(2)}) copy-start(f32[8,2]{0,1:T(2,128)} %param.15) | copy-start | bytes 196
  3.9 1.6 %copy-start.11 = (s32[64]{0:T(128)S(1)}, s32[64]{0:T(128)}, u32[]{:S(2)}) copy-start(s32[64]{0:T(128)} %param.16) | copy-start | bytes 772
  3.9 1.6 %copy-start.12 = (s32[64]{0:T(128)S(1)}, s32[64]{0:T(128)}, u32[]{:S(2)}) copy-start(s32[64]{0:T(128)} %param.17) | copy-start | bytes 772
  4.9 4.1 %collective-permute-start.4 = (bf16[352,1024]{1,0:T(8,128)(2,1)S(1)}, bf16[352,1024]{1,0:T(8,128)(2,1)S(1)}, u32[]{:S(2)}, u32[]{:S(2)}) collective-permute-start(bf16[352,1024]{1,0:T(8,128)(2,1)S(1)} %copy-done.3), channel_id=1, source_target_pairs={{0,1},{1,0},{2,3},{3,2},{4,5},{5,4},{6,7},{7,6},{8,9},{9,8},{10,11... | collective-permute-start | bytes 2162696 | tf_op jit(solution)/shard_map/ppermute | solution.py:152
  5.3 13.8 %collective-permute-start.8 = (bf16[1024,512]{1,0:T(8,128)(2,1)S(1)}, bf16[1024,512]{1,0:T(8,128)(2,1)S(1)}, u32[]{:S(2)}, u32[]{:S(2)}) collective-permute-start(bf16[1024,512]{1,0:T(8,128)(2,1)S(1)} %copy-done), channel_id=1, source_target_pairs={{0,1},{1,0},{2,3},{3,2},{4,5},{5,4},{6,7},{7,6},{8,9},{9,8},{10,11... | collective-permute-start | bytes 3145736 | tf_op jit(solution)/shard_map/ppermute | solution.py:152
  5.5 0.7 %copy-start.8 = (f32[1024]{0:T(1024)S(1)}, f32[1024]{0:T(1024)}, u32[]{:S(2)}) copy-start(f32[1024]{0:T(1024)} %param.22) | copy-start | bytes 12292
  5.5 0.7 %copy-start.7 = (f32[1024]{0:T(1024)S(1)}, f32[1024]{0:T(1024)}, u32[]{:S(2)}) copy-start(f32[1024]{0:T(1024)} %param.18) | copy-start | bytes 12292
  5.5 0.7 %copy-start.9 = (s32[8,2]{0,1:T(2,128)S(1)}, s32[8,2]{0,1:T(2,128)}, u32[]{:S(2)}) copy-start(s32[8,2]{0,1:T(2,128)} %param.14) | copy-start | bytes 196
  6.4 2.7 %copy-start.1 = (bf16[1024,352]{0,1:T(8,128)(2,1)S(1)}, bf16[1024,352]{0,1:T(8,128)(2,1)}, u32[]{:S(2)}) copy-start(bf16[1024,352]{0,1:T(8,128)(2,1)} %param.19) | copy-start | bytes 2162692
  6.4 2.7 %copy-start.2 = (bf16[1024,352]{0,1:T(8,128)(2,1)S(1)}, bf16[1024,352]{0,1:T(8,128)(2,1)}, u32[]{:S(2)}) copy-start(bf16[1024,352]{0,1:T(8,128)(2,1)} %param.20) | copy-start | bytes 2162692
  6.4 4.5 %collective-permute-start.1 = (bf16[16,1024]{1,0:T(8,128)(2,1)S(1)}, bf16[16,1024]{1,0:T(8,128)(2,1)S(1)}, u32[]{:S(2)}, u32[]{:S(2)}) collective-permute-start(bf16[16,1024]{1,0:T(8,128)(2,1)S(1)} %shard_map.150.rows_ref.first_ref), channel_id=1, source_target_pairs={{0,5},{1,4},{2,7},{3,6},{4,1},{5,0},{6,3},{7,2},{8,13},{9,12},{10,... | collective-permute-start | bytes 98312 | tf_op jit(solution)/shard_map/ppermute | solution.py:152
  10.2 2.9 %copy-start.5 = (bf16[64,512]{1,0:T(8,128)(2,1)S(1)}, bf16[64,512]{1,0:T(8,128)(2,1)}, u32[]{:S(2)}) copy-start(bf16[64,512]{1,0:T(8,128)(2,1)} %refs_9_.1) | copy-start | bytes 196612
  10.2 3.5 %collective-permute-start.6 = (bf16[16,1152]{1,0:T(8,128)(2,1)S(1)}, bf16[16,1152]{1,0:T(8,128)(2,1)S(1)}, u32[]{:S(2)}, u32[]{:S(2)}) collective-permute-start(bf16[16,1152]{1,0:T(8,128)(2,1)S(1)} %get-tuple-element.41), channel_id=1, source_target_pairs={{0,3},{1,2},{2,1},{3,0},{4,7},{5,6},{6,5},{7,4},{8,11},{9,10},{10,... | collective-permute-start | bytes 110600 | tf_op jit(solution)/shard_map/ppermute | solution.py:152
  12.1 3.6 %collective-permute-start.5 = (bf16[16,1024]{1,0:T(8,128)(2,1)S(1)}, bf16[16,1024]{1,0:T(8,128)(2,1)S(1)}, u32[]{:S(2)}, u32[]{:S(2)}) collective-permute-start(bf16[16,1024]{1,0:T(8,128)(2,1)S(1)} %get-tuple-element.35), channel_id=1, source_target_pairs={{0,3},{1,2},{2,1},{3,0},{4,7},{5,6},{6,5},{7,4},{8,11},{9,10},{10,... | collective-permute-start | bytes 98312 | tf_op jit(solution)/shard_map/ppermute | solution.py:152
  13.1 4.7 %collective-permute-start.9 = (bf16[64,512]{1,0:T(8,128)(2,1)S(1)}, bf16[64,512]{1,0:T(8,128)(2,1)S(1)}, u32[]{:S(2)}, u32[]{:S(2)}) collective-permute-start(bf16[64,512]{1,0:T(8,128)(2,1)S(1)} %copy-done.5), channel_id=1, source_target_pairs={{0,1},{1,0},{2,3},{3,2},{4,5},{5,4},{6,7},{7,6},{8,9},{9,8},{10,11... | collective-permute-start | bytes 196616 | tf_op jit(solution)/shard_map/ppermute | solution.py:152
  13.8 5.3 %collective-permute-start.7 = (bf16[16,1152]{1,0:T(8,128)(2,1)S(1)}, bf16[16,1152]{1,0:T(8,128)(2,1)S(1)}, u32[]{:S(2)}, u32[]{:S(2)}) collective-permute-start(bf16[16,1152]{1,0:T(8,128)(2,1)S(1)} %get-tuple-element.47), channel_id=1, source_target_pairs={{0,5},{1,4},{2,7},{3,6},{4,1},{5,0},{6,3},{7,2},{8,13},{9,12},{10,... | collective-permute-start | bytes 110600 | tf_op jit(solution)/shard_map/ppermute | solution.py:152
  15.7 3.4 %copy-start.4 = (bf16[1024,64]{0,1:T(8,128)(2,1)S(1)}, bf16[1024,64]{0,1:T(8,128)(2,1)}, u32[]{:S(2)}) copy-start(bf16[1024,64]{0,1:T(8,128)(2,1)} %param.24) | copy-start | bytes 393220
  15.7 4.3 %collective-permute-start.10 = (bf16[16,1024]{1,0:T(8,128)(2,1)S(1)}, bf16[16,1024]{1,0:T(8,128)(2,1)S(1)}, u32[]{:S(2)}, u32[]{:S(2)}) collective-permute-start(bf16[16,1024]{1,0:T(8,128)(2,1)S(1)} %get-tuple-element.52), channel_id=1, source_target_pairs={{0,5},{1,4},{2,7},{3,6},{4,1},{5,0},{6,3},{7,2},{8,13},{9,12},{10,... | collective-permute-start | bytes 98312 | tf_op jit(solution)/shard_map/ppermute | solution.py:152
  20.8 3.9 %collective-permute-start.11 = (f32[8,32]{1,0:T(8,128)S(1)}, f32[8,32]{1,0:T(8,128)S(1)}, u32[]{:S(2)}, u32[]{:S(2)}) collective-permute-start(f32[8,32]{1,0:T(8,128)S(1)} %shard_map.156.one_ref), channel_id=1, source_target_pairs={{0,5},{1,4},{2,7},{3,6},{4,1},{5,0},{6,3},{7,2},{8,13},{9,12},{10,... | collective-permute-start | bytes 3080 | tf_op jit(solution)/shard_map/ppermute | solution.py:152
  24.8 3.1 %collective-permute-start.12 = (f32[8,32]{1,0:T(8,128)S(1)}, f32[8,32]{1,0:T(8,128)S(1)}, u32[]{:S(2)}, u32[]{:S(2)}) collective-permute-start(f32[8,32]{1,0:T(8,128)S(1)} %shard_map.157.one_ref), channel_id=1, source_target_pairs={{0,3},{1,2},{2,1},{3,0},{4,7},{5,6},{6,5},{7,4},{8,11},{9,10},{10,... | collective-permute-start | bytes 3080 | tf_op jit(solution)/shard_map/ppermute | solution.py:152
  27.9 1.8 %collective-permute-start.13 = (f32[8,32]{1,0:T(8,128)S(1)}, f32[8,32]{1,0:T(8,128)S(1)}, u32[]{:S(2)}, u32[]{:S(2)}) collective-permute-start(f32[8,32]{1,0:T(8,128)S(1)} %shard_map.158.refs_0_), channel_id=1, source_target_pairs={{0,1},{1,0},{2,3},{3,2},{4,5},{5,4},{6,7},{7,6},{8,9},{9,8},{10,11... | collective-permute-start | bytes 3080 | tf_op jit(solution)/shard_map/ppermute | solution.py:152

commit v11 on v8

--- a/solution.py
+++ b/solution.py
@@ -9,7 +9,7 @@
 
 SPLIT = 4
 SEQS = 16
-ROUND_FLOPS = 16 << 30
+ROUND_FLOPS = 32 << 30
 
 
 epsilon = 1e-06

time: 30.7 us -> 30.7 us (level)
  no operation moved by 1% of the time
where the time goes in v11:
time: 30.7 us; the launch traced here: 30.5 us
  starting transfers between devices  15.9 us (52%)
  waiting for transfers between devices  7.29 us (24%)
  Pallas kernels  4.47 us (15%)
  local copies, waits for them, and re-layouts  2.1 us (7%)
  between operations  0.76 us (2%)
    ppermute x14, starting transfers between devices, exchange(): lax.ppermute(values, 'tensor', [(i, i ^ mask) for i in range(devices)])  15.9 us
    ppermute x14, waiting for transfers between devices, exchange(): lax.ppermute(values, 'tensor', [(i, i ^ mask) for i in range(devices)])  7.29 us
    pallas_call x12, Pallas kernels, call(): pl.pallas_call(kernel, out_shape=shapes, compiler_params=pltpu.CompilerPa...  4.47 us
    unnamed x26, local copies, waits for them, and re-layouts  2.1 us
  transfers between devices with their start and end apart: 14, of which 6 were waited for; matrix products, arithmetic and copies ran while one was open for 0% of the time, Pallas kernels for 9%

profile of v11, /device:TPU:0, one launch (start us, length us, event | category | flops | bytes accessed | tf_op | source)
XLA Modules:
  0.0 30.5 jit_solution(11500867098409092477)
XLA Ops:
  0.6 2.5 %collective-permute-start = (bf16[8,1024]{1,0:T(8,128)(2,1)}, bf16[8,1024]{1,0:T(8,128)(2,1)S(1)}, u32[]{:S(2)}, u32[]{:S(2)}) collective-permute-start(bf16[8,1024]{1,0:T(8,128)(2,1)} %refs_2_.1), channel_id=1, source_target_pairs={{0,3},{1,2},{2,1},{3,0},{4,7},{5,6},{6,5},{7,4},{8,11},{9,10},{10,... | collective-permute-start | bytes 49160 | tf_op jit(solution)/shard_map/ppermute | solution.py:152
  3.2 0.7 %collective-permute-start.2 = (bf16[352,1024]{1,0:T(8,128)(2,1)}, bf16[352,1024]{1,0:T(8,128)(2,1)S(1)}, u32[]{:S(2)}, u32[]{:S(2)}) collective-permute-start(bf16[352,1024]{1,0:T(8,128)(2,1)} %bitcast.12), channel_id=1, source_target_pairs={{0,1},{1,0},{2,3},{3,2},{4,5},{5,4},{6,7},{7,6},{8,9},{9,8},{10,11... | collective-permute-start | bytes 2162696 | tf_op jit(solution)/shard_map/ppermute | solution.py:152
  3.8 0.0 collective-permute-start.3
  3.9 1.1 %copy-done.2 = bf16[352,1024]{1,0:T(8,128)(2,1)S(1)} copy-done((bf16[352,1024]{1,0:T(8,128)(2,1)S(1)}, bf16[352,1024]{1,0:T(8,128)(2,1)}, u32[]{:S(2)}) %copy-start.2) | copy-done | bytes 720920
  5.0 0.3 %copy-done.3 = bf16[1024,512]{1,0:T(8,128)(2,1)S(1)} copy-done((bf16[1024,512]{1,0:T(8,128)(2,1)S(1)}, bf16[1024,512]{1,0:T(8,128)(2,1)}, u32[]{:S(2)}) %copy-start.3) | copy-done | bytes 1048600
  5.3 0.2 collective-permute-start.9
  5.5 0.2 copy-done.7
  5.7 0.4 %copy-done.9 = s32[8,2]{0,1:T(2,128)S(1)} copy-done((s32[8,2]{0,1:T(2,128)S(1)}, s32[8,2]{0,1:T(2,128)}, u32[]{:S(2)}) %copy-start.9) | copy-done | bytes 88
  6.1 0.2 shard_map.149
  6.3 0.0 copy-start
  6.3 0.0 copy-start.1
  6.4 2.6 %collective-permute-start.1 = (bf16[16,1024]{1,0:T(8,128)(2,1)S(1)}, bf16[16,1024]{1,0:T(8,128)(2,1)S(1)}, u32[]{:S(2)}, u32[]{:S(2)}) collective-permute-start(bf16[16,1024]{1,0:T(8,128)(2,1)S(1)} %shard_map.150.rows_ref.first_ref), channel_id=1, source_target_pairs={{0,5},{1,4},{2,7},{3,6},{4,1},{5,0},{6,3},{7,2},{8,13},{9,12},{10,... | collective-permute-start | bytes 98312 | tf_op jit(solution)/shard_map/ppermute | solution.py:152
  9.0 1.1 %shard_map.153 = (f32[16,1152]{1,0:T(8,128)S(1)}, bf16[16,1152]{1,0:T(8,128)(2,1)S(1)}) custom-call(bf16[16,1024]{1,0:T(8,128)(2,1)S(1)} %shard_map.150.rows_ref.first_ref, f32[1,1024]{1,0:T(1,128)S(1)} %get-tuple-element.30.gain_ref, bf16[352,1024]{1,0:T(8,128)(2,1)S(1)} %collective-permute-done.2.refs_0_, ...), custom_call_target="tpu_custom_call" | custom-call | flops 69206016 | bytes 4370432 | tf_op jit(solution)/shard_map/pallas_call | solution.py:389
  10.2 0.8 %collective-permute-start.6 = (bf16[16,1152]{1,0:T(8,128)(2,1)S(1)}, bf16[16,1152]{1,0:T(8,128)(2,1)S(1)}, u32[]{:S(2)}, u32[]{:S(2)}) collective-permute-start(bf16[16,1152]{1,0:T(8,128)(2,1)S(1)} %get-tuple-element.38), channel_id=1, source_target_pairs={{0,3},{1,2},{2,1},{3,0},{4,7},{5,6},{6,5},{7,4},{8,11},{9,10},{10,... | collective-permute-start | bytes 110600 | tf_op jit(solution)/shard_map/ppermute | solution.py:152
  10.9 1.1 %shard_map.151 = (f32[16,1024]{1,0:T(8,128)S(1)}, bf16[16,1024]{1,0:T(8,128)(2,1)S(1)}) custom-call(bf16[16,1024]{1,0:T(8,128)(2,1)S(1)} %collective-permute-done.1.rows_ref.second_ref, f32[1,1024]{1,0:T(1,128)S(1)} %get-tuple-element.30.gain_ref, bf16[352,1024]{1,0:T(8,128)(2,1)S(1)} %collective-permute-done.2.refs_0_, ...), custom_call_target="tpu_custom_call" | custom-call | flops 69206016 | bytes 4362240 | tf_op jit(solution)/shard_map/pallas_call | solution.py:389
  12.1 1.0 %collective-permute-start.5 = (bf16[16,1024]{1,0:T(8,128)(2,1)S(1)}, bf16[16,1024]{1,0:T(8,128)(2,1)S(1)}, u32[]{:S(2)}, u32[]{:S(2)}) collective-permute-start(bf16[16,1024]{1,0:T(8,128)(2,1)S(1)} %get-tuple-element.33), channel_id=1, source_target_pairs={{0,3},{1,2},{2,1},{3,0},{4,7},{5,6},{6,5},{7,4},{8,11},{9,10},{10,... | collective-permute-start | bytes 98312 | tf_op jit(solution)/shard_map/ppermute | solution.py:152
  13.1 0.2 collective-permute-start.10
  13.3 0.4 %collective-permute-done.6.arrived_ref = bf16[16,1152]{1,0:T(8,128)(2,1)S(1)} collective-permute-done((bf16[16,1152]{1,0:T(8,128)(2,1)S(1)}, bf16[16,1152]{1,0:T(8,128)(2,1)S(1)}, u32[]{:S(2)}, u32[]{:S(2)}) %collective-permute-start.6) | collective-permute-done | bytes 36896 | tf_op jit(solution)/shard_map/ppermute | solution.py:152
  13.7 2.0 %collective-permute-start.7 = (bf16[16,1152]{1,0:T(8,128)(2,1)S(1)}, bf16[16,1152]{1,0:T(8,128)(2,1)S(1)}, u32[]{:S(2)}, u32[]{:S(2)}) collective-permute-start(bf16[16,1152]{1,0:T(8,128)(2,1)S(1)} %get-tuple-element.43), channel_id=1, source_target_pairs={{0,5},{1,4},{2,7},{3,6},{4,1},{5,0},{6,3},{7,2},{8,13},{9,12},{10,... | collective-permute-start | bytes 110600 | tf_op jit(solution)/shard_map/ppermute | solution.py:152
  15.7 0.0 copy-start.4
  15.7 2.1 %collective-permute-start.8 = (bf16[16,1024]{1,0:T(8,128)(2,1)S(1)}, bf16[16,1024]{1,0:T(8,128)(2,1)S(1)}, u32[]{:S(2)}, u32[]{:S(2)}) collective-permute-start(bf16[16,1024]{1,0:T(8,128)(2,1)S(1)} %get-tuple-element.48), channel_id=1, source_target_pairs={{0,5},{1,4},{2,7},{3,6},{4,1},{5,0},{6,3},{7,2},{8,13},{9,12},{10,... | collective-permute-start | bytes 98312 | tf_op jit(solution)/shard_map/ppermute | solution.py:152
  17.8 1.2 %collective-permute-done.7.arrived_ref = bf16[16,1152]{1,0:T(8,128)(2,1)S(1)} collective-permute-done((bf16[16,1152]{1,0:T(8,128)(2,1)S(1)}, bf16[16,1152]{1,0:T(8,128)(2,1)S(1)}, u32[]{:S(2)}, u32[]{:S(2)}) %collective-permute-start.7) | collective-permute-done | bytes 36896 | tf_op jit(solution)/shard_map/ppermute | solution.py:152
  19.1 0.3 shard_map.155
  19.4 0.7 %collective-permute-done.8.refs_3_ = bf16[16,1024]{1,0:T(8,128)(2,1)S(1)} collective-permute-done((bf16[16,1024]{1,0:T(8,128)(2,1)S(1)}, bf16[16,1024]{1,0:T(8,128)(2,1)S(1)}, u32[]{:S(2)}, u32[]{:S(2)}) %collective-permute-start.8) | collective-permute-done | bytes 32800 | tf_op jit(solution)/shard_map/ppermute | solution.py:152
  20.1 0.9 %shard_map.156.one_ref = f32[8,32]{1,0:T(8,128)S(1)} custom-call(bf16[16,1024]{1,0:T(8,128)(2,1)S(1)} %get-tuple-element.45.refs_0_, f32[16,1024]{1,0:T(8,128)S(1)} %get-tuple-element.46.refs_1_, f32[16,128]{1,0:T(8,128)S(1)} %get-tuple-element.47.refs_2_, bf16[16,1024]{1,0:T(8,128)(2,1)S(1)} %collective-permute-done.8.refs_3_, ...), custom_call_target="tpu_custom_call" | custom-call | flops 67108864 | bytes 2551808 | tf_op jit(solution)/shard_map/pallas_call | solution.py:389
  21.0 2.1 %collective-permute-start.11 = (f32[8,32]{1,0:T(8,128)S(1)}, f32[8,32]{1,0:T(8,128)S(1)}, u32[]{:S(2)}, u32[]{:S(2)}) collective-permute-start(f32[8,32]{1,0:T(8,128)S(1)} %shard_map.156.one_ref), channel_id=1, source_target_pairs={{0,5},{1,4},{2,7},{3,6},{4,1},{5,0},{6,3},{7,2},{8,13},{9,12},{10,... | collective-permute-start | bytes 3080 | tf_op jit(solution)/shard_map/ppermute | solution.py:152
  23.0 1.9 %collective-permute-done.11.two_ref = f32[8,32]{1,0:T(8,128)S(1)} collective-permute-done((f32[8,32]{1,0:T(8,128)S(1)}, f32[8,32]{1,0:T(8,128)S(1)}, u32[]{:S(2)}, u32[]{:S(2)}) %collective-permute-start.11) | collective-permute-done | bytes 1056 | tf_op jit(solution)/shard_map/ppermute | solution.py:152
  24.9 0.9 %collective-permute-start.12 = (f32[8,32]{1,0:T(8,128)S(1)}, f32[8,32]{1,0:T(8,128)S(1)}, u32[]{:S(2)}, u32[]{:S(2)}) collective-permute-start(f32[8,32]{1,0:T(8,128)S(1)} %shard_map.157.one_ref), channel_id=1, source_target_pairs={{0,3},{1,2},{2,1},{3,0},{4,7},{5,6},{6,5},{7,4},{8,11},{9,10},{10,... | collective-permute-start | bytes 3080 | tf_op jit(solution)/shard_map/ppermute | solution.py:152
  25.8 2.2 %collective-permute-done.12.two_ref = f32[8,32]{1,0:T(8,128)S(1)} collective-permute-done((f32[8,32]{1,0:T(8,128)S(1)}, f32[8,32]{1,0:T(8,128)S(1)}, u32[]{:S(2)}, u32[]{:S(2)}) %collective-permute-start.12) | collective-permute-done | bytes 1056 | tf_op jit(solution)/shard_map/ppermute | solution.py:152
  28.0 0.9 %collective-permute-start.13 = (f32[8,32]{1,0:T(8,128)S(1)}, f32[8,32]{1,0:T(8,128)S(1)}, u32[]{:S(2)}, u32[]{:S(2)}) collective-permute-start(f32[8,32]{1,0:T(8,128)S(1)} %shard_map.158.refs_0_), channel_id=1, source_target_pairs={{0,1},{1,0},{2,3},{3,2},{4,5},{5,4},{6,7},{7,6},{8,9},{9,8},{10,11... | collective-permute-start | bytes 3080 | tf_op jit(solution)/shard_map/ppermute | solution.py:152
  29.0 0.8 %collective-permute-done.13.refs_1_ = f32[8,32]{1,0:T(8,128)S(1)} collective-permute-done((f32[8,32]{1,0:T(8,128)S(1)}, f32[8,32]{1,0:T(8,128)S(1)}, u32[]{:S(2)}, u32[]{:S(2)}) %collective-permute-start.13) | collective-permute-done | bytes 1056 | tf_op jit(solution)/shard_map/ppermute | solution.py:152
  29.8 0.7 %shard_map.159 = (f32[1,8]{1,0:T(1,128)}, f32[1,8]{1,0:T(1,128)}, f32[1,16]{1,0:T(1,128)}) custom-call(f32[8,32]{1,0:T(8,128)S(1)} %shard_map.158.refs_0_, f32[8,32]{1,0:T(8,128)S(1)} %collective-permute-done.13.refs_1_, f32[3,32,128]{2,1,0:T(8,128)S(1)} %get-tuple-element.49.refs_5_.refs_2_), custom_call_target="tpu_custom_call" | custom-call | bytes 51200 | tf_op jit(solution)/shard_map/pallas_call | solution.py:389
  (34 shorter events, 0.2 us)
Async XLA Ops:
  0.6 5.7 %collective-permute-start = (bf16[8,1024]{1,0:T(8,128)(2,1)}, bf16[8,1024]{1,0:T(8,128)(2,1)S(1)}, u32[]{:S(2)}, u32[]{:S(2)}) collective-permute-start(bf16[8,1024]{1,0:T(8,128)(2,1)} %refs_2_.1), channel_id=1, source_target_pairs={{0,3},{1,2},{2,1},{3,0},{4,7},{5,6},{6,5},{7,4},{8,11},{9,10},{10,... | collective-permute-start | bytes 49160 | tf_op jit(solution)/shard_map/ppermute | solution.py:152
  3.2 5.8 %collective-permute-start.2 = (bf16[352,1024]{1,0:T(8,128)(2,1)}, bf16[352,1024]{1,0:T(8,128)(2,1)S(1)}, u32[]{:S(2)}, u32[]{:S(2)}) collective-permute-start(bf16[352,1024]{1,0:T(8,128)(2,1)} %bitcast.12), channel_id=1, source_target_pairs={{0,1},{1,0},{2,3},{3,2},{4,5},{5,4},{6,7},{7,6},{8,9},{9,8},{10,11... | collective-permute-start | bytes 2162696 | tf_op jit(solution)/shard_map/ppermute | solution.py:152
  3.8 1.1 %copy-start.2 = (bf16[352,1024]{1,0:T(8,128)(2,1)S(1)}, bf16[352,1024]{1,0:T(8,128)(2,1)}, u32[]{:S(2)}) copy-start(bf16[352,1024]{1,0:T(8,128)(2,1)} %refs_5_.3) | copy-start | bytes 2162692
  3.8 1.4 %copy-start.3 = (bf16[1024,512]{1,0:T(8,128)(2,1)S(1)}, bf16[1024,512]{1,0:T(8,128)(2,1)}, u32[]{:S(2)}) copy-start(bf16[1024,512]{1,0:T(8,128)(2,1)} %refs_7_.1) | copy-start | bytes 3145732
  3.8 5.2 %collective-permute-start.3 = (bf16[352,1024]{1,0:T(8,128)(2,1)}, bf16[352,1024]{1,0:T(8,128)(2,1)S(1)}, u32[]{:S(2)}, u32[]{:S(2)}) collective-permute-start(bf16[352,1024]{1,0:T(8,128)(2,1)} %bitcast.15), channel_id=1, source_target_pairs={{0,1},{1,0},{2,3},{3,2},{4,5},{5,4},{6,7},{7,6},{8,9},{9,8},{10,11... | collective-permute-start | bytes 2162696 | tf_op jit(solution)/shard_map/ppermute | solution.py:152
  3.8 1.6 %copy-start.6 = (bf16[8,1024]{1,0:T(8,128)(2,1)S(1)}, bf16[8,1024]{1,0:T(8,128)(2,1)}, u32[]{:S(2)}) copy-start(bf16[8,1024]{1,0:T(8,128)(2,1)} %refs_2_.1) | copy-start | bytes 49156
  3.8 1.6 %copy-start.8 = (f32[1024]{0:T(1024)S(1)}, f32[1024]{0:T(1024)}, u32[]{:S(2)}) copy-start(f32[1024]{0:T(1024)} %param.22) | copy-start | bytes 12292
  3.9 1.6 %copy-start.10 = (f32[8,2]{0,1:T(2,128)S(1)}, f32[8,2]{0,1:T(2,128)}, u32[]{:S(2)}) copy-start(f32[8,2]{0,1:T(2,128)} %param.15) | copy-start | bytes 196
  4.9 0.8 %copy-start.7 = (f32[1024]{0:T(1024)S(1)}, f32[1024]{0:T(1024)}, u32[]{:S(2)}) copy-start(f32[1024]{0:T(1024)} %param.18) | copy-start | bytes 12292
  4.9 4.1 %collective-permute-start.4 = (bf16[352,1024]{1,0:T(8,128)(2,1)S(1)}, bf16[352,1024]{1,0:T(8,128)(2,1)S(1)}, u32[]{:S(2)}, u32[]{:S(2)}) collective-permute-start(bf16[352,1024]{1,0:T(8,128)(2,1)S(1)} %copy-done.2), channel_id=1, source_target_pairs={{0,1},{1,0},{2,3},{3,2},{4,5},{5,4},{6,7},{7,6},{8,9},{9,8},{10,11... | collective-permute-start | bytes 2162696 | tf_op jit(solution)/shard_map/ppermute | solution.py:152
  5.3 14.8 %collective-permute-start.9 = (bf16[1024,512]{1,0:T(8,128)(2,1)S(1)}, bf16[1024,512]{1,0:T(8,128)(2,1)S(1)}, u32[]{:S(2)}, u32[]{:S(2)}) collective-permute-start(bf16[1024,512]{1,0:T(8,128)(2,1)S(1)} %copy-done.3), channel_id=1, source_target_pairs={{0,1},{1,0},{2,3},{3,2},{4,5},{5,4},{6,7},{7,6},{8,9},{9,8},{10,11... | collective-permute-start | bytes 3145736 | tf_op jit(solution)/shard_map/ppermute | solution.py:152
  5.5 0.7 %copy-start.9 = (s32[8,2]{0,1:T(2,128)S(1)}, s32[8,2]{0,1:T(2,128)}, u32[]{:S(2)}) copy-start(s32[8,2]{0,1:T(2,128)} %param.14) | copy-start | bytes 196
  6.3 2.7 %copy-start = (bf16[1024,352]{0,1:T(8,128)(2,1)S(1)}, bf16[1024,352]{0,1:T(8,128)(2,1)}, u32[]{:S(2)}) copy-start(bf16[1024,352]{0,1:T(8,128)(2,1)} %param.19) | copy-start | bytes 2162692
  6.3 2.7 %copy-start.1 = (bf16[1024,352]{0,1:T(8,128)(2,1)S(1)}, bf16[1024,352]{0,1:T(8,128)(2,1)}, u32[]{:S(2)}) copy-start(bf16[1024,352]{0,1:T(8,128)(2,1)} %param.20) | copy-start | bytes 2162692
  6.4 4.5 %collective-permute-start.1 = (bf16[16,1024]{1,0:T(8,128)(2,1)S(1)}, bf16[16,1024]{1,0:T(8,128)(2,1)S(1)}, u32[]{:S(2)}, u32[]{:S(2)}) collective-permute-start(bf16[16,1024]{1,0:T(8,128)(2,1)S(1)} %shard_map.150.rows_ref.first_ref), channel_id=1, source_target_pairs={{0,5},{1,4},{2,7},{3,6},{4,1},{5,0},{6,3},{7,2},{8,13},{9,12},{10,... | collective-permute-start | bytes 98312 | tf_op jit(solution)/shard_map/ppermute | solution.py:152
  10.2 2.9 %copy-start.5 = (bf16[64,512]{1,0:T(8,128)(2,1)S(1)}, bf16[64,512]{1,0:T(8,128)(2,1)}, u32[]{:S(2)}) copy-start(bf16[64,512]{1,0:T(8,128)(2,1)} %refs_9_.1) | copy-start | bytes 196612
  10.2 3.5 %collective-permute-start.6 = (bf16[16,1152]{1,0:T(8,128)(2,1)S(1)}, bf16[16,1152]{1,0:T(8,128)(2,1)S(1)}, u32[]{:S(2)}, u32[]{:S(2)}) collective-permute-start(bf16[16,1152]{1,0:T(8,128)(2,1)S(1)} %get-tuple-element.38), channel_id=1, source_target_pairs={{0,3},{1,2},{2,1},{3,0},{4,7},{5,6},{6,5},{7,4},{8,11},{9,10},{10,... | collective-permute-start | bytes 110600 | tf_op jit(solution)/shard_map/ppermute | solution.py:152
  12.1 3.6 %collective-permute-start.5 = (bf16[16,1024]{1,0:T(8,128)(2,1)S(1)}, bf16[16,1024]{1,0:T(8,128)(2,1)S(1)}, u32[]{:S(2)}, u32[]{:S(2)}) collective-permute-start(bf16[16,1024]{1,0:T(8,128)(2,1)S(1)} %get-tuple-element.33), channel_id=1, source_target_pairs={{0,3},{1,2},{2,1},{3,0},{4,7},{5,6},{6,5},{7,4},{8,11},{9,10},{10,... | collective-permute-start | bytes 98312 | tf_op jit(solution)/shard_map/ppermute | solution.py:152
  13.1 6.2 %collective-permute-start.10 = (bf16[64,512]{1,0:T(8,128)(2,1)S(1)}, bf16[64,512]{1,0:T(8,128)(2,1)S(1)}, u32[]{:S(2)}, u32[]{:S(2)}) collective-permute-start(bf16[64,512]{1,0:T(8,128)(2,1)S(1)} %copy-done.5), channel_id=1, source_target_pairs={{0,1},{1,0},{2,3},{3,2},{4,5},{5,4},{6,7},{7,6},{8,9},{9,8},{10,11... | collective-permute-start | bytes 196616 | tf_op jit(solution)/shard_map/ppermute | solution.py:152
  13.7 5.3 %collective-permute-start.7 = (bf16[16,1152]{1,0:T(8,128)(2,1)S(1)}, bf16[16,1152]{1,0:T(8,128)(2,1)S(1)}, u32[]{:S(2)}, u32[]{:S(2)}) collective-permute-start(bf16[16,1152]{1,0:T(8,128)(2,1)S(1)} %get-tuple-element.43), channel_id=1, source_target_pairs={{0,5},{1,4},{2,7},{3,6},{4,1},{5,0},{6,3},{7,2},{8,13},{9,12},{10,... | collective-permute-start | bytes 110600 | tf_op jit(solution)/shard_map/ppermute | solution.py:152
  15.7 3.4 %copy-start.11 = (s32[64]{0:T(128)S(1)}, s32[64]{0:T(128)}, u32[]{:S(2)}) copy-start(s32[64]{0:T(128)} %param.16) | copy-start | bytes 772
  15.7 3.4 %copy-start.12 = (s32[64]{0:T(128)S(1)}, s32[64]{0:T(128)}, u32[]{:S(2)}) copy-start(s32[64]{0:T(128)} %param.17) | copy-start | bytes 772
  15.7 4.4 %copy-start.4 = (bf16[1024,64]{0,1:T(8,128)(2,1)S(1)}, bf16[1024,64]{0,1:T(8,128)(2,1)}, u32[]{:S(2)}) copy-start(bf16[1024,64]{0,1:T(8,128)(2,1)} %param.24) | copy-start | bytes 393220
  15.7 4.3 %collective-permute-start.8 = (bf16[16,1024]{1,0:T(8,128)(2,1)S(1)}, bf16[16,1024]{1,0:T(8,128)(2,1)S(1)}, u32[]{:S(2)}, u32[]{:S(2)}) collective-permute-start(bf16[16,1024]{1,0:T(8,128)(2,1)S(1)} %get-tuple-element.48), channel_id=1, source_target_pairs={{0,5},{1,4},{2,7},{3,6},{4,1},{5,0},{6,3},{7,2},{8,13},{9,12},{10,... | collective-permute-start | bytes 98312 | tf_op jit(solution)/shard_map/ppermute | solution.py:152
  21.0 3.9 %collective-permute-start.11 = (f32[8,32]{1,0:T(8,128)S(1)}, f32[8,32]{1,0:T(8,128)S(1)}, u32[]{:S(2)}, u32[]{:S(2)}) collective-permute-start(f32[8,32]{1,0:T(8,128)S(1)} %shard_map.156.one_ref), channel_id=1, source_target_pairs={{0,5},{1,4},{2,7},{3,6},{4,1},{5,0},{6,3},{7,2},{8,13},{9,12},{10,... | collective-permute-start | bytes 3080 | tf_op jit(solution)/shard_map/ppermute | solution.py:152
  24.9 3.1 %collective-permute-start.12 = (f32[8,32]{1,0:T(8,128)S(1)}, f32[8,32]{1,0:T(8,128)S(1)}, u32[]{:S(2)}, u32[]{:S(2)}) collective-permute-start(f32[8,32]{1,0:T(8,128)S(1)} %shard_map.157.one_ref), channel_id=1, source_target_pairs={{0,3},{1,2},{2,1},{3,0},{4,7},{5,6},{6,5},{7,4},{8,11},{9,10},{10,... | collective-permute-start | bytes 3080 | tf_op jit(solution)/shard_map/ppermute | solution.py:152
  28.0 1.8 %collective-permute-start.13 = (f32[8,32]{1,0:T(8,128)S(1)}, f32[8,32]{1,0:T(8,128)S(1)}, u32[]{:S(2)}, u32[]{:S(2)}) collective-permute-start(f32[8,32]{1,0:T(8,128)S(1)} %shard_map.158.refs_0_), channel_id=1, source_target_pairs={{0,1},{1,0},{2,3},{3,2},{4,5},{5,4},{6,7},{7,6},{8,9},{9,8},{10,11... | collective-permute-start | bytes 3080 | tf_op jit(solution)/shard_map/ppermute | solution.py:152

commit v12 on v10

--- a/solution.py
+++ b/solution.py
@@ -9,7 +9,7 @@
 
 SPLIT = 4
 SEQS = 16
-ROUND_FLOPS = 16 << 30
+ROUND_FLOPS = 32 << 30
 
 
 epsilon = 1e-06
@@ -183,8 +183,8 @@
 
 
 def early_kernel(tok_rows, bits, *refs):
-    (ids_ref, gates_ref), (mixing_ref,) = refs[0:2], refs[7:8]
-    for in_ref, out_ref in zip(refs[2:7], refs[8:13]):
+    (ids_ref, gates_ref), (mixing_ref,) = refs[0:2], refs[5:6]
+    for in_ref, out_ref in zip(refs[2:5], refs[6:9]):
         out_ref[...] = in_ref[...]
     my_index, parity, half = places(tok_rows, bits)
     experts = gates_ref.shape[0]
@@ -438,23 +438,19 @@
 
     flags = call(flags_kernel, array(jnp.int32, 8, 128), flops=ROUND_FLOPS)
     flags, sent_d = lax.optimization_barrier((flags, w_down))
-    mixing, held_rows, gain, last_gain, held_targets, held_seq = call(
+    mixing, held_rows, gain, last_gain = call(
         functools.partial(early_kernel, tok_rows, bits),
         [
             array(jnp.float32, 2 * tok_rows, 128),
             array(jnp.bfloat16, tok_rows, features),
             array(jnp.float32, 1, features),
             array(jnp.float32, 1, features),
-            array(jnp.int32, 1, 2 * half),
-            array(jnp.int32, 1, 2 * half),
         ],
         expert_ids.T,
         gate_weights.T,
         hidden_in,
         moe_gain[None],
         final_gain[None],
-        targets[None],
-        seq_ids[None],
     )
     first = call(
         functools.partial(order_kernel, near_bit),
@@ -490,8 +486,9 @@
         )
         totals.append(total)
         sent.append(piece)
-    sent[0], late_seq = lax.optimization_barrier((sent[0], held_seq))
-    sent[1], late_targets = lax.optimization_barrier((sent[1], held_targets))
+    sent[0], late_seq, late_targets = lax.optimization_barrier(
+        (sent[0], seq_ids[None], targets[None])
+    )
     arrived = [exchange(piece, far_mask) for piece in sent]
 
     vocabulary = [adapter_down.T, head_weight, exchange(head_weight, 1)]

time: 30.6 us -> 30.7 us (level)
  starting transfers between devices: 16.1 us -> 14.1 us
  waiting for transfers between devices: 6.52 us -> 7.89 us
  local copies, waits for them, and re-layouts: 2.09 us -> 2.76 us
    ppermute x14, starting transfers between devices: 16.1 us -> 14.1 us  [exchange(): lax.ppermute(values, 'tensor', [(i, i ^ mask) for i in range(devices)])]
    ppermute x14, waiting for transfers between devices: 6.52 us -> 7.89 us  [exchange(): lax.ppermute(values, 'tensor', [(i, i ^ mask) for i in range(devices)])]
    unnamed x26, local copies, waits for them, and re-layouts: 2.09 us -> 2.76 us
where the time goes in v12:
time: 30.7 us; the launch traced here: 30.5 us
  starting transfers between devices  14.1 us (46%)
  waiting for transfers between devices  7.89 us (26%)
  Pallas kernels  5.01 us (16%)
  local copies, waits for them, and re-layouts  2.76 us (9%)
  between operations  0.75 us (2%)
    ppermute x14, starting transfers between devices, exchange(): lax.ppermute(values, 'tensor', [(i, i ^ mask) for i in range(devices)])  14.1 us
    ppermute x14, waiting for transfers between devices, exchange(): lax.ppermute(values, 'tensor', [(i, i ^ mask) for i in range(devices)])  7.89 us
    pallas_call x12, Pallas kernels, call(): pl.pallas_call(kernel, out_shape=shapes, compiler_params=pltpu.CompilerPa...  5.01 us
    unnamed x26, local copies, waits for them, and re-layouts  2.76 us
  transfers between devices with their start and end apart: 14, of which 5 were waited for; matrix products, arithmetic and copies ran while one was open for 0% of the time, Pallas kernels for 11%

profile of v12, /device:TPU:0, one launch (start us, length us, event | category | flops | bytes accessed | tf_op | source)
XLA Modules:
  0.0 30.5 jit_solution(3354011717324379038)
XLA Ops:
  0.6 2.5 %collective-permute-start = (bf16[8,1024]{1,0:T(8,128)(2,1)}, bf16[8,1024]{1,0:T(8,128)(2,1)S(1)}, u32[]{:S(2)}, u32[]{:S(2)}) collective-permute-start(bf16[8,1024]{1,0:T(8,128)(2,1)} %refs_2_.1), channel_id=1, source_target_pairs={{0,3},{1,2},{2,1},{3,0},{4,7},{5,6},{6,5},{7,4},{8,11},{9,10},{10,... | collective-permute-start | bytes 49160 | tf_op jit(solution)/shard_map/ppermute | solution.py:152
  3.2 0.7 %collective-permute-start.1 = (bf16[352,1024]{1,0:T(8,128)(2,1)}, bf16[352,1024]{1,0:T(8,128)(2,1)S(1)}, u32[]{:S(2)}, u32[]{:S(2)}) collective-permute-start(bf16[352,1024]{1,0:T(8,128)(2,1)} %bitcast.12), channel_id=1, source_target_pairs={{0,1},{1,0},{2,3},{3,2},{4,5},{5,4},{6,7},{7,6},{8,9},{9,8},{10,11... | collective-permute-start | bytes 2162696 | tf_op jit(solution)/shard_map/ppermute | solution.py:152
  3.8 0.0 collective-permute-start.2
  3.9 1.1 %copy-done.3 = bf16[352,1024]{1,0:T(8,128)(2,1)S(1)} copy-done((bf16[352,1024]{1,0:T(8,128)(2,1)S(1)}, bf16[352,1024]{1,0:T(8,128)(2,1)}, u32[]{:S(2)}) %copy-start.3) | copy-done | bytes 720920
  5.0 0.3 %copy-done = bf16[1024,512]{1,0:T(8,128)(2,1)S(1)} copy-done((bf16[1024,512]{1,0:T(8,128)(2,1)S(1)}, bf16[1024,512]{1,0:T(8,128)(2,1)}, u32[]{:S(2)}) %copy-start) | copy-done | bytes 1048600
  5.3 0.2 collective-permute-start.8
  5.5 0.2 copy-done.7
  5.7 0.4 %copy-done.9 = s32[8,2]{0,1:T(2,128)S(1)} copy-done((s32[8,2]{0,1:T(2,128)S(1)}, s32[8,2]{0,1:T(2,128)}, u32[]{:S(2)}) %copy-start.9) | copy-done | bytes 88
  6.1 0.2 shard_map.149
  6.3 0.0 copy-start.1
  6.3 0.0 copy-start.2
  6.4 2.6 %collective-permute-start.5 = (bf16[16,1024]{1,0:T(8,128)(2,1)S(1)}, bf16[16,1024]{1,0:T(8,128)(2,1)S(1)}, u32[]{:S(2)}, u32[]{:S(2)}) collective-permute-start(bf16[16,1024]{1,0:T(8,128)(2,1)S(1)} %shard_map.150.rows_ref.first_ref), channel_id=1, source_target_pairs={{0,5},{1,4},{2,7},{3,6},{4,1},{5,0},{6,3},{7,2},{8,13},{9,12},{10,... | collective-permute-start | bytes 98312 | tf_op jit(solution)/shard_map/ppermute | solution.py:152
  9.0 1.1 %shard_map.151 = (f32[16,1152]{1,0:T(8,128)S(1)}, bf16[16,1152]{1,0:T(8,128)(2,1)S(1)}) custom-call(bf16[16,1024]{1,0:T(8,128)(2,1)S(1)} %shard_map.150.rows_ref.first_ref, f32[1,1024]{1,0:T(1,128)S(1)} %get-tuple-element.29.gain_ref, bf16[352,1024]{1,0:T(8,128)(2,1)S(1)} %collective-permute-done.1.refs_0_, ...), custom_call_target="tpu_custom_call" | custom-call | flops 69206016 | bytes 4370432 | tf_op jit(solution)/shard_map/pallas_call | solution.py:406
  10.2 0.8 %collective-permute-start.4 = (bf16[16,1152]{1,0:T(8,128)(2,1)S(1)}, bf16[16,1152]{1,0:T(8,128)(2,1)S(1)}, u32[]{:S(2)}, u32[]{:S(2)}) collective-permute-start(bf16[16,1152]{1,0:T(8,128)(2,1)S(1)} %get-tuple-element.33), channel_id=1, source_target_pairs={{0,3},{1,2},{2,1},{3,0},{4,7},{5,6},{6,5},{7,4},{8,11},{9,10},{10,... | collective-permute-start | bytes 110600 | tf_op jit(solution)/shard_map/ppermute | solution.py:152
  10.9 1.1 %shard_map.153 = (f32[16,1024]{1,0:T(8,128)S(1)}, bf16[16,1024]{1,0:T(8,128)(2,1)S(1)}) custom-call(bf16[16,1024]{1,0:T(8,128)(2,1)S(1)} %collective-permute-done.5.rows_ref.second_ref, f32[1,1024]{1,0:T(1,128)S(1)} %get-tuple-element.29.gain_ref, bf16[352,1024]{1,0:T(8,128)(2,1)S(1)} %collective-permute-done.1.refs_0_, ...), custom_call_target="tpu_custom_call" | custom-call | flops 69206016 | bytes 4362240 | tf_op jit(solution)/shard_map/pallas_call | solution.py:406
  12.1 1.0 %collective-permute-start.6 = (bf16[16,1024]{1,0:T(8,128)(2,1)S(1)}, bf16[16,1024]{1,0:T(8,128)(2,1)S(1)}, u32[]{:S(2)}, u32[]{:S(2)}) collective-permute-start(bf16[16,1024]{1,0:T(8,128)(2,1)S(1)} %get-tuple-element.39), channel_id=1, source_target_pairs={{0,3},{1,2},{2,1},{3,0},{4,7},{5,6},{6,5},{7,4},{8,11},{9,10},{10,... | collective-permute-start | bytes 98312 | tf_op jit(solution)/shard_map/ppermute | solution.py:152
  13.1 0.2 collective-permute-start.9
  13.3 0.4 %collective-permute-done.4.arrived_ref = bf16[16,1152]{1,0:T(8,128)(2,1)S(1)} collective-permute-done((bf16[16,1152]{1,0:T(8,128)(2,1)S(1)}, bf16[16,1152]{1,0:T(8,128)(2,1)S(1)}, u32[]{:S(2)}, u32[]{:S(2)}) %collective-permute-start.4) | collective-permute-done | bytes 36896 | tf_op jit(solution)/shard_map/ppermute | solution.py:152
  13.7 2.0 %collective-permute-start.7 = (bf16[16,1152]{1,0:T(8,128)(2,1)S(1)}, bf16[16,1152]{1,0:T(8,128)(2,1)S(1)}, u32[]{:S(2)}, u32[]{:S(2)}) collective-permute-start(bf16[16,1152]{1,0:T(8,128)(2,1)S(1)} %get-tuple-element.41), channel_id=1, source_target_pairs={{0,5},{1,4},{2,7},{3,6},{4,1},{5,0},{6,3},{7,2},{8,13},{9,12},{10,... | collective-permute-start | bytes 110600 | tf_op jit(solution)/shard_map/ppermute | solution.py:152
  15.7 2.1 %collective-permute-start.10 = (bf16[16,1024]{1,0:T(8,128)(2,1)S(1)}, bf16[16,1024]{1,0:T(8,128)(2,1)S(1)}, u32[]{:S(2)}, u32[]{:S(2)}) collective-permute-start(bf16[16,1024]{1,0:T(8,128)(2,1)S(1)} %get-tuple-element.46), channel_id=1, source_target_pairs={{0,5},{1,4},{2,7},{3,6},{4,1},{5,0},{6,3},{7,2},{8,13},{9,12},{10,... | collective-permute-start | bytes 98312 | tf_op jit(solution)/shard_map/ppermute | solution.py:152
  17.8 1.3 %collective-permute-done.7.arrived_ref = bf16[16,1152]{1,0:T(8,128)(2,1)S(1)} collective-permute-done((bf16[16,1152]{1,0:T(8,128)(2,1)S(1)}, bf16[16,1152]{1,0:T(8,128)(2,1)S(1)}, u32[]{:S(2)}, u32[]{:S(2)}) %collective-permute-start.7) | collective-permute-done | bytes 36896 | tf_op jit(solution)/shard_map/ppermute | solution.py:152
  19.1 0.6 %copy-done.11 = s32[64]{0:T(128)S(1)} copy-done((s32[64]{0:T(128)S(1)}, s32[64]{0:T(128)}, u32[]{:S(2)}) %copy-start.11) | copy-done | bytes 280
  19.7 0.0 copy-done.12
  19.7 0.9 %shard_map.155 = (f32[3,32,128]{2,1,0:T(8,128)S(1)}, f32[16,128]{1,0:T(8,128)S(1)}, f32[16,1024]{1,0:T(8,128)S(1)}, f32[16,128]{1,0:T(8,128)S(1)}) custom-call(s32[1,64]{1,0:T(1,128)S(1)} %bitcast.24, s32[1,64]{1,0:T(1,128)S(1)} %bitcast.25, bf16[16,1024]{1,0:T(8,128)(2,1)S(1)} %shard_map.150.rows_ref.first_ref, ...), custom_call_target="tpu_custom_call" | custom-call | bytes 2605568 | tf_op jit(solution)/shard_map/pallas_call | solution.py:406
  20.6 0.8 %shard_map.156.one_ref = f32[8,32]{1,0:T(8,128)S(1)} custom-call(f32[16,128]{1,0:T(8,128)S(1)} %get-tuple-element.43.refs_0_, f32[16,1024]{1,0:T(8,128)S(1)} %get-tuple-element.44.refs_1_, f32[16,128]{1,0:T(8,128)S(1)} %get-tuple-element.45.refs_2_, bf16[16,1024]{1,0:T(8,128)(2,1)S(1)} %collective-permute-done.10.refs_3_, ...), custom_call_target="tpu_custom_call" | custom-call | flops 67108864 | bytes 2527232 | tf_op jit(solution)/shard_map/pallas_call | solution.py:406
  21.5 1.5 %collective-permute-start.11 = (f32[8,32]{1,0:T(8,128)S(1)}, f32[8,32]{1,0:T(8,128)S(1)}, u32[]{:S(2)}, u32[]{:S(2)}) collective-permute-start(f32[8,32]{1,0:T(8,128)S(1)} %shard_map.156.one_ref), channel_id=1, source_target_pairs={{0,5},{1,4},{2,7},{3,6},{4,1},{5,0},{6,3},{7,2},{8,13},{9,12},{10,... | collective-permute-start | bytes 3080 | tf_op jit(solution)/shard_map/ppermute | solution.py:152
  22.9 2.5 %collective-permute-done.11.two_ref = f32[8,32]{1,0:T(8,128)S(1)} collective-permute-done((f32[8,32]{1,0:T(8,128)S(1)}, f32[8,32]{1,0:T(8,128)S(1)}, u32[]{:S(2)}, u32[]{:S(2)}) %collective-permute-start.11) | collective-permute-done | bytes 1056 | tf_op jit(solution)/shard_map/ppermute | solution.py:152
  25.4 0.3 %collective-permute-start.12 = (f32[8,32]{1,0:T(8,128)S(1)}, f32[8,32]{1,0:T(8,128)S(1)}, u32[]{:S(2)}, u32[]{:S(2)}) collective-permute-start(f32[8,32]{1,0:T(8,128)S(1)} %shard_map.157.one_ref), channel_id=1, source_target_pairs={{0,3},{1,2},{2,1},{3,0},{4,7},{5,6},{6,5},{7,4},{8,11},{9,10},{10,... | collective-permute-start | bytes 3080 | tf_op jit(solution)/shard_map/ppermute | solution.py:152
  25.7 2.8 %collective-permute-done.12.two_ref = f32[8,32]{1,0:T(8,128)S(1)} collective-permute-done((f32[8,32]{1,0:T(8,128)S(1)}, f32[8,32]{1,0:T(8,128)S(1)}, u32[]{:S(2)}, u32[]{:S(2)}) %collective-permute-start.12) | collective-permute-done | bytes 1056 | tf_op jit(solution)/shard_map/ppermute | solution.py:152
  28.5 0.3 %collective-permute-start.13 = (f32[8,32]{1,0:T(8,128)S(1)}, f32[8,32]{1,0:T(8,128)S(1)}, u32[]{:S(2)}, u32[]{:S(2)}) collective-permute-start(f32[8,32]{1,0:T(8,128)S(1)} %shard_map.158.refs_0_), channel_id=1, source_target_pairs={{0,1},{1,0},{2,3},{3,2},{4,5},{5,4},{6,7},{7,6},{8,9},{9,8},{10,11... | collective-permute-start | bytes 3080 | tf_op jit(solution)/shard_map/ppermute | solution.py:152
  28.9 0.9 %collective-permute-done.13.refs_1_ = f32[8,32]{1,0:T(8,128)S(1)} collective-permute-done((f32[8,32]{1,0:T(8,128)S(1)}, f32[8,32]{1,0:T(8,128)S(1)}, u32[]{:S(2)}, u32[]{:S(2)}) %collective-permute-start.13) | collective-permute-done | bytes 1056 | tf_op jit(solution)/shard_map/ppermute | solution.py:152
  29.8 0.7 %shard_map.159 = (f32[1,8]{1,0:T(1,128)}, f32[1,8]{1,0:T(1,128)}, f32[1,16]{1,0:T(1,128)}) custom-call(f32[8,32]{1,0:T(8,128)S(1)} %shard_map.158.refs_0_, f32[8,32]{1,0:T(8,128)S(1)} %collective-permute-done.13.refs_1_, f32[3,32,128]{2,1,0:T(8,128)S(1)} %get-tuple-element.47.refs_5_.refs_2_), custom_call_target="tpu_custom_call" | custom-call | bytes 51200 | tf_op jit(solution)/shard_map/pallas_call | solution.py:406
  (34 shorter events, 0.2 us)
Async XLA Ops:
  0.6 5.7 %collective-permute-start = (bf16[8,1024]{1,0:T(8,128)(2,1)}, bf16[8,1024]{1,0:T(8,128)(2,1)S(1)}, u32[]{:S(2)}, u32[]{:S(2)}) collective-permute-start(bf16[8,1024]{1,0:T(8,128)(2,1)} %refs_2_.1), channel_id=1, source_target_pairs={{0,3},{1,2},{2,1},{3,0},{4,7},{5,6},{6,5},{7,4},{8,11},{9,10},{10,... | collective-permute-start | bytes 49160 | tf_op jit(solution)/shard_map/ppermute | solution.py:152
  3.2 5.8 %collective-permute-start.1 = (bf16[352,1024]{1,0:T(8,128)(2,1)}, bf16[352,1024]{1,0:T(8,128)(2,1)S(1)}, u32[]{:S(2)}, u32[]{:S(2)}) collective-permute-start(bf16[352,1024]{1,0:T(8,128)(2,1)} %bitcast.12), channel_id=1, source_target_pairs={{0,1},{1,0},{2,3},{3,2},{4,5},{5,4},{6,7},{7,6},{8,9},{9,8},{10,11... | collective-permute-start | bytes 2162696 | tf_op jit(solution)/shard_map/ppermute | solution.py:152
  3.8 1.1 %copy-start.3 = (bf16[352,1024]{1,0:T(8,128)(2,1)S(1)}, bf16[352,1024]{1,0:T(8,128)(2,1)}, u32[]{:S(2)}) copy-start(bf16[352,1024]{1,0:T(8,128)(2,1)} %refs_5_.3) | copy-start | bytes 2162692
  3.8 1.4 %copy-start = (bf16[1024,512]{1,0:T(8,128)(2,1)S(1)}, bf16[1024,512]{1,0:T(8,128)(2,1)}, u32[]{:S(2)}) copy-start(bf16[1024,512]{1,0:T(8,128)(2,1)} %refs_7_.1) | copy-start | bytes 3145732
  3.8 5.2 %collective-permute-start.2 = (bf16[352,1024]{1,0:T(8,128)(2,1)}, bf16[352,1024]{1,0:T(8,128)(2,1)S(1)}, u32[]{:S(2)}, u32[]{:S(2)}) collective-permute-start(bf16[352,1024]{1,0:T(8,128)(2,1)} %bitcast.15), channel_id=1, source_target_pairs={{0,1},{1,0},{2,3},{3,2},{4,5},{5,4},{6,7},{7,6},{8,9},{9,8},{10,11... | collective-permute-start | bytes 2162696 | tf_op jit(solution)/shard_map/ppermute | solution.py:152
  3.8 1.6 %copy-start.6 = (bf16[8,1024]{1,0:T(8,128)(2,1)S(1)}, bf16[8,1024]{1,0:T(8,128)(2,1)}, u32[]{:S(2)}) copy-start(bf16[8,1024]{1,0:T(8,128)(2,1)} %refs_2_.1) | copy-start | bytes 49156
  3.8 1.6 %copy-start.8 = (f32[1024]{0:T(1024)S(1)}, f32[1024]{0:T(1024)}, u32[]{:S(2)}) copy-start(f32[1024]{0:T(1024)} %param.22) | copy-start | bytes 12292
  3.9 1.6 %copy-start.10 = (f32[8,2]{0,1:T(2,128)S(1)}, f32[8,2]{0,1:T(2,128)}, u32[]{:S(2)}) copy-start(f32[8,2]{0,1:T(2,128)} %param.15) | copy-start | bytes 196
  4.9 0.8 %copy-start.7 = (f32[1024]{0:T(1024)S(1)}, f32[1024]{0:T(1024)}, u32[]{:S(2)}) copy-start(f32[1024]{0:T(1024)} %param.18) | copy-start | bytes 12292
  4.9 4.1 %collective-permute-start.3 = (bf16[352,1024]{1,0:T(8,128)(2,1)S(1)}, bf16[352,1024]{1,0:T(8,128)(2,1)S(1)}, u32[]{:S(2)}, u32[]{:S(2)}) collective-permute-start(bf16[352,1024]{1,0:T(8,128)(2,1)S(1)} %copy-done.3), channel_id=1, source_target_pairs={{0,1},{1,0},{2,3},{3,2},{4,5},{5,4},{6,7},{7,6},{8,9},{9,8},{10,11... | collective-permute-start | bytes 2162696 | tf_op jit(solution)/shard_map/ppermute | solution.py:152
  5.3 13.8 %collective-permute-start.8 = (bf16[1024,512]{1,0:T(8,128)(2,1)S(1)}, bf16[1024,512]{1,0:T(8,128)(2,1)S(1)}, u32[]{:S(2)}, u32[]{:S(2)}) collective-permute-start(bf16[1024,512]{1,0:T(8,128)(2,1)S(1)} %copy-done), channel_id=1, source_target_pairs={{0,1},{1,0},{2,3},{3,2},{4,5},{5,4},{6,7},{7,6},{8,9},{9,8},{10,11... | collective-permute-start | bytes 3145736 | tf_op jit(solution)/shard_map/ppermute | solution.py:152
  5.5 0.7 %copy-start.9 = (s32[8,2]{0,1:T(2,128)S(1)}, s32[8,2]{0,1:T(2,128)}, u32[]{:S(2)}) copy-start(s32[8,2]{0,1:T(2,128)} %param.14) | copy-start | bytes 196
  6.3 2.7 %copy-start.1 = (bf16[1024,352]{0,1:T(8,128)(2,1)S(1)}, bf16[1024,352]{0,1:T(8,128)(2,1)}, u32[]{:S(2)}) copy-start(bf16[1024,352]{0,1:T(8,128)(2,1)} %param.19) | copy-start | bytes 2162692
  6.3 2.7 %copy-start.2 = (bf16[1024,352]{0,1:T(8,128)(2,1)S(1)}, bf16[1024,352]{0,1:T(8,128)(2,1)}, u32[]{:S(2)}) copy-start(bf16[1024,352]{0,1:T(8,128)(2,1)} %param.20) | copy-start | bytes 2162692
  6.4 4.5 %collective-permute-start.5 = (bf16[16,1024]{1,0:T(8,128)(2,1)S(1)}, bf16[16,1024]{1,0:T(8,128)(2,1)S(1)}, u32[]{:S(2)}, u32[]{:S(2)}) collective-permute-start(bf16[16,1024]{1,0:T(8,128)(2,1)S(1)} %shard_map.150.rows_ref.first_ref), channel_id=1, source_target_pairs={{0,5},{1,4},{2,7},{3,6},{4,1},{5,0},{6,3},{7,2},{8,13},{9,12},{10,... | collective-permute-start | bytes 98312 | tf_op jit(solution)/shard_map/ppermute | solution.py:152
  10.2 2.9 %copy-start.5 = (bf16[64,512]{1,0:T(8,128)(2,1)S(1)}, bf16[64,512]{1,0:T(8,128)(2,1)}, u32[]{:S(2)}) copy-start(bf16[64,512]{1,0:T(8,128)(2,1)} %refs_9_.1) | copy-start | bytes 196612
  10.2 3.5 %collective-permute-start.4 = (bf16[16,1152]{1,0:T(8,128)(2,1)S(1)}, bf16[16,1152]{1,0:T(8,128)(2,1)S(1)}, u32[]{:S(2)}, u32[]{:S(2)}) collective-permute-start(bf16[16,1152]{1,0:T(8,128)(2,1)S(1)} %get-tuple-element.33), channel_id=1, source_target_pairs={{0,3},{1,2},{2,1},{3,0},{4,7},{5,6},{6,5},{7,4},{8,11},{9,10},{10,... | collective-permute-start | bytes 110600 | tf_op jit(solution)/shard_map/ppermute | solution.py:152
  12.1 3.6 %collective-permute-start.6 = (bf16[16,1024]{1,0:T(8,128)(2,1)S(1)}, bf16[16,1024]{1,0:T(8,128)(2,1)S(1)}, u32[]{:S(2)}, u32[]{:S(2)}) collective-permute-start(bf16[16,1024]{1,0:T(8,128)(2,1)S(1)} %get-tuple-element.39), channel_id=1, source_target_pairs={{0,3},{1,2},{2,1},{3,0},{4,7},{5,6},{6,5},{7,4},{8,11},{9,10},{10,... | collective-permute-start | bytes 98312 | tf_op jit(solution)/shard_map/ppermute | solution.py:152
  13.1 4.7 %collective-permute-start.9 = (bf16[64,512]{1,0:T(8,128)(2,1)S(1)}, bf16[64,512]{1,0:T(8,128)(2,1)S(1)}, u32[]{:S(2)}, u32[]{:S(2)}) collective-permute-start(bf16[64,512]{1,0:T(8,128)(2,1)S(1)} %copy-done.5), channel_id=1, source_target_pairs={{0,1},{1,0},{2,3},{3,2},{4,5},{5,4},{6,7},{7,6},{8,9},{9,8},{10,11... | collective-permute-start | bytes 196616 | tf_op jit(solution)/shard_map/ppermute | solution.py:152
  13.7 5.3 %collective-permute-start.7 = (bf16[16,1152]{1,0:T(8,128)(2,1)S(1)}, bf16[16,1152]{1,0:T(8,128)(2,1)S(1)}, u32[]{:S(2)}, u32[]{:S(2)}) collective-permute-start(bf16[16,1152]{1,0:T(8,128)(2,1)S(1)} %get-tuple-element.41), channel_id=1, source_target_pairs={{0,5},{1,4},{2,7},{3,6},{4,1},{5,0},{6,3},{7,2},{8,13},{9,12},{10,... | collective-permute-start | bytes 110600 | tf_op jit(solution)/shard_map/ppermute | solution.py:152
  15.7 3.4 %copy-start.4 = (bf16[1024,64]{0,1:T(8,128)(2,1)S(1)}, bf16[1024,64]{0,1:T(8,128)(2,1)}, u32[]{:S(2)}) copy-start(bf16[1024,64]{0,1:T(8,128)(2,1)} %param.24) | copy-start | bytes 393220
  15.7 4.9 %collective-permute-start.10 = (bf16[16,1024]{1,0:T(8,128)(2,1)S(1)}, bf16[16,1024]{1,0:T(8,128)(2,1)S(1)}, u32[]{:S(2)}, u32[]{:S(2)}) collective-permute-start(bf16[16,1024]{1,0:T(8,128)(2,1)S(1)} %get-tuple-element.46), channel_id=1, source_target_pairs={{0,5},{1,4},{2,7},{3,6},{4,1},{5,0},{6,3},{7,2},{8,13},{9,12},{10,... | collective-permute-start | bytes 98312 | tf_op jit(solution)/shard_map/ppermute | solution.py:152
  19.1 0.7 %copy-start.11 = (s32[64]{0:T(128)S(1)}, s32[64]{0:T(128)}, u32[]{:S(2)}) copy-start(s32[64]{0:T(128)} %param.16) | copy-start | bytes 772
  19.1 0.7 %copy-start.12 = (s32[64]{0:T(128)S(1)}, s32[64]{0:T(128)}, u32[]{:S(2)}) copy-start(s32[64]{0:T(128)} %param.17) | copy-start | bytes 772
  21.5 3.9 %collective-permute-start.11 = (f32[8,32]{1,0:T(8,128)S(1)}, f32[8,32]{1,0:T(8,128)S(1)}, u32[]{:S(2)}, u32[]{:S(2)}) collective-permute-start(f32[8,32]{1,0:T(8,128)S(1)} %shard_map.156.one_ref), channel_id=1, source_target_pairs={{0,5},{1,4},{2,7},{3,6},{4,1},{5,0},{6,3},{7,2},{8,13},{9,12},{10,... | collective-permute-start | bytes 3080 | tf_op jit(solution)/shard_map/ppermute | solution.py:152
  25.4 3.1 %collective-permute-start.12 = (f32[8,32]{1,0:T(8,128)S(1)}, f32[8,32]{1,0:T(8,128)S(1)}, u32[]{:S(2)}, u32[]{:S(2)}) collective-permute-start(f32[8,32]{1,0:T(8,128)S(1)} %shard_map.157.one_ref), channel_id=1, source_target_pairs={{0,3},{1,2},{2,1},{3,0},{4,7},{5,6},{6,5},{7,4},{8,11},{9,10},{10,... | collective-permute-start | bytes 3080 | tf_op jit(solution)/shard_map/ppermute | solution.py:152
  28.5 1.2 %collective-permute-start.13 = (f32[8,32]{1,0:T(8,128)S(1)}, f32[8,32]{1,0:T(8,128)S(1)}, u32[]{:S(2)}, u32[]{:S(2)}) collective-permute-start(f32[8,32]{1,0:T(8,128)S(1)} %shard_map.158.refs_0_), channel_id=1, source_target_pairs={{0,1},{1,0},{2,3},{3,2},{4,5},{5,4},{6,7},{7,6},{8,9},{9,8},{10,11... | collective-permute-start | bytes 3080 | tf_op jit(solution)/shard_map/ppermute | solution.py:152
